TPU v7x, 512 devices: a whole 4x8x8 slice. The times are simulated.
512 devices in a mesh: roll: 128 (over y, z, core), rep: 4 (over x).
Axes of the slice: x: 4, y: 8, z: 8, core: 2. Of those that a mesh axis runs over, the one named last changes fastest.
Arguments:
- rollout: bfloat16 [1048576, 256], P(('roll', 'rep')), may hold values from -7.8 to 7.8
- demo: bfloat16 [262144, 256], P('roll'), may hold values from -6 to 6
- projection: bfloat16 [256, 256], replicated, may hold values from -0.375 to 0.375
- location: int32 [2048], replicated, may hold values from 0 to 2047, as said below
- pair_block: int32 [8192, 8], P(('roll', 'rep')), may hold values from 0 to 2047, as said below
- pair_count: int32 [8192], P(('roll', 'rep')), may hold values from 1 to 8, as said below
Outputs:
- reward: float32 [1048576], P(('roll', 'rep'))
- rollout_potential: float32 [1048576], P(('roll', 'rep'))
- demo_potential: float32 [262144], P('roll')
Inputs may be any that keep to these rules, and one draw needn't show every extreme that they name: location is a permutation; demonstration block d is stored block location[d], held by roll index location[d] // 16. `pair_block`: among the slots in use of the 16 rollout blocks of one device, at most 1 name blocks stored on any one roll index, and some device reaches 1. `pair_count`: on one roll index every rollout block uses all 8 slots.
All inputs are finite; a program needn't handle non-finite values.
Results may differ from a plain program's by a relative error of at most 0.0024.
Values may be sent and summed in bfloat16 or wider, within the bound.
No kernel may reach another device: no remote copies, remote signals or barrier semaphores. Data moves between devices by JAX's collectives and lax.ppermute only.
A program may use at most 128 MiB of HBM per device.

v0:
```python
import jax
import jax.numpy as jnp
from jax import lax
from jax.sharding import PartitionSpec as P

ITERS = 2


EPSILON = 0.02
UNMATCHED = 2.0
SLACK = -100.0
NEGLIGIBLE = -1e30


def joined(value, axis, join):
    pieces = jax.tree.map(lambda part: lax.all_gather(part, axis), value)
    head = jax.tree.map(lambda part: part[0], pieces)
    tail = jax.tree.map(lambda part: part[1:], pieces)
    subtotal, _ = lax.scan(lambda subtotal, share: (join(subtotal, share), None), head, tail)
    return subtotal


def tile_costs(left_codes, right_codes):
    crossed = jnp.einsum(
        "pie,pje->pij", left_codes, right_codes, preferred_element_type=jnp.float32
    )
    norm_left = jnp.einsum(
        "pie,pie->pi", left_codes, left_codes, preferred_element_type=jnp.float32
    )
    norm_right = jnp.einsum(
        "pje,pje->pj", right_codes, right_codes, preferred_element_type=jnp.float32
    )
    return (norm_left[:, :, None] + norm_right[:, None, :] - 2.0 * crossed) / left_codes.shape[2]


def row_part(costs, demo_pot, final):
    scores = (demo_pot[:, None, :] - costs) / EPSILON
    largest = jnp.max(scores, axis=2)
    shifted = jnp.exp(scores - largest[:, :, None])
    summed = jnp.sum(shifted, axis=2)
    row_lse = largest + jnp.log(summed)
    if final:
        return (row_lse, jnp.sum(shifted * costs, axis=2) / summed)
    return (row_lse, None)


def column_part(costs, roll_pot):
    scores = (roll_pot[:, :, None] - costs) / EPSILON
    largest = jnp.max(scores, axis=1)
    return largest + jnp.log(jnp.sum(jnp.exp(scores - largest[:, None, :]), axis=1))


def combine(earlier, later):
    largest = jnp.maximum(earlier[0], later[0])
    return (
        largest,
        earlier[1] * jnp.exp(earlier[0] - largest) + later[1] * jnp.exp(later[0] - largest),
    )


def demo_side(column_lse, wanted, demo_count):
    belongs = (wanted[:, None] == jnp.arange(demo_count, dtype=jnp.int32)[None, :])[:, :, None]
    largest = jnp.max(jnp.where(belongs, column_lse[:, None, :], NEGLIGIBLE), axis=0)
    summed = jnp.sum(
        jnp.where(belongs, jnp.exp(column_lse[:, None, :] - largest[None]), 0.0), axis=0
    )
    largest, summed = joined((largest, summed), "rep", combine)
    highest = jnp.maximum(largest, SLACK)
    log_total = highest + jnp.log(summed * jnp.exp(largest - highest) + jnp.exp(SLACK - highest))
    return -EPSILON * log_total


def rollout_side(row_lse, weighted, home_block, roll_blocks):
    belongs = (home_block[:, None] == jnp.arange(roll_blocks, dtype=jnp.int32)[None, :])[:, :, None]
    spread_out = jnp.where(belongs, row_lse[:, None, :], NEGLIGIBLE)
    largest = jnp.maximum(jnp.max(spread_out, axis=0), SLACK)
    summed = jnp.sum(
        jnp.where(belongs, jnp.exp(row_lse[:, None, :] - largest[None]), 0.0), axis=0
    ) + jnp.exp(SLACK - largest)
    log_total = largest + jnp.log(summed)
    potential = -EPSILON * log_total
    if weighted is None:
        return (potential, None)
    shares = jnp.where(
        belongs, jnp.exp(row_lse[:, None, :] - log_total[None]) * weighted[:, None, :], 0.0
    )
    reward = -(jnp.sum(shares, axis=0) + jnp.exp(SLACK - log_total) * UNMATCHED)
    return (potential, reward)


def body(rollout, demo, projection, location, pair_block, pair_count):
    roll_blocks, pair_slots = pair_block.shape
    block_len = rollout.shape[0] // roll_blocks
    features = projection.shape[1]
    demo_count = demo.shape[0] // block_len
    owners_n = lax.axis_size("roll")
    slot_count = roll_blocks * pair_slots
    capacity = max(1, slot_count // owners_n)
    positions = owners_n * capacity
    roll_codes = jnp.dot(rollout, projection, preferred_element_type=jnp.float32).astype(
        jnp.bfloat16
    )
    demo_codes = jnp.dot(demo, projection, preferred_element_type=jnp.float32).astype(jnp.bfloat16)
    roll_tiles = roll_codes.reshape(roll_blocks, block_len, features)
    demo_tiles = demo_codes.reshape(demo_count, block_len, features)
    chosen = pair_block.reshape(slot_count)
    active = (jnp.arange(pair_slots, dtype=jnp.int32)[None, :] < pair_count[:, None]).reshape(
        slot_count
    )
    stored = location[chosen]
    owner_roll = stored // demo_count
    local_block = stored % demo_count
    slot_ids = jnp.arange(slot_count, dtype=jnp.int32)
    earlier = (
        (owner_roll[:, None] == owner_roll[None, :])
        & active[None, :]
        & (slot_ids[None, :] < slot_ids[:, None])
    )
    position_rank = jnp.sum(earlier.astype(jnp.int32), axis=1)
    slot_place = jnp.where(active, owner_roll * capacity + position_rank, positions)
    requested = jnp.full((positions,), -1, jnp.int32).at[slot_place].set(local_block, mode="drop")
    home_block = (
        jnp.full((positions,), -1, jnp.int32)
        .at[slot_place]
        .set(slot_ids // pair_slots, mode="drop")
    )
    wanted = lax.all_to_all(
        requested.reshape(owners_n, capacity), "roll", split_axis=0, concat_axis=0, tiled=True
    ).reshape(positions)
    serve_index = jnp.maximum(wanted, 0)
    home_index = jnp.maximum(home_block, 0)
    roll_pot = jnp.zeros((roll_blocks, block_len), jnp.float32)
    demo_pot = jnp.zeros((demo_count, block_len), jnp.float32)
    reward = jnp.zeros((roll_blocks, block_len), jnp.float32)
    outgoing = demo_tiles[serve_index]
    arrived = lax.all_to_all(
        outgoing.reshape(owners_n, capacity, block_len, features),
        "roll",
        split_axis=0,
        concat_axis=0,
        tiled=True,
    )
    left_codes = roll_tiles[home_index]
    right_codes = arrived.reshape(positions, block_len, features)
    stored_costs = tile_costs(left_codes, right_codes)
    for iteration in range(ITERS):
        costs = stored_costs
        column_lse = column_part(costs, roll_pot[home_index])
        returned = lax.all_to_all(
            column_lse.reshape(owners_n, capacity, block_len),
            "roll",
            split_axis=0,
            concat_axis=0,
            tiled=True,
        )
        demo_pot = demo_side(returned.reshape(positions, block_len), wanted, demo_count)
        pot_sent = lax.all_to_all(
            demo_pot[serve_index].reshape(owners_n, capacity, block_len),
            "roll",
            split_axis=0,
            concat_axis=0,
            tiled=True,
        )
        costs = stored_costs
        final = iteration == ITERS - 1
        row_lse, weighted = row_part(costs, pot_sent.reshape(positions, block_len), final)
        roll_pot, row_reward = rollout_side(row_lse, weighted, home_block, roll_blocks)
        if final:
            reward = row_reward
    return (reward.reshape(-1), roll_pot.reshape(-1), demo_pot.reshape(-1))


def solution(mesh):
    placed = (
        P(("roll", "rep"), None),
        P("roll", None),
        P(),
        P(),
        P(("roll", "rep"), None),
        P(("roll", "rep")),
    )
    return jax.shard_map(
        body,
        mesh=mesh,
        in_specs=placed,
        out_specs=(P(("roll", "rep")), P(("roll", "rep")), P("roll")),
        check_vma=False,
    )
```

profile of v0, /device:TPU:1, one launch (start us, length us, event | category | flops | bytes accessed | tf_op | source)
XLA Modules:
  0.0 513.8 jit_solution(9999728730605393680)
XLA Ops:
  0.6 0.8 iota_compare_fusion.3
  1.7 0.8 copy.19
  2.5 1.6 gather_fusion
  4.4 1.0 scatter_custom_fusion.1
  5.4 0.7 copy.20
  6.1 18.4 %all-to-all-start = ((s32[128,1,1]{2,1,0:T(1,128)}), s32[128,1,1]{2,1,0:T(1,128)S(1)}, u32[]{:S(2)}, u32[]{:S(2)}) async-start(s32[128,1,1]{2,1,0:T(1,128)} %copy.20), calls=%async_computation | async-start | bytes 131072 | tf_op jit(solution)/shard_map/all_to_all | solution.py:127
  24.5 1.3 convolution_convert_fusion
  25.9 10.2 %all-to-all-done = s32[128,1,1]{2,1,0:T(1,128)S(1)} async-done(((s32[128,1,1]{2,1,0:T(1,128)}), s32[128,1,1]{2,1,0:T(1,128)S(1)}, u32[]{:S(2)}, u32[]{:S(2)}) %all-to-all-start) | async-done | bytes 544 | tf_op jit(solution)/shard_map/all_to_all | solution.py:127
  36.1 4.7 fusion.39
  40.8 6.5 %gather_fusion.3 = bf16[128,128,256]{2,1,0:T(8,128)(2,1)} fusion(bf16[16,128,256]{2,1,0:T(8,128)(2,1)S(1)} %bitcast.107, s32[1024]{0:T(1024)S(1)} %pad_clamp_fusion), kind=kCustom, calls=%fused_computation.3 | custom fusion | bytes 16777728 | tf_op jit(solution)/shard_map/gather | solution.py:135
  47.3 7.1 %all-to-all-start.1 = ((bf16[128,1,128,256]{3,2,1,0:T(8,128)(2,1)}), bf16[128,1,128,256]{3,2,1,0:T(8,128)(2,1)}, u32[]{:S(2)}, u32[]{:S(2)}) async-start(bf16[128,1,128,256]{3,2,1,0:T(8,128)(2,1)} %bitcast.110), calls=%async_computation.1 | async-start | bytes 16777216 | tf_op jit(solution)/shard_map/all_to_all | solution.py:136
  54.4 1.1 scatter_custom_fusion
  55.6 0.4 convolution_convert_fusion.1
  56.0 6.5 %gather_fusion.2 = bf16[128,128,256]{2,1,0:T(8,128)(2,1)} fusion(bf16[16,128,256]{2,1,0:T(8,128)(2,1)S(1)} %bitcast.108, s32[1024]{0:T(1024)S(1)} %pad_clamp_fusion.1), kind=kCustom, calls=%fused_computation.2 | custom fusion | bytes 16777728 | tf_op jit(solution)/shard_map/gather | solution.py:143
  62.5 0.6 gather_fusion.1
  63.1 5.6 %fusion.5 = f32[128,128]{1,0:T(8,128)S(1)} fusion(bf16[128,128,256]{2,1,0:T(8,128)(2,1)} %gather_fusion.2), kind=kLoop, calls=%fused_computation.22 | loop fusion | flops 12566528 | bytes 8454144 | tf_op jit(solution)/shard_map/pie,pie->pi/dot_general | solution.py:27
  68.7 211.6 %all-to-all-done.1 = bf16[128,1,128,256]{3,2,1,0:T(8,128)(2,1)} async-done(((bf16[128,1,128,256]{3,2,1,0:T(8,128)(2,1)}), bf16[128,1,128,256]{3,2,1,0:T(8,128)(2,1)}, u32[]{:S(2)}, u32[]{:S(2)}) %all-to-all-start.1) | async-done | bytes 8388640 | tf_op jit(solution)/shard_map/all_to_all | solution.py:136
  280.4 5.6 %fusion.4 = f32[128,128]{1,0:T(8,128)S(1)} fusion(bf16[128,1,128,256]{3,2,1,0:T(8,128)(2,1)} %all-to-all-done.1), kind=kLoop, calls=%fused_computation.20 | loop fusion | flops 12566528 | bytes 8454144 | tf_op jit(solution)/shard_map/pje,pje->pj/dot_general | solution.py:30
  286.0 8.9 %fusion.8 = (f32[128,128]{1,0:T(8,128)S(1)}, f32[128,128,128]{1,2,0:T(8,128)S(1)}) fusion(f32[128,128]{1,0:T(8,128)S(1)} %gather_fusion.1, bf16[128,128,256]{2,1,0:T(8,128)(2,1)} %gather_fusion.2, bf16[128,1,128,256]{3,2,1,0:T(8,128)(2,1)} %all-to-all-done.1, f32[128,128]{1,0:T(8,128)S(1)} %fusion.4, f32[128,128]{1,0:T(8,128)S(1)} %fusion.5), kind=kOutput, calls=%fused_computation.35 | convolution fusion | flops 1088405504 | bytes 25427968 | tf_op jit(solution)/shard_map/pie,pje->pij/dot_general | solution.py:24
  294.9 3.2 copy-done.1
  298.1 4.8 exponential_reduce_fusion.2
  302.9 0.7 log_add_fusion.3
  303.5 55.7 %all-to-all-start.2 = ((f32[128,1,128]{2,1,0:T(1,128)}), f32[128,1,128]{2,1,0:T(1,128)S(1)}, u32[]{:S(2)}, u32[]{:S(2)}) async-start(f32[128,1,128]{2,1,0:T(1,128)} %bitcast.13), calls=%async_computation.2 | async-start | bytes 131072 | tf_op jit(solution)/shard_map/all_to_all | solution.py:149
  359.3 11.3 %all-to-all-done.2 = f32[128,1,128]{2,1,0:T(1,128)S(1)} async-done(((f32[128,1,128]{2,1,0:T(1,128)}), f32[128,1,128]{2,1,0:T(1,128)S(1)}, u32[]{:S(2)}, u32[]{:S(2)}) %all-to-all-start.2) | async-done | bytes 65568 | tf_op jit(solution)/shard_map/all_to_all | solution.py:149
  370.9 0.4 select_reduce_fusion.7
  371.4 9.3 %all-gather.1 = f32[64,128]{1,0:T(8,128)S(1)} all-gather(f32[16,128]{1,0:T(8,128)S(1)} %select_reduce_fusion.7), channel_id=3, replica_groups=mesh['roll'=128,'rep'=4] {'rep'}, dimensions={0}, use_global_device_ids=true | all-gather | bytes 40960 | tf_op jit(solution)/shard_map/all_gather | solution.py:16
  380.7 9.0 %all-gather = f32[64,128]{1,0:T(8,128)S(1)} all-gather(f32[16,128]{1,0:T(8,128)S(1)} %select_reduce_fusion.8), channel_id=2, replica_groups=mesh['roll'=128,'rep'=4] {'rep'}, dimensions={0}, use_global_device_ids=true | all-gather | bytes 40960 | tf_op jit(solution)/shard_map/all_gather | solution.py:16
  389.9 1.2 gather_fusion.4
  391.1 11.4 %all-to-all-start.3 = ((f32[128,1,128]{2,1,0:T(1,128)}), f32[128,1,128]{2,1,0:T(1,128)S(1)}, u32[]{:S(2)}, u32[]{:S(2)}) async-start(f32[128,1,128]{2,1,0:T(1,128)} %bitcast.18), calls=%async_computation.3 | async-start | bytes 131072 | tf_op jit(solution)/shard_map/all_to_all | solution.py:157
  402.6 11.6 %all-to-all-done.3 = f32[128,1,128]{2,1,0:T(1,128)S(1)} async-done(((f32[128,1,128]{2,1,0:T(1,128)}), f32[128,1,128]{2,1,0:T(1,128)S(1)}, u32[]{:S(2)}, u32[]{:S(2)}) %all-to-all-start.3) | async-done | bytes 65568 | tf_op jit(solution)/shard_map/all_to_all | solution.py:157
  414.2 5.7 %fusion.9 = f32[128,128]{1,0:T(8,128)S(1)} fusion(f32[128,128,128]{1,2,0:T(8,128)} %copy-done.1, f32[128,128]{1,0:T(8,128)S(1)} %bitcast.111), kind=kLoop, calls=%fused_computation.36 | loop fusion | flops 6275072 | bytes 8519680 | tf_op jit(solution)/shard_map/reduce_max | solution.py:38
  420.1 4.9 exponential_reduce_fusion.1
  425.1 0.3 select_reduce_fusion.6
  425.4 0.4 select_reduce_fusion.5
  425.9 0.6 gather_fusion.5
  426.5 5.6 %fusion.10 = f32[128,128]{1,0:T(8,128)S(1)} fusion(f32[128,128,128]{1,2,0:T(8,128)} %copy-done.1, f32[128,128]{1,0:T(8,128)S(1)} %gather_fusion.5), kind=kLoop, calls=%fused_computation.37 | loop fusion | flops 6275072 | bytes 8519680 | tf_op jit(solution)/shard_map/reduce_max | solution.py:49
  432.2 6.9 %exponential_reduce_fusion = f32[128,128]{1,0:T(8,128)S(1)} fusion(f32[128,128,128]{1,2,0:T(8,128)} %copy-done.1, f32[128,128]{1,0:T(8,128)S(1)} %fusion.10, f32[128,128]{1,0:T(8,128)S(1)} %gather_fusion.5), kind=kLoop, calls=%fused_computation.28 | loop fusion | flops 8372224 | bytes 8585216 | tf_op jit(solution)/shard_map/reduce_sum | solution.py:50
  439.1 16.8 %all_to_all.34 = f32[128,1,128]{2,1,0:T(1,128)S(1)} all-to-all(f32[128,1,128]{2,1,0:T(1,128)S(1)} %bitcast.115), channel_id=1, replica_groups=mesh['roll'=128,'rep'=4] {'roll'}, dimensions={0} | all-to-all | bytes 131072 | tf_op jit(solution)/shard_map/all_to_all | solution.py:149
  456.2 0.4 select_reduce_fusion.3
  456.6 9.0 %all-gather.3 = f32[64,128]{1,0:T(8,128)S(1)} all-gather(f32[16,128]{1,0:T(8,128)S(1)} %select_reduce_fusion.3), channel_id=5, replica_groups=mesh['roll'=128,'rep'=4] {'rep'}, dimensions={0}, use_global_device_ids=true | all-gather | bytes 40960 | tf_op jit(solution)/shard_map/all_gather | solution.py:16
  465.7 9.0 %all-gather.2 = f32[64,128]{1,0:T(8,128)S(1)} all-gather(f32[16,128]{1,0:T(8,128)S(1)} %select_reduce_fusion.4), channel_id=4, replica_groups=mesh['roll'=128,'rep'=4] {'rep'}, dimensions={0}, use_global_device_ids=true | all-gather | bytes 40960 | tf_op jit(solution)/shard_map/all_gather | solution.py:16
  474.8 0.6 gather_fusion.6
  475.5 22.8 %all_to_all.35 = f32[128,1,128]{2,1,0:T(1,128)S(1)} all-to-all(f32[128,1,128]{2,1,0:T(1,128)S(1)} %bitcast.120), channel_id=1, replica_groups=mesh['roll'=128,'rep'=4] {'roll'}, dimensions={0} | all-to-all | bytes 131072 | tf_op jit(solution)/shard_map/all_to_all | solution.py:157
  498.2 5.2 %fusion.11 = f32[128,128]{1,0:T(8,128)S(1)} fusion(f32[128,128,128]{1,2,0:T(8,128)} %copy-done.1, f32[128,128]{1,0:T(8,128)S(1)} %bitcast.113), kind=kLoop, calls=%fused_computation.38 | loop fusion | flops 6275072 | bytes 8519680 | tf_op jit(solution)/shard_map/reduce_max | solution.py:38
  503.5 7.9 %fusion.12 = (f32[128,128]{1,0:T(8,128)S(1)}, f32[128,128]{1,0:T(8,128)S(1)}) fusion(f32[128,128,128]{1,2,0:T(8,128)} %copy-done.1, f32[128,128]{1,0:T(8,128)S(1)} %fusion.11, f32[128,128]{1,0:T(8,128)S(1)} %bitcast.114), kind=kLoop, calls=%fused_computation.39 | loop fusion | flops 12550144 | bytes 8650752 | tf_op jit(solution)/shard_map/reduce_sum | solution.py:40
  511.8 0.4 select_reduce_fusion.1
  512.3 0.4 select_reduce_fusion
  512.7 0.6 broadcast_multiply_fusion
  (54 shorter events, 2.4 us)
Async XLA Ops:
  0.6 23.9 %copy-start = (bf16[2048,256]{1,0:T(8,128)(2,1)S(1)}, bf16[2048,256]{1,0:T(8,128)(2,1)}, u32[]{:S(2)}) copy-start(bf16[2048,256]{1,0:T(8,128)(2,1)} %param.11) | copy-start | bytes 3145732
  6.1 30.0 %all-to-all-start = ((s32[128,1,1]{2,1,0:T(1,128)}), s32[128,1,1]{2,1,0:T(1,128)S(1)}, u32[]{:S(2)}, u32[]{:S(2)}) async-start(s32[128,1,1]{2,1,0:T(1,128)} %copy.20), calls=%async_computation | async-start | bytes 131072 | tf_op jit(solution)/shard_map/all_to_all | solution.py:127
  47.3 8.3 %copy-start.4 = (bf16[2048,256]{1,0:T(8,128)(2,1)S(1)}, bf16[2048,256]{1,0:T(8,128)(2,1)}, u32[]{:S(2)}) copy-start(bf16[2048,256]{1,0:T(8,128)(2,1)} %param.10) | copy-start | bytes 3145732
  47.3 8.3 %copy-start.5 = (bf16[256,256]{1,0:T(8,128)(2,1)S(1)}, bf16[256,256]{1,0:T(8,128)(2,1)}, u32[]{:S(2)}) copy-start(bf16[256,256]{1,0:T(8,128)(2,1)} %param.12) | copy-start | bytes 393220
  47.3 233.1 %all-to-all-start.1 = ((bf16[128,1,128,256]{3,2,1,0:T(8,128)(2,1)}), bf16[128,1,128,256]{3,2,1,0:T(8,128)(2,1)}, u32[]{:S(2)}, u32[]{:S(2)}) async-start(bf16[128,1,128,256]{3,2,1,0:T(8,128)(2,1)} %bitcast.110), calls=%async_computation.1 | async-start | bytes 16777216 | tf_op jit(solution)/shard_map/all_to_all | solution.py:136
  294.9 3.2 copy-start.1
  303.5 67.0 %all-to-all-start.2 = ((f32[128,1,128]{2,1,0:T(1,128)}), f32[128,1,128]{2,1,0:T(1,128)S(1)}, u32[]{:S(2)}, u32[]{:S(2)}) async-start(f32[128,1,128]{2,1,0:T(1,128)} %bitcast.13), calls=%async_computation.2 | async-start | bytes 131072 | tf_op jit(solution)/shard_map/all_to_all | solution.py:149
  391.1 23.1 %all-to-all-start.3 = ((f32[128,1,128]{2,1,0:T(1,128)}), f32[128,1,128]{2,1,0:T(1,128)S(1)}, u32[]{:S(2)}, u32[]{:S(2)}) async-start(f32[128,1,128]{2,1,0:T(1,128)} %bitcast.18), calls=%async_computation.3 | async-start | bytes 131072 | tf_op jit(solution)/shard_map/all_to_all | solution.py:157
  414.2 5.9 %copy-start.2 = (f32[128,128,128]{1,2,0:T(8,128)S(1)}, f32[128,128,128]{1,2,0:T(8,128)}, u32[]{:S(2)}) copy-start(f32[128,128,128]{1,2,0:T(8,128)} %copy-done.1) | copy-start | bytes 25165828
  474.8 36.6 %copy-start.3 = (f32[16,128]{1,0:T(8,128)}, f32[16,128]{1,0:T(8,128)S(1)}, u32[]{:S(2)}) copy-start(f32[16,128]{1,0:T(8,128)S(1)} %fusion.27) | copy-start | bytes 24580
where the time goes:
time: 522 us; the launch traced here: 514 us
  waiting for transfers between devices  245 us (47%)
  starting transfers between devices  92.6 us (18%)
  blocking collectives  75.9 us (15%)
  other arithmetic  63.2 us (12%)
  local copies, waits for them, and re-layouts  25.2 us (5%)
  matrix products  10.6 us (2%)
    all_to_all x1, waiting for transfers between devices, body(): lax.all_to_all(outgoing.reshape(owners_n, capacity, block_len, features),...  212 us
    all_to_all x1, starting transfers between devices, body(): lax.all_to_all(column_lse.reshape(owners_n, capacity, block_len), 'roll',...  55.7 us
    all_gather x4, blocking collectives, joined(): pieces = jax.tree.map(lambda part: lax.all_gather(part, axis), value)  36.4 us
    all_to_all x1, blocking collectives, body(): lax.all_to_all(demo_pot[serve_index].reshape(owners_n, capacity, block_le...  22.8 us
    all_to_all x1, starting transfers between devices, body(): lax.all_to_all(requested.reshape(owners_n, capacity), 'roll', split_axis=...  18.4 us
    all_to_all x1, blocking collectives, body(): lax.all_to_all(column_lse.reshape(owners_n, capacity, block_len), 'roll',...  16.8 us
    reduce_sum x2, other arithmetic, row_part(): summed = jnp.sum(shifted, axis=2)  12.8 us
    reduce_sum x2, other arithmetic, column_part(): jnp.sum(jnp.exp(scores - largest[:, None, :]), axis=1)  11.7 us
  transfers between devices with their start and end apart: 4, of which 4 were waited for; matrix products, arithmetic and copies ran while one was open for 3% of the time, Pallas kernels for 0%

commit v1 on v0

v1 whole, which is shorter than its diff:
```python
import functools
import math

import jax
import jax.numpy as jnp
from jax import lax
from jax.experimental import pallas as pl
from jax.experimental.pallas import tpu as pltpu
from jax.sharding import Mesh
from jax.sharding import PartitionSpec as P

EPSILON = 0.02
UNMATCHED = 2.0
SLACK = 100.0
SHIFT = 46.0
LOG2E = 1.4426950408889634
SHIFT2 = SHIFT * LOG2E
FLOOR = math.exp(SHIFT - SLACK)
OFF = -1.0e30

BLK = 128
E = 256
NY, NZ, NC, NX = 8, 8, 2, 4
KB = 16
ROWS = KB * BLK
AUX = 2 * KB
LOAD = ROWS + AUX
SOURCES = NY * NC
POS = SOURCES * NZ
BETA = LOG2E * 2.0 / (E * EPSILON)
VMEM = 52 * 2**20

NT = (((1,), (1,)), ((), ()))
TN = (((0,), (0,)), ((), ()))
NN = (((1,), (0,)), ((), ()))


def exact_sum(onehot, values):
    return lax.dot_general(
        onehot,
        values,
        NN,
        precision=lax.Precision.HIGHEST,
        preferred_element_type=jnp.float32,
    )


def spread(places, count):
    rows = lax.broadcasted_iota(jnp.int32, (count, POS), 0)
    return jnp.where(rows == places, 1.0, 0.0)


def project_kernel(frames, projection, out, norms):
    for k in range(KB):
        rows = pl.ds(k * BLK, BLK)
        codes = jnp.dot(
            frames[rows, :], projection[...], preferred_element_type=jnp.float32
        ).astype(jnp.bfloat16)
        out[rows, :] = codes
        wide = codes.astype(jnp.float32)
        square = wide * wide
        high = square.astype(jnp.bfloat16)
        low = (square - high.astype(jnp.float32)).astype(jnp.bfloat16)
        ones = jnp.ones((16, E), jnp.bfloat16)
        total = lax.dot_general(ones, high, NT, preferred_element_type=jnp.float32)
        total += lax.dot_general(ones, low, NT, preferred_element_type=jnp.float32)
        norms[k : k + 1, :] = total[0:1, :]
    norm = norms[...]
    high = norm.astype(jnp.bfloat16)
    rest = norm - high.astype(jnp.float32)
    middle = rest.astype(jnp.bfloat16)
    low = (rest - middle.astype(jnp.float32)).astype(jnp.bfloat16)
    out[ROWS : ROWS + KB, 0:BLK] = high
    out[ROWS : ROWS + KB, BLK:E] = middle
    out[ROWS + KB : LOAD, 0:BLK] = low
    out[ROWS + KB : LOAD, BLK:E] = jnp.zeros((KB, BLK), jnp.bfloat16)


def project(frames, projection):
    return pl.pallas_call(
        project_kernel,
        out_shape=jax.ShapeDtypeStruct((LOAD, E), jnp.bfloat16),
        in_specs=[pl.BlockSpec(memory_space=pltpu.VMEM)] * 2,
        out_specs=pl.BlockSpec(memory_space=pltpu.VMEM),
        scratch_shapes=[pltpu.VMEM((KB, BLK), jnp.float32)],
        compiler_params=pltpu.CompilerParams(vmem_limit_bytes=VMEM),
        cost_estimate=pl.CostEstimate(
            flops=2 * ROWS * E * E, bytes_accessed=4 * ROWS * E, transcendentals=0
        ),
    )(frames, projection)


def picked(which):
    rows = lax.broadcasted_iota(jnp.int32, (4 * KB, BLK), 0)
    return jnp.where(rows % KB == which, -0.5, 0.0).astype(jnp.bfloat16)


def parts(held):
    aux = held[ROWS:LOAD, :]
    return jnp.concatenate([aux[:, 0:BLK], aux[:, BLK:E]], axis=0)


def first_kernel(code, col_place, left, *rest):
    rights, (cross, columns, sums) = rest[:NZ], rest[NZ:]
    step = pl.program_id(0)
    left_parts = parts(left)
    rows = []
    for z in range(NZ):
        value = code[step * NZ + z]
        active = value >= 0
        value = jnp.maximum(value, 0)
        k, t = value // KB, value % KB
        u = left[pl.ds(pl.multiple_of(k * BLK, BLK), BLK), :]
        v = rights[z][pl.ds(pl.multiple_of(t * BLK, BLK), BLK), :]
        w = lax.dot_general(u, v, NT, preferred_element_type=jnp.float32)
        w += lax.dot_general(
            jnp.concatenate([left_parts, picked(t)], axis=0),
            jnp.concatenate([picked(k), parts(rights[z])], axis=0),
            TN,
            preferred_element_type=jnp.float32,
        )
        cross[z] = w
        shifted = jnp.exp2(w * BETA + jnp.where(active, SHIFT2, OFF))
        rows.append(jnp.sum(shifted, axis=0, keepdims=True))
    sums[pl.ds(pl.multiple_of(step * NZ, NZ), NZ), :] = jnp.concatenate(rows, axis=0)

    @pl.when(step == SOURCES - 1)
    def _():
        columns[...] = exact_sum(spread(col_place[...], NZ * KB), sums[...])


def first_pass(code, col_place, left, rights):
    whole = pl.BlockSpec(memory_space=pltpu.VMEM)
    return pl.pallas_call(
        first_kernel,
        grid_spec=pltpu.PrefetchScalarGridSpec(
            num_scalar_prefetch=1,
            grid=(SOURCES,),
            in_specs=[whole, pl.BlockSpec((None, LOAD, E), lambda s, *_: (s, 0, 0))]
            + [whole] * NZ,
            out_specs=[pl.BlockSpec((NZ, BLK, BLK), lambda s, *_: (s, 0, 0)), whole],
            scratch_shapes=[pltpu.VMEM((POS, BLK), jnp.float32)],
        ),
        out_shape=[
            jax.ShapeDtypeStruct((POS, BLK, BLK), jnp.float32),
            jax.ShapeDtypeStruct((NZ * KB, BLK), jnp.float32),
        ],
        compiler_params=pltpu.CompilerParams(vmem_limit_bytes=VMEM),
        cost_estimate=pl.CostEstimate(
            flops=2 * POS * BLK * BLK * 384,
            bytes_accessed=32 * 2**20,
            transcendentals=POS * BLK * BLK,
        ),
    )(code, col_place, left, *rights)


TILES = 16


def second_kernel(col_at, row_place, column_sum, cross, kernel, costed, rows_out, potential, sums):
    step = pl.program_id(0)

    @pl.when(step == 0)
    def _():
        potential[...] = 2.0 * SHIFT2 - jnp.log2(FLOOR + column_sum[...])

    ones = jnp.ones((16, BLK), jnp.bfloat16)
    rows = []
    for n in range(TILES):
        at = col_at[step * TILES + n]
        pot = potential[pl.ds(jnp.maximum(at, 0), 1), :] + jnp.where(at >= 0, 0.0, OFF)
        w = cross[n]
        rounded = jnp.exp2(w * BETA + pot).astype(jnp.bfloat16)
        kernel[n] = rounded
        costed[n] = (rounded.astype(jnp.float32) * (w * (-2.0 / E))).astype(jnp.bfloat16)
        rows.append(
            lax.dot_general(ones, rounded, NT, preferred_element_type=jnp.float32)[0:1, :]
        )
    sums[pl.ds(pl.multiple_of(step * TILES, TILES), TILES), :] = jnp.concatenate(rows, axis=0)

    @pl.when(step == POS // TILES - 1)
    def _():
        rows_out[...] = exact_sum(spread(row_place[...], SOURCES * KB), sums[...])


def tiles_spec():
    return pl.BlockSpec((TILES, BLK, BLK), lambda s, *_: (s, 0, 0))


def second_pass(col_at, row_place, column_sum, cross):
    whole = pl.BlockSpec(memory_space=pltpu.VMEM)
    return pl.pallas_call(
        second_kernel,
        grid_spec=pltpu.PrefetchScalarGridSpec(
            num_scalar_prefetch=1,
            grid=(POS // TILES,),
            in_specs=[whole, whole, tiles_spec()],
            out_specs=[tiles_spec(), tiles_spec(), whole],
            scratch_shapes=[
                pltpu.VMEM((NZ * KB, BLK), jnp.float32),
                pltpu.VMEM((POS, BLK), jnp.float32),
            ],
        ),
        out_shape=[
            jax.ShapeDtypeStruct((POS, BLK, BLK), jnp.bfloat16),
            jax.ShapeDtypeStruct((POS, BLK, BLK), jnp.bfloat16),
            jax.ShapeDtypeStruct((SOURCES * KB, BLK), jnp.float32),
        ],
        compiler_params=pltpu.CompilerParams(vmem_limit_bytes=VMEM),
    )(col_at, row_place, column_sum, cross)


def two_parts(row):
    high = row.astype(jnp.bfloat16).astype(jnp.float32)
    at = lax.broadcasted_iota(jnp.int32, (16, BLK), 0)
    return jnp.where(at == 0, high, jnp.where(at == 1, row - high, 0.0)).astype(jnp.bfloat16)


def third_kernel(row_at, col_place, scale, kernel, columns, sums):
    step = pl.program_id(0)
    rows = []
    for n in range(TILES):
        at = jnp.maximum(row_at[step * TILES + n], 0)
        both = lax.dot_general(
            two_parts(scale[pl.ds(at, 1), :]),
            kernel[n],
            NN,
            preferred_element_type=jnp.float32,
        )
        rows.append(both[0:1, :] + both[1:2, :])
    sums[pl.ds(pl.multiple_of(step * TILES, TILES), TILES), :] = jnp.concatenate(rows, axis=0)

    @pl.when(step == POS // TILES - 1)
    def _():
        columns[...] = exact_sum(spread(col_place[...], NZ * KB), sums[...])


def third_pass(row_at, col_place, scale, kernel):
    whole = pl.BlockSpec(memory_space=pltpu.VMEM)
    return pl.pallas_call(
        third_kernel,
        grid_spec=pltpu.PrefetchScalarGridSpec(
            num_scalar_prefetch=1,
            grid=(POS // TILES,),
            in_specs=[whole, whole, tiles_spec()],
            out_specs=whole,
            scratch_shapes=[pltpu.VMEM((POS, BLK), jnp.float32)],
        ),
        out_shape=jax.ShapeDtypeStruct((NZ * KB, BLK), jnp.float32),
        compiler_params=pltpu.CompilerParams(vmem_limit_bytes=VMEM),
    )(row_at, col_place, scale, kernel)


def fourth_kernel(col_at, row_place, scale, kernel, costed, rows_out, sums, weighed):
    step = pl.program_id(0)
    rows, heavy = [], []
    for n in range(TILES):
        at = jnp.maximum(col_at[step * TILES + n], 0)
        pair = two_parts(scale[pl.ds(at, 1), :])
        both = lax.dot_general(pair, kernel[n], NT, preferred_element_type=jnp.float32)
        rows.append(both[0:1, :] + both[1:2, :])
        both = lax.dot_general(pair, costed[n], NT, preferred_element_type=jnp.float32)
        heavy.append(both[0:1, :] + both[1:2, :])
    place = pl.ds(pl.multiple_of(step * TILES, TILES), TILES)
    sums[place, :] = jnp.concatenate(rows, axis=0)
    weighed[place, :] = jnp.concatenate(heavy, axis=0)

    @pl.when(step == POS // TILES - 1)
    def _():
        which = spread(row_place[...], SOURCES * KB)
        total = exact_sum(which, sums[...])
        heavy_total = exact_sum(which, weighed[...])
        for s in range(SOURCES):
            rows_out[s, 0:KB, :] = total[s * KB : (s + 1) * KB, :]
            rows_out[s, KB : 2 * KB, :] = heavy_total[s * KB : (s + 1) * KB, :]


def fourth_pass(col_at, row_place, scale, kernel, costed):
    whole = pl.BlockSpec(memory_space=pltpu.VMEM)
    return pl.pallas_call(
        fourth_kernel,
        grid_spec=pltpu.PrefetchScalarGridSpec(
            num_scalar_prefetch=1,
            grid=(POS // TILES,),
            in_specs=[whole, whole, tiles_spec(), tiles_spec()],
            out_specs=whole,
            scratch_shapes=[pltpu.VMEM((POS, BLK), jnp.float32)] * 2,
        ),
        out_shape=jax.ShapeDtypeStruct((SOURCES, 2 * KB, BLK), jnp.float32),
        compiler_params=pltpu.CompilerParams(vmem_limit_bytes=VMEM),
    )(col_at, row_place, scale, kernel, costed)


def ring_pieces(block, axis, n):
    up = [(i, (i + 1) % n) for i in range(n)]
    down = [(i, (i - 1) % n) for i in range(n)]
    half = block.shape[0] // 2
    held = [block] + [None] * (n - 1)
    right = left = block
    for k in range(1, n // 2):
        right = lax.ppermute(right, axis, up)
        left = lax.ppermute(left, axis, down)
        held[n - k], held[k] = right, left
    first = lax.ppermute(right[:half], axis, up)
    second = lax.ppermute(left[half:], axis, down)
    held[n // 2] = jnp.concatenate([first, second], axis=0)
    return held


def swap(value, axes):
    return lax.all_to_all(value, axes, split_axis=0, concat_axis=0, tiled=True)


def to_all(value, axes, n):
    return swap(jnp.broadcast_to(value[None], (n,) + value.shape), axes)


def column_total(columns):
    mine = jnp.sum(swap(columns.reshape(NZ, KB, BLK), "z"), axis=0)
    return jnp.sum(to_all(mine, "x", NX), axis=0)


def slot_codes(location, pair_block, pair_count):
    slots = pair_block.shape[1]
    stored = location[pair_block.reshape(-1)]
    used = (
        jnp.arange(slots, dtype=jnp.int32)[None, :] < pair_count[:, None]
    ).reshape(-1)
    block = jnp.arange(KB * slots, dtype=jnp.int32) // slots
    owner, local = stored // KB, stored % KB
    holders = jnp.arange(NY * NZ * NC, dtype=jnp.int32)
    match = (owner[None, :] == holders[:, None]) & used[None, :]
    return jnp.max(jnp.where(match, (block * KB + local)[None, :], -1), axis=1)


def body(rollout, demo, projection, location, pair_block, pair_count):
    codes = slot_codes(location, pair_block, pair_count)
    codes = codes.reshape(NY, NZ, NC).transpose(0, 2, 1).reshape(SOURCES, NZ)
    codes = swap(codes[:, None, :], ("y", "c")).reshape(SOURCES, NZ)
    turned = (lax.axis_index("z") + jnp.arange(NZ, dtype=jnp.int32)) % NZ
    pick = turned[:, None] == jnp.arange(NZ, dtype=jnp.int32)[None, :]
    codes = jnp.max(jnp.where(pick[None], codes[:, None, :], -1), axis=2)
    used = codes >= 0
    col_at = jnp.where(used, turned[None, :] * KB + codes % KB, -1).reshape(POS)
    sources = jnp.arange(SOURCES, dtype=jnp.int32)[:, None]
    row_at = jnp.where(used, sources * KB + codes // KB, -1).reshape(POS)
    col_place, row_place = col_at.reshape(1, POS), row_at.reshape(1, POS)
    codes = codes.reshape(POS)

    left = lax.all_gather(project(rollout, projection), ("y", "c"))
    rights = ring_pieces(project(demo, projection), "z", NZ)

    cross, columns = first_pass(codes, col_place, left, rights)
    column_sum = column_total(columns)
    kernel, costed, rows = second_pass(
        col_at, row_place, to_all(column_sum, "z", NZ).reshape(NZ * KB, BLK), cross
    )
    row_sum = jnp.sum(swap(rows.reshape(SOURCES, KB, BLK), ("y", "c")), axis=0)
    roll_scale = 1.0 / (FLOOR + row_sum)
    columns = third_pass(
        row_at,
        col_place,
        to_all(roll_scale, ("y", "c"), SOURCES).reshape(SOURCES * KB, BLK),
        kernel,
    )
    plan_sum = column_total(columns)
    demo_scale = 1.0 / (FLOOR / (FLOOR + column_sum) + plan_sum)
    demo_pot = EPSILON * (SHIFT - jnp.log(FLOOR + (FLOOR + column_sum) * plan_sum))
    both = fourth_pass(
        col_at,
        row_place,
        to_all(demo_scale, "z", NZ).reshape(NZ * KB, BLK),
        kernel,
        costed,
    )
    both = jnp.sum(swap(both, ("y", "c")), axis=0)
    total = FLOOR + both[:KB]
    reward = -(both[KB:] + UNMATCHED * FLOOR) / total
    roll_pot = EPSILON * (SHIFT - jnp.log(total))
    return reward.reshape(-1), roll_pot.reshape(-1), demo_pot.reshape(-1)


def solution(mesh):
    grid = Mesh(mesh.devices.reshape(NY, NZ, NC, NX), ("y", "z", "c", "x"))
    every, roll = ("y", "z", "c", "x"), ("y", "z", "c")
    return jax.shard_map(
        body,
        mesh=grid,
        in_specs=(P(every, None), P(roll, None), P(), P(), P(every, None), P(every)),
        out_specs=(P(every), P(every), P(roll)),
        check_vma=False,
    )
```

time: 522 us -> 292 us (0.56); the launches traced: 514 us -> 291 us
  waiting for transfers between devices: 245 us -> 68.9 us
  other arithmetic: 63.2 us -> 4.01 us
  Pallas kernels: 0 us -> 52.9 us
  starting transfers between devices: 92.6 us -> 49.8 us
  local copies, waits for them, and re-layouts: 25.2 us -> 9.4 us
  blocking collectives: 75.9 us -> 91.1 us
  between operations: 1.49 us -> 14.4 us
  matrix products: 10.6 us -> 0 us
    all_to_all x4 -> x3, waiting for transfers between devices: 245 us -> 11.3 us  [swap(): return lax.all_to_all(value, axes, split_axis=0, concat_axis=0, tiled=True)]
    all_to_all x4 -> x3, starting transfers between devices: 92.6 us -> 16.9 us  [swap(): return lax.all_to_all(value, axes, split_axis=0, concat_axis=0, tiled=True)]
    ppermute x0 -> x8, waiting for transfers between devices: none -> 57.6 us  [the longest x3 49.7 us: ring_pieces(): right = lax.ppermute(right, axis, up)]
    pallas_call x0 -> x6, Pallas kernels: none -> 52.9 us  [the longest x1 20 us: first_pass(): pl.pallas_call(first_kernel, grid_spec=pltpu.PrefetchScalarGridSpec(num_s...]
    all_to_all x2 -> x7, blocking collectives: 39.5 us -> 91.1 us  [swap(): return lax.all_to_all(value, axes, split_axis=0, concat_axis=0, tiled=True)]
    all_gather x4 -> x0, blocking collectives: 36.4 us -> none  [joined(): pieces = jax.tree.map(lambda part: lax.all_gather(part, axis), value)]
    ppermute x0 -> x8, starting transfers between devices: none -> 32.8 us  [the longest x3 17.7 us: ring_pieces(): left = lax.ppermute(left, axis, down)]
    reduce_sum x10 -> x6, other arithmetic: 26.9 us -> 0.07 us  [the longest x1 0.02 us: body(): both = jnp.sum(swap(both, ('y', 'c')), axis=0)]
  transfers between devices with their start and end apart: 4 -> 12, of which waited for: 4 -> 7; matrix products, arithmetic and copies ran while one was open for 3% -> 3% of each run, Pallas kernels for 0% -> 1%
where the time goes in v1:
time: 292 us; the launch traced here: 291 us
  blocking collectives  91.1 us (31%)
  waiting for transfers between devices  68.9 us (24%)
  Pallas kernels  52.9 us (18%)
  starting transfers between devices  49.8 us (17%)
  between operations  14.4 us (5%)
  local copies, waits for them, and re-layouts  9.4 us (3%)
  other arithmetic  4.01 us (1%)
    all_to_all x7, blocking collectives, swap(): return lax.all_to_all(value, axes, split_axis=0, concat_axis=0, tiled=True)  91.1 us
    ppermute x3, waiting for transfers between devices, ring_pieces(): right = lax.ppermute(right, axis, up)  49.7 us
    pallas_call x1, Pallas kernels, first_pass(): pl.pallas_call(first_kernel, grid_spec=pltpu.PrefetchScalarGridSpec(num_s...  20 us
    ppermute x3, starting transfers between devices, ring_pieces(): left = lax.ppermute(left, axis, down)  17.7 us
    all_to_all x3, starting transfers between devices, swap(): return lax.all_to_all(value, axes, split_axis=0, concat_axis=0, tiled=True)  16.9 us
    all_to_all x3, waiting for transfers between devices, swap(): return lax.all_to_all(value, axes, split_axis=0, concat_axis=0, tiled=True)  11.3 us
    pallas_call x1, Pallas kernels, second_pass(): pl.pallas_call(second_kernel, grid_spec=pltpu.PrefetchScalarGridSpec(num_...  11.1 us
    pallas_call x1, Pallas kernels, fourth_pass(): pl.pallas_call(fourth_kernel, grid_spec=pltpu.PrefetchScalarGridSpec(num_...  9.27 us
  transfers between devices with their start and end apart: 12, of which 7 were waited for; matrix products, arithmetic and copies ran while one was open for 3% of the time, Pallas kernels for 1%

profile of v1, /device:TPU:1, one launch (start us, length us, event | category | flops | bytes accessed | tf_op | source)
XLA Modules:
  0.0 290.6 jit_solution(18128290651194290913)
XLA Ops:
  7.2 1.2 copy-done.2
  8.5 0.9 copy-done.4
  9.4 3.1 %shard_map.85 = bf16[2080,256]{1,0:T(8,128)(2,1)} custom-call(bf16[2048,256]{1,0:T(8,128)(2,1)S(1)} %copy-done.2, bf16[256,256]{1,0:T(8,128)(2,1)S(1)} %copy-done.4), custom_call_target="tpu_custom_call" | custom-call | flops 268435456 | bytes 2097152 | tf_op jit(solution)/shard_map/pallas_call | solution.py:80
  12.5 1.2 copy-done.3
  13.7 3.1 %shard_map.86.rest_0_ = bf16[2080,256]{1,0:T(8,128)(2,1)} custom-call(bf16[2048,256]{1,0:T(8,128)(2,1)S(1)} %copy-done.3, bf16[256,256]{1,0:T(8,128)(2,1)S(1)} %copy-done.5), custom_call_target="tpu_custom_call" | custom-call | flops 268435456 | bytes 2097152 | tf_op jit(solution)/shard_map/pallas_call | solution.py:80
  16.8 4.8 %collective-permute-start.3 = (bf16[2080,256]{1,0:T(8,128)(2,1)}, bf16[2080,256]{1,0:T(8,128)(2,1)S(1)}, u32[]{:S(2)}, u32[]{:S(2)}) collective-permute-start(bf16[2080,256]{1,0:T(8,128)(2,1)} %shard_map.86.rest_0_), channel_id=1, source_target_pairs={{0,8},{8,16},{16,24},{24,32},{32,40},{40,48},{48,56},{56,0},{1,9},... | collective-permute-start | bytes 3194888 | tf_op jit(solution)/shard_map/ppermute | solution.py:301
  21.6 8.6 %collective-permute-start = (bf16[2080,256]{1,0:T(8,128)(2,1)}, bf16[2080,256]{1,0:T(8,128)(2,1)S(1)}, u32[]{:S(2)}, u32[]{:S(2)}) collective-permute-start(bf16[2080,256]{1,0:T(8,128)(2,1)} %shard_map.86.rest_0_), channel_id=1, source_target_pairs={{0,56},{8,0},{16,8},{24,16},{32,24},{40,32},{48,40},{56,48},{1,57}... | collective-permute-start | bytes 3194888 | tf_op jit(solution)/shard_map/ppermute | solution.py:302
  30.2 21.6 %collective-permute-done.3.rest_7_ = bf16[2080,256]{1,0:T(8,128)(2,1)S(1)} collective-permute-done((bf16[2080,256]{1,0:T(8,128)(2,1)}, bf16[2080,256]{1,0:T(8,128)(2,1)S(1)}, u32[]{:S(2)}, u32[]{:S(2)}) %collective-permute-start.3) | collective-permute-done | bytes 1064992 | tf_op jit(solution)/shard_map/ppermute | solution.py:301
  51.9 1.9 collective-permute-start.4
  53.8 4.6 %collective-permute-start.1 = (bf16[2080,256]{1,0:T(8,128)(2,1)S(1)}, bf16[2080,256]{1,0:T(8,128)(2,1)}, u32[]{:S(2)}, u32[]{:S(2)}) collective-permute-start(bf16[2080,256]{1,0:T(8,128)(2,1)S(1)} %collective-permute-done.rest_1_), channel_id=1, source_target_pairs={{0,56},{8,0},{16,8},{24,16},{32,24},{40,32},{48,40},{56,48},{1,57}... | collective-permute-start | bytes 3194888 | tf_op jit(solution)/shard_map/ppermute | solution.py:302
  58.4 20.6 %collective-permute-done.4.rest_6_ = bf16[2080,256]{1,0:T(8,128)(2,1)S(1)} collective-permute-done((bf16[2080,256]{1,0:T(8,128)(2,1)S(1)}, bf16[2080,256]{1,0:T(8,128)(2,1)S(1)}, u32[]{:S(2)}, u32[]{:S(2)}) %collective-permute-start.4) | collective-permute-done | bytes 1064992 | tf_op jit(solution)/shard_map/ppermute | solution.py:301
  78.9 1.9 collective-permute-start.5
  80.9 4.6 %collective-permute-start.2 = (bf16[2080,256]{1,0:T(8,128)(2,1)}, bf16[2080,256]{1,0:T(8,128)(2,1)S(1)}, u32[]{:S(2)}, u32[]{:S(2)}) collective-permute-start(bf16[2080,256]{1,0:T(8,128)(2,1)} %collective-permute-done.1.rest_2_), channel_id=1, source_target_pairs={{0,56},{8,0},{16,8},{24,16},{32,24},{40,32},{48,40},{56,48},{1,57}... | collective-permute-start | bytes 3194888 | tf_op jit(solution)/shard_map/ppermute | solution.py:302
  85.6 0.1 lt.59
  85.9 1.1 gather_fusion
  87.0 0.1 select_reduce_fusion
  87.2 0.1 reshape.356
  87.3 0.7 copy.23
  88.0 9.6 %all-to-all-start = ((s32[16,1,8]{2,1,0:T(1,128)}), s32[16,1,8]{2,1,0:T(1,128)S(1)}, u32[]{:S(2)}, u32[]{:S(2)}) async-start(s32[16,1,8]{2,1,0:T(1,128)} %bitcast.3), calls=%async_computation | async-start | bytes 16384 | tf_op jit(solution)/shard_map/all_to_all | solution.py:311
  97.7 7.5 %collective-permute-done.5.rest_5_ = bf16[2080,256]{1,0:T(8,128)(2,1)S(1)} collective-permute-done((bf16[2080,256]{1,0:T(8,128)(2,1)S(1)}, bf16[2080,256]{1,0:T(8,128)(2,1)S(1)}, u32[]{:S(2)}, u32[]{:S(2)}) %collective-permute-start.5) | collective-permute-done | bytes 1064992 | tf_op jit(solution)/shard_map/ppermute | solution.py:301
  105.2 0.9 slice.18
  106.1 1.9 collective-permute-start.6
  108.1 0.9 slice.19
  109.0 4.6 %collective-permute-start.7 = (bf16[1040,256]{1,0:T(8,128)(2,1)}, bf16[1040,256]{1,0:T(8,128)(2,1)}, u32[]{:S(2)}, u32[]{:S(2)}) collective-permute-start(bf16[1040,256]{1,0:T(8,128)(2,1)} %slice.19), channel_id=1, source_target_pairs={{0,56},{8,0},{16,8},{24,16},{32,24},{40,32},{48,40},{56,48},{1,57}... | collective-permute-start | bytes 1597448 | tf_op jit(solution)/shard_map/ppermute | solution.py:305
  113.6 0.1 add.189
  113.9 0.1 select_reduce_fusion.1
  114.3 6.1 %collective-permute-done.6 = bf16[1040,256]{1,0:T(8,128)(2,1)} collective-permute-done((bf16[1040,256]{1,0:T(8,128)(2,1)}, bf16[1040,256]{1,0:T(8,128)(2,1)}, u32[]{:S(2)}, u32[]{:S(2)}) %collective-permute-start.6) | collective-permute-done | bytes 532512 | tf_op jit(solution)/shard_map/ppermute | solution.py:304
  120.4 1.8 collective-permute-done.7
  122.2 2.3 pad_maximum_fusion.rest_4_
  124.5 20.0 %shard_map.87 = (f32[128,128,128]{2,1,0:T(8,128)}, f32[128,128]{1,0:T(8,128)S(1)}) custom-call(s32[128]{0:T(128)S(1)} %reduce_max.24.code, s32[1,128]{1,0:T(1,128)S(1)} %get-tuple-element.17.col_place, bf16[16,2080,256]{2,1,0:T(8,128)(2,1)} %bitcast.26, bf16[2080,256]{1,0:T(8,128)(2,1)S(1)} %copy-done.1, bf16[2080,256]{1,0:T(8,128)(2,1)} %copy-done.9, ...), custom_call_target="tpu_custom_call" | custom-call | flops 1610612736 | bytes 33554432 | tf_op jit(solution)/shard_map/pallas_call | solution.py:134
  144.5 11.7 %all_to_all.50 = f32[8,16,128]{2,1,0:T(8,128)S(1)} all-to-all(f32[8,16,128]{2,1,0:T(8,128)S(1)} %bitcast.25), channel_id=1, replica_groups=mesh['y'=8,'z'=8,'c'=2,'x'=4] {'z'}, dimensions={0} | all-to-all | bytes 131072 | tf_op jit(solution)/shard_map/all_to_all | solution.py:311
  156.2 0.6 broadcast_in_dim.53
  156.8 4.0 %all-to-all-start.2 = ((f32[4,16,128]{2,1,0:T(8,128)}), f32[4,16,128]{2,1,0:T(8,128)S(1)}, u32[]{:S(2)}, u32[]{:S(2)}) async-start(f32[4,16,128]{2,1,0:T(8,128)} %broadcast_in_dim.53), calls=%async_computation.2 | async-start | bytes 65536 | tf_op jit(solution)/shard_map/all_to_all | solution.py:311
  161.0 4.1 %all-to-all-done.2 = f32[4,16,128]{2,1,0:T(8,128)S(1)} async-done(((f32[4,16,128]{2,1,0:T(8,128)}), f32[4,16,128]{2,1,0:T(8,128)S(1)}, u32[]{:S(2)}, u32[]{:S(2)}) %all-to-all-start.2) | async-done | bytes 32800 | tf_op jit(solution)/shard_map/all_to_all | solution.py:311
  165.1 0.6 broadcast_in_dim.54
  165.8 3.3 %all-to-all-start.3 = ((f32[8,16,128]{2,1,0:T(8,128)}), f32[8,16,128]{2,1,0:T(8,128)S(1)}, u32[]{:S(2)}, u32[]{:S(2)}) async-start(f32[8,16,128]{2,1,0:T(8,128)} %broadcast_in_dim.54), calls=%async_computation.3 | async-start | bytes 131072 | tf_op jit(solution)/shard_map/all_to_all | solution.py:311
  169.1 7.1 %all-to-all-done.3 = f32[8,16,128]{2,1,0:T(8,128)S(1)} async-done(((f32[8,16,128]{2,1,0:T(8,128)}), f32[8,16,128]{2,1,0:T(8,128)S(1)}, u32[]{:S(2)}, u32[]{:S(2)}) %all-to-all-start.3) | async-done | bytes 65568 | tf_op jit(solution)/shard_map/all_to_all | solution.py:311
  176.3 11.1 %shard_map.88 = (bf16[128,128,128]{2,1,0:T(8,128)(2,1)}, bf16[128,128,128]{2,1,0:T(8,128)(2,1)}, f32[256,128]{1,0:T(8,128)S(1)}) custom-call(s32[128]{0:T(128)S(1)} %get-tuple-element.20.col_at, s32[1,128]{1,0:T(1,128)S(1)} %get-tuple-element.18.row_place, f32[128,128]{1,0:T(8,128)S(1)} %bitcast.21, f32[128,128,128]{2,1,0:T(8,128)} %get-tuple-element.9.cross), custom_call_target="tpu_custom_call" | custom-call | tf_op jit(solution)/shard_map/pallas_call | solution.py:192
  187.3 24.0 %all_to_all.51 = f32[16,16,128]{2,1,0:T(8,128)S(1)} all-to-all(f32[16,16,128]{2,1,0:T(8,128)S(1)} %bitcast.24), channel_id=1, replica_groups=mesh['y'=8,'z'=8,'c'=2,'x'=4] {'y','c'}, dimensions={0} | all-to-all | bytes 262144 | tf_op jit(solution)/shard_map/all_to_all | solution.py:311
  211.4 11.6 %all_to_all.52 = f32[16,16,128]{2,1,0:T(8,128)S(1)} all-to-all(f32[16,16,128]{2,1,0:T(8,128)S(1)} %broadcast_in_dim.86), channel_id=1, replica_groups=mesh['y'=8,'z'=8,'c'=2,'x'=4] {'y','c'}, dimensions={0} | all-to-all | bytes 262144 | tf_op jit(solution)/shard_map/all_to_all | solution.py:311
  223.0 6.3 %shard_map.89 = f32[128,128]{1,0:T(8,128)S(1)} custom-call(s32[128]{0:T(128)S(1)} %get-tuple-element.19.row_at, s32[1,128]{1,0:T(1,128)S(1)} %get-tuple-element.17.col_place, f32[256,128]{1,0:T(8,128)S(1)} %bitcast.20, bf16[128,128,128]{2,1,0:T(8,128)(2,1)} %get-tuple-element.11.kernel), custom_call_target="tpu_custom_call" | custom-call | tf_op jit(solution)/shard_map/pallas_call | solution.py:240
  229.3 10.2 %all_to_all.53 = f32[8,16,128]{2,1,0:T(8,128)S(1)} all-to-all(f32[8,16,128]{2,1,0:T(8,128)S(1)} %bitcast.23), channel_id=1, replica_groups=mesh['y'=8,'z'=8,'c'=2,'x'=4] {'z'}, dimensions={0} | all-to-all | bytes 131072 | tf_op jit(solution)/shard_map/all_to_all | solution.py:311
  239.6 6.7 %all_to_all.54 = f32[4,16,128]{2,1,0:T(8,128)S(1)} all-to-all(f32[4,16,128]{2,1,0:T(8,128)S(1)} %broadcast_in_dim.87), channel_id=1, replica_groups=mesh['y'=8,'z'=8,'c'=2,'x'=4] {'x'}, dimensions={0} | all-to-all | bytes 65536 | tf_op jit(solution)/shard_map/all_to_all | solution.py:311
  246.2 0.6 multiply_bitcast_fusion
  246.8 9.7 %all_to_all.55 = f32[8,16,128]{2,1,0:T(8,128)S(1)} all-to-all(f32[8,16,128]{2,1,0:T(8,128)S(1)} %broadcast_in_dim.88), channel_id=1, replica_groups=mesh['y'=8,'z'=8,'c'=2,'x'=4] {'z'}, dimensions={0} | all-to-all | bytes 131072 | tf_op jit(solution)/shard_map/all_to_all | solution.py:311
  256.5 9.3 %shard_map.90 = f32[16,32,128]{2,1,0:T(8,128)S(1)} custom-call(s32[128]{0:T(128)S(1)} %get-tuple-element.20.col_at, s32[1,128]{1,0:T(1,128)S(1)} %get-tuple-element.18.row_place, f32[128,128]{1,0:T(8,128)S(1)} %bitcast.22, bf16[128,128,128]{2,1,0:T(8,128)(2,1)} %get-tuple-element.11.kernel, bf16[128,128,128]{2,1,0:T(8,128)(2,1)} %get-tuple-element.12.costed), custom_call_target="tpu_custom_call" | custom-call | tf_op jit(solution)/shard_map/pallas_call | solution.py:280
  265.8 17.3 %all_to_all.56 = f32[16,32,128]{2,1,0:T(8,128)S(1)} all-to-all(f32[16,32,128]{2,1,0:T(8,128)S(1)} %shard_map.90), channel_id=1, replica_groups=mesh['y'=8,'z'=8,'c'=2,'x'=4] {'y','c'}, dimensions={0} | all-to-all | bytes 524288 | tf_op jit(solution)/shard_map/all_to_all | solution.py:311
  283.1 0.6 multiply_bitcast_fusion.1
  (61 shorter events, 1.2 us)
Async XLA Ops:
  7.2 78.7 %copy-start = (s32[2048]{0:T(1024)S(1)}, s32[2048]{0:T(1024)}, u32[]{:S(2)}) copy-start(s32[2048]{0:T(1024)} %param.9) | copy-start | bytes 24580
  7.2 117.3 %all-gather.3.cloned.1.call-start = ((), (), s32[]{:S(2)}) async-start(), calls=%async_computation.10 | async-start | bytes 18104320 | tf_op jit(solution)/shard_map/all_gather | solution.py:350
  7.2 1.2 copy-start.2
  8.5 0.9 copy-start.4
  9.4 3.2 %copy-start.5 = (bf16[256,256]{1,0:T(8,128)(2,1)S(1)}, bf16[256,256]{1,0:T(8,128)(2,1)}, u32[]{:S(2)}) copy-start(bf16[256,256]{1,0:T(8,128)(2,1)} %projection.3) | copy-start | bytes 393220
  12.5 1.2 copy-start.3
  13.7 71.8 %copy-start.12 = (s32[16]{0:T(128)S(1)}, s32[16]{0:T(128)}, u32[]{:S(2)}) copy-start(s32[16]{0:T(128)} %param.11) | copy-start | bytes 196
  13.7 71.9 %copy-start.11 = (s32[16,8]{0,1:T(8,128)S(1)}, s32[16,8]{0,1:T(8,128)}, u32[]{:S(2)}) copy-start(s32[16,8]{0,1:T(8,128)} %param.10) | copy-start | bytes 1540
  16.8 35.0 %collective-permute-start.3 = (bf16[2080,256]{1,0:T(8,128)(2,1)}, bf16[2080,256]{1,0:T(8,128)(2,1)S(1)}, u32[]{:S(2)}, u32[]{:S(2)}) collective-permute-start(bf16[2080,256]{1,0:T(8,128)(2,1)} %shard_map.86.rest_0_), channel_id=1, source_target_pairs={{0,8},{8,16},{16,24},{24,32},{32,40},{40,48},{48,56},{56,0},{1,9},... | collective-permute-start | bytes 3194888 | tf_op jit(solution)/shard_map/ppermute | solution.py:301
  21.6 32.1 %collective-permute-start = (bf16[2080,256]{1,0:T(8,128)(2,1)}, bf16[2080,256]{1,0:T(8,128)(2,1)S(1)}, u32[]{:S(2)}, u32[]{:S(2)}) collective-permute-start(bf16[2080,256]{1,0:T(8,128)(2,1)} %shard_map.86.rest_0_), channel_id=1, source_target_pairs={{0,56},{8,0},{16,8},{24,16},{32,24},{40,32},{48,40},{56,48},{1,57}... | collective-permute-start | bytes 3194888 | tf_op jit(solution)/shard_map/ppermute | solution.py:302
  51.9 29.0 %copy-start.8 = (bf16[2080,256]{1,0:T(8,128)(2,1)}, bf16[2080,256]{1,0:T(8,128)(2,1)S(1)}, u32[]{:S(2)}) copy-start(bf16[2080,256]{1,0:T(8,128)(2,1)S(1)} %collective-permute-done.3.rest_7_) | copy-start | bytes 3194884
  51.9 27.1 %collective-permute-start.4 = (bf16[2080,256]{1,0:T(8,128)(2,1)S(1)}, bf16[2080,256]{1,0:T(8,128)(2,1)S(1)}, u32[]{:S(2)}, u32[]{:S(2)}) collective-permute-start(bf16[2080,256]{1,0:T(8,128)(2,1)S(1)} %collective-permute-done.3.rest_7_), channel_id=1, source_target_pairs={{0,8},{8,16},{16,24},{24,32},{32,40},{40,48},{48,56},{56,0},{1,9},... | collective-permute-start | bytes 3194888 | tf_op jit(solution)/shard_map/ppermute | solution.py:301
  53.8 27.1 %copy-start.9 = (bf16[2080,256]{1,0:T(8,128)(2,1)}, bf16[2080,256]{1,0:T(8,128)(2,1)S(1)}, u32[]{:S(2)}) copy-start(bf16[2080,256]{1,0:T(8,128)(2,1)S(1)} %collective-permute-done.rest_1_) | copy-start | bytes 3194884
  53.8 27.1 %collective-permute-start.1 = (bf16[2080,256]{1,0:T(8,128)(2,1)S(1)}, bf16[2080,256]{1,0:T(8,128)(2,1)}, u32[]{:S(2)}, u32[]{:S(2)}) collective-permute-start(bf16[2080,256]{1,0:T(8,128)(2,1)S(1)} %collective-permute-done.rest_1_), channel_id=1, source_target_pairs={{0,56},{8,0},{16,8},{24,16},{32,24},{40,32},{48,40},{56,48},{1,57}... | collective-permute-start | bytes 3194888 | tf_op jit(solution)/shard_map/ppermute | solution.py:302
  78.9 30.0 %copy-start.10 = (bf16[2080,256]{1,0:T(8,128)(2,1)}, bf16[2080,256]{1,0:T(8,128)(2,1)S(1)}, u32[]{:S(2)}) copy-start(bf16[2080,256]{1,0:T(8,128)(2,1)S(1)} %collective-permute-done.4.rest_6_) | copy-start | bytes 3194884
  78.9 26.3 %collective-permute-start.5 = (bf16[2080,256]{1,0:T(8,128)(2,1)S(1)}, bf16[2080,256]{1,0:T(8,128)(2,1)S(1)}, u32[]{:S(2)}, u32[]{:S(2)}) collective-permute-start(bf16[2080,256]{1,0:T(8,128)(2,1)S(1)} %collective-permute-done.4.rest_6_), channel_id=1, source_target_pairs={{0,8},{8,16},{16,24},{24,32},{32,40},{40,48},{48,56},{56,0},{1,9},... | collective-permute-start | bytes 3194888 | tf_op jit(solution)/shard_map/ppermute | solution.py:301
  80.9 27.2 %collective-permute-start.2 = (bf16[2080,256]{1,0:T(8,128)(2,1)}, bf16[2080,256]{1,0:T(8,128)(2,1)S(1)}, u32[]{:S(2)}, u32[]{:S(2)}) collective-permute-start(bf16[2080,256]{1,0:T(8,128)(2,1)} %collective-permute-done.1.rest_2_), channel_id=1, source_target_pairs={{0,56},{8,0},{16,8},{24,16},{32,24},{40,32},{48,40},{56,48},{1,57}... | collective-permute-start | bytes 3194888 | tf_op jit(solution)/shard_map/ppermute | solution.py:302
  88.0 25.8 %all-to-all-start = ((s32[16,1,8]{2,1,0:T(1,128)}), s32[16,1,8]{2,1,0:T(1,128)S(1)}, u32[]{:S(2)}, u32[]{:S(2)}) async-start(s32[16,1,8]{2,1,0:T(1,128)} %bitcast.3), calls=%async_computation | async-start | bytes 16384 | tf_op jit(solution)/shard_map/all_to_all | solution.py:311
  105.2 3.7 %copy-start.6 = (bf16[2080,256]{1,0:T(8,128)(2,1)}, bf16[2080,256]{1,0:T(8,128)(2,1)S(1)}, u32[]{:S(2)}) copy-start(bf16[2080,256]{1,0:T(8,128)(2,1)S(1)} %collective-permute-done.5.rest_5_) | copy-start | bytes 3194884
  106.1 14.2 %collective-permute-start.6 = (bf16[1040,256]{1,0:T(8,128)(2,1)}, bf16[1040,256]{1,0:T(8,128)(2,1)}, u32[]{:S(2)}, u32[]{:S(2)}) collective-permute-start(bf16[1040,256]{1,0:T(8,128)(2,1)} %slice.18), channel_id=1, source_target_pairs={{0,8},{8,16},{16,24},{24,32},{32,40},{40,48},{48,56},{56,0},{1,9},... | collective-permute-start | bytes 1597448 | tf_op jit(solution)/shard_map/ppermute | solution.py:304
  108.1 16.4 %copy-start.7 = (bf16[2080,256]{1,0:T(8,128)(2,1)}, bf16[2080,256]{1,0:T(8,128)(2,1)S(1)}, u32[]{:S(2)}) copy-start(bf16[2080,256]{1,0:T(8,128)(2,1)S(1)} %collective-permute-done.2.rest_3_) | copy-start | bytes 3194884
  109.0 13.2 %collective-permute-start.7 = (bf16[1040,256]{1,0:T(8,128)(2,1)}, bf16[1040,256]{1,0:T(8,128)(2,1)}, u32[]{:S(2)}, u32[]{:S(2)}) collective-permute-start(bf16[1040,256]{1,0:T(8,128)(2,1)} %slice.19), channel_id=1, source_target_pairs={{0,56},{8,0},{16,8},{24,16},{32,24},{40,32},{48,40},{56,48},{1,57}... | collective-permute-start | bytes 1597448 | tf_op jit(solution)/shard_map/ppermute | solution.py:305
  114.3 10.2 %copy-start.1 = (bf16[2080,256]{1,0:T(8,128)(2,1)S(1)}, bf16[2080,256]{1,0:T(8,128)(2,1)}, u32[]{:S(2)}) copy-start(bf16[2080,256]{1,0:T(8,128)(2,1)} %shard_map.86.rest_0_) | copy-start | bytes 3194884
  156.8 8.3 %all-to-all-start.2 = ((f32[4,16,128]{2,1,0:T(8,128)}), f32[4,16,128]{2,1,0:T(8,128)S(1)}, u32[]{:S(2)}, u32[]{:S(2)}) async-start(f32[4,16,128]{2,1,0:T(8,128)} %broadcast_in_dim.53), calls=%async_computation.2 | async-start | bytes 65536 | tf_op jit(solution)/shard_map/all_to_all | solution.py:311
  165.8 10.5 %all-to-all-start.3 = ((f32[8,16,128]{2,1,0:T(8,128)}), f32[8,16,128]{2,1,0:T(8,128)S(1)}, u32[]{:S(2)}, u32[]{:S(2)}) async-start(f32[8,16,128]{2,1,0:T(8,128)} %broadcast_in_dim.54), calls=%async_computation.3 | async-start | bytes 131072 | tf_op jit(solution)/shard_map/all_to_all | solution.py:311
Sparse Core Ops, SparseCore 0:
  12.6 105.0 all-gather.2

commit v2 on v1

v2 whole, which is shorter than its diff:
```python
import math

import jax
import jax.numpy as jnp
from jax import lax
from jax.experimental import pallas as pl
from jax.experimental.pallas import tpu as pltpu
from jax.sharding import Mesh
from jax.sharding import PartitionSpec as P

EPSILON = 0.02
UNMATCHED = 2.0
SLACK = 100.0
SHIFT = 46.0
LOG2E = 1.4426950408889634
SHIFT2 = SHIFT * LOG2E
FLOOR = math.exp(SHIFT - SLACK)
OFF = -1.0e30

BLK = 128
E = 256
NY, NZ, NC, NX = 8, 8, 2, 4
KB = 16
HB = KB // 2
HALF = HB * BLK + 2 * HB
SOURCES = NY * NC
POS = SOURCES * NZ
TILES = 16
STEPS = POS // TILES
BETA = LOG2E * 2.0 / (E * EPSILON)
MIB = 2**20

F32, BF16 = jnp.float32, jnp.bfloat16
NT = (((1,), (1,)), ((), ()))
NN = (((1,), (0,)), ((), ()))
VMEM_WHOLE = pl.BlockSpec(memory_space=pltpu.VMEM)
SMEM_WHOLE = pl.BlockSpec(memory_space=pltpu.SMEM)
ANYWHERE = pl.BlockSpec(memory_space=pl.ANY)
TILE_BLOCK = pl.BlockSpec((TILES, BLK, BLK), lambda s: (s, 0, 0))


def dot(left, right, dims):
    return lax.dot_general(left, right, dims, preferred_element_type=F32)


def exact_sum(onehot, values):
    return lax.dot_general(
        onehot, values, NN, precision=lax.Precision.HIGHEST, preferred_element_type=F32
    )


def spread(places, count):
    rows = lax.broadcasted_iota(jnp.int32, (count, POS), 0)
    return jnp.where(rows == places, 1.0, 0.0)


def project_kernel(frames, projection, out, norms):
    for k in range(KB):
        codes = dot(frames[pl.ds(k * BLK, BLK), :], projection[...], NN).astype(BF16)
        out[k // HB, pl.ds(k % HB * BLK, BLK), :] = codes
        wide = codes.astype(F32)
        square = wide * wide
        high = square.astype(BF16)
        low = (square - high.astype(F32)).astype(BF16)
        ones = jnp.ones((16, E), BF16)
        norms[k : k + 1, :] = (dot(ones, high, NT) + dot(ones, low, NT))[0:1, :]
    for h in range(2):
        norm = norms[h * HB : (h + 1) * HB, :]
        high = norm.astype(BF16).astype(F32)
        middle = (norm - high).astype(BF16).astype(F32)
        low = norm - high - middle
        left = jnp.concatenate([high, low], axis=0)
        right = jnp.concatenate([middle, jnp.zeros_like(low)], axis=0)
        out[h, HB * BLK : HALF, :] = jnp.concatenate([left, right], axis=1).astype(BF16)


def project(frames, projection):
    return pl.pallas_call(
        project_kernel,
        out_shape=jax.ShapeDtypeStruct((2, HALF, E), BF16),
        in_specs=[VMEM_WHOLE] * 2,
        out_specs=VMEM_WHOLE,
        scratch_shapes=[pltpu.VMEM((KB, BLK), F32)],
        compiler_params=pltpu.CompilerParams(vmem_limit_bytes=60 * MIB),
    )(frames, projection)


def first_kernel(code, col_place, left, *rest):
    rights = rest[: 2 * NZ]
    cross, columns, sums, taken, tails, held, picks, norms, sems, right_sem = rest[2 * NZ :]
    step = pl.program_id(0)

    def moves(step):
        slot = step % 2
        copies = []
        for z in range(NZ):
            k = jnp.maximum(code[step * NZ + z], 0) // KB
            start = pl.multiple_of(k % HB * BLK, BLK)
            copies.append((left.at[step, k // HB, pl.ds(start, BLK)], taken.at[slot, z]))
        for h in range(2):
            copies.append((left.at[step, h, pl.ds(HB * BLK, 2 * HB)], tails.at[slot, h]))
        return [
            pltpu.make_async_copy(a, b, sems.at[slot, n]) for n, (a, b) in enumerate(copies)
        ]

    into = [
        pltpu.make_async_copy(rights[i], held.at[i // 2, i % 2], right_sem.at[i])
        for i in range(2 * NZ)
    ]
    @pl.when(step == 0)
    def _():
        for copy in moves(0) + into:
            copy.start()
        row = lax.broadcasted_iota(jnp.int32, (4 * KB, BLK), 0)
        for k in range(KB):
            ours = (row // (2 * KB) == k // HB) & (row % HB == k % HB)
            picks[k] = jnp.where(ours, -0.5, 0.0).astype(BF16)
        for copy in into:
            copy.wait()
        for i in range(2 * NZ):
            tail = held[i // 2, i % 2, HB * BLK : HALF, :].astype(F32)
            norm = tail[0:HB, 0:BLK] + tail[0:HB, BLK:E] + tail[HB : 2 * HB, 0:BLK]
            norms[i * HB : (i + 1) * HB, :] = 0.5 * norm

    @pl.when(step + 1 < SOURCES)
    def _():
        for copy in moves(step + 1):
            copy.start()

    for copy in moves(step):
        copy.wait()
    slot = step % 2
    stacked = []
    for h in range(2):
        tail = tails[slot, h].astype(F32)
        stacked += [tail[:, 0:BLK], tail[:, BLK:E]]
    parts = jnp.concatenate(stacked, axis=0).T.astype(BF16)
    rows = []
    for z in range(NZ):
        value = code[step * NZ + z]
        off = jnp.where(value >= 0, SHIFT2, OFF)
        value = jnp.maximum(value, 0)
        k, t = value // KB, value % KB
        v = held[z, t // HB, pl.ds(pl.multiple_of(t % HB * BLK, BLK), BLK), :]
        w = dot(taken[slot, z], v, NT) + dot(parts, picks[k], NN)
        w = w - norms[pl.ds(z * KB + t, 1), :]
        cross[z] = w
        rows.append(jnp.sum(jnp.exp2(w * BETA + off), axis=0, keepdims=True))
    sums[pl.ds(pl.multiple_of(step * NZ, NZ), NZ), :] = jnp.concatenate(rows, axis=0)

    @pl.when(step == SOURCES - 1)
    def _():
        columns[...] = exact_sum(spread(col_place[...], NZ * KB), sums[...]).astype(BF16)


def first_pass(code, col_place, left, rights):
    return pl.pallas_call(
        first_kernel,
        grid=(SOURCES,),
        in_specs=[SMEM_WHOLE, VMEM_WHOLE, ANYWHERE] + [ANYWHERE] * (2 * NZ),
        out_specs=[pl.BlockSpec((NZ, BLK, BLK), lambda s: (s, 0, 0)), VMEM_WHOLE],
        scratch_shapes=[
            pltpu.VMEM((POS, BLK), F32),
            pltpu.VMEM((2, NZ, BLK, E), BF16),
            pltpu.VMEM((2, 2, 2 * HB, E), BF16),
            pltpu.VMEM((NZ, 2, HALF, E), BF16),
            pltpu.VMEM((KB, 4 * KB, BLK), BF16),
            pltpu.VMEM((NZ * KB, BLK), F32),
            pltpu.SemaphoreType.DMA((2, NZ + 2)),
            pltpu.SemaphoreType.DMA((2 * NZ,)),
        ],
        out_shape=[
            jax.ShapeDtypeStruct((POS, BLK, BLK), F32),
            jax.ShapeDtypeStruct((NZ * KB, BLK), BF16),
        ],
        compiler_params=pltpu.CompilerParams(vmem_limit_bytes=60 * MIB),
    )(code, col_place, left, *rights)


def total_of(received):
    total = received[0].astype(F32)
    for n in range(1, received.shape[0]):
        total += received[n].astype(F32)
    return total


def second_kernel(col_at, row_place, received, cross, kernel, costed, rows_out, column_sum, potential, sums):
    step = pl.program_id(0)

    @pl.when(step == 0)
    def _():
        column_sum[...] = total_of(received)
        potential[...] = 2.0 * SHIFT2 - jnp.log2(FLOOR + column_sum[...])

    ones = jnp.ones((16, BLK), BF16)
    rows = []
    for n in range(TILES):
        at = col_at[step * TILES + n]
        pot = potential[pl.ds(jnp.maximum(at, 0), 1), :] + jnp.where(at >= 0, 0.0, OFF)
        w = cross[n]
        rounded = jnp.exp2(w * BETA + pot).astype(BF16)
        kernel[n] = rounded
        costed[n] = (rounded.astype(F32) * (w * (-2.0 / E))).astype(BF16)
        rows.append(dot(ones, rounded, NT)[0:1, :])
    sums[pl.ds(pl.multiple_of(step * TILES, TILES), TILES), :] = jnp.concatenate(rows, axis=0)

    @pl.when(step == STEPS - 1)
    def _():
        rows_out[...] = exact_sum(spread(row_place[...], SOURCES * KB), sums[...]).astype(BF16)


def second_pass(col_at, row_place, received, cross):
    return pl.pallas_call(
        second_kernel,
        grid=(STEPS,),
        in_specs=[SMEM_WHOLE, VMEM_WHOLE, VMEM_WHOLE, TILE_BLOCK],
        out_specs=[TILE_BLOCK, TILE_BLOCK, VMEM_WHOLE, VMEM_WHOLE],
        scratch_shapes=[pltpu.VMEM((NZ * KB, BLK), F32), pltpu.VMEM((POS, BLK), F32)],
        out_shape=[
            jax.ShapeDtypeStruct((POS, BLK, BLK), BF16),
            jax.ShapeDtypeStruct((POS, BLK, BLK), BF16),
            jax.ShapeDtypeStruct((SOURCES * KB, BLK), BF16),
            jax.ShapeDtypeStruct((NZ * KB, BLK), F32),
        ],
        compiler_params=pltpu.CompilerParams(vmem_limit_bytes=60 * MIB),
    )(col_at, row_place, received, cross)


def two_parts(row):
    high = row.astype(BF16).astype(F32)
    at = lax.broadcasted_iota(jnp.int32, (16, BLK), 0)
    return jnp.where(at == 0, high, jnp.where(at == 1, row - high, 0.0)).astype(BF16)


def third_kernel(row_at, col_place, received, kernel, columns, scale, sums):
    step = pl.program_id(0)

    @pl.when(step == 0)
    def _():
        scale[...] = 1.0 / (FLOOR + received[...].astype(F32))

    rows = []
    for n in range(TILES):
        at = jnp.maximum(row_at[step * TILES + n], 0)
        both = dot(two_parts(scale[pl.ds(at, 1), :]), kernel[n], NN)
        rows.append(both[0:1, :] + both[1:2, :])
    sums[pl.ds(pl.multiple_of(step * TILES, TILES), TILES), :] = jnp.concatenate(rows, axis=0)

    @pl.when(step == STEPS - 1)
    def _():
        columns[...] = exact_sum(spread(col_place[...], NZ * KB), sums[...]).astype(BF16)


def third_pass(row_at, col_place, received, kernel):
    return pl.pallas_call(
        third_kernel,
        grid=(STEPS,),
        in_specs=[SMEM_WHOLE, VMEM_WHOLE, VMEM_WHOLE, TILE_BLOCK],
        out_specs=VMEM_WHOLE,
        scratch_shapes=[pltpu.VMEM((SOURCES * KB, BLK), F32), pltpu.VMEM((POS, BLK), F32)],
        out_shape=jax.ShapeDtypeStruct((NZ * KB, BLK), BF16),
        compiler_params=pltpu.CompilerParams(vmem_limit_bytes=60 * MIB),
    )(row_at, col_place, received, kernel)


def fourth_kernel(col_at, row_place, received, column_sum, kernel, costed, rows_out, plan_out, scale, sums, weighed):
    step = pl.program_id(0)

    @pl.when(step == 0)
    def _():
        plan_sum = total_of(received)
        plan_out[...] = plan_sum
        scale[...] = 1.0 / (FLOOR / (FLOOR + column_sum[...]) + plan_sum)

    rows, heavy = [], []
    for n in range(TILES):
        pair = two_parts(scale[pl.ds(jnp.maximum(col_at[step * TILES + n], 0), 1), :])
        both = dot(pair, kernel[n], NT)
        rows.append(both[0:1, :] + both[1:2, :])
        both = dot(pair, costed[n], NT)
        heavy.append(both[0:1, :] + both[1:2, :])
    place = pl.ds(pl.multiple_of(step * TILES, TILES), TILES)
    sums[place, :] = jnp.concatenate(rows, axis=0)
    weighed[place, :] = jnp.concatenate(heavy, axis=0)

    @pl.when(step == STEPS - 1)
    def _():
        which = spread(row_place[...], SOURCES * KB)
        total = exact_sum(which, sums[...])
        heavy_total = exact_sum(which, weighed[...])
        for s in range(SOURCES):
            c, y = s // NY, s % NY
            rows_out[y * NC + c, 0:KB, :] = total[s * KB : (s + 1) * KB, :]
            rows_out[y * NC + c, KB : 2 * KB, :] = heavy_total[s * KB : (s + 1) * KB, :]


def fourth_pass(col_at, row_place, received, column_sum, kernel, costed):
    return pl.pallas_call(
        fourth_kernel,
        grid=(STEPS,),
        in_specs=[SMEM_WHOLE] + [VMEM_WHOLE] * 3 + [TILE_BLOCK] * 2,
        out_specs=[VMEM_WHOLE] * 2,
        scratch_shapes=[pltpu.VMEM((NZ * KB, BLK), F32)] + [pltpu.VMEM((POS, BLK), F32)] * 2,
        out_shape=[
            jax.ShapeDtypeStruct((SOURCES, 2 * KB, BLK), F32),
            jax.ShapeDtypeStruct((NZ * KB, BLK), F32),
        ],
        compiler_params=pltpu.CompilerParams(vmem_limit_bytes=60 * MIB),
    )(col_at, row_place, received, column_sum, kernel, costed)


def ring_pieces(block, axis, n):
    up = [(i, (i + 1) % n) for i in range(n)]
    down = [(i, (i - 1) % n) for i in range(n)]
    top, low = block[0], block[1]
    held = [[top, low]] + [[None, None] for _ in range(n - 1)]
    right, left = [top, low], [low, top]
    for k in range(1, n // 2 + 1):
        for i in range(2 if k < n // 2 else 1):
            right[i] = lax.ppermute(right[i], axis, up)
            left[i] = lax.ppermute(left[i], axis, down)
            held[n - k][i] = right[i]
            held[k][1 - i] = left[i]
    return [half for pair in held for half in pair]


def swap(value, axes):
    return lax.all_to_all(value, axes, split_axis=0, concat_axis=0, tiled=True)


def to_all(value, axes, n):
    return swap(jnp.broadcast_to(value[None], (n,) + value.shape), axes)


def columns_to_row(columns):
    over_rep = jnp.sum(to_all(columns, "x", NX).astype(F32), axis=0)
    return to_all(over_rep.astype(BF16), "z", NZ)


def own_columns(columns):
    at = lax.axis_index("z") * KB
    return lax.dynamic_slice_in_dim(columns, at, KB, 0)


def slot_codes(location, pair_block, pair_count):
    slots = pair_block.shape[1]
    stored = location[pair_block.reshape(-1)]
    used = (
        jnp.arange(slots, dtype=jnp.int32)[None, :] < pair_count[:, None]
    ).reshape(-1)
    block = jnp.arange(KB * slots, dtype=jnp.int32) // slots
    owner, local = stored // KB, stored % KB
    holders = jnp.arange(NY * NZ * NC, dtype=jnp.int32)
    match = (owner[None, :] == holders[:, None]) & used[None, :]
    return jnp.max(jnp.where(match, (block * KB + local)[None, :], -1), axis=1)


def body(rollout, demo, projection, location, pair_block, pair_count):
    codes = slot_codes(location, pair_block, pair_count)
    codes = codes.reshape(NY, NZ, NC).transpose(0, 2, 1).reshape(SOURCES, NZ)
    codes = swap(codes[:, None, :], ("y", "c")).reshape(SOURCES, NZ)
    turned = (lax.axis_index("z") + jnp.arange(NZ, dtype=jnp.int32)) % NZ
    pick = turned[:, None] == jnp.arange(NZ, dtype=jnp.int32)[None, :]
    codes = jnp.max(jnp.where(pick[None], codes[:, None, :], -1), axis=2)
    used = codes >= 0
    col_at = jnp.where(used, turned[None, :] * KB + codes % KB, -1).reshape(POS)
    source = jnp.arange(SOURCES, dtype=jnp.int32)
    source = (source % NC * NY + source // NC)[:, None]
    row_at = jnp.where(used, source * KB + codes // KB, -1).reshape(POS)
    col_place, row_place = col_at.reshape(1, POS), row_at.reshape(1, POS)
    codes = codes.reshape(POS)

    left = lax.all_gather(project(rollout, projection), ("y", "c"))
    rights = ring_pieces(project(demo, projection), "z", NZ)

    cross, columns = first_pass(codes, col_place, left, rights)
    kernel, costed, rows, column_sum = second_pass(
        col_at, row_place, columns_to_row(columns), cross
    )
    rows = jnp.sum(swap(rows.reshape(NC, NY * KB, BLK), "c").astype(F32), axis=0)
    rows = jnp.sum(to_all(rows.astype(BF16), "y", NY).astype(F32), axis=0)
    rows = to_all(rows.astype(BF16), "c", NC).reshape(SOURCES * KB, BLK)
    columns = third_pass(row_at, col_place, rows, kernel)
    both, plan_sum = fourth_pass(
        col_at, row_place, columns_to_row(columns), column_sum, kernel, costed
    )
    both = jnp.sum(swap(both, ("y", "c")), axis=0)
    total = FLOOR + both[:KB]
    reward = -(both[KB:] + UNMATCHED * FLOOR) / total
    roll_pot = EPSILON * (SHIFT - jnp.log(total))
    reached = FLOOR + (FLOOR + own_columns(column_sum)) * own_columns(plan_sum)
    demo_pot = EPSILON * (SHIFT - jnp.log(reached))
    return reward.reshape(-1), roll_pot.reshape(-1), demo_pot.reshape(-1)


def solution(mesh):
    grid = Mesh(mesh.devices.reshape(NY, NZ, NC, NX), ("y", "z", "c", "x"))
    every, roll = ("y", "z", "c", "x"), ("y", "z", "c")
    return jax.shard_map(
        body,
        mesh=grid,
        in_specs=(P(every, None), P(roll, None), P(), P(), P(every, None), P(every)),
        out_specs=(P(every), P(every), P(roll)),
        check_vma=False,
    )
```

time: 292 us -> 270 us (0.925)
  blocking collectives: 91.1 us -> 58 us
  starting transfers between devices: 49.8 us -> 76.3 us
  waiting for transfers between devices: 68.9 us -> 50.9 us
    all_to_all x7 -> x6, blocking collectives: 91.1 us -> 58 us  [swap(): return lax.all_to_all(value, axes, split_axis=0, concat_axis=0, tiled=True)]
    ppermute x8 -> x14, waiting for transfers between devices: 57.6 us -> 28.1 us  [the longest x7 18 us: ring_pieces(): right[i] = lax.ppermute(right[i], axis, up)]
    ppermute x8 -> x14, starting transfers between devices: 32.8 us -> 52.9 us  [the longest x7 39.5 us: ring_pieces(): left[i] = lax.ppermute(left[i], axis, down)]
    all_to_all x3, waiting for transfers between devices: 11.3 us -> 19 us  [swap(): return lax.all_to_all(value, axes, split_axis=0, concat_axis=0, tiled=True)]
    all_to_all x3, starting transfers between devices: 16.9 us -> 23.4 us  [swap(): return lax.all_to_all(value, axes, split_axis=0, concat_axis=0, tiled=True)]
    all_gather x1, waiting for transfers between devices: 0.01 us -> 3.73 us  [body(): left = lax.all_gather(project(rollout, projection), ('y', 'c'))]
  transfers between devices with their start and end apart: 12 -> 18, of which waited for: 7 -> 8; matrix products, arithmetic and copies ran while one was open for 3% -> 3% of each run, Pallas kernels for 1% -> 2%
where the time goes in v2:
time: 270 us; the launch traced here: 267 us
  starting transfers between devices  76.3 us (28%)
  blocking collectives  58 us (21%)
  Pallas kernels  55.8 us (21%)
  waiting for transfers between devices  50.9 us (19%)
  between operations  14.5 us (5%)
  local copies, waits for them, and re-layouts  7.88 us (3%)
  other arithmetic  3.61 us (1%)
    all_to_all x6, blocking collectives, swap(): return lax.all_to_all(value, axes, split_axis=0, concat_axis=0, tiled=True)  58 us
    ppermute x7, starting transfers between devices, ring_pieces(): left[i] = lax.ppermute(left[i], axis, down)  39.5 us
    all_to_all x3, starting transfers between devices, swap(): return lax.all_to_all(value, axes, split_axis=0, concat_axis=0, tiled=True)  23.4 us
    pallas_call x1, Pallas kernels, first_pass(): pl.pallas_call(first_kernel, grid=(SOURCES,), in_specs=[SMEM_WHOLE, VMEM_...  20.4 us
    all_to_all x3, waiting for transfers between devices, swap(): return lax.all_to_all(value, axes, split_axis=0, concat_axis=0, tiled=True)  19 us
    ppermute x7, waiting for transfers between devices, ring_pieces(): right[i] = lax.ppermute(right[i], axis, up)  18 us
    ppermute x7, starting transfers between devices, ring_pieces(): right[i] = lax.ppermute(right[i], axis, up)  13.4 us
    pallas_call x1, Pallas kernels, second_pass(): pl.pallas_call(second_kernel, grid=(STEPS,), in_specs=[SMEM_WHOLE, VMEM_W...  10.7 us
  transfers between devices with their start and end apart: 18, of which 8 were waited for; matrix products, arithmetic and copies ran while one was open for 3% of the time, Pallas kernels for 2%

profile of v2, /device:TPU:1, one launch (start us, length us, event | category | flops | bytes accessed | tf_op | source)
XLA Modules:
  0.0 267.0 jit_solution(2630200743859409310)
XLA Ops:
  7.2 4.3 %shard_map.85 = bf16[2,1040,256]{2,1,0:T(8,128)(2,1)} custom-call(bf16[2048,256]{1,0:T(8,128)(2,1)} %frames.2, bf16[256,256]{1,0:T(8,128)(2,1)} %projection.3), custom_call_target="tpu_custom_call" | custom-call | tf_op jit(solution)/shard_map/pallas_call | solution.py:78
  11.6 4.3 %shard_map.86 = bf16[2,1040,256]{2,1,0:T(8,128)(2,1)} custom-call(bf16[2048,256]{1,0:T(8,128)(2,1)} %frames.3, bf16[256,256]{1,0:T(8,128)(2,1)} %projection.3), custom_call_target="tpu_custom_call" | custom-call | tf_op jit(solution)/shard_map/pallas_call | solution.py:78
  15.9 1.3 slice_bitcast_fusion
  17.2 11.5 %collective-permute-start.1 = (bf16[1040,256]{1,0:T(8,128)(2,1)S(1)}, bf16[1040,256]{1,0:T(8,128)(2,1)S(1)}, u32[]{:S(2)}, u32[]{:S(2)}) collective-permute-start(bf16[1040,256]{1,0:T(8,128)(2,1)S(1)} %get-tuple-element.19.rest_1_), channel_id=1, source_target_pairs={{0,56},{8,0},{16,8},{24,16},{32,24},{40,32},{48,40},{56,48},{1,57}... | collective-permute-start | bytes 1597448 | tf_op jit(solution)/shard_map/ppermute | solution.py:321
  28.7 1.9 collective-permute-start.6
  30.7 1.9 collective-permute-start.11
  32.6 4.6 %collective-permute-start = (bf16[1040,256]{1,0:T(8,128)(2,1)S(1)}, bf16[1040,256]{1,0:T(8,128)(2,1)S(1)}, u32[]{:S(2)}, u32[]{:S(2)}) collective-permute-start(bf16[1040,256]{1,0:T(8,128)(2,1)S(1)} %get-tuple-element.20.rest_0_), channel_id=1, source_target_pairs={{0,56},{8,0},{16,8},{24,16},{32,24},{40,32},{48,40},{56,48},{1,57}... | collective-permute-start | bytes 1597448 | tf_op jit(solution)/shard_map/ppermute | solution.py:321
  37.3 2.1 collective-permute-done.1.rest_3_
  39.5 5.4 %collective-permute-start.3 = (bf16[1040,256]{1,0:T(8,128)(2,1)S(1)}, bf16[1040,256]{1,0:T(8,128)(2,1)}, u32[]{:S(2)}, u32[]{:S(2)}) collective-permute-start(bf16[1040,256]{1,0:T(8,128)(2,1)S(1)} %collective-permute-done.1.rest_3_), channel_id=1, source_target_pairs={{0,56},{8,0},{16,8},{24,16},{32,24},{40,32},{48,40},{56,48},{1,57}... | collective-permute-start | bytes 1597448 | tf_op jit(solution)/shard_map/ppermute | solution.py:321
  44.9 1.9 collective-permute-start.7
  46.9 1.1 gather_fusion
  48.1 7.9 %collective-permute-done.11.rest_15_ = bf16[1040,256]{1,0:T(8,128)(2,1)S(1)} collective-permute-done((bf16[1040,256]{1,0:T(8,128)(2,1)S(1)}, bf16[1040,256]{1,0:T(8,128)(2,1)S(1)}, u32[]{:S(2)}, u32[]{:S(2)}) %collective-permute-start.11) | collective-permute-done | bytes 532512 | tf_op jit(solution)/shard_map/ppermute | solution.py:320
  56.0 1.9 collective-permute-start.12
  58.0 4.6 %collective-permute-start.2 = (bf16[1040,256]{1,0:T(8,128)(2,1)S(1)}, bf16[1040,256]{1,0:T(8,128)(2,1)}, u32[]{:S(2)}, u32[]{:S(2)}) collective-permute-start(bf16[1040,256]{1,0:T(8,128)(2,1)S(1)} %collective-permute-done.rest_2_), channel_id=1, source_target_pairs={{0,56},{8,0},{16,8},{24,16},{32,24},{40,32},{48,40},{56,48},{1,57}... | collective-permute-start | bytes 1597448 | tf_op jit(solution)/shard_map/ppermute | solution.py:321
  62.5 5.2 %collective-permute-start.5 = (bf16[1040,256]{1,0:T(8,128)(2,1)}, bf16[1040,256]{1,0:T(8,128)(2,1)}, u32[]{:S(2)}, u32[]{:S(2)}) collective-permute-start(bf16[1040,256]{1,0:T(8,128)(2,1)} %collective-permute-done.3.rest_5_), channel_id=1, source_target_pairs={{0,56},{8,0},{16,8},{24,16},{32,24},{40,32},{48,40},{56,48},{1,57}... | collective-permute-start | bytes 1597448 | tf_op jit(solution)/shard_map/ppermute | solution.py:321
  67.7 1.9 collective-permute-start.8
  70.0 0.7 copy.23
  70.8 10.1 %all-to-all-start = ((s32[16,1,8]{2,1,0:T(1,128)}), s32[16,1,8]{2,1,0:T(1,128)S(1)}, u32[]{:S(2)}, u32[]{:S(2)}) async-start(s32[16,1,8]{2,1,0:T(1,128)} %bitcast.3), calls=%async_computation | async-start | bytes 16384 | tf_op jit(solution)/shard_map/all_to_all | solution.py:328
  81.0 1.9 collective-permute-start.13
  82.9 4.9 %collective-permute-start.4 = (bf16[1040,256]{1,0:T(8,128)(2,1)}, bf16[1040,256]{1,0:T(8,128)(2,1)}, u32[]{:S(2)}, u32[]{:S(2)}) collective-permute-start(bf16[1040,256]{1,0:T(8,128)(2,1)} %collective-permute-done.2.rest_4_), channel_id=1, source_target_pairs={{0,56},{8,0},{16,8},{24,16},{32,24},{40,32},{48,40},{56,48},{1,57}... | collective-permute-start | bytes 1597448 | tf_op jit(solution)/shard_map/ppermute | solution.py:321
  87.8 3.4 %collective-permute-start.10 = (bf16[1040,256]{1,0:T(8,128)(2,1)}, bf16[1040,256]{1,0:T(8,128)(2,1)}, u32[]{:S(2)}, u32[]{:S(2)}) collective-permute-start(bf16[1040,256]{1,0:T(8,128)(2,1)} %collective-permute-done.5.rest_7_), channel_id=1, source_target_pairs={{0,56},{8,0},{16,8},{24,16},{32,24},{40,32},{48,40},{56,48},{1,57}... | collective-permute-start | bytes 1597448 | tf_op jit(solution)/shard_map/ppermute | solution.py:321
  91.2 1.9 collective-permute-start.9
  93.7 0.6 reduce_max.24.code
  94.3 0.6 compare_select_fusion.12
  95.0 6.7 %collective-permute-done.13.rest_11_ = bf16[1040,256]{1,0:T(8,128)(2,1)} collective-permute-done((bf16[1040,256]{1,0:T(8,128)(2,1)}, bf16[1040,256]{1,0:T(8,128)(2,1)}, u32[]{:S(2)}, u32[]{:S(2)}) %collective-permute-start.13) | collective-permute-done | bytes 532512 | tf_op jit(solution)/shard_map/ppermute | solution.py:320
  101.7 8.0 %collective-permute-done.10.rest_9_ = bf16[1040,256]{1,0:T(8,128)(2,1)} collective-permute-done((bf16[1040,256]{1,0:T(8,128)(2,1)}, bf16[1040,256]{1,0:T(8,128)(2,1)}, u32[]{:S(2)}, u32[]{:S(2)}) %collective-permute-start.10) | collective-permute-done | bytes 532512 | tf_op jit(solution)/shard_map/ppermute | solution.py:321
  109.7 3.4 %collective-permute-done.9.rest_8_ = bf16[1040,256]{1,0:T(8,128)(2,1)} collective-permute-done((bf16[1040,256]{1,0:T(8,128)(2,1)}, bf16[1040,256]{1,0:T(8,128)(2,1)}, u32[]{:S(2)}, u32[]{:S(2)}) %collective-permute-start.9) | collective-permute-done | bytes 532512 | tf_op jit(solution)/shard_map/ppermute | solution.py:320
  113.1 3.7 %all-gather.3.cloned.1.call-done = bf16[32,1040,256]{2,1,0:T(8,128)(2,1)} async-done(((bf16[2,1040,256]{2,1,0:T(8,128)(2,1)}), bf16[32,1040,256]{2,1,0:T(8,128)(2,1)}) %all-gather.3.cloned.1.call-update) | async-done | bytes 17039376 | tf_op jit(solution)/shard_map/all_gather | solution.py:373
  116.8 20.4 %shard_map.87 = (f32[128,128,128]{2,1,0:T(8,128)}, bf16[128,128]{1,0:T(8,128)(2,1)}) custom-call(s32[128]{0:T(128)} %reduce_max.24.code, s32[1,128]{1,0:T(1,128)} %get-tuple-element.23.col_place, bf16[16,2,1040,256]{3,2,1,0:T(8,128)(2,1)} %bitcast.20, bf16[1040,256]{1,0:T(8,128)(2,1)} %copy-done.2, bf16[1040,256]{1,0:T(8,128)(2,1)} %copy-done.1, ...), custom_call_target="tpu_custom_call" | custom-call | tf_op jit(solution)/shard_map/pallas_call | solution.py:157
  137.2 0.8 broadcast_in_dim.55
  138.0 8.3 %all_to_all.45 = bf16[4,128,128]{2,1,0:T(8,128)(2,1)S(1)} all-to-all(bf16[4,128,128]{2,1,0:T(8,128)(2,1)S(1)} %broadcast_in_dim.55), channel_id=1, replica_groups=mesh['y'=8,'z'=8,'c'=2,'x'=4] {'x'}, dimensions={0} | all-to-all | bytes 262144 | tf_op jit(solution)/shard_map/all_to_all | solution.py:328
  146.3 0.7 broadcast_in_dim.56
  147.1 7.3 %all-to-all-start.2 = ((bf16[8,128,128]{2,1,0:T(8,128)(2,1)}), bf16[8,128,128]{2,1,0:T(8,128)(2,1)S(1)}, u32[]{:S(2)}, u32[]{:S(2)}) async-start(bf16[8,128,128]{2,1,0:T(8,128)(2,1)} %broadcast_in_dim.56), calls=%async_computation.2 | async-start | bytes 524288 | tf_op jit(solution)/shard_map/all_to_all | solution.py:328
  155.1 8.5 %all-to-all-done.2.received = bf16[8,128,128]{2,1,0:T(8,128)(2,1)S(1)} async-done(((bf16[8,128,128]{2,1,0:T(8,128)(2,1)}), bf16[8,128,128]{2,1,0:T(8,128)(2,1)S(1)}, u32[]{:S(2)}, u32[]{:S(2)}) %all-to-all-start.2) | async-done | bytes 262176 | tf_op jit(solution)/shard_map/all_to_all | solution.py:328
  163.6 0.7 copy-done.3
  164.3 10.7 %shard_map.88 = (bf16[128,128,128]{2,1,0:T(8,128)(2,1)}, bf16[128,128,128]{2,1,0:T(8,128)(2,1)}, bf16[256,128]{1,0:T(8,128)(2,1)}, f32[128,128]{1,0:T(8,128)}) custom-call(s32[128]{0:T(128)} %get-tuple-element.26.col_at, s32[1,128]{1,0:T(1,128)} %get-tuple-element.24.row_place, bf16[8,128,128]{2,1,0:T(8,128)(2,1)} %copy-done.3, ...), custom_call_target="tpu_custom_call" | custom-call | tf_op jit(solution)/shard_map/pallas_call | solution.py:213
  175.0 8.0 %all_to_all.46 = bf16[2,128,128]{2,1,0:T(8,128)(2,1)S(1)} all-to-all(bf16[2,128,128]{2,1,0:T(8,128)(2,1)} %bitcast.23), channel_id=1, replica_groups=mesh['y'=8,'z'=8,'c'=2,'x'=4] {'c'}, dimensions={0} | all-to-all | bytes 131072 | tf_op jit(solution)/shard_map/all_to_all | solution.py:328
  183.1 15.4 %all_to_all.47 = bf16[8,128,128]{2,1,0:T(8,128)(2,1)S(1)} all-to-all(bf16[8,128,128]{2,1,0:T(8,128)(2,1)S(1)} %broadcast_in_dim.57), channel_id=1, replica_groups=mesh['y'=8,'z'=8,'c'=2,'x'=4] {'y'}, dimensions={0} | all-to-all | bytes 524288 | tf_op jit(solution)/shard_map/all_to_all | solution.py:328
  198.5 5.8 %all_to_all.48 = bf16[2,128,128]{2,1,0:T(8,128)(2,1)} all-to-all(bf16[2,128,128]{2,1,0:T(8,128)(2,1)S(1)} %broadcast_in_dim.58), channel_id=1, replica_groups=mesh['y'=8,'z'=8,'c'=2,'x'=4] {'c'}, dimensions={0} | all-to-all | bytes 131072 | tf_op jit(solution)/shard_map/all_to_all | solution.py:328
  204.3 6.4 %shard_map.89 = bf16[128,128]{1,0:T(8,128)(2,1)} custom-call(s32[128]{0:T(128)} %get-tuple-element.25.row_at, s32[1,128]{1,0:T(1,128)} %get-tuple-element.23.col_place, bf16[256,128]{1,0:T(8,128)(2,1)} %bitcast.21, bf16[128,128,128]{2,1,0:T(8,128)(2,1)} %get-tuple-element.14.kernel), custom_call_target="tpu_custom_call" | custom-call | tf_op jit(solution)/shard_map/pallas_call | solution.py:255
  210.8 0.8 broadcast_in_dim.94
  211.5 7.2 %all_to_all.49 = bf16[4,128,128]{2,1,0:T(8,128)(2,1)S(1)} all-to-all(bf16[4,128,128]{2,1,0:T(8,128)(2,1)S(1)} %broadcast_in_dim.94), channel_id=1, replica_groups=mesh['y'=8,'z'=8,'c'=2,'x'=4] {'x'}, dimensions={0} | all-to-all | bytes 262144 | tf_op jit(solution)/shard_map/all_to_all | solution.py:328
  218.8 13.2 %all_to_all.50.received = bf16[8,128,128]{2,1,0:T(8,128)(2,1)} all-to-all(bf16[8,128,128]{2,1,0:T(8,128)(2,1)S(1)} %broadcast_in_dim.95), channel_id=1, replica_groups=mesh['y'=8,'z'=8,'c'=2,'x'=4] {'z'}, dimensions={0} | all-to-all | bytes 524288 | tf_op jit(solution)/shard_map/all_to_all | solution.py:328
  232.1 9.6 %shard_map.90 = (f32[16,32,128]{2,1,0:T(8,128)}, f32[128,128]{1,0:T(8,128)}) custom-call(s32[128]{0:T(128)} %get-tuple-element.26.col_at, s32[1,128]{1,0:T(1,128)} %get-tuple-element.24.row_place, bf16[8,128,128]{2,1,0:T(8,128)(2,1)} %all_to_all.50.received, f32[128,128]{1,0:T(8,128)} %get-tuple-element.15.column_sum, ...), custom_call_target="tpu_custom_call" | custom-call | tf_op jit(solution)/shard_map/pallas_call | solution.py:298
  241.7 6.0 %all-to-all-start.8 = ((f32[16,32,128]{2,1,0:T(8,128)}), f32[16,32,128]{2,1,0:T(8,128)S(1)}, u32[]{:S(2)}, u32[]{:S(2)}) async-start(f32[16,32,128]{2,1,0:T(8,128)} %get-tuple-element.17), calls=%async_computation.8 | async-start | bytes 524288 | tf_op jit(solution)/shard_map/all_to_all | solution.py:328
  247.7 1.3 multiply_bitcast_fusion
  249.0 10.5 %all-to-all-done.8 = f32[16,32,128]{2,1,0:T(8,128)S(1)} async-done(((f32[16,32,128]{2,1,0:T(8,128)}), f32[16,32,128]{2,1,0:T(8,128)S(1)}, u32[]{:S(2)}, u32[]{:S(2)}) %all-to-all-start.8) | async-done | bytes 262176 | tf_op jit(solution)/shard_map/all_to_all | solution.py:328
  259.6 0.6 multiply_bitcast_fusion.1
  (65 shorter events, 2.3 us)
Async XLA Ops:
  7.2 39.7 %copy-start = (s32[2048]{0:T(1024)S(1)}, s32[2048]{0:T(1024)}, u32[]{:S(2)}) copy-start(s32[2048]{0:T(1024)} %param.9) | copy-start | bytes 24580
  7.2 30.0 %copy-start.9 = (s32[16,8]{0,1:T(8,128)S(1)}, s32[16,8]{0,1:T(8,128)}, u32[]{:S(2)}) copy-start(s32[16,8]{0,1:T(8,128)} %param.10) | copy-start | bytes 1540
  7.2 40.9 %copy-start.10 = (s32[16]{0:T(128)S(1)}, s32[16]{0:T(128)}, u32[]{:S(2)}) copy-start(s32[16]{0:T(128)} %param.11) | copy-start | bytes 196
  7.2 109.6 %all-gather.3.cloned.1.call-start = ((), (), s32[]{:S(2)}) async-start(), calls=%async_computation.9 | async-start | bytes 18104320 | tf_op jit(solution)/shard_map/all_gather | solution.py:373
  17.2 99.6 %copy-start.1 = (bf16[1040,256]{1,0:T(8,128)(2,1)}, bf16[1040,256]{1,0:T(8,128)(2,1)S(1)}, u32[]{:S(2)}) copy-start(bf16[1040,256]{1,0:T(8,128)(2,1)S(1)} %get-tuple-element.19.rest_1_) | copy-start | bytes 1597444
  17.2 99.6 %copy-start.2 = (bf16[1040,256]{1,0:T(8,128)(2,1)}, bf16[1040,256]{1,0:T(8,128)(2,1)S(1)}, u32[]{:S(2)}) copy-start(bf16[1040,256]{1,0:T(8,128)(2,1)S(1)} %get-tuple-element.20.rest_0_) | copy-start | bytes 1597444
  17.2 22.3 %collective-permute-start.1 = (bf16[1040,256]{1,0:T(8,128)(2,1)S(1)}, bf16[1040,256]{1,0:T(8,128)(2,1)S(1)}, u32[]{:S(2)}, u32[]{:S(2)}) collective-permute-start(bf16[1040,256]{1,0:T(8,128)(2,1)S(1)} %get-tuple-element.19.rest_1_), channel_id=1, source_target_pairs={{0,56},{8,0},{16,8},{24,16},{32,24},{40,32},{48,40},{56,48},{1,57}... | collective-permute-start | bytes 1597448 | tf_op jit(solution)/shard_map/ppermute | solution.py:321
  28.7 16.2 %collective-permute-start.6 = (bf16[1040,256]{1,0:T(8,128)(2,1)S(1)}, bf16[1040,256]{1,0:T(8,128)(2,1)S(1)}, u32[]{:S(2)}, u32[]{:S(2)}) collective-permute-start(bf16[1040,256]{1,0:T(8,128)(2,1)S(1)} %get-tuple-element.20.rest_0_), channel_id=1, source_target_pairs={{0,8},{8,16},{16,24},{24,32},{32,40},{40,48},{48,56},{56,0},{1,9},... | collective-permute-start | bytes 1597448 | tf_op jit(solution)/shard_map/ppermute | solution.py:320
  30.7 25.3 %collective-permute-start.11 = (bf16[1040,256]{1,0:T(8,128)(2,1)S(1)}, bf16[1040,256]{1,0:T(8,128)(2,1)S(1)}, u32[]{:S(2)}, u32[]{:S(2)}) collective-permute-start(bf16[1040,256]{1,0:T(8,128)(2,1)S(1)} %get-tuple-element.19.rest_1_), channel_id=1, source_target_pairs={{0,8},{8,16},{16,24},{24,32},{32,40},{40,48},{48,56},{56,0},{1,9},... | collective-permute-start | bytes 1597448 | tf_op jit(solution)/shard_map/ppermute | solution.py:320
  32.6 25.3 %collective-permute-start = (bf16[1040,256]{1,0:T(8,128)(2,1)S(1)}, bf16[1040,256]{1,0:T(8,128)(2,1)S(1)}, u32[]{:S(2)}, u32[]{:S(2)}) collective-permute-start(bf16[1040,256]{1,0:T(8,128)(2,1)S(1)} %get-tuple-element.20.rest_0_), channel_id=1, source_target_pairs={{0,56},{8,0},{16,8},{24,16},{32,24},{40,32},{48,40},{56,48},{1,57}... | collective-permute-start | bytes 1597448 | tf_op jit(solution)/shard_map/ppermute | solution.py:321
  39.5 77.3 %copy-start.4 = (bf16[1040,256]{1,0:T(8,128)(2,1)}, bf16[1040,256]{1,0:T(8,128)(2,1)S(1)}, u32[]{:S(2)}) copy-start(bf16[1040,256]{1,0:T(8,128)(2,1)S(1)} %collective-permute-done.1.rest_3_) | copy-start | bytes 1597444
  39.5 23.0 %collective-permute-start.3 = (bf16[1040,256]{1,0:T(8,128)(2,1)S(1)}, bf16[1040,256]{1,0:T(8,128)(2,1)}, u32[]{:S(2)}, u32[]{:S(2)}) collective-permute-start(bf16[1040,256]{1,0:T(8,128)(2,1)S(1)} %collective-permute-done.1.rest_3_), channel_id=1, source_target_pairs={{0,56},{8,0},{16,8},{24,16},{32,24},{40,32},{48,40},{56,48},{1,57}... | collective-permute-start | bytes 1597448 | tf_op jit(solution)/shard_map/ppermute | solution.py:321
  44.9 71.9 %copy-start.5 = (bf16[1040,256]{1,0:T(8,128)(2,1)}, bf16[1040,256]{1,0:T(8,128)(2,1)S(1)}, u32[]{:S(2)}) copy-start(bf16[1040,256]{1,0:T(8,128)(2,1)S(1)} %collective-permute-done.6.rest_14_) | copy-start | bytes 1597444
  44.9 22.8 %collective-permute-start.7 = (bf16[1040,256]{1,0:T(8,128)(2,1)S(1)}, bf16[1040,256]{1,0:T(8,128)(2,1)}, u32[]{:S(2)}, u32[]{:S(2)}) collective-permute-start(bf16[1040,256]{1,0:T(8,128)(2,1)S(1)} %collective-permute-done.6.rest_14_), channel_id=1, source_target_pairs={{0,8},{8,16},{16,24},{24,32},{32,40},{40,48},{48,56},{56,0},{1,9},... | collective-permute-start | bytes 1597448 | tf_op jit(solution)/shard_map/ppermute | solution.py:320
  56.0 60.8 %copy-start.6 = (bf16[1040,256]{1,0:T(8,128)(2,1)}, bf16[1040,256]{1,0:T(8,128)(2,1)S(1)}, u32[]{:S(2)}) copy-start(bf16[1040,256]{1,0:T(8,128)(2,1)S(1)} %collective-permute-done.11.rest_15_) | copy-start | bytes 1597444
  56.0 25.0 %collective-permute-start.12 = (bf16[1040,256]{1,0:T(8,128)(2,1)S(1)}, bf16[1040,256]{1,0:T(8,128)(2,1)}, u32[]{:S(2)}, u32[]{:S(2)}) collective-permute-start(bf16[1040,256]{1,0:T(8,128)(2,1)S(1)} %collective-permute-done.11.rest_15_), channel_id=1, source_target_pairs={{0,8},{8,16},{16,24},{24,32},{32,40},{40,48},{48,56},{56,0},{1,9},... | collective-permute-start | bytes 1597448 | tf_op jit(solution)/shard_map/ppermute | solution.py:320
  57.9 58.9 %copy-start.7 = (bf16[1040,256]{1,0:T(8,128)(2,1)}, bf16[1040,256]{1,0:T(8,128)(2,1)S(1)}, u32[]{:S(2)}) copy-start(bf16[1040,256]{1,0:T(8,128)(2,1)S(1)} %collective-permute-done.rest_2_) | copy-start | bytes 1597444
  58.0 24.9 %collective-permute-start.2 = (bf16[1040,256]{1,0:T(8,128)(2,1)S(1)}, bf16[1040,256]{1,0:T(8,128)(2,1)}, u32[]{:S(2)}, u32[]{:S(2)}) collective-permute-start(bf16[1040,256]{1,0:T(8,128)(2,1)S(1)} %collective-permute-done.rest_2_), channel_id=1, source_target_pairs={{0,56},{8,0},{16,8},{24,16},{32,24},{40,32},{48,40},{56,48},{1,57}... | collective-permute-start | bytes 1597448 | tf_op jit(solution)/shard_map/ppermute | solution.py:321
  62.5 25.2 %collective-permute-start.5 = (bf16[1040,256]{1,0:T(8,128)(2,1)}, bf16[1040,256]{1,0:T(8,128)(2,1)}, u32[]{:S(2)}, u32[]{:S(2)}) collective-permute-start(bf16[1040,256]{1,0:T(8,128)(2,1)} %collective-permute-done.3.rest_5_), channel_id=1, source_target_pairs={{0,56},{8,0},{16,8},{24,16},{32,24},{40,32},{48,40},{56,48},{1,57}... | collective-permute-start | bytes 1597448 | tf_op jit(solution)/shard_map/ppermute | solution.py:321
  67.7 23.4 %collective-permute-start.8 = (bf16[1040,256]{1,0:T(8,128)(2,1)}, bf16[1040,256]{1,0:T(8,128)(2,1)}, u32[]{:S(2)}, u32[]{:S(2)}) collective-permute-start(bf16[1040,256]{1,0:T(8,128)(2,1)} %collective-permute-done.7.rest_12_), channel_id=1, source_target_pairs={{0,8},{8,16},{16,24},{24,32},{32,40},{40,48},{48,56},{56,0},{1,9},... | collective-permute-start | bytes 1597448 | tf_op jit(solution)/shard_map/ppermute | solution.py:320
  70.8 22.6 %all-to-all-start = ((s32[16,1,8]{2,1,0:T(1,128)}), s32[16,1,8]{2,1,0:T(1,128)S(1)}, u32[]{:S(2)}, u32[]{:S(2)}) async-start(s32[16,1,8]{2,1,0:T(1,128)} %bitcast.3), calls=%async_computation | async-start | bytes 16384 | tf_op jit(solution)/shard_map/all_to_all | solution.py:328
  81.0 20.7 %collective-permute-start.13 = (bf16[1040,256]{1,0:T(8,128)(2,1)}, bf16[1040,256]{1,0:T(8,128)(2,1)}, u32[]{:S(2)}, u32[]{:S(2)}) collective-permute-start(bf16[1040,256]{1,0:T(8,128)(2,1)} %collective-permute-done.12.rest_13_), channel_id=1, source_target_pairs={{0,8},{8,16},{16,24},{24,32},{32,40},{40,48},{48,56},{56,0},{1,9},... | collective-permute-start | bytes 1597448 | tf_op jit(solution)/shard_map/ppermute | solution.py:320
  82.9 18.8 %collective-permute-start.4 = (bf16[1040,256]{1,0:T(8,128)(2,1)}, bf16[1040,256]{1,0:T(8,128)(2,1)}, u32[]{:S(2)}, u32[]{:S(2)}) collective-permute-start(bf16[1040,256]{1,0:T(8,128)(2,1)} %collective-permute-done.2.rest_4_), channel_id=1, source_target_pairs={{0,56},{8,0},{16,8},{24,16},{32,24},{40,32},{48,40},{56,48},{1,57}... | collective-permute-start | bytes 1597448 | tf_op jit(solution)/shard_map/ppermute | solution.py:321
  87.8 21.9 %collective-permute-start.10 = (bf16[1040,256]{1,0:T(8,128)(2,1)}, bf16[1040,256]{1,0:T(8,128)(2,1)}, u32[]{:S(2)}, u32[]{:S(2)}) collective-permute-start(bf16[1040,256]{1,0:T(8,128)(2,1)} %collective-permute-done.5.rest_7_), channel_id=1, source_target_pairs={{0,56},{8,0},{16,8},{24,16},{32,24},{40,32},{48,40},{56,48},{1,57}... | collective-permute-start | bytes 1597448 | tf_op jit(solution)/shard_map/ppermute | solution.py:321
  91.2 21.9 %collective-permute-start.9 = (bf16[1040,256]{1,0:T(8,128)(2,1)}, bf16[1040,256]{1,0:T(8,128)(2,1)}, u32[]{:S(2)}, u32[]{:S(2)}) collective-permute-start(bf16[1040,256]{1,0:T(8,128)(2,1)} %collective-permute-done.8.rest_10_), channel_id=1, source_target_pairs={{0,8},{8,16},{16,24},{24,32},{32,40},{40,48},{48,56},{56,0},{1,9},... | collective-permute-start | bytes 1597448 | tf_op jit(solution)/shard_map/ppermute | solution.py:320
  116.8 37.7 %copy-start.8 = (s32[128]{0:T(128)S(1)}, s32[128]{0:T(128)}, u32[]{:S(2)}) copy-start(s32[128]{0:T(128)} %reduce_max.24.code) | copy-start | bytes 1540
  147.1 16.5 %all-to-all-start.2 = ((bf16[8,128,128]{2,1,0:T(8,128)(2,1)}), bf16[8,128,128]{2,1,0:T(8,128)(2,1)S(1)}, u32[]{:S(2)}, u32[]{:S(2)}) async-start(bf16[8,128,128]{2,1,0:T(8,128)(2,1)} %broadcast_in_dim.56), calls=%async_computation.2 | async-start | bytes 524288 | tf_op jit(solution)/shard_map/all_to_all | solution.py:328
  163.6 0.7 copy-start.3
  241.7 17.8 %all-to-all-start.8 = ((f32[16,32,128]{2,1,0:T(8,128)}), f32[16,32,128]{2,1,0:T(8,128)S(1)}, u32[]{:S(2)}, u32[]{:S(2)}) async-start(f32[16,32,128]{2,1,0:T(8,128)} %get-tuple-element.17), calls=%async_computation.8 | async-start | bytes 524288 | tf_op jit(solution)/shard_map/all_to_all | solution.py:328
Sparse Core Ops, SparseCore 0:
  11.7 105.0 all-gather.2

commit v3 on v2

v3 whole, which is shorter than its diff:
```python
import math

import jax
import jax.numpy as jnp
from jax import lax
from jax.experimental import pallas as pl
from jax.experimental.pallas import tpu as pltpu
from jax.sharding import Mesh
from jax.sharding import PartitionSpec as P

EPSILON = 0.02
UNMATCHED = 2.0
SLACK = 100.0
SHIFT = 46.0
LOG2E = 1.4426950408889634
SHIFT2 = SHIFT * LOG2E
FLOOR = math.exp(SHIFT - SLACK)
OFF = -1.0e30

BLK = 128
E = 256
NY, NZ, NC, NX = 8, 8, 2, 4
KB = 16
HB = KB // 2
HALF = HB * BLK + 2 * HB
SOURCES = NY * NC
POS = SOURCES * NZ
ROWS = KB * BLK
PART = 512
BETA = LOG2E * 2.0 / (E * EPSILON)
MIB = 2**20

F32, BF16 = jnp.float32, jnp.bfloat16
NT = (((1,), (1,)), ((), ()))
NN = (((1,), (0,)), ((), ()))
VMEM_WHOLE = pl.BlockSpec(memory_space=pltpu.VMEM)
SMEM_WHOLE = pl.BlockSpec(memory_space=pltpu.SMEM)
ANYWHERE = pl.BlockSpec(memory_space=pl.ANY)
IN_HBM = pl.BlockSpec(memory_space=pltpu.HBM)
GRANT = 40 * MIB


def dot(left, right, dims):
    return lax.dot_general(left, right, dims, preferred_element_type=F32)


def exact_sum(onehot, values):
    return lax.dot_general(
        onehot, values, NN, precision=lax.Precision.HIGHEST, preferred_element_type=F32
    )


def spread(places, count):
    rows = lax.broadcasted_iota(jnp.int32, (count, POS), 0)
    return jnp.where(rows == places, 1.0, 0.0)


def project_kernel(frames, projection, out, here, made, norms, sems, out_sems):
    def inward(n):
        rows = pl.ds(n * PART, PART)
        return pltpu.make_async_copy(frames.at[rows], here.at[rows], sems.at[n])

    def outward(h):
        return pltpu.make_async_copy(made.at[h], out.at[h], out_sems.at[h])

    for n in range(ROWS // PART):
        inward(n).start()
    ones = jnp.ones((16, E), BF16)
    for h in range(2):
        for j in range(HB):
            k = h * HB + j
            if k * BLK % PART == 0:
                inward(k * BLK // PART).wait()
            codes = dot(here[pl.ds(k * BLK, BLK), :], projection[...], NN).astype(BF16)
            made[h, pl.ds(j * BLK, BLK), :] = codes
            wide = codes.astype(F32)
            square = wide * wide
            high = square.astype(BF16)
            low = (square - high.astype(F32)).astype(BF16)
            norms[j : j + 1, :] = (dot(ones, high, NT) + dot(ones, low, NT))[0:1, :]
        norm = norms[...]
        high = norm.astype(BF16).astype(F32)
        middle = (norm - high).astype(BF16).astype(F32)
        low = norm - high - middle
        left = jnp.concatenate([high, low], axis=0)
        right = jnp.concatenate([middle, jnp.zeros_like(low)], axis=0)
        made[h, HB * BLK : HALF, :] = jnp.concatenate([left, right], axis=1).astype(BF16)
        outward(h).start()
    for h in range(2):
        outward(h).wait()


def project(frames, projection):
    return pl.pallas_call(
        project_kernel,
        out_shape=pltpu.HBM((2, HALF, E), BF16),
        in_specs=[IN_HBM, VMEM_WHOLE],
        out_specs=IN_HBM,
        scratch_shapes=[
            pltpu.VMEM((ROWS, E), BF16),
            pltpu.VMEM((2, HALF, E), BF16),
            pltpu.VMEM((HB, BLK), F32),
            pltpu.SemaphoreType.DMA((ROWS // PART,)),
            pltpu.SemaphoreType.DMA((2,)),
        ],
        compiler_params=pltpu.CompilerParams(vmem_limit_bytes=GRANT),
    )(in_hbm(frames), projection)


def in_hbm(value):
    return pltpu.with_memory_space_constraint(value, pltpu.HBM)


AHEAD = 2
SLOTS = AHEAD + 1
CHUNK = 32
CHUNKS = POS // CHUNK


def first_kernel(code, col_at, row_at, col_place, row_place, left, *rest):
    rights = rest[: 2 * NZ]
    (
        cross, columns, sums, taken, tails, held, picks, parts, norms, made,
        sems, tail_sem, right_sem, out_sem,
    ) = rest[2 * NZ :]

    def moves(z):
        slot = z % SLOTS
        copies = []
        for n in range(SOURCES):
            k = jnp.maximum(code[z * SOURCES + n], 0) // KB
            start = pl.multiple_of(k % HB * BLK, BLK)
            copies.append(
                pltpu.make_async_copy(
                    left.at[n, k // HB, pl.ds(start, BLK)], taken.at[slot, n], sems.at[slot, n]
                )
            )
        return copies

    def away(z):
        slot = z % SLOTS
        to = cross.at[pl.ds(z * SOURCES, SOURCES)]
        return pltpu.make_async_copy(made.at[slot], to, out_sem.at[slot])

    into = [
        pltpu.make_async_copy(rights[i], held.at[i // 2, i % 2], right_sem.at[i])
        for i in range(2 * NZ)
    ]
    tail_copy = pltpu.make_async_copy(
        left.at[:, :, pl.ds(HB * BLK, 2 * HB)], tails, tail_sem
    )
    tail_copy.start()
    for z in range(AHEAD):
        for copy in into[2 * z : 2 * z + 2] + moves(z):
            copy.start()
    for copy in into[2 * AHEAD :]:
        copy.start()
    row = lax.broadcasted_iota(jnp.int32, (4 * KB, BLK), 0)
    for k in range(KB):
        ours = (row // (2 * KB) == k // HB) & (row % HB == k % HB)
        picks[k] = jnp.where(ours, -0.5, 0.0).astype(BF16)
    tail_copy.wait()
    for n in range(SOURCES):
        stacked = []
        for h in range(2):
            tail = tails[n, h].astype(F32)
            stacked += [tail[:, 0:BLK], tail[:, BLK:E]]
        parts[n] = jnp.concatenate(stacked, axis=0).T.astype(BF16)

    @pl.loop(0, NZ)
    def _(z):
        slot = z % SLOTS

        @pl.when(z + AHEAD < NZ)
        def _():
            for copy in moves(z + AHEAD):
                copy.start()

        @pl.when(z >= SLOTS)
        def _():
            away(z - SLOTS).wait()

        for h in range(2):
            pltpu.make_async_copy(rights[h], held.at[z, h], right_sem.at[2 * z + h]).wait()
            tail = held[z, h, HB * BLK : HALF, :].astype(F32)
            norm = tail[0:HB, 0:BLK] + tail[0:HB, BLK:E] + tail[HB : 2 * HB, 0:BLK]
            norms[h * HB : (h + 1) * HB, :] = 0.5 * norm
        for copy in moves(z):
            copy.wait()
        rows = []
        for n in range(SOURCES):
            value = code[z * SOURCES + n]
            off = jnp.where(value >= 0, SHIFT2, OFF)
            value = jnp.maximum(value, 0)
            k, t = value // KB, value % KB
            v = held[z, t // HB, pl.ds(pl.multiple_of(t % HB * BLK, BLK), BLK), :]
            w = dot(taken[slot, n], v, NT) + dot(parts[n], picks[k], NN)
            w = w - norms[pl.ds(t, 1), :]
            made[slot, n] = w
            rows.append(jnp.sum(jnp.exp2(w * BETA + off), axis=0, keepdims=True))
        away(z).start()
        place = pl.ds(pl.multiple_of(z * SOURCES, SOURCES), SOURCES)
        sums[place, :] = jnp.concatenate(rows, axis=0)

    columns[...] = exact_sum(spread(col_place[...], NZ * KB), sums[...]).astype(BF16)
    for z in range(NZ - SLOTS, NZ):
        away(z).wait()


def first_pass(code, col_at, row_at, col_place, row_place, left, rights):
    return pl.pallas_call(
        first_kernel,
        in_specs=[SMEM_WHOLE] * 3 + [VMEM_WHOLE] * 2 + [ANYWHERE] * (2 * NZ + 1),
        out_specs=[IN_HBM, VMEM_WHOLE],
        scratch_shapes=[
            pltpu.VMEM((POS, BLK), F32),
            pltpu.VMEM((SLOTS, SOURCES, BLK, E), BF16),
            pltpu.VMEM((SOURCES, 2, 2 * HB, E), BF16),
            pltpu.VMEM((NZ, 2, HALF, E), BF16),
            pltpu.VMEM((KB, 4 * KB, BLK), BF16),
            pltpu.VMEM((SOURCES, BLK, 4 * KB), BF16),
            pltpu.VMEM((KB, BLK), F32),
            pltpu.VMEM((SLOTS, SOURCES, BLK, BLK), F32),
            pltpu.SemaphoreType.DMA((SLOTS, SOURCES)),
            pltpu.SemaphoreType.DMA,
            pltpu.SemaphoreType.DMA((2 * NZ,)),
            pltpu.SemaphoreType.DMA((SLOTS,)),
        ],
        out_shape=[
            pltpu.HBM((POS, BLK, BLK), F32),
            jax.ShapeDtypeStruct((NZ * KB, BLK), BF16),
        ],
        compiler_params=pltpu.CompilerParams(vmem_limit_bytes=GRANT),
    )(code, col_at, row_at, col_place, row_place, left, *rights)


def total_of(received):
    total = received[0].astype(F32)
    for n in range(1, received.shape[0]):
        total += received[n].astype(F32)
    return total


def one_chunk(source, target, sems, n):
    part = pl.ds(n * CHUNK, CHUNK)
    return pltpu.make_async_copy(source.at[part], target.at[part], sems.at[n])


def start_all(source, target, sems):
    for n in range(CHUNKS):
        one_chunk(source, target, sems, n).start()


def second_kernel(
    col_at, row_place, received, cross, kernel, rows_out, column_sum,
    cross_here, kernel_here, potential, sums, in_sem, kernel_sem,
):
    start_all(cross, cross_here, in_sem)
    column_sum[...] = total_of(received)
    potential[...] = 2.0 * SHIFT2 - jnp.log2(FLOOR + column_sum[...])
    ones = jnp.ones((16, BLK), BF16)

    @pl.loop(0, CHUNKS)
    def _(step):
        one_chunk(cross, cross_here, in_sem, step).wait()
        rows = []
        for n in range(CHUNK):
            tile = step * CHUNK + n
            at = col_at[tile]
            pot = potential[pl.ds(jnp.maximum(at, 0), 1), :] + jnp.where(at >= 0, 0.0, OFF)
            w = cross_here[tile]
            rounded = jnp.exp2(w * BETA + pot).astype(BF16)
            kernel_here[tile, 0:BLK, :] = rounded
            kernel_here[tile, BLK : 2 * BLK, :] = (
                rounded.astype(F32) * (w * (-2.0 / E))
            ).astype(BF16)
            rows.append(dot(ones, rounded, NT)[0:1, :])
        one_chunk(kernel_here, kernel, kernel_sem, step).start()
        sums[pl.ds(pl.multiple_of(step * CHUNK, CHUNK), CHUNK), :] = jnp.concatenate(rows, axis=0)

    rows_out[...] = exact_sum(spread(row_place[...], SOURCES * KB), sums[...]).astype(BF16)

    @pl.loop(0, CHUNKS)
    def _(step):
        one_chunk(kernel_here, kernel, kernel_sem, step).wait()


def second_pass(col_at, row_place, received, cross):
    return pl.pallas_call(
        second_kernel,
        in_specs=[SMEM_WHOLE, VMEM_WHOLE, VMEM_WHOLE, IN_HBM],
        out_specs=[IN_HBM, VMEM_WHOLE, VMEM_WHOLE],
        scratch_shapes=[
            pltpu.VMEM((POS, BLK, BLK), F32),
            pltpu.VMEM((POS, 2 * BLK, BLK), BF16),
            pltpu.VMEM((NZ * KB, BLK), F32),
            pltpu.VMEM((POS, BLK), F32),
            pltpu.SemaphoreType.DMA((CHUNKS,)),
            pltpu.SemaphoreType.DMA((CHUNKS,)),
        ],
        out_shape=[
            pltpu.HBM((POS, 2 * BLK, BLK), BF16),
            jax.ShapeDtypeStruct((SOURCES * KB, BLK), BF16),
            jax.ShapeDtypeStruct((NZ * KB, BLK), F32),
        ],
        compiler_params=pltpu.CompilerParams(vmem_limit_bytes=GRANT),
    )(col_at, row_place, received, in_hbm(cross))


def two_parts(row):
    high = row.astype(BF16).astype(F32)
    at = lax.broadcasted_iota(jnp.int32, (16, BLK), 0)
    return jnp.where(at == 0, high, jnp.where(at == 1, row - high, 0.0)).astype(BF16)


def third_kernel(row_at, col_place, received, kernel, columns, kernel_here, scale, sums, in_sem):
    upper = kernel.at[:, pl.ds(0, BLK)]
    start_all(upper, kernel_here, in_sem)
    scale[...] = 1.0 / (FLOOR + received[...].astype(F32))

    @pl.loop(0, CHUNKS)
    def _(step):
        one_chunk(upper, kernel_here, in_sem, step).wait()
        rows = []
        for n in range(CHUNK):
            tile = step * CHUNK + n
            at = jnp.maximum(row_at[tile], 0)
            both = dot(two_parts(scale[pl.ds(at, 1), :]), kernel_here[tile], NN)
            rows.append(both[0:1, :] + both[1:2, :])
        sums[pl.ds(pl.multiple_of(step * CHUNK, CHUNK), CHUNK), :] = jnp.concatenate(rows, axis=0)

    columns[...] = exact_sum(spread(col_place[...], NZ * KB), sums[...]).astype(BF16)


def third_pass(row_at, col_place, received, kernel):
    return pl.pallas_call(
        third_kernel,
        in_specs=[SMEM_WHOLE, VMEM_WHOLE, VMEM_WHOLE, IN_HBM],
        out_specs=VMEM_WHOLE,
        scratch_shapes=[
            pltpu.VMEM((POS, BLK, BLK), BF16),
            pltpu.VMEM((SOURCES * KB, BLK), F32),
            pltpu.VMEM((POS, BLK), F32),
            pltpu.SemaphoreType.DMA((CHUNKS,)),
        ],
        out_shape=jax.ShapeDtypeStruct((NZ * KB, BLK), BF16),
        compiler_params=pltpu.CompilerParams(vmem_limit_bytes=GRANT),
    )(row_at, col_place, received, in_hbm(kernel))


def fourth_kernel(
    col_at, row_place, received, column_sum, kernel, rows_out, plan_out,
    kernel_here, scale, sums, weighed, kernel_sem,
):
    start_all(kernel, kernel_here, kernel_sem)
    plan_sum = total_of(received)
    plan_out[...] = plan_sum
    scale[...] = 1.0 / (FLOOR / (FLOOR + column_sum[...]) + plan_sum)

    @pl.loop(0, CHUNKS)
    def _(step):
        one_chunk(kernel, kernel_here, kernel_sem, step).wait()
        rows, heavy = [], []
        for n in range(CHUNK):
            tile = step * CHUNK + n
            pair = two_parts(scale[pl.ds(jnp.maximum(col_at[tile], 0), 1), :])
            both = dot(pair, kernel_here[tile], NT)
            both = both[0:1, :] + both[1:2, :]
            rows.append(both[:, 0:BLK])
            heavy.append(both[:, BLK : 2 * BLK])
        place = pl.ds(pl.multiple_of(step * CHUNK, CHUNK), CHUNK)
        sums[place, :] = jnp.concatenate(rows, axis=0)
        weighed[place, :] = jnp.concatenate(heavy, axis=0)

    which = spread(row_place[...], SOURCES * KB)
    total = exact_sum(which, sums[...])
    heavy_total = exact_sum(which, weighed[...])
    for s in range(SOURCES):
        c, y = s // NY, s % NY
        rows_out[y * NC + c, 0:KB, :] = total[s * KB : (s + 1) * KB, :]
        rows_out[y * NC + c, KB : 2 * KB, :] = heavy_total[s * KB : (s + 1) * KB, :]


def fourth_pass(col_at, row_place, received, column_sum, kernel):
    return pl.pallas_call(
        fourth_kernel,
        in_specs=[SMEM_WHOLE] + [VMEM_WHOLE] * 3 + [IN_HBM],
        out_specs=[VMEM_WHOLE] * 2,
        scratch_shapes=[
            pltpu.VMEM((POS, 2 * BLK, BLK), BF16),
            pltpu.VMEM((NZ * KB, BLK), F32),
            pltpu.VMEM((POS, BLK), F32),
            pltpu.VMEM((POS, BLK), F32),
            pltpu.SemaphoreType.DMA((CHUNKS,)),
        ],
        out_shape=[
            jax.ShapeDtypeStruct((SOURCES, 2 * KB, BLK), F32),
            jax.ShapeDtypeStruct((NZ * KB, BLK), F32),
        ],
        compiler_params=pltpu.CompilerParams(vmem_limit_bytes=GRANT),
    )(col_at, row_place, received, column_sum, in_hbm(kernel))


def ring_pieces(block, axis, n):
    up = [(i, (i + 1) % n) for i in range(n)]
    down = [(i, (i - 1) % n) for i in range(n)]
    top, low = block[0], block[1]
    held = [[top, low]] + [[None, None] for _ in range(n - 1)]
    right, left = [top, low], [low, top]
    for k in range(1, n // 2 + 1):
        for i in range(2 if k < n // 2 else 1):
            right[i] = lax.ppermute(right[i], axis, up)
            left[i] = lax.ppermute(left[i], axis, down)
            held[n - k][i] = right[i]
            held[k][1 - i] = left[i]
    return [half for pair in held for half in pair]


def swap(value, axes):
    return lax.all_to_all(value, axes, split_axis=0, concat_axis=0, tiled=True)


def to_all(value, axes, n):
    return swap(jnp.broadcast_to(value[None], (n,) + value.shape), axes)


def columns_to_row(columns):
    over_rep = jnp.sum(to_all(columns, "x", NX).astype(F32), axis=0)
    return to_all(over_rep.astype(BF16), "z", NZ)


def own_columns(columns):
    at = lax.axis_index("z") * KB
    return lax.dynamic_slice_in_dim(columns, at, KB, 0)


def slot_codes(location, pair_block, pair_count):
    slots = pair_block.shape[1]
    stored = location[pair_block.reshape(-1)]
    used = (
        jnp.arange(slots, dtype=jnp.int32)[None, :] < pair_count[:, None]
    ).reshape(-1)
    block = jnp.arange(KB * slots, dtype=jnp.int32) // slots
    owner, local = stored // KB, stored % KB
    holders = jnp.arange(NY * NZ * NC, dtype=jnp.int32)
    match = (owner[None, :] == holders[:, None]) & used[None, :]
    return jnp.max(jnp.where(match, (block * KB + local)[None, :], -1), axis=1)


def body(rollout, demo, projection, location, pair_block, pair_count):
    codes = slot_codes(location, pair_block, pair_count)
    codes = codes.reshape(NY, NZ, NC).transpose(0, 2, 1).reshape(SOURCES, NZ)
    codes = swap(codes[:, None, :], ("y", "c")).reshape(SOURCES, NZ)
    turned = (lax.axis_index("z") + jnp.arange(NZ, dtype=jnp.int32)) % NZ
    pick = turned[:, None] == jnp.arange(NZ, dtype=jnp.int32)[None, :]
    codes = jnp.max(jnp.where(pick[:, None, :], codes[None], -1), axis=2)
    used = codes >= 0
    col_at = jnp.where(used, turned[:, None] * KB + codes % KB, -1).reshape(POS)
    source = jnp.arange(SOURCES, dtype=jnp.int32)
    source = (source % NC * NY + source // NC)[None, :]
    row_at = jnp.where(used, source * KB + codes // KB, -1).reshape(POS)
    col_place, row_place = col_at.reshape(1, POS), row_at.reshape(1, POS)
    codes = codes.reshape(POS)

    left = lax.all_gather(project(rollout, projection), ("y", "c"))
    rights = ring_pieces(project(demo, projection), "z", NZ)

    cross, columns = first_pass(codes, col_at, row_at, col_place, row_place, left, rights)
    kernel, rows, column_sum = second_pass(
        col_at, row_place, columns_to_row(columns), cross
    )
    rows = jnp.sum(swap(rows.reshape(NC, NY * KB, BLK), "c").astype(F32), axis=0)
    rows = jnp.sum(to_all(rows.astype(BF16), "y", NY).astype(F32), axis=0)
    rows = to_all(rows.astype(BF16), "c", NC).reshape(SOURCES * KB, BLK)
    columns = third_pass(row_at, col_place, rows, kernel)
    both, plan_sum = fourth_pass(
        col_at, row_place, columns_to_row(columns), column_sum, kernel
    )
    both = jnp.sum(swap(both, ("y", "c")), axis=0)
    total = FLOOR + both[:KB]
    reward = -(both[KB:] + UNMATCHED * FLOOR) / total
    roll_pot = EPSILON * (SHIFT - jnp.log(total))
    reached = FLOOR + (FLOOR + own_columns(column_sum)) * own_columns(plan_sum)
    demo_pot = EPSILON * (SHIFT - jnp.log(reached))
    return reward.reshape(-1), roll_pot.reshape(-1), demo_pot.reshape(-1)


def solution(mesh):
    grid = Mesh(mesh.devices.reshape(NY, NZ, NC, NX), ("y", "z", "c", "x"))
    every, roll = ("y", "z", "c", "x"), ("y", "z", "c")
    return jax.shard_map(
        body,
        mesh=grid,
        in_specs=(P(every, None), P(roll, None), P(), P(), P(every, None), P(every)),
        out_specs=(P(every), P(every), P(roll)),
        check_vma=False,
    )
```

time: 270 us -> 244 us (0.904)
  Pallas kernels: 55.8 us -> 36.9 us
  blocking collectives: 58 us -> 71.6 us
  waiting for transfers between devices: 50.9 us -> 42 us
  starting transfers between devices: 76.3 us -> 69.1 us
    pallas_call x6, Pallas kernels: 55.8 us -> 36.9 us  [the longest x1 12 us: first_pass(): pl.pallas_call(first_kernel, in_specs=[SMEM_WHOLE] * 3 + [VMEM_WHOLE] * 2...]
    all_to_all x6 -> x7, blocking collectives: 58 us -> 71.6 us  [swap(): return lax.all_to_all(value, axes, split_axis=0, concat_axis=0, tiled=True)]
    all_to_all x3 -> x2, waiting for transfers between devices: 19 us -> 11.3 us  [swap(): return lax.all_to_all(value, axes, split_axis=0, concat_axis=0, tiled=True)]
    all_to_all x3 -> x2, starting transfers between devices: 23.4 us -> 16 us  [swap(): return lax.all_to_all(value, axes, split_axis=0, concat_axis=0, tiled=True)]
    ppermute x7, waiting for transfers between devices: 18 us -> 13.9 us  [ring_pieces(): right[i] = lax.ppermute(right[i], axis, up)]
    ppermute x7, waiting for transfers between devices: 10.2 us -> 14 us  [ring_pieces(): left[i] = lax.ppermute(left[i], axis, down)]
  transfers between devices with their start and end apart: 18 -> 17, of which waited for: 8 -> 8; matrix products, arithmetic and copies ran while one was open for 3% -> 3% of each run, Pallas kernels for 2% -> 2%
where the time goes in v3:
time: 244 us; the launch traced here: 243 us
  blocking collectives  71.6 us (29%)
  starting transfers between devices  69.1 us (28%)
  waiting for transfers between devices  42 us (17%)
  Pallas kernels  36.9 us (15%)
  between operations  14.4 us (6%)
  local copies, waits for them, and re-layouts  6.8 us (3%)
    all_to_all x7, blocking collectives, swap(): return lax.all_to_all(value, axes, split_axis=0, concat_axis=0, tiled=True)  71.6 us
    ppermute x7, starting transfers between devices, ring_pieces(): left[i] = lax.ppermute(left[i], axis, down)  39.6 us
    all_to_all x2, starting transfers between devices, swap(): return lax.all_to_all(value, axes, split_axis=0, concat_axis=0, tiled=True)  16 us
    ppermute x7, waiting for transfers between devices, ring_pieces(): left[i] = lax.ppermute(left[i], axis, down)  14 us
    ppermute x7, waiting for transfers between devices, ring_pieces(): right[i] = lax.ppermute(right[i], axis, up)  13.9 us
    ppermute x7, starting transfers between devices, ring_pieces(): right[i] = lax.ppermute(right[i], axis, up)  13.4 us
    pallas_call x1, Pallas kernels, first_pass(): pl.pallas_call(first_kernel, in_specs=[SMEM_WHOLE] * 3 + [VMEM_WHOLE] * 2...  12 us
    all_to_all x2, waiting for transfers between devices, swap(): return lax.all_to_all(value, axes, split_axis=0, concat_axis=0, tiled=True)  11.3 us
  transfers between devices with their start and end apart: 17, of which 8 were waited for; matrix products, arithmetic and copies ran while one was open for 3% of the time, Pallas kernels for 2%

profile of v3, /device:TPU:1, one launch (start us, length us, event | category | flops | bytes accessed | tf_op | source)
XLA Modules:
  0.0 243.3 jit_solution(10318720797769143846)
XLA Ops:
  7.2 0.9 copy-done.1
  8.1 4.3 %shard_map.85 = bf16[2,1040,256]{2,1,0:T(8,128)(2,1)} custom-call(bf16[2048,256]{1,0:T(8,128)(2,1)} %frames.2, bf16[256,256]{1,0:T(8,128)(2,1)S(1)} %copy-done.1), custom_call_target="tpu_custom_call" | custom-call | tf_op jit(solution)/shard_map/pallas_call | solution.py:94
  12.5 0.9 copy-done.2
  13.4 4.3 %shard_map.86 = bf16[2,1040,256]{2,1,0:T(8,128)(2,1)} custom-call(bf16[2048,256]{1,0:T(8,128)(2,1)} %frames.3, bf16[256,256]{1,0:T(8,128)(2,1)S(1)} %copy-done.2), custom_call_target="tpu_custom_call" | custom-call | tf_op jit(solution)/shard_map/pallas_call | solution.py:94
  17.7 1.3 slice_bitcast_fusion
  19.0 11.5 %collective-permute-start.1 = (bf16[1040,256]{1,0:T(8,128)(2,1)S(1)}, bf16[1040,256]{1,0:T(8,128)(2,1)S(1)}, u32[]{:S(2)}, u32[]{:S(2)}) collective-permute-start(bf16[1040,256]{1,0:T(8,128)(2,1)S(1)} %get-tuple-element.17.rest_1_), channel_id=1, source_target_pairs={{0,56},{8,0},{16,8},{24,16},{32,24},{40,32},{48,40},{56,48},{1,57}... | collective-permute-start | bytes 1597448 | tf_op jit(solution)/shard_map/ppermute | solution.py:413
  30.5 1.9 collective-permute-start.6
  32.4 1.9 collective-permute-start.11
  34.3 4.6 %collective-permute-start = (bf16[1040,256]{1,0:T(8,128)(2,1)S(1)}, bf16[1040,256]{1,0:T(8,128)(2,1)S(1)}, u32[]{:S(2)}, u32[]{:S(2)}) collective-permute-start(bf16[1040,256]{1,0:T(8,128)(2,1)S(1)} %get-tuple-element.18.rest_0_), channel_id=1, source_target_pairs={{0,56},{8,0},{16,8},{24,16},{32,24},{40,32},{48,40},{56,48},{1,57}... | collective-permute-start | bytes 1597448 | tf_op jit(solution)/shard_map/ppermute | solution.py:413
  38.9 0.8 copy.22
  39.8 0.7 iota_compare_fusion.1
  40.5 0.7 collective-permute-done.1.rest_3_
  41.2 5.4 %collective-permute-start.3 = (bf16[1040,256]{1,0:T(8,128)(2,1)S(1)}, bf16[1040,256]{1,0:T(8,128)(2,1)}, u32[]{:S(2)}, u32[]{:S(2)}) collective-permute-start(bf16[1040,256]{1,0:T(8,128)(2,1)S(1)} %collective-permute-done.1.rest_3_), channel_id=1, source_target_pairs={{0,56},{8,0},{16,8},{24,16},{32,24},{40,32},{48,40},{56,48},{1,57}... | collective-permute-start | bytes 1597448 | tf_op jit(solution)/shard_map/ppermute | solution.py:413
  46.7 1.9 collective-permute-start.7
  48.7 1.1 gather_fusion
  49.9 0.1 select_reduce_fusion
  50.0 0.1 reshape.334
  50.1 0.7 copy.23
  50.9 10.0 %all-to-all-start = ((s32[16,1,8]{2,1,0:T(1,128)}), s32[16,1,8]{2,1,0:T(1,128)S(1)}, u32[]{:S(2)}, u32[]{:S(2)}) async-start(s32[16,1,8]{2,1,0:T(1,128)} %bitcast.3), calls=%async_computation | async-start | bytes 16384 | tf_op jit(solution)/shard_map/all_to_all | solution.py:420
  60.9 1.9 collective-permute-start.12
  62.8 4.9 %collective-permute-start.2 = (bf16[1040,256]{1,0:T(8,128)(2,1)S(1)}, bf16[1040,256]{1,0:T(8,128)(2,1)}, u32[]{:S(2)}, u32[]{:S(2)}) collective-permute-start(bf16[1040,256]{1,0:T(8,128)(2,1)S(1)} %collective-permute-done.rest_2_), channel_id=1, source_target_pairs={{0,56},{8,0},{16,8},{24,16},{32,24},{40,32},{48,40},{56,48},{1,57}... | collective-permute-start | bytes 1597448 | tf_op jit(solution)/shard_map/ppermute | solution.py:413
  67.7 3.4 %collective-permute-start.5 = (bf16[1040,256]{1,0:T(8,128)(2,1)}, bf16[1040,256]{1,0:T(8,128)(2,1)}, u32[]{:S(2)}, u32[]{:S(2)}) collective-permute-start(bf16[1040,256]{1,0:T(8,128)(2,1)} %collective-permute-done.3.rest_5_), channel_id=1, source_target_pairs={{0,56},{8,0},{16,8},{24,16},{32,24},{40,32},{48,40},{56,48},{1,57}... | collective-permute-start | bytes 1597448 | tf_op jit(solution)/shard_map/ppermute | solution.py:413
  71.1 1.9 collective-permute-start.8
  73.6 6.9 %collective-permute-done.12.rest_13_ = bf16[1040,256]{1,0:T(8,128)(2,1)} collective-permute-done((bf16[1040,256]{1,0:T(8,128)(2,1)S(1)}, bf16[1040,256]{1,0:T(8,128)(2,1)}, u32[]{:S(2)}, u32[]{:S(2)}) %collective-permute-start.12) | collective-permute-done | bytes 532512 | tf_op jit(solution)/shard_map/ppermute | solution.py:412
  80.6 1.9 collective-permute-start.13
  82.5 4.6 %collective-permute-start.4 = (bf16[1040,256]{1,0:T(8,128)(2,1)}, bf16[1040,256]{1,0:T(8,128)(2,1)}, u32[]{:S(2)}, u32[]{:S(2)}) collective-permute-start(bf16[1040,256]{1,0:T(8,128)(2,1)} %collective-permute-done.2.rest_4_), channel_id=1, source_target_pairs={{0,56},{8,0},{16,8},{24,16},{32,24},{40,32},{48,40},{56,48},{1,57}... | collective-permute-start | bytes 1597448 | tf_op jit(solution)/shard_map/ppermute | solution.py:413
  87.1 3.6 %collective-permute-done.5.rest_7_ = bf16[1040,256]{1,0:T(8,128)(2,1)} collective-permute-done((bf16[1040,256]{1,0:T(8,128)(2,1)}, bf16[1040,256]{1,0:T(8,128)(2,1)}, u32[]{:S(2)}, u32[]{:S(2)}) %collective-permute-start.5) | collective-permute-done | bytes 532512 | tf_op jit(solution)/shard_map/ppermute | solution.py:413
  90.6 5.3 %collective-permute-start.10 = (bf16[1040,256]{1,0:T(8,128)(2,1)}, bf16[1040,256]{1,0:T(8,128)(2,1)}, u32[]{:S(2)}, u32[]{:S(2)}) collective-permute-start(bf16[1040,256]{1,0:T(8,128)(2,1)} %collective-permute-done.5.rest_7_), channel_id=1, source_target_pairs={{0,56},{8,0},{16,8},{24,16},{32,24},{40,32},{48,40},{56,48},{1,57}... | collective-permute-start | bytes 1597448 | tf_op jit(solution)/shard_map/ppermute | solution.py:413
  96.0 1.9 collective-permute-start.9
  98.2 5.2 %collective-permute-done.13.rest_11_ = bf16[1040,256]{1,0:T(8,128)(2,1)} collective-permute-done((bf16[1040,256]{1,0:T(8,128)(2,1)}, bf16[1040,256]{1,0:T(8,128)(2,1)}, u32[]{:S(2)}, u32[]{:S(2)}) %collective-permute-start.13) | collective-permute-done | bytes 532512 | tf_op jit(solution)/shard_map/ppermute | solution.py:412
  103.4 9.7 %collective-permute-done.10.rest_9_ = bf16[1040,256]{1,0:T(8,128)(2,1)} collective-permute-done((bf16[1040,256]{1,0:T(8,128)(2,1)}, bf16[1040,256]{1,0:T(8,128)(2,1)}, u32[]{:S(2)}, u32[]{:S(2)}) %collective-permute-start.10) | collective-permute-done | bytes 532512 | tf_op jit(solution)/shard_map/ppermute | solution.py:413
  113.1 1.7 collective-permute-done.9.rest_8_
  114.8 2.9 %all-gather.3.cloned.1.call-done = bf16[32,1040,256]{2,1,0:T(8,128)(2,1)} async-done(((bf16[2,1040,256]{2,1,0:T(8,128)(2,1)}), bf16[32,1040,256]{2,1,0:T(8,128)(2,1)}) %all-gather.3.cloned.1.call-update) | async-done | bytes 17039376 | tf_op jit(solution)/shard_map/all_gather | solution.py:465
  117.7 12.0 %shard_map.87 = (f32[128,128,128]{2,1,0:T(8,128)}, bf16[128,128]{1,0:T(8,128)(2,1)S(1)}) custom-call(s32[128]{0:T(128)S(1)} %reduce_max.24.code, s32[128]{0:T(128)S(1)} %get-tuple-element.24.col_at, s32[128]{0:T(128)S(1)} %get-tuple-element.23.row_at, s32[1,128]{1,0:T(1,128)S(1)} %get-tuple-element.21.col_place, s32[1,128]{1,0:T(1,128)S(1)} %get-tuple-element.22.row_place, ...), custom_call_target="tpu_custom_call" | custom-call | tf_op jit(solution)/shard_map/pallas_call | solution.py:211
  129.8 8.1 %all_to_all.45 = bf16[4,128,128]{2,1,0:T(8,128)(2,1)S(1)} all-to-all(bf16[4,128,128]{2,1,0:T(8,128)(2,1)S(1)} %broadcast_in_dim.55), channel_id=1, replica_groups=mesh['y'=8,'z'=8,'c'=2,'x'=4] {'x'}, dimensions={0} | all-to-all | bytes 262144 | tf_op jit(solution)/shard_map/all_to_all | solution.py:420
  138.0 16.5 %all_to_all.46.received = bf16[8,128,128]{2,1,0:T(8,128)(2,1)S(1)} all-to-all(bf16[8,128,128]{2,1,0:T(8,128)(2,1)S(1)} %broadcast_in_dim.56), channel_id=1, replica_groups=mesh['y'=8,'z'=8,'c'=2,'x'=4] {'z'}, dimensions={0} | all-to-all | bytes 524288 | tf_op jit(solution)/shard_map/all_to_all | solution.py:420
  154.5 6.8 %shard_map.88 = (bf16[128,256,128]{2,1,0:T(8,128)(2,1)}, bf16[256,128]{1,0:T(8,128)(2,1)S(1)}, f32[128,128]{1,0:T(8,128)S(1)}) custom-call(s32[128]{0:T(128)S(1)} %get-tuple-element.24.col_at, s32[1,128]{1,0:T(1,128)S(1)} %get-tuple-element.22.row_place, bf16[8,128,128]{2,1,0:T(8,128)(2,1)S(1)} %all_to_all.46.received, f32[128,128,128]{2,1,0:T(8,128)} %get-tuple-element.11.cross), custom_call_target="tpu_custom_call" | custom-call | tf_op jit(solution)/shard_map/pallas_call | solution.py:289
  161.3 7.1 %all_to_all.47 = bf16[2,128,128]{2,1,0:T(8,128)(2,1)S(1)} all-to-all(bf16[2,128,128]{2,1,0:T(8,128)(2,1)S(1)} %bitcast.21), channel_id=1, replica_groups=mesh['y'=8,'z'=8,'c'=2,'x'=4] {'c'}, dimensions={0} | all-to-all | bytes 131072 | tf_op jit(solution)/shard_map/all_to_all | solution.py:420
  168.4 14.9 %all_to_all.48 = bf16[8,128,128]{2,1,0:T(8,128)(2,1)S(1)} all-to-all(bf16[8,128,128]{2,1,0:T(8,128)(2,1)S(1)} %broadcast_in_dim.57), channel_id=1, replica_groups=mesh['y'=8,'z'=8,'c'=2,'x'=4] {'y'}, dimensions={0} | all-to-all | bytes 524288 | tf_op jit(solution)/shard_map/all_to_all | solution.py:420
  183.4 5.1 %all_to_all.49 = bf16[2,128,128]{2,1,0:T(8,128)(2,1)S(1)} all-to-all(bf16[2,128,128]{2,1,0:T(8,128)(2,1)S(1)} %broadcast_in_dim.58), channel_id=1, replica_groups=mesh['y'=8,'z'=8,'c'=2,'x'=4] {'c'}, dimensions={0} | all-to-all | bytes 131072 | tf_op jit(solution)/shard_map/all_to_all | solution.py:420
  188.5 3.6 %shard_map.89 = bf16[128,128]{1,0:T(8,128)(2,1)S(1)} custom-call(s32[128]{0:T(128)S(1)} %get-tuple-element.23.row_at, s32[1,128]{1,0:T(1,128)S(1)} %get-tuple-element.21.col_place, bf16[256,128]{1,0:T(8,128)(2,1)S(1)} %bitcast.20, bf16[128,256,128]{2,1,0:T(8,128)(2,1)} %get-tuple-element.13.kernel), custom_call_target="tpu_custom_call" | custom-call | tf_op jit(solution)/shard_map/pallas_call | solution.py:336
  192.1 7.2 %all_to_all.50 = bf16[4,128,128]{2,1,0:T(8,128)(2,1)S(1)} all-to-all(bf16[4,128,128]{2,1,0:T(8,128)(2,1)S(1)} %broadcast_in_dim.94), channel_id=1, replica_groups=mesh['y'=8,'z'=8,'c'=2,'x'=4] {'x'}, dimensions={0} | all-to-all | bytes 262144 | tf_op jit(solution)/shard_map/all_to_all | solution.py:420
  199.4 12.6 %all_to_all.51.received = bf16[8,128,128]{2,1,0:T(8,128)(2,1)S(1)} all-to-all(bf16[8,128,128]{2,1,0:T(8,128)(2,1)S(1)} %broadcast_in_dim.95), channel_id=1, replica_groups=mesh['y'=8,'z'=8,'c'=2,'x'=4] {'z'}, dimensions={0} | all-to-all | bytes 524288 | tf_op jit(solution)/shard_map/all_to_all | solution.py:420
  212.0 5.9 %shard_map.90 = (f32[16,32,128]{2,1,0:T(8,128)}, f32[128,128]{1,0:T(8,128)S(1)}) custom-call(s32[128]{0:T(128)S(1)} %get-tuple-element.24.col_at, s32[1,128]{1,0:T(1,128)S(1)} %get-tuple-element.22.row_place, bf16[8,128,128]{2,1,0:T(8,128)(2,1)S(1)} %all_to_all.51.received, f32[128,128]{1,0:T(8,128)S(1)} %get-tuple-element.14.column_sum, ...), custom_call_target="tpu_custom_call" | custom-call | tf_op jit(solution)/shard_map/pallas_call | solution.py:385
  217.9 6.0 %all-to-all-start.8 = ((f32[16,32,128]{2,1,0:T(8,128)}), f32[16,32,128]{2,1,0:T(8,128)S(1)}, u32[]{:S(2)}, u32[]{:S(2)}) async-start(f32[16,32,128]{2,1,0:T(8,128)} %get-tuple-element.15), calls=%async_computation.8 | async-start | bytes 524288 | tf_op jit(solution)/shard_map/all_to_all | solution.py:420
  223.9 0.6 multiply_bitcast_fusion
  224.5 11.2 %all-to-all-done.8 = f32[16,32,128]{2,1,0:T(8,128)S(1)} async-done(((f32[16,32,128]{2,1,0:T(8,128)}), f32[16,32,128]{2,1,0:T(8,128)S(1)}, u32[]{:S(2)}, u32[]{:S(2)}) %all-to-all-start.8) | async-done | bytes 262176 | tf_op jit(solution)/shard_map/all_to_all | solution.py:420
  235.8 0.6 multiply_bitcast_fusion.1
  (47 shorter events, 1.4 us)
Async XLA Ops:
  7.2 41.5 %copy-start = (s32[2048]{0:T(1024)S(1)}, s32[2048]{0:T(1024)}, u32[]{:S(2)}) copy-start(s32[2048]{0:T(1024)} %param.9) | copy-start | bytes 24580
  7.2 110.5 %all-gather.3.cloned.1.call-start = ((), (), s32[]{:S(2)}) async-start(), calls=%async_computation.9 | async-start | bytes 18104320 | tf_op jit(solution)/shard_map/all_gather | solution.py:465
  7.2 0.9 copy-start.1
  12.5 0.9 copy-start.2
  19.0 22.3 %collective-permute-start.1 = (bf16[1040,256]{1,0:T(8,128)(2,1)S(1)}, bf16[1040,256]{1,0:T(8,128)(2,1)S(1)}, u32[]{:S(2)}, u32[]{:S(2)}) collective-permute-start(bf16[1040,256]{1,0:T(8,128)(2,1)S(1)} %get-tuple-element.17.rest_1_), channel_id=1, source_target_pairs={{0,56},{8,0},{16,8},{24,16},{32,24},{40,32},{48,40},{56,48},{1,57}... | collective-permute-start | bytes 1597448 | tf_op jit(solution)/shard_map/ppermute | solution.py:413
  30.5 16.2 %collective-permute-start.6 = (bf16[1040,256]{1,0:T(8,128)(2,1)S(1)}, bf16[1040,256]{1,0:T(8,128)(2,1)S(1)}, u32[]{:S(2)}, u32[]{:S(2)}) collective-permute-start(bf16[1040,256]{1,0:T(8,128)(2,1)S(1)} %get-tuple-element.18.rest_0_), channel_id=1, source_target_pairs={{0,8},{8,16},{16,24},{24,32},{32,40},{40,48},{48,56},{56,0},{1,9},... | collective-permute-start | bytes 1597448 | tf_op jit(solution)/shard_map/ppermute | solution.py:412
  32.4 28.5 %collective-permute-start.11 = (bf16[1040,256]{1,0:T(8,128)(2,1)S(1)}, bf16[1040,256]{1,0:T(8,128)(2,1)S(1)}, u32[]{:S(2)}, u32[]{:S(2)}) collective-permute-start(bf16[1040,256]{1,0:T(8,128)(2,1)S(1)} %get-tuple-element.17.rest_1_), channel_id=1, source_target_pairs={{0,8},{8,16},{16,24},{24,32},{32,40},{40,48},{48,56},{56,0},{1,9},... | collective-permute-start | bytes 1597448 | tf_op jit(solution)/shard_map/ppermute | solution.py:412
  34.3 28.5 %collective-permute-start = (bf16[1040,256]{1,0:T(8,128)(2,1)S(1)}, bf16[1040,256]{1,0:T(8,128)(2,1)S(1)}, u32[]{:S(2)}, u32[]{:S(2)}) collective-permute-start(bf16[1040,256]{1,0:T(8,128)(2,1)S(1)} %get-tuple-element.18.rest_0_), channel_id=1, source_target_pairs={{0,56},{8,0},{16,8},{24,16},{32,24},{40,32},{48,40},{56,48},{1,57}... | collective-permute-start | bytes 1597448 | tf_op jit(solution)/shard_map/ppermute | solution.py:413
  41.2 26.5 %collective-permute-start.3 = (bf16[1040,256]{1,0:T(8,128)(2,1)S(1)}, bf16[1040,256]{1,0:T(8,128)(2,1)}, u32[]{:S(2)}, u32[]{:S(2)}) collective-permute-start(bf16[1040,256]{1,0:T(8,128)(2,1)S(1)} %collective-permute-done.1.rest_3_), channel_id=1, source_target_pairs={{0,56},{8,0},{16,8},{24,16},{32,24},{40,32},{48,40},{56,48},{1,57}... | collective-permute-start | bytes 1597448 | tf_op jit(solution)/shard_map/ppermute | solution.py:413
  46.7 24.4 %collective-permute-start.7 = (bf16[1040,256]{1,0:T(8,128)(2,1)S(1)}, bf16[1040,256]{1,0:T(8,128)(2,1)}, u32[]{:S(2)}, u32[]{:S(2)}) collective-permute-start(bf16[1040,256]{1,0:T(8,128)(2,1)S(1)} %collective-permute-done.6.rest_14_), channel_id=1, source_target_pairs={{0,8},{8,16},{16,24},{24,32},{32,40},{40,48},{48,56},{56,0},{1,9},... | collective-permute-start | bytes 1597448 | tf_op jit(solution)/shard_map/ppermute | solution.py:412
  50.9 22.7 %all-to-all-start = ((s32[16,1,8]{2,1,0:T(1,128)}), s32[16,1,8]{2,1,0:T(1,128)S(1)}, u32[]{:S(2)}, u32[]{:S(2)}) async-start(s32[16,1,8]{2,1,0:T(1,128)} %bitcast.3), calls=%async_computation | async-start | bytes 16384 | tf_op jit(solution)/shard_map/all_to_all | solution.py:420
  60.9 19.7 %collective-permute-start.12 = (bf16[1040,256]{1,0:T(8,128)(2,1)S(1)}, bf16[1040,256]{1,0:T(8,128)(2,1)}, u32[]{:S(2)}, u32[]{:S(2)}) collective-permute-start(bf16[1040,256]{1,0:T(8,128)(2,1)S(1)} %collective-permute-done.11.rest_15_), channel_id=1, source_target_pairs={{0,8},{8,16},{16,24},{24,32},{32,40},{40,48},{48,56},{56,0},{1,9},... | collective-permute-start | bytes 1597448 | tf_op jit(solution)/shard_map/ppermute | solution.py:412
  62.8 19.7 %collective-permute-start.2 = (bf16[1040,256]{1,0:T(8,128)(2,1)S(1)}, bf16[1040,256]{1,0:T(8,128)(2,1)}, u32[]{:S(2)}, u32[]{:S(2)}) collective-permute-start(bf16[1040,256]{1,0:T(8,128)(2,1)S(1)} %collective-permute-done.rest_2_), channel_id=1, source_target_pairs={{0,56},{8,0},{16,8},{24,16},{32,24},{40,32},{48,40},{56,48},{1,57}... | collective-permute-start | bytes 1597448 | tf_op jit(solution)/shard_map/ppermute | solution.py:413
  67.7 22.9 %collective-permute-start.5 = (bf16[1040,256]{1,0:T(8,128)(2,1)}, bf16[1040,256]{1,0:T(8,128)(2,1)}, u32[]{:S(2)}, u32[]{:S(2)}) collective-permute-start(bf16[1040,256]{1,0:T(8,128)(2,1)} %collective-permute-done.3.rest_5_), channel_id=1, source_target_pairs={{0,56},{8,0},{16,8},{24,16},{32,24},{40,32},{48,40},{56,48},{1,57}... | collective-permute-start | bytes 1597448 | tf_op jit(solution)/shard_map/ppermute | solution.py:413
  71.1 24.9 %collective-permute-start.8 = (bf16[1040,256]{1,0:T(8,128)(2,1)}, bf16[1040,256]{1,0:T(8,128)(2,1)}, u32[]{:S(2)}, u32[]{:S(2)}) collective-permute-start(bf16[1040,256]{1,0:T(8,128)(2,1)} %collective-permute-done.7.rest_12_), channel_id=1, source_target_pairs={{0,8},{8,16},{16,24},{24,32},{32,40},{40,48},{48,56},{56,0},{1,9},... | collective-permute-start | bytes 1597448 | tf_op jit(solution)/shard_map/ppermute | solution.py:412
  80.6 22.8 %collective-permute-start.13 = (bf16[1040,256]{1,0:T(8,128)(2,1)}, bf16[1040,256]{1,0:T(8,128)(2,1)}, u32[]{:S(2)}, u32[]{:S(2)}) collective-permute-start(bf16[1040,256]{1,0:T(8,128)(2,1)} %collective-permute-done.12.rest_13_), channel_id=1, source_target_pairs={{0,8},{8,16},{16,24},{24,32},{32,40},{40,48},{48,56},{56,0},{1,9},... | collective-permute-start | bytes 1597448 | tf_op jit(solution)/shard_map/ppermute | solution.py:412
  82.5 20.9 %collective-permute-start.4 = (bf16[1040,256]{1,0:T(8,128)(2,1)}, bf16[1040,256]{1,0:T(8,128)(2,1)}, u32[]{:S(2)}, u32[]{:S(2)}) collective-permute-start(bf16[1040,256]{1,0:T(8,128)(2,1)} %collective-permute-done.2.rest_4_), channel_id=1, source_target_pairs={{0,56},{8,0},{16,8},{24,16},{32,24},{40,32},{48,40},{56,48},{1,57}... | collective-permute-start | bytes 1597448 | tf_op jit(solution)/shard_map/ppermute | solution.py:413
  90.6 22.4 %collective-permute-start.10 = (bf16[1040,256]{1,0:T(8,128)(2,1)}, bf16[1040,256]{1,0:T(8,128)(2,1)}, u32[]{:S(2)}, u32[]{:S(2)}) collective-permute-start(bf16[1040,256]{1,0:T(8,128)(2,1)} %collective-permute-done.5.rest_7_), channel_id=1, source_target_pairs={{0,56},{8,0},{16,8},{24,16},{32,24},{40,32},{48,40},{56,48},{1,57}... | collective-permute-start | bytes 1597448 | tf_op jit(solution)/shard_map/ppermute | solution.py:413
  96.0 18.8 %collective-permute-start.9 = (bf16[1040,256]{1,0:T(8,128)(2,1)}, bf16[1040,256]{1,0:T(8,128)(2,1)}, u32[]{:S(2)}, u32[]{:S(2)}) collective-permute-start(bf16[1040,256]{1,0:T(8,128)(2,1)} %collective-permute-done.8.rest_10_), channel_id=1, source_target_pairs={{0,8},{8,16},{16,24},{24,32},{32,40},{40,48},{48,56},{56,0},{1,9},... | collective-permute-start | bytes 1597448 | tf_op jit(solution)/shard_map/ppermute | solution.py:412
  217.9 17.8 %all-to-all-start.8 = ((f32[16,32,128]{2,1,0:T(8,128)}), f32[16,32,128]{2,1,0:T(8,128)S(1)}, u32[]{:S(2)}, u32[]{:S(2)}) async-start(f32[16,32,128]{2,1,0:T(8,128)} %get-tuple-element.15), calls=%async_computation.8 | async-start | bytes 524288 | tf_op jit(solution)/shard_map/all_to_all | solution.py:420
Sparse Core Ops, SparseCore 0:
  12.6 105.0 all-gather.2

commit v4 on v3

--- a/solution.py
+++ b/solution.py
@@ -35,7 +35,6 @@
 NN = (((1,), (0,)), ((), ()))
 VMEM_WHOLE = pl.BlockSpec(memory_space=pltpu.VMEM)
 SMEM_WHOLE = pl.BlockSpec(memory_space=pltpu.SMEM)
-ANYWHERE = pl.BlockSpec(memory_space=pl.ANY)
 IN_HBM = pl.BlockSpec(memory_space=pltpu.HBM)
 GRANT = 40 * MIB
 
@@ -55,7 +54,7 @@
     return jnp.where(rows == places, 1.0, 0.0)
 
 
-def project_kernel(frames, projection, out, here, made, norms, sems, out_sems):
+def project_kernel(frames, head, out, here, projection, made, norms, sems, head_sem, out_sems):
     def inward(n):
         rows = pl.ds(n * PART, PART)
         return pltpu.make_async_copy(frames.at[rows], here.at[rows], sems.at[n])
@@ -63,9 +62,13 @@
     def outward(h):
         return pltpu.make_async_copy(made.at[h], out.at[h], out_sems.at[h])
 
-    for n in range(ROWS // PART):
+    head_copy = pltpu.make_async_copy(head, projection, head_sem)
+    inward(0).start()
+    head_copy.start()
+    for n in range(1, ROWS // PART):
         inward(n).start()
     ones = jnp.ones((16, E), BF16)
+    head_copy.wait()
     for h in range(2):
         for j in range(HB):
             k = h * HB + j
@@ -94,17 +97,19 @@
     return pl.pallas_call(
         project_kernel,
         out_shape=pltpu.HBM((2, HALF, E), BF16),
-        in_specs=[IN_HBM, VMEM_WHOLE],
+        in_specs=[IN_HBM, IN_HBM],
         out_specs=IN_HBM,
         scratch_shapes=[
             pltpu.VMEM((ROWS, E), BF16),
+            pltpu.VMEM((E, E), BF16),
             pltpu.VMEM((2, HALF, E), BF16),
             pltpu.VMEM((HB, BLK), F32),
             pltpu.SemaphoreType.DMA((ROWS // PART,)),
+            pltpu.SemaphoreType.DMA,
             pltpu.SemaphoreType.DMA((2,)),
         ],
         compiler_params=pltpu.CompilerParams(vmem_limit_bytes=GRANT),
-    )(in_hbm(frames), projection)
+    )(in_hbm(frames), in_hbm(projection))
 
 
 def in_hbm(value):
@@ -113,33 +118,44 @@
 
 AHEAD = 2
 SLOTS = AHEAD + 1
-CHUNK = 32
+CHUNK = 16
 CHUNKS = POS // CHUNK
 
 
-def first_kernel(code, col_at, row_at, col_place, row_place, left, *rest):
+def chunks_of(count):
+    return (count[0] + CHUNK - 1) // CHUNK
+
+
+def first_kernel(count, place, col_at, row_at, col_place, row_place, left, *rest):
     rights = rest[: 2 * NZ]
     (
         cross, columns, sums, taken, tails, held, picks, parts, norms, made,
         sems, tail_sem, right_sem, out_sem,
     ) = rest[2 * NZ :]
-
-    def moves(z):
-        slot = z % SLOTS
+    chunks = chunks_of(count)
+
+    def taken_apart(at):
+        value = place[at]
+        return value // (256 * SOURCES), value // 256 % SOURCES, value // KB % KB, value % KB
+
+    def moves(i):
+        slot = i % SLOTS
         copies = []
-        for n in range(SOURCES):
-            k = jnp.maximum(code[z * SOURCES + n], 0) // KB
+        for n in range(CHUNK):
+            _, source, k, _ = taken_apart(i * CHUNK + n)
             start = pl.multiple_of(k % HB * BLK, BLK)
             copies.append(
                 pltpu.make_async_copy(
-                    left.at[n, k // HB, pl.ds(start, BLK)], taken.at[slot, n], sems.at[slot, n]
+                    left.at[source, k // HB, pl.ds(start, BLK)],
+                    taken.at[slot, n],
+                    sems.at[slot, n],
                 )
             )
         return copies
 
-    def away(z):
-        slot = z % SLOTS
-        to = cross.at[pl.ds(z * SOURCES, SOURCES)]
+    def away(i):
+        slot = i % SLOTS
+        to = cross.at[pl.ds(i * CHUNK, CHUNK)]
         return pltpu.make_async_copy(made.at[slot], to, out_sem.at[slot])
 
     into = [
@@ -150,11 +166,18 @@
         left.at[:, :, pl.ds(HB * BLK, 2 * HB)], tails, tail_sem
     )
     tail_copy.start()
-    for z in range(AHEAD):
-        for copy in into[2 * z : 2 * z + 2] + moves(z):
+    for i in range(AHEAD):
+        for copy in into[2 * i : 2 * i + 2]:
             copy.start()
+
+        @pl.when(i < chunks)
+        def _():
+            for copy in moves(i):
+                copy.start()
+
     for copy in into[2 * AHEAD :]:
         copy.start()
+    sums[...] = jnp.zeros_like(sums)
     row = lax.broadcasted_iota(jnp.int32, (4 * KB, BLK), 0)
     for k in range(KB):
         ours = (row // (2 * KB) == k // HB) & (row % HB == k % HB)
@@ -167,61 +190,79 @@
             stacked += [tail[:, 0:BLK], tail[:, BLK:E]]
         parts[n] = jnp.concatenate(stacked, axis=0).T.astype(BF16)
 
-    @pl.loop(0, NZ)
-    def _(z):
-        slot = z % SLOTS
-
-        @pl.when(z + AHEAD < NZ)
+    def last_piece(i):
+        return place[i * CHUNK + CHUNK - 1] // (256 * SOURCES)
+
+    def one(i, seen):
+        slot = i % SLOTS
+
+        @pl.when(i + AHEAD < chunks)
         def _():
-            for copy in moves(z + AHEAD):
+            for copy in moves(i + AHEAD):
                 copy.start()
 
-        @pl.when(z >= SLOTS)
+        @pl.when(i >= SLOTS)
         def _():
-            away(z - SLOTS).wait()
-
-        for h in range(2):
-            pltpu.make_async_copy(rights[h], held.at[z, h], right_sem.at[2 * z + h]).wait()
-            tail = held[z, h, HB * BLK : HALF, :].astype(F32)
-            norm = tail[0:HB, 0:BLK] + tail[0:HB, BLK:E] + tail[HB : 2 * HB, 0:BLK]
-            norms[h * HB : (h + 1) * HB, :] = 0.5 * norm
-        for copy in moves(z):
+            away(i - SLOTS).wait()
+
+        needed = last_piece(i)
+        for z in range(NZ):
+
+            @pl.when((z > seen) & (z <= needed))
+            def _():
+                for h in range(2):
+                    into[2 * z + h].wait()
+                    tail = held[z, h, HB * BLK : HALF, :].astype(F32)
+                    norm = tail[0:HB, 0:BLK] + tail[0:HB, BLK:E] + tail[HB : 2 * HB, 0:BLK]
+                    norms[z * KB + h * HB : z * KB + (h + 1) * HB, :] = 0.5 * norm
+
+        for copy in moves(i):
             copy.wait()
         rows = []
-        for n in range(SOURCES):
-            value = code[z * SOURCES + n]
-            off = jnp.where(value >= 0, SHIFT2, OFF)
-            value = jnp.maximum(value, 0)
-            k, t = value // KB, value % KB
+        for n in range(CHUNK):
+            z, source, k, t = taken_apart(i * CHUNK + n)
+            off = jnp.where(i * CHUNK + n < count[0], SHIFT2, OFF)
             v = held[z, t // HB, pl.ds(pl.multiple_of(t % HB * BLK, BLK), BLK), :]
-            w = dot(taken[slot, n], v, NT) + dot(parts[n], picks[k], NN)
-            w = w - norms[pl.ds(t, 1), :]
+            w = dot(taken[slot, n], v, NT) + dot(parts[source], picks[k], NN)
+            w = w - norms[pl.ds(z * KB + t, 1), :]
             made[slot, n] = w
             rows.append(jnp.sum(jnp.exp2(w * BETA + off), axis=0, keepdims=True))
-        away(z).start()
-        place = pl.ds(pl.multiple_of(z * SOURCES, SOURCES), SOURCES)
-        sums[place, :] = jnp.concatenate(rows, axis=0)
-
+        away(i).start()
+        sums[pl.ds(pl.multiple_of(i * CHUNK, CHUNK), CHUNK), :] = jnp.concatenate(rows, axis=0)
+        return needed
+
+    seen = lax.fori_loop(0, chunks, one, -1)
     columns[...] = exact_sum(spread(col_place[...], NZ * KB), sums[...]).astype(BF16)
-    for z in range(NZ - SLOTS, NZ):
-        away(z).wait()
-
-
-def first_pass(code, col_at, row_at, col_place, row_place, left, rights):
+    for z in range(NZ):
+
+        @pl.when(z > seen)
+        def _():
+            for h in range(2):
+                into[2 * z + h].wait()
+
+    for n in range(SLOTS):
+        i = chunks - 1 - n
+
+        @pl.when(i >= 0)
+        def _():
+            away(i).wait()
+
+
+def first_pass(count, place, col_at, row_at, col_place, row_place, left, rights):
     return pl.pallas_call(
         first_kernel,
-        in_specs=[SMEM_WHOLE] * 3 + [VMEM_WHOLE] * 2 + [ANYWHERE] * (2 * NZ + 1),
+        in_specs=[SMEM_WHOLE] * 4 + [VMEM_WHOLE] * 2 + [IN_HBM] * (2 * NZ + 1),
         out_specs=[IN_HBM, VMEM_WHOLE],
         scratch_shapes=[
             pltpu.VMEM((POS, BLK), F32),
-            pltpu.VMEM((SLOTS, SOURCES, BLK, E), BF16),
+            pltpu.VMEM((SLOTS, CHUNK, BLK, E), BF16),
             pltpu.VMEM((SOURCES, 2, 2 * HB, E), BF16),
             pltpu.VMEM((NZ, 2, HALF, E), BF16),
             pltpu.VMEM((KB, 4 * KB, BLK), BF16),
             pltpu.VMEM((SOURCES, BLK, 4 * KB), BF16),
-            pltpu.VMEM((KB, BLK), F32),
-            pltpu.VMEM((SLOTS, SOURCES, BLK, BLK), F32),
-            pltpu.SemaphoreType.DMA((SLOTS, SOURCES)),
+            pltpu.VMEM((NZ * KB, BLK), F32),
+            pltpu.VMEM((SLOTS, CHUNK, BLK, BLK), F32),
+            pltpu.SemaphoreType.DMA((SLOTS, CHUNK)),
             pltpu.SemaphoreType.DMA,
             pltpu.SemaphoreType.DMA((2 * NZ,)),
             pltpu.SemaphoreType.DMA((SLOTS,)),
@@ -231,7 +272,7 @@
             jax.ShapeDtypeStruct((NZ * KB, BLK), BF16),
         ],
         compiler_params=pltpu.CompilerParams(vmem_limit_bytes=GRANT),
-    )(code, col_at, row_at, col_place, row_place, left, *rights)
+    )(count, place, col_at, row_at, col_place, row_place, in_hbm(left), *map(in_hbm, rights))
 
 
 def total_of(received):
@@ -246,28 +287,33 @@
     return pltpu.make_async_copy(source.at[part], target.at[part], sems.at[n])
 
 
-def start_all(source, target, sems):
+def start_all(source, target, sems, chunks):
     for n in range(CHUNKS):
-        one_chunk(source, target, sems, n).start()
+
+        @pl.when(n < chunks)
+        def _():
+            one_chunk(source, target, sems, n).start()
 
 
 def second_kernel(
-    col_at, row_place, received, cross, kernel, rows_out, column_sum,
+    count, col_at, row_place, received, cross, kernel, rows_out, column_sum,
     cross_here, kernel_here, potential, sums, in_sem, kernel_sem,
 ):
-    start_all(cross, cross_here, in_sem)
+    chunks = chunks_of(count)
+    start_all(cross, cross_here, in_sem, chunks)
+    sums[...] = jnp.zeros_like(sums)
     column_sum[...] = total_of(received)
     potential[...] = 2.0 * SHIFT2 - jnp.log2(FLOOR + column_sum[...])
     ones = jnp.ones((16, BLK), BF16)
 
-    @pl.loop(0, CHUNKS)
+    @pl.loop(0, chunks)
     def _(step):
         one_chunk(cross, cross_here, in_sem, step).wait()
         rows = []
         for n in range(CHUNK):
             tile = step * CHUNK + n
-            at = col_at[tile]
-            pot = potential[pl.ds(jnp.maximum(at, 0), 1), :] + jnp.where(at >= 0, 0.0, OFF)
+            off = jnp.where(tile < count[0], 0.0, OFF)
+            pot = potential[pl.ds(col_at[tile], 1), :] + off
             w = cross_here[tile]
             rounded = jnp.exp2(w * BETA + pot).astype(BF16)
             kernel_here[tile, 0:BLK, :] = rounded
@@ -280,15 +326,15 @@
 
     rows_out[...] = exact_sum(spread(row_place[...], SOURCES * KB), sums[...]).astype(BF16)
 
-    @pl.loop(0, CHUNKS)
+    @pl.loop(0, chunks)
     def _(step):
         one_chunk(kernel_here, kernel, kernel_sem, step).wait()
 
 
-def second_pass(col_at, row_place, received, cross):
+def second_pass(count, col_at, row_place, received, cross):
     return pl.pallas_call(
         second_kernel,
-        in_specs=[SMEM_WHOLE, VMEM_WHOLE, VMEM_WHOLE, IN_HBM],
+        in_specs=[SMEM_WHOLE, SMEM_WHOLE, VMEM_WHOLE, VMEM_WHOLE, IN_HBM],
         out_specs=[IN_HBM, VMEM_WHOLE, VMEM_WHOLE],
         scratch_shapes=[
             pltpu.VMEM((POS, BLK, BLK), F32),
@@ -304,7 +350,7 @@
             jax.ShapeDtypeStruct((NZ * KB, BLK), F32),
         ],
         compiler_params=pltpu.CompilerParams(vmem_limit_bytes=GRANT),
-    )(col_at, row_place, received, in_hbm(cross))
+    )(count, col_at, row_place, received, in_hbm(cross))
 
 
 def two_parts(row):
@@ -313,29 +359,32 @@
     return jnp.where(at == 0, high, jnp.where(at == 1, row - high, 0.0)).astype(BF16)
 
 
-def third_kernel(row_at, col_place, received, kernel, columns, kernel_here, scale, sums, in_sem):
+def third_kernel(
+    count, row_at, col_place, received, kernel, columns, kernel_here, scale, sums, in_sem
+):
+    chunks = chunks_of(count)
+    sums[...] = jnp.zeros_like(sums)
     upper = kernel.at[:, pl.ds(0, BLK)]
-    start_all(upper, kernel_here, in_sem)
+    start_all(upper, kernel_here, in_sem, chunks)
     scale[...] = 1.0 / (FLOOR + received[...].astype(F32))
 
-    @pl.loop(0, CHUNKS)
+    @pl.loop(0, chunks)
     def _(step):
         one_chunk(upper, kernel_here, in_sem, step).wait()
         rows = []
         for n in range(CHUNK):
             tile = step * CHUNK + n
-            at = jnp.maximum(row_at[tile], 0)
-            both = dot(two_parts(scale[pl.ds(at, 1), :]), kernel_here[tile], NN)
+            both = dot(two_parts(scale[pl.ds(row_at[tile], 1), :]), kernel_here[tile], NN)
             rows.append(both[0:1, :] + both[1:2, :])
         sums[pl.ds(pl.multiple_of(step * CHUNK, CHUNK), CHUNK), :] = jnp.concatenate(rows, axis=0)
 
     columns[...] = exact_sum(spread(col_place[...], NZ * KB), sums[...]).astype(BF16)
 
 
-def third_pass(row_at, col_place, received, kernel):
+def third_pass(count, row_at, col_place, received, kernel):
     return pl.pallas_call(
         third_kernel,
-        in_specs=[SMEM_WHOLE, VMEM_WHOLE, VMEM_WHOLE, IN_HBM],
+        in_specs=[SMEM_WHOLE, SMEM_WHOLE, VMEM_WHOLE, VMEM_WHOLE, IN_HBM],
         out_specs=VMEM_WHOLE,
         scratch_shapes=[
             pltpu.VMEM((POS, BLK, BLK), BF16),
@@ -345,25 +394,28 @@
         ],
         out_shape=jax.ShapeDtypeStruct((NZ * KB, BLK), BF16),
         compiler_params=pltpu.CompilerParams(vmem_limit_bytes=GRANT),
-    )(row_at, col_place, received, in_hbm(kernel))
+    )(count, row_at, col_place, received, in_hbm(kernel))
 
 
 def fourth_kernel(
-    col_at, row_place, received, column_sum, kernel, rows_out, plan_out,
+    count, col_at, row_place, received, column_sum, kernel, rows_out, plan_out,
     kernel_here, scale, sums, weighed, kernel_sem,
 ):
-    start_all(kernel, kernel_here, kernel_sem)
+    chunks = chunks_of(count)
+    start_all(kernel, kernel_here, kernel_sem, chunks)
+    sums[...] = jnp.zeros_like(sums)
+    weighed[...] = jnp.zeros_like(weighed)
     plan_sum = total_of(received)
     plan_out[...] = plan_sum
     scale[...] = 1.0 / (FLOOR / (FLOOR + column_sum[...]) + plan_sum)
 
-    @pl.loop(0, CHUNKS)
+    @pl.loop(0, chunks)
     def _(step):
         one_chunk(kernel, kernel_here, kernel_sem, step).wait()
         rows, heavy = [], []
         for n in range(CHUNK):
             tile = step * CHUNK + n
-            pair = two_parts(scale[pl.ds(jnp.maximum(col_at[tile], 0), 1), :])
+            pair = two_parts(scale[pl.ds(col_at[tile], 1), :])
             both = dot(pair, kernel_here[tile], NT)
             both = both[0:1, :] + both[1:2, :]
             rows.append(both[:, 0:BLK])
@@ -381,10 +433,10 @@
         rows_out[y * NC + c, KB : 2 * KB, :] = heavy_total[s * KB : (s + 1) * KB, :]
 
 
-def fourth_pass(col_at, row_place, received, column_sum, kernel):
+def fourth_pass(count, col_at, row_place, received, column_sum, kernel):
     return pl.pallas_call(
         fourth_kernel,
-        in_specs=[SMEM_WHOLE] + [VMEM_WHOLE] * 3 + [IN_HBM],
+        in_specs=[SMEM_WHOLE] * 2 + [VMEM_WHOLE] * 3 + [IN_HBM],
         out_specs=[VMEM_WHOLE] * 2,
         scratch_shapes=[
             pltpu.VMEM((POS, 2 * BLK, BLK), BF16),
@@ -398,7 +450,7 @@
             jax.ShapeDtypeStruct((NZ * KB, BLK), F32),
         ],
         compiler_params=pltpu.CompilerParams(vmem_limit_bytes=GRANT),
-    )(col_at, row_place, received, column_sum, in_hbm(kernel))
+    )(count, col_at, row_place, received, column_sum, in_hbm(kernel))
 
 
 def ring_pieces(block, axis, n):
@@ -447,6 +499,18 @@
     return jnp.max(jnp.where(match, (block * KB + local)[None, :], -1), axis=1)
 
 
+def in_use(codes):
+    at = jnp.arange(POS, dtype=jnp.int32)
+    active = codes >= 0
+    rank = jnp.sum((active[None, :] & (at[None, :] < at[:, None])).astype(jnp.int32), axis=1)
+    count = jnp.sum(active.astype(jnp.int32))
+    place = jnp.where(active, at * 256 + codes, 0)
+    lands = active[None, :] & (rank[None, :] == at[:, None])
+    sorted_ = jnp.max(jnp.where(lands, place[None, :], 0), axis=1)
+    used = at < count
+    return count.reshape(1), jnp.where(used, sorted_, jnp.max(place)), used
+
+
 def body(rollout, demo, projection, location, pair_block, pair_count):
     codes = slot_codes(location, pair_block, pair_count)
     codes = codes.reshape(NY, NZ, NC).transpose(0, 2, 1).reshape(SOURCES, NZ)
@@ -454,27 +518,28 @@
     turned = (lax.axis_index("z") + jnp.arange(NZ, dtype=jnp.int32)) % NZ
     pick = turned[:, None] == jnp.arange(NZ, dtype=jnp.int32)[None, :]
     codes = jnp.max(jnp.where(pick[:, None, :], codes[None], -1), axis=2)
-    used = codes >= 0
-    col_at = jnp.where(used, turned[:, None] * KB + codes % KB, -1).reshape(POS)
-    source = jnp.arange(SOURCES, dtype=jnp.int32)
-    source = (source % NC * NY + source // NC)[None, :]
-    row_at = jnp.where(used, source * KB + codes // KB, -1).reshape(POS)
-    col_place, row_place = col_at.reshape(1, POS), row_at.reshape(1, POS)
-    codes = codes.reshape(POS)
+    count, place, used = in_use(codes.reshape(POS))
+    piece, source = place // (256 * SOURCES), place // 256 % SOURCES
+    col_at = (lax.axis_index("z") + piece) % NZ * KB + place % KB
+    row_at = (source % NC * NY + source // NC) * KB + place // KB % KB
+    col_place = jnp.where(used, col_at, -1).reshape(1, POS)
+    row_place = jnp.where(used, row_at, -1).reshape(1, POS)
 
     left = lax.all_gather(project(rollout, projection), ("y", "c"))
     rights = ring_pieces(project(demo, projection), "z", NZ)
 
-    cross, columns = first_pass(codes, col_at, row_at, col_place, row_place, left, rights)
+    cross, columns = first_pass(
+        count, place, col_at, row_at, col_place, row_place, left, rights
+    )
     kernel, rows, column_sum = second_pass(
-        col_at, row_place, columns_to_row(columns), cross
+        count, col_at, row_place, columns_to_row(columns), cross
     )
     rows = jnp.sum(swap(rows.reshape(NC, NY * KB, BLK), "c").astype(F32), axis=0)
     rows = jnp.sum(to_all(rows.astype(BF16), "y", NY).astype(F32), axis=0)
     rows = to_all(rows.astype(BF16), "c", NC).reshape(SOURCES * KB, BLK)
-    columns = third_pass(row_at, col_place, rows, kernel)
+    columns = third_pass(count, row_at, col_place, rows, kernel)
     both, plan_sum = fourth_pass(
-        col_at, row_place, columns_to_row(columns), column_sum, kernel
+        count, col_at, row_place, columns_to_row(columns), column_sum, kernel
     )
     both = jnp.sum(swap(both, ("y", "c")), axis=0)
     total = FLOOR + both[:KB]

time: 244 us -> 242 us (level)
  starting transfers between devices: 69.1 us -> 65.6 us
  other arithmetic: 2.43 us -> 5.93 us
    ppermute x7, starting transfers between devices: 39.6 us -> 32.9 us  [ring_pieces(): left[i] = lax.ppermute(left[i], axis, down)]
    ppermute x7, starting transfers between devices: 13.4 us -> 17.7 us  [ring_pieces(): right[i] = lax.ppermute(right[i], axis, up)]
    pallas_call x4, Pallas kernels: 28.3 us -> 25.5 us  [the longest x1 10.8 us: first_pass(): pl.pallas_call(first_kernel, in_specs=[SMEM_WHOLE] * 4 + [VMEM_WHOLE] * 2...]
  transfers between devices with their start and end apart: 17 -> 17, of which waited for: 8 -> 9; matrix products, arithmetic and copies ran while one was open for 3% -> 4% of each run, Pallas kernels for 2% -> 2%
where the time goes in v4:
time: 242 us; the launch traced here: 241 us
  blocking collectives  72 us (30%)
  starting transfers between devices  65.6 us (27%)
  waiting for transfers between devices  42.6 us (18%)
  Pallas kernels  34.5 us (14%)
  between operations  14.5 us (6%)
  other arithmetic  5.93 us (2%)
  local copies, waits for them, and re-layouts  5.36 us (2%)
    all_to_all x7, blocking collectives, swap(): return lax.all_to_all(value, axes, split_axis=0, concat_axis=0, tiled=True)  72 us
    ppermute x7, starting transfers between devices, ring_pieces(): left[i] = lax.ppermute(left[i], axis, down)  32.9 us
    ppermute x7, starting transfers between devices, ring_pieces(): right[i] = lax.ppermute(right[i], axis, up)  17.7 us
    all_to_all x2, starting transfers between devices, swap(): return lax.all_to_all(value, axes, split_axis=0, concat_axis=0, tiled=True)  15 us
    ppermute x7, waiting for transfers between devices, ring_pieces(): right[i] = lax.ppermute(right[i], axis, up)  14.7 us
    all_to_all x2, waiting for transfers between devices, swap(): return lax.all_to_all(value, axes, split_axis=0, concat_axis=0, tiled=True)  12.8 us
    ppermute x7, waiting for transfers between devices, ring_pieces(): left[i] = lax.ppermute(left[i], axis, down)  12.1 us
    pallas_call x1, Pallas kernels, first_pass(): pl.pallas_call(first_kernel, in_specs=[SMEM_WHOLE] * 4 + [VMEM_WHOLE] * 2...  10.8 us
  transfers between devices with their start and end apart: 17, of which 9 were waited for; matrix products, arithmetic and copies ran while one was open for 4% of the time, Pallas kernels for 2%

profile of v4, /device:TPU:1, one launch (start us, length us, event | category | flops | bytes accessed | tf_op | source)
XLA Modules:
  0.0 240.6 jit_solution(13675016890514485459)
XLA Ops:
  7.2 4.5 %shard_map.85 = bf16[2,1040,256]{2,1,0:T(8,128)(2,1)} custom-call(bf16[2048,256]{1,0:T(8,128)(2,1)} %frames.2, bf16[256,256]{1,0:T(8,128)(2,1)} %head.3), custom_call_target="tpu_custom_call" | custom-call | tf_op jit(solution)/shard_map/pallas_call | solution.py:97
  11.8 4.5 %shard_map.86 = bf16[2,1040,256]{2,1,0:T(8,128)(2,1)} custom-call(bf16[2048,256]{1,0:T(8,128)(2,1)} %frames.3, bf16[256,256]{1,0:T(8,128)(2,1)} %head.3), custom_call_target="tpu_custom_call" | custom-call | tf_op jit(solution)/shard_map/pallas_call | solution.py:97
  16.3 1.3 slice_bitcast_fusion
  17.6 4.8 %collective-permute-start.11 = (bf16[1040,256]{1,0:T(8,128)(2,1)S(1)}, bf16[1040,256]{1,0:T(8,128)(2,1)S(1)}, u32[]{:S(2)}, u32[]{:S(2)}) collective-permute-start(bf16[1040,256]{1,0:T(8,128)(2,1)S(1)} %get-tuple-element.21.rest_1_), channel_id=1, source_target_pairs={{0,8},{8,16},{16,24},{24,32},{32,40},{40,48},{48,56},{56,0},{1,9},... | collective-permute-start | bytes 1597448 | tf_op jit(solution)/shard_map/ppermute | solution.py:464
  22.4 8.6 %collective-permute-start.1 = (bf16[1040,256]{1,0:T(8,128)(2,1)S(1)}, bf16[1040,256]{1,0:T(8,128)(2,1)S(1)}, u32[]{:S(2)}, u32[]{:S(2)}) collective-permute-start(bf16[1040,256]{1,0:T(8,128)(2,1)S(1)} %get-tuple-element.21.rest_1_), channel_id=1, source_target_pairs={{0,56},{8,0},{16,8},{24,16},{32,24},{40,32},{48,40},{56,48},{1,57}... | collective-permute-start | bytes 1597448 | tf_op jit(solution)/shard_map/ppermute | solution.py:465
  31.0 1.9 collective-permute-start.6
  32.9 4.6 %collective-permute-start = (bf16[1040,256]{1,0:T(8,128)(2,1)S(1)}, bf16[1040,256]{1,0:T(8,128)(2,1)S(1)}, u32[]{:S(2)}, u32[]{:S(2)}) collective-permute-start(bf16[1040,256]{1,0:T(8,128)(2,1)S(1)} %get-tuple-element.22.rest_0_), channel_id=1, source_target_pairs={{0,56},{8,0},{16,8},{24,16},{32,24},{40,32},{48,40},{56,48},{1,57}... | collective-permute-start | bytes 1597448 | tf_op jit(solution)/shard_map/ppermute | solution.py:465
  37.5 0.7 iota_compare_fusion.3
  38.3 0.8 copy.22
  39.2 1.1 gather_fusion
  40.6 0.7 copy.23
  41.4 8.6 %all-to-all-start = ((s32[16,1,8]{2,1,0:T(1,128)}), s32[16,1,8]{2,1,0:T(1,128)S(1)}, u32[]{:S(2)}, u32[]{:S(2)}) async-start(s32[16,1,8]{2,1,0:T(1,128)} %bitcast.3), calls=%async_computation | async-start | bytes 16384 | tf_op jit(solution)/shard_map/all_to_all | solution.py:472
  50.0 2.5 %collective-permute-start.3 = (bf16[1040,256]{1,0:T(8,128)(2,1)S(1)}, bf16[1040,256]{1,0:T(8,128)(2,1)}, u32[]{:S(2)}, u32[]{:S(2)}) collective-permute-start(bf16[1040,256]{1,0:T(8,128)(2,1)S(1)} %collective-permute-done.1.rest_3_), channel_id=1, source_target_pairs={{0,56},{8,0},{16,8},{24,16},{32,24},{40,32},{48,40},{56,48},{1,57}... | collective-permute-start | bytes 1597448 | tf_op jit(solution)/shard_map/ppermute | solution.py:465
  52.5 2.9 %collective-permute-start.7 = (bf16[1040,256]{1,0:T(8,128)(2,1)S(1)}, bf16[1040,256]{1,0:T(8,128)(2,1)}, u32[]{:S(2)}, u32[]{:S(2)}) collective-permute-start(bf16[1040,256]{1,0:T(8,128)(2,1)S(1)} %collective-permute-done.6.rest_14_), channel_id=1, source_target_pairs={{0,8},{8,16},{16,24},{24,32},{32,40},{40,48},{48,56},{56,0},{1,9},... | collective-permute-start | bytes 1597448 | tf_op jit(solution)/shard_map/ppermute | solution.py:464
  55.5 1.6 all-to-all-done
  57.3 1.9 collective-permute-start.12
  59.2 4.6 %collective-permute-start.2 = (bf16[1040,256]{1,0:T(8,128)(2,1)S(1)}, bf16[1040,256]{1,0:T(8,128)(2,1)S(1)}, u32[]{:S(2)}, u32[]{:S(2)}) collective-permute-start(bf16[1040,256]{1,0:T(8,128)(2,1)S(1)} %collective-permute-done.rest_2_), channel_id=1, source_target_pairs={{0,56},{8,0},{16,8},{24,16},{32,24},{40,32},{48,40},{56,48},{1,57}... | collective-permute-start | bytes 1597448 | tf_op jit(solution)/shard_map/ppermute | solution.py:465
  63.8 1.9 collective-permute-done.3.rest_5_
  65.7 4.3 %collective-permute-start.5 = (bf16[1040,256]{1,0:T(8,128)(2,1)}, bf16[1040,256]{1,0:T(8,128)(2,1)S(1)}, u32[]{:S(2)}, u32[]{:S(2)}) collective-permute-start(bf16[1040,256]{1,0:T(8,128)(2,1)} %collective-permute-done.3.rest_5_), channel_id=1, source_target_pairs={{0,56},{8,0},{16,8},{24,16},{32,24},{40,32},{48,40},{56,48},{1,57}... | collective-permute-start | bytes 1597448 | tf_op jit(solution)/shard_map/ppermute | solution.py:465
  70.0 1.9 collective-permute-start.8
  71.9 0.6 select_reduce_fusion.3
  72.8 7.0 %collective-permute-done.12.rest_13_ = bf16[1040,256]{1,0:T(8,128)(2,1)S(1)} collective-permute-done((bf16[1040,256]{1,0:T(8,128)(2,1)S(1)}, bf16[1040,256]{1,0:T(8,128)(2,1)S(1)}, u32[]{:S(2)}, u32[]{:S(2)}) %collective-permute-start.12) | collective-permute-done | bytes 532512 | tf_op jit(solution)/shard_map/ppermute | solution.py:464
  79.8 2.3 collective-permute-start.13
  82.1 4.1 %collective-permute-start.4 = (bf16[1040,256]{1,0:T(8,128)(2,1)S(1)}, bf16[1040,256]{1,0:T(8,128)(2,1)S(1)}, u32[]{:S(2)}, u32[]{:S(2)}) collective-permute-start(bf16[1040,256]{1,0:T(8,128)(2,1)S(1)} %collective-permute-done.2.rest_4_), channel_id=1, source_target_pairs={{0,56},{8,0},{16,8},{24,16},{32,24},{40,32},{48,40},{56,48},{1,57}... | collective-permute-start | bytes 1597448 | tf_op jit(solution)/shard_map/ppermute | solution.py:465
  86.3 2.2 collective-permute-done.5.rest_7_
  88.5 4.3 %collective-permute-start.10 = (bf16[1040,256]{1,0:T(8,128)(2,1)S(1)}, bf16[1040,256]{1,0:T(8,128)(2,1)S(1)}, u32[]{:S(2)}, u32[]{:S(2)}) collective-permute-start(bf16[1040,256]{1,0:T(8,128)(2,1)S(1)} %collective-permute-done.5.rest_7_), channel_id=1, source_target_pairs={{0,56},{8,0},{16,8},{24,16},{32,24},{40,32},{48,40},{56,48},{1,57}... | collective-permute-start | bytes 1597448 | tf_op jit(solution)/shard_map/ppermute | solution.py:465
  92.8 1.9 collective-permute-start.9
  94.8 1.3 fusion.9
  96.1 1.3 fusion.11
  97.4 5.1 %collective-permute-done.13.rest_11_ = bf16[1040,256]{1,0:T(8,128)(2,1)S(1)} collective-permute-done((bf16[1040,256]{1,0:T(8,128)(2,1)S(1)}, bf16[1040,256]{1,0:T(8,128)(2,1)S(1)}, u32[]{:S(2)}, u32[]{:S(2)}) %collective-permute-start.13) | collective-permute-done | bytes 532512 | tf_op jit(solution)/shard_map/ppermute | solution.py:464
  102.6 8.0 %collective-permute-done.10.rest_9_ = bf16[1040,256]{1,0:T(8,128)(2,1)S(1)} collective-permute-done((bf16[1040,256]{1,0:T(8,128)(2,1)S(1)}, bf16[1040,256]{1,0:T(8,128)(2,1)S(1)}, u32[]{:S(2)}, u32[]{:S(2)}) %collective-permute-start.10) | collective-permute-done | bytes 532512 | tf_op jit(solution)/shard_map/ppermute | solution.py:465
  110.6 0.8 copy-done.13
  111.4 2.6 %collective-permute-done.9.rest_8_ = bf16[1040,256]{1,0:T(8,128)(2,1)} collective-permute-done((bf16[1040,256]{1,0:T(8,128)(2,1)S(1)}, bf16[1040,256]{1,0:T(8,128)(2,1)}, u32[]{:S(2)}, u32[]{:S(2)}) %collective-permute-start.9) | collective-permute-done | bytes 532512 | tf_op jit(solution)/shard_map/ppermute | solution.py:464
  114.0 3.0 %all-gather.3.cloned.1.call-done = bf16[32,1040,256]{2,1,0:T(8,128)(2,1)} async-done(((bf16[2,1040,256]{2,1,0:T(8,128)(2,1)}), bf16[32,1040,256]{2,1,0:T(8,128)(2,1)}) %all-gather.3.cloned.1.call-update) | async-done | bytes 17039376 | tf_op jit(solution)/shard_map/all_gather | solution.py:528
  117.0 10.8 %shard_map.87 = (f32[128,128,128]{2,1,0:T(8,128)}, bf16[128,128]{1,0:T(8,128)(2,1)S(1)}) custom-call(s32[1]{0:T(128)} %bitcast.5.count, s32[128]{0:T(128)S(1)} %get-tuple-element.20.place, s32[128]{0:T(128)S(1)} %fusion.7.col_at, s32[128]{0:T(128)S(1)} %get-tuple-element.19.row_at, s32[1,128]{1,0:T(1,128)S(1)} %get-tuple-element.25.col_place, ...), custom_call_target="tpu_custom_call" | custom-call | tf_op jit(solution)/shard_map/pallas_call | solution.py:252
  127.8 8.7 %all_to_all.45 = bf16[4,128,128]{2,1,0:T(8,128)(2,1)S(1)} all-to-all(bf16[4,128,128]{2,1,0:T(8,128)(2,1)S(1)} %broadcast_in_dim.114), channel_id=1, replica_groups=mesh['y'=8,'z'=8,'c'=2,'x'=4] {'x'}, dimensions={0} | all-to-all | bytes 262144 | tf_op jit(solution)/shard_map/all_to_all | solution.py:472
  136.5 19.3 %all_to_all.46.received = bf16[8,128,128]{2,1,0:T(8,128)(2,1)S(1)} all-to-all(bf16[8,128,128]{2,1,0:T(8,128)(2,1)S(1)} %broadcast_in_dim.115), channel_id=1, replica_groups=mesh['y'=8,'z'=8,'c'=2,'x'=4] {'z'}, dimensions={0} | all-to-all | bytes 524288 | tf_op jit(solution)/shard_map/all_to_all | solution.py:472
  155.8 5.4 %shard_map.88 = (bf16[128,256,128]{2,1,0:T(8,128)(2,1)}, bf16[256,128]{1,0:T(8,128)(2,1)S(1)}, f32[128,128]{1,0:T(8,128)S(1)}) custom-call(s32[1]{0:T(128)} %bitcast.5.count, s32[128]{0:T(128)S(1)} %fusion.7.col_at, s32[1,128]{1,0:T(1,128)S(1)} %get-tuple-element.26.row_place, bf16[8,128,128]{2,1,0:T(8,128)(2,1)S(1)} %all_to_all.46.received, ...), custom_call_target="tpu_custom_call" | custom-call | tf_op jit(solution)/shard_map/pallas_call | solution.py:335
  161.3 5.5 %all_to_all.47 = bf16[2,128,128]{2,1,0:T(8,128)(2,1)S(1)} all-to-all(bf16[2,128,128]{2,1,0:T(8,128)(2,1)S(1)} %bitcast.28), channel_id=1, replica_groups=mesh['y'=8,'z'=8,'c'=2,'x'=4] {'c'}, dimensions={0} | all-to-all | bytes 131072 | tf_op jit(solution)/shard_map/all_to_all | solution.py:472
  166.8 13.9 %all_to_all.48 = bf16[8,128,128]{2,1,0:T(8,128)(2,1)S(1)} all-to-all(bf16[8,128,128]{2,1,0:T(8,128)(2,1)S(1)} %broadcast_in_dim.116), channel_id=1, replica_groups=mesh['y'=8,'z'=8,'c'=2,'x'=4] {'y'}, dimensions={0} | all-to-all | bytes 524288 | tf_op jit(solution)/shard_map/all_to_all | solution.py:472
  180.8 5.1 %all_to_all.49 = bf16[2,128,128]{2,1,0:T(8,128)(2,1)S(1)} all-to-all(bf16[2,128,128]{2,1,0:T(8,128)(2,1)S(1)} %broadcast_in_dim.117), channel_id=1, replica_groups=mesh['y'=8,'z'=8,'c'=2,'x'=4] {'c'}, dimensions={0} | all-to-all | bytes 131072 | tf_op jit(solution)/shard_map/all_to_all | solution.py:472
  185.9 3.8 %shard_map.89 = bf16[128,128]{1,0:T(8,128)(2,1)S(1)} custom-call(s32[1]{0:T(128)} %bitcast.5.count, s32[128]{0:T(128)S(1)} %get-tuple-element.19.row_at, s32[1,128]{1,0:T(1,128)S(1)} %get-tuple-element.25.col_place, bf16[256,128]{1,0:T(8,128)(2,1)S(1)} %bitcast.27, bf16[128,256,128]{2,1,0:T(8,128)(2,1)} %get-tuple-element.13.kernel), custom_call_target="tpu_custom_call" | custom-call | tf_op jit(solution)/shard_map/pallas_call | solution.py:385
  189.7 7.2 %all_to_all.50 = bf16[4,128,128]{2,1,0:T(8,128)(2,1)S(1)} all-to-all(bf16[4,128,128]{2,1,0:T(8,128)(2,1)S(1)} %broadcast_in_dim.118), channel_id=1, replica_groups=mesh['y'=8,'z'=8,'c'=2,'x'=4] {'x'}, dimensions={0} | all-to-all | bytes 262144 | tf_op jit(solution)/shard_map/all_to_all | solution.py:472
  197.0 12.3 %all_to_all.51.received = bf16[8,128,128]{2,1,0:T(8,128)(2,1)S(1)} all-to-all(bf16[8,128,128]{2,1,0:T(8,128)(2,1)S(1)} %broadcast_in_dim.119), channel_id=1, replica_groups=mesh['y'=8,'z'=8,'c'=2,'x'=4] {'z'}, dimensions={0} | all-to-all | bytes 524288 | tf_op jit(solution)/shard_map/all_to_all | solution.py:472
  209.3 5.5 %shard_map.90 = (f32[16,32,128]{2,1,0:T(8,128)}, f32[128,128]{1,0:T(8,128)S(1)}) custom-call(s32[1]{0:T(128)} %bitcast.5.count, s32[128]{0:T(128)S(1)} %fusion.7.col_at, s32[1,128]{1,0:T(1,128)S(1)} %get-tuple-element.26.row_place, bf16[8,128,128]{2,1,0:T(8,128)(2,1)S(1)} %all_to_all.51.received, f32[128,128]{1,0:T(8,128)S(1)} %get-tuple-element.14.column_sum, ...), custom_call_target="tpu_custom_call" | custom-call | tf_op jit(solution)/shard_map/pallas_call | solution.py:437
  214.9 6.4 %all-to-all-start.8 = ((f32[16,32,128]{2,1,0:T(8,128)}), f32[16,32,128]{2,1,0:T(8,128)S(1)}, u32[]{:S(2)}, u32[]{:S(2)}) async-start(f32[16,32,128]{2,1,0:T(8,128)} %get-tuple-element.15), calls=%async_computation.8 | async-start | bytes 524288 | tf_op jit(solution)/shard_map/all_to_all | solution.py:472
  221.8 11.2 %all-to-all-done.8 = f32[16,32,128]{2,1,0:T(8,128)S(1)} async-done(((f32[16,32,128]{2,1,0:T(8,128)}), f32[16,32,128]{2,1,0:T(8,128)S(1)}, u32[]{:S(2)}, u32[]{:S(2)}) %all-to-all-start.8) | async-done | bytes 262176 | tf_op jit(solution)/shard_map/all_to_all | solution.py:472
  233.1 0.6 multiply_bitcast_fusion.1
  (66 shorter events, 2.0 us)
Async XLA Ops:
  7.2 32.0 %copy-start = (s32[2048]{0:T(1024)S(1)}, s32[2048]{0:T(1024)}, u32[]{:S(2)}) copy-start(s32[2048]{0:T(1024)} %param.9) | copy-start | bytes 24580
  7.2 109.8 %all-gather.3.cloned.1.call-start = ((), (), s32[]{:S(2)}) async-start(), calls=%async_computation.9 | async-start | bytes 18104320 | tf_op jit(solution)/shard_map/all_gather | solution.py:528
  17.5 99.4 %copy-start.1 = (bf16[1040,256]{1,0:T(8,128)(2,1)}, bf16[1040,256]{1,0:T(8,128)(2,1)S(1)}, u32[]{:S(2)}) copy-start(bf16[1040,256]{1,0:T(8,128)(2,1)S(1)} %get-tuple-element.21.rest_1_) | copy-start | bytes 1597444
  17.5 99.4 %copy-start.2 = (bf16[1040,256]{1,0:T(8,128)(2,1)}, bf16[1040,256]{1,0:T(8,128)(2,1)S(1)}, u32[]{:S(2)}) copy-start(bf16[1040,256]{1,0:T(8,128)(2,1)S(1)} %get-tuple-element.22.rest_0_) | copy-start | bytes 1597444
  17.6 39.7 %collective-permute-start.11 = (bf16[1040,256]{1,0:T(8,128)(2,1)S(1)}, bf16[1040,256]{1,0:T(8,128)(2,1)S(1)}, u32[]{:S(2)}, u32[]{:S(2)}) collective-permute-start(bf16[1040,256]{1,0:T(8,128)(2,1)S(1)} %get-tuple-element.21.rest_1_), channel_id=1, source_target_pairs={{0,8},{8,16},{16,24},{24,32},{32,40},{40,48},{48,56},{56,0},{1,9},... | collective-permute-start | bytes 1597448 | tf_op jit(solution)/shard_map/ppermute | solution.py:464
  22.4 27.6 %collective-permute-start.1 = (bf16[1040,256]{1,0:T(8,128)(2,1)S(1)}, bf16[1040,256]{1,0:T(8,128)(2,1)S(1)}, u32[]{:S(2)}, u32[]{:S(2)}) collective-permute-start(bf16[1040,256]{1,0:T(8,128)(2,1)S(1)} %get-tuple-element.21.rest_1_), channel_id=1, source_target_pairs={{0,56},{8,0},{16,8},{24,16},{32,24},{40,32},{48,40},{56,48},{1,57}... | collective-permute-start | bytes 1597448 | tf_op jit(solution)/shard_map/ppermute | solution.py:465
  31.0 21.5 %collective-permute-start.6 = (bf16[1040,256]{1,0:T(8,128)(2,1)S(1)}, bf16[1040,256]{1,0:T(8,128)(2,1)S(1)}, u32[]{:S(2)}, u32[]{:S(2)}) collective-permute-start(bf16[1040,256]{1,0:T(8,128)(2,1)S(1)} %get-tuple-element.22.rest_0_), channel_id=1, source_target_pairs={{0,8},{8,16},{16,24},{24,32},{32,40},{40,48},{48,56},{56,0},{1,9},... | collective-permute-start | bytes 1597448 | tf_op jit(solution)/shard_map/ppermute | solution.py:464
  32.9 26.3 %collective-permute-start = (bf16[1040,256]{1,0:T(8,128)(2,1)S(1)}, bf16[1040,256]{1,0:T(8,128)(2,1)S(1)}, u32[]{:S(2)}, u32[]{:S(2)}) collective-permute-start(bf16[1040,256]{1,0:T(8,128)(2,1)S(1)} %get-tuple-element.22.rest_0_), channel_id=1, source_target_pairs={{0,56},{8,0},{16,8},{24,16},{32,24},{40,32},{48,40},{56,48},{1,57}... | collective-permute-start | bytes 1597448 | tf_op jit(solution)/shard_map/ppermute | solution.py:465
  41.4 15.7 %all-to-all-start = ((s32[16,1,8]{2,1,0:T(1,128)}), s32[16,1,8]{2,1,0:T(1,128)S(1)}, u32[]{:S(2)}, u32[]{:S(2)}) async-start(s32[16,1,8]{2,1,0:T(1,128)} %bitcast.3), calls=%async_computation | async-start | bytes 16384 | tf_op jit(solution)/shard_map/all_to_all | solution.py:472
  50.0 67.0 %copy-start.4 = (bf16[1040,256]{1,0:T(8,128)(2,1)}, bf16[1040,256]{1,0:T(8,128)(2,1)S(1)}, u32[]{:S(2)}) copy-start(bf16[1040,256]{1,0:T(8,128)(2,1)S(1)} %collective-permute-done.1.rest_3_) | copy-start | bytes 1597444
  50.0 15.7 %collective-permute-start.3 = (bf16[1040,256]{1,0:T(8,128)(2,1)S(1)}, bf16[1040,256]{1,0:T(8,128)(2,1)}, u32[]{:S(2)}, u32[]{:S(2)}) collective-permute-start(bf16[1040,256]{1,0:T(8,128)(2,1)S(1)} %collective-permute-done.1.rest_3_), channel_id=1, source_target_pairs={{0,56},{8,0},{16,8},{24,16},{32,24},{40,32},{48,40},{56,48},{1,57}... | collective-permute-start | bytes 1597448 | tf_op jit(solution)/shard_map/ppermute | solution.py:465
  52.5 64.5 %copy-start.5 = (bf16[1040,256]{1,0:T(8,128)(2,1)}, bf16[1040,256]{1,0:T(8,128)(2,1)S(1)}, u32[]{:S(2)}) copy-start(bf16[1040,256]{1,0:T(8,128)(2,1)S(1)} %collective-permute-done.6.rest_14_) | copy-start | bytes 1597444
  52.5 17.5 %collective-permute-start.7 = (bf16[1040,256]{1,0:T(8,128)(2,1)S(1)}, bf16[1040,256]{1,0:T(8,128)(2,1)}, u32[]{:S(2)}, u32[]{:S(2)}) collective-permute-start(bf16[1040,256]{1,0:T(8,128)(2,1)S(1)} %collective-permute-done.6.rest_14_), channel_id=1, source_target_pairs={{0,8},{8,16},{16,24},{24,32},{32,40},{40,48},{48,56},{56,0},{1,9},... | collective-permute-start | bytes 1597448 | tf_op jit(solution)/shard_map/ppermute | solution.py:464
  57.3 59.7 %copy-start.3 = (bf16[1040,256]{1,0:T(8,128)(2,1)}, bf16[1040,256]{1,0:T(8,128)(2,1)S(1)}, u32[]{:S(2)}) copy-start(bf16[1040,256]{1,0:T(8,128)(2,1)S(1)} %collective-permute-done.11.rest_15_) | copy-start | bytes 1597444
  57.3 22.5 %collective-permute-start.12 = (bf16[1040,256]{1,0:T(8,128)(2,1)S(1)}, bf16[1040,256]{1,0:T(8,128)(2,1)S(1)}, u32[]{:S(2)}, u32[]{:S(2)}) collective-permute-start(bf16[1040,256]{1,0:T(8,128)(2,1)S(1)} %collective-permute-done.11.rest_15_), channel_id=1, source_target_pairs={{0,8},{8,16},{16,24},{24,32},{32,40},{40,48},{48,56},{56,0},{1,9},... | collective-permute-start | bytes 1597448 | tf_op jit(solution)/shard_map/ppermute | solution.py:464
  59.2 57.8 %copy-start.6 = (bf16[1040,256]{1,0:T(8,128)(2,1)}, bf16[1040,256]{1,0:T(8,128)(2,1)S(1)}, u32[]{:S(2)}) copy-start(bf16[1040,256]{1,0:T(8,128)(2,1)S(1)} %collective-permute-done.rest_2_) | copy-start | bytes 1597444
  59.2 22.9 %collective-permute-start.2 = (bf16[1040,256]{1,0:T(8,128)(2,1)S(1)}, bf16[1040,256]{1,0:T(8,128)(2,1)S(1)}, u32[]{:S(2)}, u32[]{:S(2)}) collective-permute-start(bf16[1040,256]{1,0:T(8,128)(2,1)S(1)} %collective-permute-done.rest_2_), channel_id=1, source_target_pairs={{0,56},{8,0},{16,8},{24,16},{32,24},{40,32},{48,40},{56,48},{1,57}... | collective-permute-start | bytes 1597448 | tf_op jit(solution)/shard_map/ppermute | solution.py:465
  65.7 22.8 %collective-permute-start.5 = (bf16[1040,256]{1,0:T(8,128)(2,1)}, bf16[1040,256]{1,0:T(8,128)(2,1)S(1)}, u32[]{:S(2)}, u32[]{:S(2)}) collective-permute-start(bf16[1040,256]{1,0:T(8,128)(2,1)} %collective-permute-done.3.rest_5_), channel_id=1, source_target_pairs={{0,56},{8,0},{16,8},{24,16},{32,24},{40,32},{48,40},{56,48},{1,57}... | collective-permute-start | bytes 1597448 | tf_op jit(solution)/shard_map/ppermute | solution.py:465
  70.0 22.8 %collective-permute-start.8 = (bf16[1040,256]{1,0:T(8,128)(2,1)}, bf16[1040,256]{1,0:T(8,128)(2,1)S(1)}, u32[]{:S(2)}, u32[]{:S(2)}) collective-permute-start(bf16[1040,256]{1,0:T(8,128)(2,1)} %collective-permute-done.7.rest_12_), channel_id=1, source_target_pairs={{0,8},{8,16},{16,24},{24,32},{32,40},{40,48},{48,56},{56,0},{1,9},... | collective-permute-start | bytes 1597448 | tf_op jit(solution)/shard_map/ppermute | solution.py:464
  79.8 16.3 %copy-start.7 = (bf16[1040,256]{1,0:T(8,128)(2,1)}, bf16[1040,256]{1,0:T(8,128)(2,1)S(1)}, u32[]{:S(2)}) copy-start(bf16[1040,256]{1,0:T(8,128)(2,1)S(1)} %collective-permute-done.12.rest_13_) | copy-start | bytes 1597444
  79.8 22.8 %collective-permute-start.13 = (bf16[1040,256]{1,0:T(8,128)(2,1)S(1)}, bf16[1040,256]{1,0:T(8,128)(2,1)S(1)}, u32[]{:S(2)}, u32[]{:S(2)}) collective-permute-start(bf16[1040,256]{1,0:T(8,128)(2,1)S(1)} %collective-permute-done.12.rest_13_), channel_id=1, source_target_pairs={{0,8},{8,16},{16,24},{24,32},{32,40},{40,48},{48,56},{56,0},{1,9},... | collective-permute-start | bytes 1597448 | tf_op jit(solution)/shard_map/ppermute | solution.py:464
  82.1 20.5 %copy-start.8 = (bf16[1040,256]{1,0:T(8,128)(2,1)}, bf16[1040,256]{1,0:T(8,128)(2,1)S(1)}, u32[]{:S(2)}) copy-start(bf16[1040,256]{1,0:T(8,128)(2,1)S(1)} %collective-permute-done.2.rest_4_) | copy-start | bytes 1597444
  82.1 20.5 %collective-permute-start.4 = (bf16[1040,256]{1,0:T(8,128)(2,1)S(1)}, bf16[1040,256]{1,0:T(8,128)(2,1)S(1)}, u32[]{:S(2)}, u32[]{:S(2)}) collective-permute-start(bf16[1040,256]{1,0:T(8,128)(2,1)S(1)} %collective-permute-done.2.rest_4_), channel_id=1, source_target_pairs={{0,56},{8,0},{16,8},{24,16},{32,24},{40,32},{48,40},{56,48},{1,57}... | collective-permute-start | bytes 1597448 | tf_op jit(solution)/shard_map/ppermute | solution.py:465
  88.5 14.1 %copy-start.9 = (bf16[1040,256]{1,0:T(8,128)(2,1)}, bf16[1040,256]{1,0:T(8,128)(2,1)S(1)}, u32[]{:S(2)}) copy-start(bf16[1040,256]{1,0:T(8,128)(2,1)S(1)} %collective-permute-done.5.rest_7_) | copy-start | bytes 1597444
  88.5 22.1 %collective-permute-start.10 = (bf16[1040,256]{1,0:T(8,128)(2,1)S(1)}, bf16[1040,256]{1,0:T(8,128)(2,1)S(1)}, u32[]{:S(2)}, u32[]{:S(2)}) collective-permute-start(bf16[1040,256]{1,0:T(8,128)(2,1)S(1)} %collective-permute-done.5.rest_7_), channel_id=1, source_target_pairs={{0,56},{8,0},{16,8},{24,16},{32,24},{40,32},{48,40},{56,48},{1,57}... | collective-permute-start | bytes 1597448 | tf_op jit(solution)/shard_map/ppermute | solution.py:465
  92.8 17.8 %copy-start.10 = (bf16[1040,256]{1,0:T(8,128)(2,1)}, bf16[1040,256]{1,0:T(8,128)(2,1)S(1)}, u32[]{:S(2)}) copy-start(bf16[1040,256]{1,0:T(8,128)(2,1)S(1)} %collective-permute-done.8.rest_10_) | copy-start | bytes 1597444
  92.8 21.2 %collective-permute-start.9 = (bf16[1040,256]{1,0:T(8,128)(2,1)S(1)}, bf16[1040,256]{1,0:T(8,128)(2,1)}, u32[]{:S(2)}, u32[]{:S(2)}) collective-permute-start(bf16[1040,256]{1,0:T(8,128)(2,1)S(1)} %collective-permute-done.8.rest_10_), channel_id=1, source_target_pairs={{0,8},{8,16},{16,24},{24,32},{32,40},{40,48},{48,56},{56,0},{1,9},... | collective-permute-start | bytes 1597448 | tf_op jit(solution)/shard_map/ppermute | solution.py:464
  102.6 8.0 %copy-start.11 = (bf16[1040,256]{1,0:T(8,128)(2,1)}, bf16[1040,256]{1,0:T(8,128)(2,1)S(1)}, u32[]{:S(2)}) copy-start(bf16[1040,256]{1,0:T(8,128)(2,1)S(1)} %collective-permute-done.13.rest_11_) | copy-start | bytes 1597444
  102.6 8.0 %copy-start.12 = (bf16[1040,256]{1,0:T(8,128)(2,1)}, bf16[1040,256]{1,0:T(8,128)(2,1)S(1)}, u32[]{:S(2)}) copy-start(bf16[1040,256]{1,0:T(8,128)(2,1)S(1)} %collective-permute-done.4.rest_6_) | copy-start | bytes 1597444
  110.6 0.8 copy-start.13
  214.9 18.2 %all-to-all-start.8 = ((f32[16,32,128]{2,1,0:T(8,128)}), f32[16,32,128]{2,1,0:T(8,128)S(1)}, u32[]{:S(2)}, u32[]{:S(2)}) async-start(f32[16,32,128]{2,1,0:T(8,128)} %get-tuple-element.15), calls=%async_computation.8 | async-start | bytes 524288 | tf_op jit(solution)/shard_map/all_to_all | solution.py:472
Sparse Core Ops, SparseCore 0:
  11.9 105.0 all-gather.2

commit v5 on v4

--- a/solution.py
+++ b/solution.py
@@ -54,20 +54,114 @@
     return jnp.where(rows == places, 1.0, 0.0)
 
 
-def project_kernel(frames, head, out, here, projection, made, norms, sems, head_sem, out_sems):
+def norms_of(codes):
+    wide = codes.astype(F32)
+    square = wide * wide
+    high = square.astype(BF16)
+    low = (square - high.astype(F32)).astype(BF16)
+    ones = jnp.ones((16, E), BF16)
+    return (dot(ones, high, NT) + dot(ones, low, NT))[0:1, :]
+
+
+def three_parts(norm):
+    high = norm.astype(BF16).astype(F32)
+    middle = (norm - high).astype(BF16).astype(F32)
+    return high, middle, norm - high - middle
+
+
+def codes_kernel(frames, head, out, here, projection, made, sems, head_sem, out_sems):
     def inward(n):
         rows = pl.ds(n * PART, PART)
         return pltpu.make_async_copy(frames.at[rows], here.at[rows], sems.at[n])
 
-    def outward(h):
-        return pltpu.make_async_copy(made.at[h], out.at[h], out_sems.at[h])
+    def outward(n):
+        rows = pl.ds(n * PART, PART)
+        return pltpu.make_async_copy(made.at[rows], out.at[rows], out_sems.at[n])
 
     head_copy = pltpu.make_async_copy(head, projection, head_sem)
     inward(0).start()
     head_copy.start()
     for n in range(1, ROWS // PART):
         inward(n).start()
-    ones = jnp.ones((16, E), BF16)
+    head_copy.wait()
+    for n in range(ROWS // PART):
+        rows = pl.ds(n * PART, PART)
+        inward(n).wait()
+        made[rows, :] = dot(here[rows, :], projection[...], NN).astype(BF16)
+        outward(n).start()
+    for n in range(ROWS // PART):
+        outward(n).wait()
+
+
+def project_codes(frames, projection):
+    return pl.pallas_call(
+        codes_kernel,
+        out_shape=pltpu.HBM((ROWS, E), BF16),
+        in_specs=[IN_HBM, IN_HBM],
+        out_specs=IN_HBM,
+        scratch_shapes=[
+            pltpu.VMEM((ROWS, E), BF16),
+            pltpu.VMEM((E, E), BF16),
+            pltpu.VMEM((ROWS, E), BF16),
+            pltpu.SemaphoreType.DMA((ROWS // PART,)),
+            pltpu.SemaphoreType.DMA,
+            pltpu.SemaphoreType.DMA((ROWS // PART,)),
+        ],
+        compiler_params=pltpu.CompilerParams(vmem_limit_bytes=GRANT),
+    )(in_hbm(frames), in_hbm(projection))
+
+
+def norms_kernel(codes, after, out):
+    for k in range(KB):
+        out[k : k + 1, :] = norms_of(codes[pl.ds(k * BLK, BLK), :])
+
+
+def block_norms(codes, after):
+    return pl.pallas_call(
+        norms_kernel,
+        out_shape=jax.ShapeDtypeStruct((KB, BLK), F32),
+        in_specs=[VMEM_WHOLE, IN_HBM],
+        out_specs=VMEM_WHOLE,
+        compiler_params=pltpu.CompilerParams(vmem_limit_bytes=GRANT),
+    )(codes, in_hbm(after))
+
+
+def parts_kernel(received, parts, picks):
+    for n in range(SOURCES):
+        stacked = [*three_parts(received[n, 0:KB, :]), jnp.zeros((KB, BLK), F32)]
+        parts[n] = jnp.concatenate(stacked, axis=0).T.astype(BF16)
+    row = lax.broadcasted_iota(jnp.int32, (4 * KB, BLK), 0)
+    for k in range(KB):
+        ours = (row % KB == k) & (row < 3 * KB)
+        picks[k] = jnp.where(ours, -0.5, 0.0).astype(BF16)
+
+
+def norm_parts(received):
+    return pl.pallas_call(
+        parts_kernel,
+        out_shape=[
+            jax.ShapeDtypeStruct((SOURCES, BLK, 4 * KB), BF16),
+            jax.ShapeDtypeStruct((KB, 4 * KB, BLK), BF16),
+        ],
+        in_specs=[VMEM_WHOLE],
+        out_specs=[VMEM_WHOLE] * 2,
+        compiler_params=pltpu.CompilerParams(vmem_limit_bytes=GRANT),
+    )(received)
+
+
+def project_kernel(frames, head, out, here, projection, made, norms, sems, head_sem, out_sems):
+    def inward(n):
+        rows = pl.ds(n * PART, PART)
+        return pltpu.make_async_copy(frames.at[rows], here.at[rows], sems.at[n])
+
+    def outward(h):
+        return pltpu.make_async_copy(made.at[h], out.at[h], out_sems.at[h])
+
+    head_copy = pltpu.make_async_copy(head, projection, head_sem)
+    inward(0).start()
+    head_copy.start()
+    for n in range(1, ROWS // PART):
+        inward(n).start()
     head_copy.wait()
     for h in range(2):
         for j in range(HB):
@@ -76,15 +170,8 @@
                 inward(k * BLK // PART).wait()
             codes = dot(here[pl.ds(k * BLK, BLK), :], projection[...], NN).astype(BF16)
             made[h, pl.ds(j * BLK, BLK), :] = codes
-            wide = codes.astype(F32)
-            square = wide * wide
-            high = square.astype(BF16)
-            low = (square - high.astype(F32)).astype(BF16)
-            norms[j : j + 1, :] = (dot(ones, high, NT) + dot(ones, low, NT))[0:1, :]
-        norm = norms[...]
-        high = norm.astype(BF16).astype(F32)
-        middle = (norm - high).astype(BF16).astype(F32)
-        low = norm - high - middle
+            norms[j : j + 1, :] = norms_of(codes)
+        high, middle, low = three_parts(norms[...])
         left = jnp.concatenate([high, low], axis=0)
         right = jnp.concatenate([middle, jnp.zeros_like(low)], axis=0)
         made[h, HB * BLK : HALF, :] = jnp.concatenate([left, right], axis=1).astype(BF16)
@@ -116,7 +203,7 @@
     return pltpu.with_memory_space_constraint(value, pltpu.HBM)
 
 
-AHEAD = 2
+AHEAD = 3
 SLOTS = AHEAD + 1
 CHUNK = 16
 CHUNKS = POS // CHUNK
@@ -126,11 +213,10 @@
     return (count[0] + CHUNK - 1) // CHUNK
 
 
-def first_kernel(count, place, col_at, row_at, col_place, row_place, left, *rest):
+def first_kernel(count, place, col_at, row_at, col_place, row_place, parts, picks, left, *rest):
     rights = rest[: 2 * NZ]
     (
-        cross, columns, sums, taken, tails, held, picks, parts, norms, made,
-        sems, tail_sem, right_sem, out_sem,
+        cross, columns, sums, taken, held, norms, made, sems, right_sem, out_sem,
     ) = rest[2 * NZ :]
     chunks = chunks_of(count)
 
@@ -143,10 +229,10 @@
         copies = []
         for n in range(CHUNK):
             _, source, k, _ = taken_apart(i * CHUNK + n)
-            start = pl.multiple_of(k % HB * BLK, BLK)
+            start = pl.multiple_of(k * BLK, BLK)
             copies.append(
                 pltpu.make_async_copy(
-                    left.at[source, k // HB, pl.ds(start, BLK)],
+                    left.at[source, pl.ds(start, BLK)],
                     taken.at[slot, n],
                     sems.at[slot, n],
                 )
@@ -162,10 +248,6 @@
         pltpu.make_async_copy(rights[i], held.at[i // 2, i % 2], right_sem.at[i])
         for i in range(2 * NZ)
     ]
-    tail_copy = pltpu.make_async_copy(
-        left.at[:, :, pl.ds(HB * BLK, 2 * HB)], tails, tail_sem
-    )
-    tail_copy.start()
     for i in range(AHEAD):
         for copy in into[2 * i : 2 * i + 2]:
             copy.start()
@@ -178,17 +260,6 @@
     for copy in into[2 * AHEAD :]:
         copy.start()
     sums[...] = jnp.zeros_like(sums)
-    row = lax.broadcasted_iota(jnp.int32, (4 * KB, BLK), 0)
-    for k in range(KB):
-        ours = (row // (2 * KB) == k // HB) & (row % HB == k % HB)
-        picks[k] = jnp.where(ours, -0.5, 0.0).astype(BF16)
-    tail_copy.wait()
-    for n in range(SOURCES):
-        stacked = []
-        for h in range(2):
-            tail = tails[n, h].astype(F32)
-            stacked += [tail[:, 0:BLK], tail[:, BLK:E]]
-        parts[n] = jnp.concatenate(stacked, axis=0).T.astype(BF16)
 
     def last_piece(i):
         return place[i * CHUNK + CHUNK - 1] // (256 * SOURCES)
@@ -248,22 +319,18 @@
             away(i).wait()
 
 
-def first_pass(count, place, col_at, row_at, col_place, row_place, left, rights):
+def first_pass(count, place, col_at, row_at, col_place, row_place, parts, picks, left, rights):
     return pl.pallas_call(
         first_kernel,
-        in_specs=[SMEM_WHOLE] * 4 + [VMEM_WHOLE] * 2 + [IN_HBM] * (2 * NZ + 1),
+        in_specs=[SMEM_WHOLE] * 4 + [VMEM_WHOLE] * 4 + [IN_HBM] * (2 * NZ + 1),
         out_specs=[IN_HBM, VMEM_WHOLE],
         scratch_shapes=[
             pltpu.VMEM((POS, BLK), F32),
             pltpu.VMEM((SLOTS, CHUNK, BLK, E), BF16),
-            pltpu.VMEM((SOURCES, 2, 2 * HB, E), BF16),
             pltpu.VMEM((NZ, 2, HALF, E), BF16),
-            pltpu.VMEM((KB, 4 * KB, BLK), BF16),
-            pltpu.VMEM((SOURCES, BLK, 4 * KB), BF16),
             pltpu.VMEM((NZ * KB, BLK), F32),
             pltpu.VMEM((SLOTS, CHUNK, BLK, BLK), F32),
             pltpu.SemaphoreType.DMA((SLOTS, CHUNK)),
-            pltpu.SemaphoreType.DMA,
             pltpu.SemaphoreType.DMA((2 * NZ,)),
             pltpu.SemaphoreType.DMA((SLOTS,)),
         ],
@@ -272,7 +339,10 @@
             jax.ShapeDtypeStruct((NZ * KB, BLK), BF16),
         ],
         compiler_params=pltpu.CompilerParams(vmem_limit_bytes=GRANT),
-    )(count, place, col_at, row_at, col_place, row_place, in_hbm(left), *map(in_hbm, rights))
+    )(
+        count, place, col_at, row_at, col_place, row_place, parts, picks,
+        in_hbm(left), *map(in_hbm, rights),
+    )
 
 
 def total_of(received):
@@ -398,7 +468,7 @@
 
 
 def fourth_kernel(
-    count, col_at, row_place, received, column_sum, kernel, rows_out, plan_out,
+    count, col_at, row_place, received, column_sum, kernel, rows_out, potential,
     kernel_here, scale, sums, weighed, kernel_sem,
 ):
     chunks = chunks_of(count)
@@ -406,7 +476,8 @@
     sums[...] = jnp.zeros_like(sums)
     weighed[...] = jnp.zeros_like(weighed)
     plan_sum = total_of(received)
-    plan_out[...] = plan_sum
+    scale[...] = EPSILON * (SHIFT - jnp.log(FLOOR + (FLOOR + column_sum[...]) * plan_sum))
+    potential[...] = scale[pl.ds(pl.multiple_of(count[1] * KB, KB), KB), :]
     scale[...] = 1.0 / (FLOOR / (FLOOR + column_sum[...]) + plan_sum)
 
     @pl.loop(0, chunks)
@@ -447,7 +518,7 @@
         ],
         out_shape=[
             jax.ShapeDtypeStruct((SOURCES, 2 * KB, BLK), F32),
-            jax.ShapeDtypeStruct((NZ * KB, BLK), F32),
+            jax.ShapeDtypeStruct((KB, BLK), F32),
         ],
         compiler_params=pltpu.CompilerParams(vmem_limit_bytes=GRANT),
     )(count, col_at, row_place, received, column_sum, in_hbm(kernel))
@@ -481,11 +552,6 @@
     return to_all(over_rep.astype(BF16), "z", NZ)
 
 
-def own_columns(columns):
-    at = lax.axis_index("z") * KB
-    return lax.dynamic_slice_in_dim(columns, at, KB, 0)
-
-
 def slot_codes(location, pair_block, pair_count):
     slots = pair_block.shape[1]
     stored = location[pair_block.reshape(-1)]
@@ -508,28 +574,34 @@
     lands = active[None, :] & (rank[None, :] == at[:, None])
     sorted_ = jnp.max(jnp.where(lands, place[None, :], 0), axis=1)
     used = at < count
-    return count.reshape(1), jnp.where(used, sorted_, jnp.max(place)), used
+    return count, jnp.where(used, sorted_, jnp.max(place)), used
 
 
 def body(rollout, demo, projection, location, pair_block, pair_count):
     codes = slot_codes(location, pair_block, pair_count)
-    codes = codes.reshape(NY, NZ, NC).transpose(0, 2, 1).reshape(SOURCES, NZ)
-    codes = swap(codes[:, None, :], ("y", "c")).reshape(SOURCES, NZ)
+    codes = codes.reshape(NY, NZ, NC).transpose(0, 2, 1).reshape(SOURCES, 1, NZ)
+    own_codes = project_codes(rollout, projection)
+    left = lax.all_gather(own_codes, ("y", "c"))
+    rights = ring_pieces(project(demo, projection), "z", NZ)
+    norms = jnp.broadcast_to(block_norms(own_codes, rights[-1])[None], (SOURCES, KB, BLK))
+    wide = jnp.pad(codes.astype(F32), ((0, 0), (0, 7), (0, BLK - NZ)))
+    received = swap(jnp.concatenate([norms, wide], axis=1), ("y", "c"))
+    parts, picks = norm_parts(received)
+    codes = received[:, KB, :NZ].astype(jnp.int32)
     turned = (lax.axis_index("z") + jnp.arange(NZ, dtype=jnp.int32)) % NZ
     pick = turned[:, None] == jnp.arange(NZ, dtype=jnp.int32)[None, :]
     codes = jnp.max(jnp.where(pick[:, None, :], codes[None], -1), axis=2)
     count, place, used = in_use(codes.reshape(POS))
+    count = jnp.stack([count, lax.axis_index("z").astype(jnp.int32)])
     piece, source = place // (256 * SOURCES), place // 256 % SOURCES
     col_at = (lax.axis_index("z") + piece) % NZ * KB + place % KB
     row_at = (source % NC * NY + source // NC) * KB + place // KB % KB
     col_place = jnp.where(used, col_at, -1).reshape(1, POS)
     row_place = jnp.where(used, row_at, -1).reshape(1, POS)
 
-    left = lax.all_gather(project(rollout, projection), ("y", "c"))
-    rights = ring_pieces(project(demo, projection), "z", NZ)
 
     cross, columns = first_pass(
-        count, place, col_at, row_at, col_place, row_place, left, rights
+        count, place, col_at, row_at, col_place, row_place, parts, picks, left, rights
     )
     kernel, rows, column_sum = second_pass(
         count, col_at, row_place, columns_to_row(columns), cross
@@ -538,15 +610,13 @@
     rows = jnp.sum(to_all(rows.astype(BF16), "y", NY).astype(F32), axis=0)
     rows = to_all(rows.astype(BF16), "c", NC).reshape(SOURCES * KB, BLK)
     columns = third_pass(count, row_at, col_place, rows, kernel)
-    both, plan_sum = fourth_pass(
+    both, demo_pot = fourth_pass(
         count, col_at, row_place, columns_to_row(columns), column_sum, kernel
     )
     both = jnp.sum(swap(both, ("y", "c")), axis=0)
     total = FLOOR + both[:KB]
     reward = -(both[KB:] + UNMATCHED * FLOOR) / total
     roll_pot = EPSILON * (SHIFT - jnp.log(total))
-    reached = FLOOR + (FLOOR + own_columns(column_sum)) * own_columns(plan_sum)
-    demo_pot = EPSILON * (SHIFT - jnp.log(reached))
     return reward.reshape(-1), roll_pot.reshape(-1), demo_pot.reshape(-1)
 
 

time: 242 us -> 254 us (1.050)
  blocking collectives: 72 us -> 90.4 us
  starting transfers between devices: 65.6 us -> 58.5 us
  Pallas kernels: 34.5 us -> 30.3 us
  waiting for transfers between devices: 42.6 us -> 45.4 us
    ppermute x7, waiting for transfers between devices: 14.7 us -> 36.5 us  [ring_pieces(): right[i] = lax.ppermute(right[i], axis, up)]
    all_to_all x7 -> x8, blocking collectives: 72 us -> 90.4 us  [swap(): return lax.all_to_all(value, axes, split_axis=0, concat_axis=0, tiled=True)]
    all_to_all x2 -> x1, waiting for transfers between devices: 12.8 us -> 0.64 us  [swap(): return lax.all_to_all(value, axes, split_axis=0, concat_axis=0, tiled=True)]
    all_to_all x2 -> x1, starting transfers between devices: 15 us -> 8.23 us  [swap(): return lax.all_to_all(value, axes, split_axis=0, concat_axis=0, tiled=True)]
    pallas_call x2 -> x1, Pallas kernels: 8.99 us -> 4.47 us  [project(): pl.pallas_call(project_kernel, out_shape=pltpu.HBM((2, HALF, E), BF16), i...]
    ppermute x7, waiting for transfers between devices: 12.1 us -> 8.25 us  [ring_pieces(): left[i] = lax.ppermute(left[i], axis, down)]
    all_gather x1, waiting for transfers between devices: 2.98 us -> 0.01 us  [body(): left = lax.all_gather(own_codes, ('y', 'c'))]
    pallas_call x1 -> x4, Pallas kernels: 10.8 us -> 13.5 us  [the longest x1 9.52 us: first_pass(): pl.pallas_call(first_kernel, in_specs=[SMEM_WHOLE] * 4 + [VMEM_WHOLE] * 4...]
  transfers between devices with their start and end apart: 17 -> 16, of which waited for: 9 -> 9; matrix products, arithmetic and copies ran while one was open for 4% -> 4% of each run, Pallas kernels for 2% -> 2%
where the time goes in v5:
time: 254 us; the launch traced here: 253 us
  blocking collectives  90.4 us (36%)
  starting transfers between devices  58.5 us (23%)
  waiting for transfers between devices  45.4 us (18%)
  Pallas kernels  30.3 us (12%)
  between operations  14.5 us (6%)
  local copies, waits for them, and re-layouts  6.85 us (3%)
  other arithmetic  6.75 us (3%)
    all_to_all x8, blocking collectives, swap(): return lax.all_to_all(value, axes, split_axis=0, concat_axis=0, tiled=True)  90.4 us
    ppermute x7, waiting for transfers between devices, ring_pieces(): right[i] = lax.ppermute(right[i], axis, up)  36.5 us
    ppermute x7, starting transfers between devices, ring_pieces(): left[i] = lax.ppermute(left[i], axis, down)  32.5 us
    ppermute x7, starting transfers between devices, ring_pieces(): right[i] = lax.ppermute(right[i], axis, up)  17.8 us
    pallas_call x1, Pallas kernels, first_pass(): pl.pallas_call(first_kernel, in_specs=[SMEM_WHOLE] * 4 + [VMEM_WHOLE] * 4...  9.52 us
    ppermute x7, waiting for transfers between devices, ring_pieces(): left[i] = lax.ppermute(left[i], axis, down)  8.25 us
    all_to_all x1, starting transfers between devices, swap(): return lax.all_to_all(value, axes, split_axis=0, concat_axis=0, tiled=True)  8.23 us
  transfers between devices with their start and end apart: 16, of which 9 were waited for; matrix products, arithmetic and copies ran while one was open for 4% of the time, Pallas kernels for 2%

profile of v5, /device:TPU:1, one launch (start us, length us, event | category | flops | bytes accessed | tf_op | source)
XLA Modules:
  0.0 252.7 jit_solution(5438579058239724656)
XLA Ops:
  7.2 3.1 %shard_map.85.codes = bf16[2048,256]{1,0:T(8,128)(2,1)} custom-call(bf16[2048,256]{1,0:T(8,128)(2,1)} %frames.2, bf16[256,256]{1,0:T(8,128)(2,1)} %head.3), custom_call_target="tpu_custom_call" | custom-call | tf_op jit(solution)/shard_map/pallas_call | solution.py:97
  10.3 4.5 %shard_map.86 = bf16[2,1040,256]{2,1,0:T(8,128)(2,1)} custom-call(bf16[2048,256]{1,0:T(8,128)(2,1)} %frames.3, bf16[256,256]{1,0:T(8,128)(2,1)} %head.3), custom_call_target="tpu_custom_call" | custom-call | tf_op jit(solution)/shard_map/pallas_call | solution.py:184
  14.8 1.3 slice_bitcast_fusion
  16.1 4.8 %collective-permute-start.7 = (bf16[1040,256]{1,0:T(8,128)(2,1)S(1)}, bf16[1040,256]{1,0:T(8,128)(2,1)S(1)}, u32[]{:S(2)}, u32[]{:S(2)}) collective-permute-start(bf16[1040,256]{1,0:T(8,128)(2,1)S(1)} %get-tuple-element.25.rest_0_), channel_id=1, source_target_pairs={{0,8},{8,16},{16,24},{24,32},{32,40},{40,48},{48,56},{56,0},{1,9},... | collective-permute-start | bytes 1597448 | tf_op jit(solution)/shard_map/ppermute | solution.py:535
  20.9 8.6 %collective-permute-start.1 = (bf16[1040,256]{1,0:T(8,128)(2,1)S(1)}, bf16[1040,256]{1,0:T(8,128)(2,1)}, u32[]{:S(2)}, u32[]{:S(2)}) collective-permute-start(bf16[1040,256]{1,0:T(8,128)(2,1)S(1)} %get-tuple-element.25.rest_0_), channel_id=1, source_target_pairs={{0,56},{8,0},{16,8},{24,16},{32,24},{40,32},{48,40},{56,48},{1,57}... | collective-permute-start | bytes 1597448 | tf_op jit(solution)/shard_map/ppermute | solution.py:536
  29.5 3.4 %collective-permute-start.2 = (bf16[1040,256]{1,0:T(8,128)(2,1)S(1)}, bf16[1040,256]{1,0:T(8,128)(2,1)}, u32[]{:S(2)}, u32[]{:S(2)}) collective-permute-start(bf16[1040,256]{1,0:T(8,128)(2,1)S(1)} %get-tuple-element.26.rest_1_), channel_id=1, source_target_pairs={{0,56},{8,0},{16,8},{24,16},{32,24},{40,32},{48,40},{56,48},{1,57}... | collective-permute-start | bytes 1597448 | tf_op jit(solution)/shard_map/ppermute | solution.py:536
  32.9 1.9 collective-permute-start
  34.8 0.8 copy.23
  35.7 0.7 iota_compare_fusion.4
  36.5 1.1 gather_fusion
  38.1 12.8 %collective-permute-done.after.rest_15_ = bf16[1040,256]{1,0:T(8,128)(2,1)S(1)} collective-permute-done((bf16[1040,256]{1,0:T(8,128)(2,1)S(1)}, bf16[1040,256]{1,0:T(8,128)(2,1)S(1)}, u32[]{:S(2)}, u32[]{:S(2)}) %collective-permute-start) | collective-permute-done | bytes 532512 | tf_op jit(solution)/shard_map/ppermute | solution.py:535
  50.9 0.9 copy-done.2
  51.8 1.2 copy-done.1
  53.0 0.7 shard_map.87
  53.7 0.7 select_maximum_fusion
  54.4 8.2 %all-to-all-start = ((f32[16,24,128]{2,1,0:T(8,128)}), f32[16,24,128]{2,1,0:T(8,128)S(1)}, u32[]{:S(2)}, u32[]{:S(2)}) async-start(f32[16,24,128]{2,1,0:T(8,128)} %select_maximum_fusion), calls=%async_computation | async-start | bytes 393216 | tf_op jit(solution)/shard_map/all_to_all | solution.py:543
  62.7 1.9 collective-permute-start.12
  64.6 1.9 collective-permute-start.8
  66.6 4.6 %collective-permute-start.3 = (bf16[1040,256]{1,0:T(8,128)(2,1)}, bf16[1040,256]{1,0:T(8,128)(2,1)}, u32[]{:S(2)}, u32[]{:S(2)}) collective-permute-start(bf16[1040,256]{1,0:T(8,128)(2,1)} %collective-permute-done.1.rest_2_), channel_id=1, source_target_pairs={{0,56},{8,0},{16,8},{24,16},{32,24},{40,32},{48,40},{56,48},{1,57}... | collective-permute-start | bytes 1597448 | tf_op jit(solution)/shard_map/ppermute | solution.py:536
  71.2 3.4 %collective-permute-start.4 = (bf16[1040,256]{1,0:T(8,128)(2,1)}, bf16[1040,256]{1,0:T(8,128)(2,1)}, u32[]{:S(2)}, u32[]{:S(2)}) collective-permute-start(bf16[1040,256]{1,0:T(8,128)(2,1)} %collective-permute-done.2.rest_3_), channel_id=1, source_target_pairs={{0,56},{8,0},{16,8},{24,16},{32,24},{40,32},{48,40},{56,48},{1,57}... | collective-permute-start | bytes 1597448 | tf_op jit(solution)/shard_map/ppermute | solution.py:536
  76.5 14.7 %collective-permute-done.8.rest_12_ = bf16[1040,256]{1,0:T(8,128)(2,1)} collective-permute-done((bf16[1040,256]{1,0:T(8,128)(2,1)S(1)}, bf16[1040,256]{1,0:T(8,128)(2,1)}, u32[]{:S(2)}, u32[]{:S(2)}) %collective-permute-start.8) | collective-permute-done | bytes 532512 | tf_op jit(solution)/shard_map/ppermute | solution.py:535
  91.2 1.9 collective-permute-start.9
  93.1 0.9 collective-permute-done.4.rest_5_
  94.0 5.3 %collective-permute-start.6 = (bf16[1040,256]{1,0:T(8,128)(2,1)}, bf16[1040,256]{1,0:T(8,128)(2,1)S(1)}, u32[]{:S(2)}, u32[]{:S(2)}) collective-permute-start(bf16[1040,256]{1,0:T(8,128)(2,1)} %collective-permute-done.4.rest_5_), channel_id=1, source_target_pairs={{0,56},{8,0},{16,8},{24,16},{32,24},{40,32},{48,40},{56,48},{1,57}... | collective-permute-start | bytes 1597448 | tf_op jit(solution)/shard_map/ppermute | solution.py:536
  99.5 1.3 fusion.9
  100.8 1.9 collective-permute-start.5
  102.7 3.4 %collective-permute-start.13 = (bf16[1040,256]{1,0:T(8,128)(2,1)S(1)}, bf16[1040,256]{1,0:T(8,128)(2,1)S(1)}, u32[]{:S(2)}, u32[]{:S(2)}) collective-permute-start(bf16[1040,256]{1,0:T(8,128)(2,1)S(1)} %collective-permute-done.12.rest_13_), channel_id=1, source_target_pairs={{0,8},{8,16},{16,24},{24,32},{32,40},{40,48},{48,56},{56,0},{1,9},... | collective-permute-start | bytes 1597448 | tf_op jit(solution)/shard_map/ppermute | solution.py:535
  106.1 1.2 collective-permute-done.9.rest_10_
  107.3 1.9 collective-permute-start.10
  109.8 5.3 %collective-permute-start.11 = (bf16[1040,256]{1,0:T(8,128)(2,1)S(1)}, bf16[1040,256]{1,0:T(8,128)(2,1)}, u32[]{:S(2)}, u32[]{:S(2)}) collective-permute-start(bf16[1040,256]{1,0:T(8,128)(2,1)S(1)} %collective-permute-done.6.rest_7_), channel_id=1, source_target_pairs={{0,56},{8,0},{16,8},{24,16},{32,24},{40,32},{48,40},{56,48},{1,57}... | collective-permute-start | bytes 1597448 | tf_op jit(solution)/shard_map/ppermute | solution.py:536
  115.1 0.7 pad_add_fusion.count
  115.9 1.3 fusion.11
  117.2 4.0 %collective-permute-done.5.rest_6_ = bf16[1040,256]{1,0:T(8,128)(2,1)S(1)} collective-permute-done((bf16[1040,256]{1,0:T(8,128)(2,1)}, bf16[1040,256]{1,0:T(8,128)(2,1)S(1)}, u32[]{:S(2)}, u32[]{:S(2)}) %collective-permute-start.5) | collective-permute-done | bytes 532512 | tf_op jit(solution)/shard_map/ppermute | solution.py:536
  121.3 7.7 %collective-permute-done.10.rest_8_ = bf16[1040,256]{1,0:T(8,128)(2,1)S(1)} collective-permute-done((bf16[1040,256]{1,0:T(8,128)(2,1)S(1)}, bf16[1040,256]{1,0:T(8,128)(2,1)S(1)}, u32[]{:S(2)}, u32[]{:S(2)}) %collective-permute-start.10) | collective-permute-done | bytes 532512 | tf_op jit(solution)/shard_map/ppermute | solution.py:535
  129.0 0.8 copy-done.11
  129.8 2.8 %collective-permute-done.11.rest_9_ = bf16[1040,256]{1,0:T(8,128)(2,1)} collective-permute-done((bf16[1040,256]{1,0:T(8,128)(2,1)S(1)}, bf16[1040,256]{1,0:T(8,128)(2,1)}, u32[]{:S(2)}, u32[]{:S(2)}) %collective-permute-start.11) | collective-permute-done | bytes 532512 | tf_op jit(solution)/shard_map/ppermute | solution.py:536
  132.6 9.5 %shard_map.89 = (f32[128,128,128]{2,1,0:T(8,128)}, bf16[128,128]{1,0:T(8,128)(2,1)S(1)}) custom-call(s32[2]{0:T(128)S(1)} %pad_add_fusion.count, s32[128]{0:T(128)S(1)} %get-tuple-element.24.place, s32[128]{0:T(128)S(1)} %fusion.7.col_at, s32[128]{0:T(128)S(1)} %get-tuple-element.23.row_at, s32[1,128]{1,0:T(1,128)S(1)} %get-tuple-element.29.col_place, ...), custom_call_target="tpu_custom_call" | custom-call | tf_op jit(solution)/shard_map/pallas_call | solution.py:323
  142.1 8.7 %all_to_all.45 = bf16[4,128,128]{2,1,0:T(8,128)(2,1)S(1)} all-to-all(bf16[4,128,128]{2,1,0:T(8,128)(2,1)S(1)} %broadcast_in_dim.119), channel_id=1, replica_groups=mesh['y'=8,'z'=8,'c'=2,'x'=4] {'x'}, dimensions={0} | all-to-all | bytes 262144 | tf_op jit(solution)/shard_map/all_to_all | solution.py:543
  150.9 15.3 %all_to_all.46.received = bf16[8,128,128]{2,1,0:T(8,128)(2,1)S(1)} all-to-all(bf16[8,128,128]{2,1,0:T(8,128)(2,1)S(1)} %broadcast_in_dim.120), channel_id=1, replica_groups=mesh['y'=8,'z'=8,'c'=2,'x'=4] {'z'}, dimensions={0} | all-to-all | bytes 524288 | tf_op jit(solution)/shard_map/all_to_all | solution.py:543
  166.2 4.8 %shard_map.90 = (bf16[128,256,128]{2,1,0:T(8,128)(2,1)}, bf16[256,128]{1,0:T(8,128)(2,1)S(1)}, f32[128,128]{1,0:T(8,128)S(1)}) custom-call(s32[2]{0:T(128)S(1)} %pad_add_fusion.count, s32[128]{0:T(128)S(1)} %fusion.7.col_at, s32[1,128]{1,0:T(1,128)S(1)} %get-tuple-element.30.row_place, bf16[8,128,128]{2,1,0:T(8,128)(2,1)S(1)} %all_to_all.46.received, ...), custom_call_target="tpu_custom_call" | custom-call | tf_op jit(solution)/shard_map/pallas_call | solution.py:405
  171.0 8.1 %all_to_all.47 = bf16[2,128,128]{2,1,0:T(8,128)(2,1)S(1)} all-to-all(bf16[2,128,128]{2,1,0:T(8,128)(2,1)S(1)} %bitcast.28), channel_id=1, replica_groups=mesh['y'=8,'z'=8,'c'=2,'x'=4] {'c'}, dimensions={0} | all-to-all | bytes 131072 | tf_op jit(solution)/shard_map/all_to_all | solution.py:543
  179.1 16.1 %all_to_all.48 = bf16[8,128,128]{2,1,0:T(8,128)(2,1)S(1)} all-to-all(bf16[8,128,128]{2,1,0:T(8,128)(2,1)S(1)} %broadcast_in_dim.121), channel_id=1, replica_groups=mesh['y'=8,'z'=8,'c'=2,'x'=4] {'y'}, dimensions={0} | all-to-all | bytes 524288 | tf_op jit(solution)/shard_map/all_to_all | solution.py:543
  195.3 5.1 %all_to_all.49 = bf16[2,128,128]{2,1,0:T(8,128)(2,1)S(1)} all-to-all(bf16[2,128,128]{2,1,0:T(8,128)(2,1)S(1)} %broadcast_in_dim.122), channel_id=1, replica_groups=mesh['y'=8,'z'=8,'c'=2,'x'=4] {'c'}, dimensions={0} | all-to-all | bytes 131072 | tf_op jit(solution)/shard_map/all_to_all | solution.py:543
  200.4 3.2 %shard_map.91 = bf16[128,128]{1,0:T(8,128)(2,1)S(1)} custom-call(s32[2]{0:T(128)S(1)} %pad_add_fusion.count, s32[128]{0:T(128)S(1)} %get-tuple-element.23.row_at, s32[1,128]{1,0:T(1,128)S(1)} %get-tuple-element.29.col_place, bf16[256,128]{1,0:T(8,128)(2,1)S(1)} %bitcast.27, bf16[128,256,128]{2,1,0:T(8,128)(2,1)} %get-tuple-element.17.kernel), custom_call_target="tpu_custom_call" | custom-call | tf_op jit(solution)/shard_map/pallas_call | solution.py:455
  203.6 7.2 %all_to_all.50 = bf16[4,128,128]{2,1,0:T(8,128)(2,1)S(1)} all-to-all(bf16[4,128,128]{2,1,0:T(8,128)(2,1)S(1)} %broadcast_in_dim.123), channel_id=1, replica_groups=mesh['y'=8,'z'=8,'c'=2,'x'=4] {'x'}, dimensions={0} | all-to-all | bytes 262144 | tf_op jit(solution)/shard_map/all_to_all | solution.py:543
  210.9 12.1 %all_to_all.51.received = bf16[8,128,128]{2,1,0:T(8,128)(2,1)S(1)} all-to-all(bf16[8,128,128]{2,1,0:T(8,128)(2,1)S(1)} %broadcast_in_dim.124), channel_id=1, replica_groups=mesh['y'=8,'z'=8,'c'=2,'x'=4] {'z'}, dimensions={0} | all-to-all | bytes 524288 | tf_op jit(solution)/shard_map/all_to_all | solution.py:543
  222.9 4.4 %shard_map.92 = (f32[16,32,128]{2,1,0:T(8,128)S(1)}, f32[16,128]{1,0:T(8,128)}) custom-call(s32[2]{0:T(128)S(1)} %pad_add_fusion.count, s32[128]{0:T(128)S(1)} %fusion.7.col_at, s32[1,128]{1,0:T(1,128)S(1)} %get-tuple-element.30.row_place, bf16[8,128,128]{2,1,0:T(8,128)(2,1)S(1)} %all_to_all.51.received, f32[128,128]{1,0:T(8,128)S(1)} %get-tuple-element.18.column_sum, ...), custom_call_target="tpu_custom_call" | custom-call | tf_op jit(solution)/shard_map/pallas_call | solution.py:508
  227.4 17.8 %all_to_all.52 = f32[16,32,128]{2,1,0:T(8,128)S(1)} all-to-all(f32[16,32,128]{2,1,0:T(8,128)S(1)} %get-tuple-element.19), channel_id=1, replica_groups=mesh['y'=8,'z'=8,'c'=2,'x'=4] {'y','c'}, dimensions={0} | all-to-all | bytes 524288 | tf_op jit(solution)/shard_map/all_to_all | solution.py:543
  (67 shorter events, 4.2 us)
Async XLA Ops:
  7.2 29.4 %copy-start = (s32[2048]{0:T(1024)S(1)}, s32[2048]{0:T(1024)}, u32[]{:S(2)}) copy-start(s32[2048]{0:T(1024)} %param.9) | copy-start | bytes 24580
  7.2 125.4 %all-gather.3.cloned.1.call-start = ((), (), s32[]{:S(2)}) async-start(), calls=%async_computation.9 | async-start | bytes 17825792 | tf_op jit(solution)/shard_map/all_gather | solution.py:584
  16.1 116.5 %copy-start.3 = (bf16[1040,256]{1,0:T(8,128)(2,1)}, bf16[1040,256]{1,0:T(8,128)(2,1)S(1)}, u32[]{:S(2)}) copy-start(bf16[1040,256]{1,0:T(8,128)(2,1)S(1)} %get-tuple-element.25.rest_0_) | copy-start | bytes 1597444
  16.1 116.5 %copy-start.4 = (bf16[1040,256]{1,0:T(8,128)(2,1)}, bf16[1040,256]{1,0:T(8,128)(2,1)S(1)}, u32[]{:S(2)}) copy-start(bf16[1040,256]{1,0:T(8,128)(2,1)S(1)} %get-tuple-element.26.rest_1_) | copy-start | bytes 1597444
  16.1 48.5 %collective-permute-start.7 = (bf16[1040,256]{1,0:T(8,128)(2,1)S(1)}, bf16[1040,256]{1,0:T(8,128)(2,1)S(1)}, u32[]{:S(2)}, u32[]{:S(2)}) collective-permute-start(bf16[1040,256]{1,0:T(8,128)(2,1)S(1)} %get-tuple-element.25.rest_0_), channel_id=1, source_target_pairs={{0,8},{8,16},{16,24},{24,32},{32,40},{40,48},{48,56},{56,0},{1,9},... | collective-permute-start | bytes 1597448 | tf_op jit(solution)/shard_map/ppermute | solution.py:535
  20.9 45.6 %collective-permute-start.1 = (bf16[1040,256]{1,0:T(8,128)(2,1)S(1)}, bf16[1040,256]{1,0:T(8,128)(2,1)}, u32[]{:S(2)}, u32[]{:S(2)}) collective-permute-start(bf16[1040,256]{1,0:T(8,128)(2,1)S(1)} %get-tuple-element.25.rest_0_), channel_id=1, source_target_pairs={{0,56},{8,0},{16,8},{24,16},{32,24},{40,32},{48,40},{56,48},{1,57}... | collective-permute-start | bytes 1597448 | tf_op jit(solution)/shard_map/ppermute | solution.py:536
  29.5 41.7 %collective-permute-start.2 = (bf16[1040,256]{1,0:T(8,128)(2,1)S(1)}, bf16[1040,256]{1,0:T(8,128)(2,1)}, u32[]{:S(2)}, u32[]{:S(2)}) collective-permute-start(bf16[1040,256]{1,0:T(8,128)(2,1)S(1)} %get-tuple-element.26.rest_1_), channel_id=1, source_target_pairs={{0,56},{8,0},{16,8},{24,16},{32,24},{40,32},{48,40},{56,48},{1,57}... | collective-permute-start | bytes 1597448 | tf_op jit(solution)/shard_map/ppermute | solution.py:536
  32.9 18.0 %collective-permute-start = (bf16[1040,256]{1,0:T(8,128)(2,1)S(1)}, bf16[1040,256]{1,0:T(8,128)(2,1)S(1)}, u32[]{:S(2)}, u32[]{:S(2)}) collective-permute-start(bf16[1040,256]{1,0:T(8,128)(2,1)S(1)} %get-tuple-element.26.rest_1_), channel_id=1, source_target_pairs={{0,8},{8,16},{16,24},{24,32},{32,40},{40,48},{48,56},{56,0},{1,9},... | collective-permute-start | bytes 1597448 | tf_op jit(solution)/shard_map/ppermute | solution.py:535
  50.9 0.9 copy-start.2
  51.8 1.2 copy-start.1
  54.4 20.8 %all-to-all-start = ((f32[16,24,128]{2,1,0:T(8,128)}), f32[16,24,128]{2,1,0:T(8,128)S(1)}, u32[]{:S(2)}, u32[]{:S(2)}) async-start(f32[16,24,128]{2,1,0:T(8,128)} %select_maximum_fusion), calls=%async_computation | async-start | bytes 393216 | tf_op jit(solution)/shard_map/all_to_all | solution.py:543
  62.7 40.0 %collective-permute-start.12 = (bf16[1040,256]{1,0:T(8,128)(2,1)}, bf16[1040,256]{1,0:T(8,128)(2,1)S(1)}, u32[]{:S(2)}, u32[]{:S(2)}) collective-permute-start(bf16[1040,256]{1,0:T(8,128)(2,1)} %copy-done.2), channel_id=1, source_target_pairs={{0,8},{8,16},{16,24},{24,32},{32,40},{40,48},{48,56},{56,0},{1,9},... | collective-permute-start | bytes 1597448 | tf_op jit(solution)/shard_map/ppermute | solution.py:535
  64.6 67.9 %copy-start.5 = (bf16[1040,256]{1,0:T(8,128)(2,1)}, bf16[1040,256]{1,0:T(8,128)(2,1)S(1)}, u32[]{:S(2)}) copy-start(bf16[1040,256]{1,0:T(8,128)(2,1)S(1)} %collective-permute-done.7.rest_14_) | copy-start | bytes 1597444
  64.6 26.6 %collective-permute-start.8 = (bf16[1040,256]{1,0:T(8,128)(2,1)S(1)}, bf16[1040,256]{1,0:T(8,128)(2,1)}, u32[]{:S(2)}, u32[]{:S(2)}) collective-permute-start(bf16[1040,256]{1,0:T(8,128)(2,1)S(1)} %collective-permute-done.7.rest_14_), channel_id=1, source_target_pairs={{0,8},{8,16},{16,24},{24,32},{32,40},{40,48},{48,56},{56,0},{1,9},... | collective-permute-start | bytes 1597448 | tf_op jit(solution)/shard_map/ppermute | solution.py:535
  66.6 34.2 %collective-permute-start.3 = (bf16[1040,256]{1,0:T(8,128)(2,1)}, bf16[1040,256]{1,0:T(8,128)(2,1)}, u32[]{:S(2)}, u32[]{:S(2)}) collective-permute-start(bf16[1040,256]{1,0:T(8,128)(2,1)} %collective-permute-done.1.rest_2_), channel_id=1, source_target_pairs={{0,56},{8,0},{16,8},{24,16},{32,24},{40,32},{48,40},{56,48},{1,57}... | collective-permute-start | bytes 1597448 | tf_op jit(solution)/shard_map/ppermute | solution.py:536
  71.2 22.8 %collective-permute-start.4 = (bf16[1040,256]{1,0:T(8,128)(2,1)}, bf16[1040,256]{1,0:T(8,128)(2,1)}, u32[]{:S(2)}, u32[]{:S(2)}) collective-permute-start(bf16[1040,256]{1,0:T(8,128)(2,1)} %collective-permute-done.2.rest_3_), channel_id=1, source_target_pairs={{0,56},{8,0},{16,8},{24,16},{32,24},{40,32},{48,40},{56,48},{1,57}... | collective-permute-start | bytes 1597448 | tf_op jit(solution)/shard_map/ppermute | solution.py:536
  91.2 16.2 %collective-permute-start.9 = (bf16[1040,256]{1,0:T(8,128)(2,1)}, bf16[1040,256]{1,0:T(8,128)(2,1)S(1)}, u32[]{:S(2)}, u32[]{:S(2)}) collective-permute-start(bf16[1040,256]{1,0:T(8,128)(2,1)} %collective-permute-done.8.rest_12_), channel_id=1, source_target_pairs={{0,8},{8,16},{16,24},{24,32},{32,40},{40,48},{48,56},{56,0},{1,9},... | collective-permute-start | bytes 1597448 | tf_op jit(solution)/shard_map/ppermute | solution.py:535
  94.0 15.8 %collective-permute-start.6 = (bf16[1040,256]{1,0:T(8,128)(2,1)}, bf16[1040,256]{1,0:T(8,128)(2,1)S(1)}, u32[]{:S(2)}, u32[]{:S(2)}) collective-permute-start(bf16[1040,256]{1,0:T(8,128)(2,1)} %collective-permute-done.4.rest_5_), channel_id=1, source_target_pairs={{0,56},{8,0},{16,8},{24,16},{32,24},{40,32},{48,40},{56,48},{1,57}... | collective-permute-start | bytes 1597448 | tf_op jit(solution)/shard_map/ppermute | solution.py:536
  100.8 20.4 %collective-permute-start.5 = (bf16[1040,256]{1,0:T(8,128)(2,1)}, bf16[1040,256]{1,0:T(8,128)(2,1)S(1)}, u32[]{:S(2)}, u32[]{:S(2)}) collective-permute-start(bf16[1040,256]{1,0:T(8,128)(2,1)} %collective-permute-done.3.rest_4_), channel_id=1, source_target_pairs={{0,56},{8,0},{16,8},{24,16},{32,24},{40,32},{48,40},{56,48},{1,57}... | collective-permute-start | bytes 1597448 | tf_op jit(solution)/shard_map/ppermute | solution.py:536
  102.7 29.8 %copy-start.6 = (bf16[1040,256]{1,0:T(8,128)(2,1)}, bf16[1040,256]{1,0:T(8,128)(2,1)S(1)}, u32[]{:S(2)}) copy-start(bf16[1040,256]{1,0:T(8,128)(2,1)S(1)} %collective-permute-done.12.rest_13_) | copy-start | bytes 1597444
  102.7 18.5 %collective-permute-start.13 = (bf16[1040,256]{1,0:T(8,128)(2,1)S(1)}, bf16[1040,256]{1,0:T(8,128)(2,1)S(1)}, u32[]{:S(2)}, u32[]{:S(2)}) collective-permute-start(bf16[1040,256]{1,0:T(8,128)(2,1)S(1)} %collective-permute-done.12.rest_13_), channel_id=1, source_target_pairs={{0,8},{8,16},{16,24},{24,32},{32,40},{40,48},{48,56},{56,0},{1,9},... | collective-permute-start | bytes 1597448 | tf_op jit(solution)/shard_map/ppermute | solution.py:535
  107.3 13.9 %copy-start.7 = (bf16[1040,256]{1,0:T(8,128)(2,1)}, bf16[1040,256]{1,0:T(8,128)(2,1)S(1)}, u32[]{:S(2)}) copy-start(bf16[1040,256]{1,0:T(8,128)(2,1)S(1)} %collective-permute-done.9.rest_10_) | copy-start | bytes 1597444
  107.3 21.6 %collective-permute-start.10 = (bf16[1040,256]{1,0:T(8,128)(2,1)S(1)}, bf16[1040,256]{1,0:T(8,128)(2,1)S(1)}, u32[]{:S(2)}, u32[]{:S(2)}) collective-permute-start(bf16[1040,256]{1,0:T(8,128)(2,1)S(1)} %collective-permute-done.9.rest_10_), channel_id=1, source_target_pairs={{0,8},{8,16},{16,24},{24,32},{32,40},{40,48},{48,56},{56,0},{1,9},... | collective-permute-start | bytes 1597448 | tf_op jit(solution)/shard_map/ppermute | solution.py:535
  109.8 19.2 %copy-start.8 = (bf16[1040,256]{1,0:T(8,128)(2,1)}, bf16[1040,256]{1,0:T(8,128)(2,1)S(1)}, u32[]{:S(2)}) copy-start(bf16[1040,256]{1,0:T(8,128)(2,1)S(1)} %collective-permute-done.6.rest_7_) | copy-start | bytes 1597444
  109.8 22.7 %collective-permute-start.11 = (bf16[1040,256]{1,0:T(8,128)(2,1)S(1)}, bf16[1040,256]{1,0:T(8,128)(2,1)}, u32[]{:S(2)}, u32[]{:S(2)}) collective-permute-start(bf16[1040,256]{1,0:T(8,128)(2,1)S(1)} %collective-permute-done.6.rest_7_), channel_id=1, source_target_pairs={{0,56},{8,0},{16,8},{24,16},{32,24},{40,32},{48,40},{56,48},{1,57}... | collective-permute-start | bytes 1597448 | tf_op jit(solution)/shard_map/ppermute | solution.py:536
  121.2 7.7 %copy-start.9 = (bf16[1040,256]{1,0:T(8,128)(2,1)}, bf16[1040,256]{1,0:T(8,128)(2,1)S(1)}, u32[]{:S(2)}) copy-start(bf16[1040,256]{1,0:T(8,128)(2,1)S(1)} %collective-permute-done.5.rest_6_) | copy-start | bytes 1597444
  121.2 7.7 %copy-start.10 = (bf16[1040,256]{1,0:T(8,128)(2,1)}, bf16[1040,256]{1,0:T(8,128)(2,1)S(1)}, u32[]{:S(2)}) copy-start(bf16[1040,256]{1,0:T(8,128)(2,1)S(1)} %collective-permute-done.13.rest_11_) | copy-start | bytes 1597444
  129.0 0.8 copy-start.11
Sparse Core Ops, SparseCore 0:
  10.4 107.8 all-gather.2

commit v6 on v5

--- a/solution.py
+++ b/solution.py
@@ -580,14 +580,12 @@
 def body(rollout, demo, projection, location, pair_block, pair_count):
     codes = slot_codes(location, pair_block, pair_count)
     codes = codes.reshape(NY, NZ, NC).transpose(0, 2, 1).reshape(SOURCES, 1, NZ)
+    codes = swap(codes, ("y", "c")).reshape(SOURCES, NZ)
     own_codes = project_codes(rollout, projection)
     left = lax.all_gather(own_codes, ("y", "c"))
     rights = ring_pieces(project(demo, projection), "z", NZ)
-    norms = jnp.broadcast_to(block_norms(own_codes, rights[-1])[None], (SOURCES, KB, BLK))
-    wide = jnp.pad(codes.astype(F32), ((0, 0), (0, 7), (0, BLK - NZ)))
-    received = swap(jnp.concatenate([norms, wide], axis=1), ("y", "c"))
-    parts, picks = norm_parts(received)
-    codes = received[:, KB, :NZ].astype(jnp.int32)
+    norms = block_norms(own_codes, rights[2 * (NZ - 3) + 1])
+    parts, picks = norm_parts(to_all(norms, ("y", "c"), SOURCES))
     turned = (lax.axis_index("z") + jnp.arange(NZ, dtype=jnp.int32)) % NZ
     pick = turned[:, None] == jnp.arange(NZ, dtype=jnp.int32)[None, :]
     codes = jnp.max(jnp.where(pick[:, None, :], codes[None], -1), axis=2)

time: 254 us -> 240 us (0.945)
  waiting for transfers between devices: 45.4 us -> 29.9 us
  blocking collectives: 90.4 us -> 82.4 us
  starting transfers between devices: 58.5 us -> 65.2 us
  Pallas kernels: 30.3 us -> 33.3 us
    ppermute x7, waiting for transfers between devices: 36.5 us -> 15.8 us  [ring_pieces(): right[i] = lax.ppermute(right[i], axis, up)]
    all_to_all x1 -> x2, waiting for transfers between devices: 0.64 us -> 14.1 us  [swap(): return lax.all_to_all(value, axes, split_axis=0, concat_axis=0, tiled=True)]
    ppermute x7, waiting for transfers between devices: 8.25 us -> 0.02 us  [ring_pieces(): left[i] = lax.ppermute(left[i], axis, down)]
    all_to_all x8, blocking collectives: 90.4 us -> 82.4 us  [swap(): return lax.all_to_all(value, axes, split_axis=0, concat_axis=0, tiled=True)]
    all_to_all x1 -> x2, starting transfers between devices: 8.23 us -> 13.7 us  [swap(): return lax.all_to_all(value, axes, split_axis=0, concat_axis=0, tiled=True)]
    ppermute x7, starting transfers between devices: 32.5 us -> 35.1 us  [ring_pieces(): left[i] = lax.ppermute(left[i], axis, down)]
  transfers between devices with their start and end apart: 16 -> 17, of which waited for: 9 -> 6; matrix products, arithmetic and copies ran while one was open for 4% -> 4% of each run, Pallas kernels for 2% -> 2%
where the time goes in v6:
time: 240 us; the launch traced here: 239 us
  blocking collectives  82.4 us (34%)
  starting transfers between devices  65.2 us (27%)
  Pallas kernels  33.3 us (14%)
  waiting for transfers between devices  29.9 us (12%)
  between operations  14.5 us (6%)
  local copies, waits for them, and re-layouts  7.31 us (3%)
  other arithmetic  6.04 us (3%)
    all_to_all x8, blocking collectives, swap(): return lax.all_to_all(value, axes, split_axis=0, concat_axis=0, tiled=True)  82.4 us
    ppermute x7, starting transfers between devices, ring_pieces(): left[i] = lax.ppermute(left[i], axis, down)  35.1 us
    ppermute x7, starting transfers between devices, ring_pieces(): right[i] = lax.ppermute(right[i], axis, up)  16.3 us
    ppermute x7, waiting for transfers between devices, ring_pieces(): right[i] = lax.ppermute(right[i], axis, up)  15.8 us
    all_to_all x2, waiting for transfers between devices, swap(): return lax.all_to_all(value, axes, split_axis=0, concat_axis=0, tiled=True)  14.1 us
    all_to_all x2, starting transfers between devices, swap(): return lax.all_to_all(value, axes, split_axis=0, concat_axis=0, tiled=True)  13.7 us
    pallas_call x1, Pallas kernels, first_pass(): pl.pallas_call(first_kernel, in_specs=[SMEM_WHOLE] * 4 + [VMEM_WHOLE] * 4...  10.9 us
    pallas_call x1, Pallas kernels, second_pass(): pl.pallas_call(second_kernel, in_specs=[SMEM_WHOLE, SMEM_WHOLE, VMEM_WHOL...  5.71 us
  transfers between devices with their start and end apart: 17, of which 6 were waited for; matrix products, arithmetic and copies ran while one was open for 4% of the time, Pallas kernels for 2%

profile of v6, /device:TPU:1, one launch (start us, length us, event | category | flops | bytes accessed | tf_op | source)
XLA Modules:
  0.0 238.7 jit_solution(7087390771368521447)
XLA Ops:
  7.2 3.1 %shard_map.85.codes = bf16[2048,256]{1,0:T(8,128)(2,1)} custom-call(bf16[2048,256]{1,0:T(8,128)(2,1)} %frames.2, bf16[256,256]{1,0:T(8,128)(2,1)} %head.3), custom_call_target="tpu_custom_call" | custom-call | tf_op jit(solution)/shard_map/pallas_call | solution.py:97
  10.3 4.5 %shard_map.86 = bf16[2,1040,256]{2,1,0:T(8,128)(2,1)} custom-call(bf16[2048,256]{1,0:T(8,128)(2,1)} %frames.3, bf16[256,256]{1,0:T(8,128)(2,1)} %head.3), custom_call_target="tpu_custom_call" | custom-call | tf_op jit(solution)/shard_map/pallas_call | solution.py:184
  14.8 1.3 slice_bitcast_fusion
  16.1 4.8 %collective-permute-start.9 = (bf16[1040,256]{1,0:T(8,128)(2,1)S(1)}, bf16[1040,256]{1,0:T(8,128)(2,1)S(1)}, u32[]{:S(2)}, u32[]{:S(2)}) collective-permute-start(bf16[1040,256]{1,0:T(8,128)(2,1)S(1)} %get-tuple-element.25.rest_0_), channel_id=1, source_target_pairs={{0,8},{8,16},{16,24},{24,32},{32,40},{40,48},{48,56},{56,0},{1,9},... | collective-permute-start | bytes 1597448 | tf_op jit(solution)/shard_map/ppermute | solution.py:535
  21.0 8.6 %collective-permute-start.3 = (bf16[1040,256]{1,0:T(8,128)(2,1)S(1)}, bf16[1040,256]{1,0:T(8,128)(2,1)S(1)}, u32[]{:S(2)}, u32[]{:S(2)}) collective-permute-start(bf16[1040,256]{1,0:T(8,128)(2,1)S(1)} %get-tuple-element.25.rest_0_), channel_id=1, source_target_pairs={{0,56},{8,0},{16,8},{24,16},{32,24},{40,32},{48,40},{56,48},{1,57}... | collective-permute-start | bytes 1597448 | tf_op jit(solution)/shard_map/ppermute | solution.py:536
  29.5 3.4 %collective-permute-start.4 = (bf16[1040,256]{1,0:T(8,128)(2,1)S(1)}, bf16[1040,256]{1,0:T(8,128)(2,1)S(1)}, u32[]{:S(2)}, u32[]{:S(2)}) collective-permute-start(bf16[1040,256]{1,0:T(8,128)(2,1)S(1)} %get-tuple-element.26.rest_1_), channel_id=1, source_target_pairs={{0,56},{8,0},{16,8},{24,16},{32,24},{40,32},{48,40},{56,48},{1,57}... | collective-permute-start | bytes 1597448 | tf_op jit(solution)/shard_map/ppermute | solution.py:536
  32.9 1.9 collective-permute-start
  34.8 0.8 copy.22
  35.7 1.1 gather_fusion
  36.9 0.7 iota_compare_fusion.3
  38.0 0.7 copy.23
  38.7 8.6 %all-to-all-start = ((s32[16,1,8]{2,1,0:T(1,128)}), s32[16,1,8]{2,1,0:T(1,128)S(1)}, u32[]{:S(2)}, u32[]{:S(2)}) async-start(s32[16,1,8]{2,1,0:T(1,128)} %bitcast.3), calls=%async_computation | async-start | bytes 16384 | tf_op jit(solution)/shard_map/all_to_all | solution.py:543
  47.4 6.9 %all-to-all-done = s32[16,1,8]{2,1,0:T(1,128)S(1)} async-done(((s32[16,1,8]{2,1,0:T(1,128)}), s32[16,1,8]{2,1,0:T(1,128)S(1)}, u32[]{:S(2)}, u32[]{:S(2)}) %all-to-all-start) | async-done | bytes 544 | tf_op jit(solution)/shard_map/all_to_all | solution.py:543
  54.4 1.9 collective-permute-start.10
  56.4 4.9 %collective-permute-start.6 = (bf16[1040,256]{1,0:T(8,128)(2,1)S(1)}, bf16[1040,256]{1,0:T(8,128)(2,1)}, u32[]{:S(2)}, u32[]{:S(2)}) collective-permute-start(bf16[1040,256]{1,0:T(8,128)(2,1)S(1)} %collective-permute-done.4.rest_3_), channel_id=1, source_target_pairs={{0,56},{8,0},{16,8},{24,16},{32,24},{40,32},{48,40},{56,48},{1,57}... | collective-permute-start | bytes 1597448 | tf_op jit(solution)/shard_map/ppermute | solution.py:536
  61.4 1.9 collective-permute-start.1
  63.4 4.6 %collective-permute-start.5 = (bf16[1040,256]{1,0:T(8,128)(2,1)S(1)}, bf16[1040,256]{1,0:T(8,128)(2,1)}, u32[]{:S(2)}, u32[]{:S(2)}) collective-permute-start(bf16[1040,256]{1,0:T(8,128)(2,1)S(1)} %collective-permute-done.3.rest_2_), channel_id=1, source_target_pairs={{0,56},{8,0},{16,8},{24,16},{32,24},{40,32},{48,40},{56,48},{1,57}... | collective-permute-start | bytes 1597448 | tf_op jit(solution)/shard_map/ppermute | solution.py:536
  68.0 3.3 %collective-permute-done.10.rest_12_ = bf16[1040,256]{1,0:T(8,128)(2,1)} collective-permute-done((bf16[1040,256]{1,0:T(8,128)(2,1)S(1)}, bf16[1040,256]{1,0:T(8,128)(2,1)}, u32[]{:S(2)}, u32[]{:S(2)}) %collective-permute-start.10) | collective-permute-done | bytes 532512 | tf_op jit(solution)/shard_map/ppermute | solution.py:535
  71.3 1.9 collective-permute-start.11
  73.2 4.6 %collective-permute-start.8 = (bf16[1040,256]{1,0:T(8,128)(2,1)}, bf16[1040,256]{1,0:T(8,128)(2,1)}, u32[]{:S(2)}, u32[]{:S(2)}) collective-permute-start(bf16[1040,256]{1,0:T(8,128)(2,1)} %collective-permute-done.6.rest_5_), channel_id=1, source_target_pairs={{0,56},{8,0},{16,8},{24,16},{32,24},{40,32},{48,40},{56,48},{1,57}... | collective-permute-start | bytes 1597448 | tf_op jit(solution)/shard_map/ppermute | solution.py:536
  78.0 4.7 %collective-permute-done.1.rest_13_ = bf16[1040,256]{1,0:T(8,128)(2,1)S(1)} collective-permute-done((bf16[1040,256]{1,0:T(8,128)(2,1)}, bf16[1040,256]{1,0:T(8,128)(2,1)S(1)}, u32[]{:S(2)}, u32[]{:S(2)}) %collective-permute-start.1) | collective-permute-done | bytes 532512 | tf_op jit(solution)/shard_map/ppermute | solution.py:535
  82.7 1.9 collective-permute-start.2
  85.3 1.3 fusion.9
  86.6 4.6 %collective-permute-start.7 = (bf16[1040,256]{1,0:T(8,128)(2,1)}, bf16[1040,256]{1,0:T(8,128)(2,1)}, u32[]{:S(2)}, u32[]{:S(2)}) collective-permute-start(bf16[1040,256]{1,0:T(8,128)(2,1)} %collective-permute-done.5.rest_4_), channel_id=1, source_target_pairs={{0,56},{8,0},{16,8},{24,16},{32,24},{40,32},{48,40},{56,48},{1,57}... | collective-permute-start | bytes 1597448 | tf_op jit(solution)/shard_map/ppermute | solution.py:536
  91.2 2.9 %collective-permute-done.11.rest_10_ = bf16[1040,256]{1,0:T(8,128)(2,1)} collective-permute-done((bf16[1040,256]{1,0:T(8,128)(2,1)}, bf16[1040,256]{1,0:T(8,128)(2,1)}, u32[]{:S(2)}, u32[]{:S(2)}) %collective-permute-start.11) | collective-permute-done | bytes 532512 | tf_op jit(solution)/shard_map/ppermute | solution.py:535
  94.1 1.9 collective-permute-start.12
  96.0 4.6 %collective-permute-start.13 = (bf16[1040,256]{1,0:T(8,128)(2,1)}, bf16[1040,256]{1,0:T(8,128)(2,1)}, u32[]{:S(2)}, u32[]{:S(2)}) collective-permute-start(bf16[1040,256]{1,0:T(8,128)(2,1)} %collective-permute-done.8.rest_7_), channel_id=1, source_target_pairs={{0,56},{8,0},{16,8},{24,16},{32,24},{40,32},{48,40},{56,48},{1,57}... | collective-permute-start | bytes 1597448 | tf_op jit(solution)/shard_map/ppermute | solution.py:536
  100.6 4.9 %collective-permute-done.2.after.rest_11_ = bf16[1040,256]{1,0:T(8,128)(2,1)S(1)} collective-permute-done((bf16[1040,256]{1,0:T(8,128)(2,1)S(1)}, bf16[1040,256]{1,0:T(8,128)(2,1)S(1)}, u32[]{:S(2)}, u32[]{:S(2)}) %collective-permute-start.2) | collective-permute-done | bytes 532512 | tf_op jit(solution)/shard_map/ppermute | solution.py:535
  105.5 0.8 copy-done.2
  106.4 1.2 copy-done.1
  107.6 0.7 shard_map.87
  108.3 0.7 broadcast_in_dim.120
  108.9 5.1 %all-to-all-start.1 = ((f32[16,16,128]{2,1,0:T(8,128)}), f32[16,16,128]{2,1,0:T(8,128)S(1)}, u32[]{:S(2)}, u32[]{:S(2)}) async-start(f32[16,16,128]{2,1,0:T(8,128)} %broadcast_in_dim.120), calls=%async_computation.1 | async-start | bytes 262144 | tf_op jit(solution)/shard_map/all_to_all | solution.py:543
  114.0 0.7 pad_add_fusion.count
  114.7 1.3 fusion.11
  116.1 7.2 %all-to-all-done.1.received = f32[16,16,128]{2,1,0:T(8,128)S(1)} async-done(((f32[16,16,128]{2,1,0:T(8,128)}), f32[16,16,128]{2,1,0:T(8,128)S(1)}, u32[]{:S(2)}, u32[]{:S(2)}) %all-to-all-start.1) | async-done | bytes 131104 | tf_op jit(solution)/shard_map/all_to_all | solution.py:543
  123.6 10.9 %shard_map.89 = (f32[128,128,128]{2,1,0:T(8,128)}, bf16[128,128]{1,0:T(8,128)(2,1)S(1)}) custom-call(s32[2]{0:T(128)S(1)} %pad_add_fusion.count, s32[128]{0:T(128)S(1)} %get-tuple-element.24.place, s32[128]{0:T(128)S(1)} %fusion.7.col_at, s32[128]{0:T(128)S(1)} %get-tuple-element.23.row_at, s32[1,128]{1,0:T(1,128)S(1)} %get-tuple-element.29.col_place, ...), custom_call_target="tpu_custom_call" | custom-call | tf_op jit(solution)/shard_map/pallas_call | solution.py:323
  134.5 7.2 %all_to_all.50 = bf16[4,128,128]{2,1,0:T(8,128)(2,1)S(1)} all-to-all(bf16[4,128,128]{2,1,0:T(8,128)(2,1)S(1)} %broadcast_in_dim.121), channel_id=1, replica_groups=mesh['y'=8,'z'=8,'c'=2,'x'=4] {'x'}, dimensions={0} | all-to-all | bytes 262144 | tf_op jit(solution)/shard_map/all_to_all | solution.py:543
  141.8 15.3 %all_to_all.51.received = bf16[8,128,128]{2,1,0:T(8,128)(2,1)S(1)} all-to-all(bf16[8,128,128]{2,1,0:T(8,128)(2,1)S(1)} %broadcast_in_dim.122), channel_id=1, replica_groups=mesh['y'=8,'z'=8,'c'=2,'x'=4] {'z'}, dimensions={0} | all-to-all | bytes 524288 | tf_op jit(solution)/shard_map/all_to_all | solution.py:543
  157.1 5.7 %shard_map.90 = (bf16[128,256,128]{2,1,0:T(8,128)(2,1)}, bf16[256,128]{1,0:T(8,128)(2,1)S(1)}, f32[128,128]{1,0:T(8,128)S(1)}) custom-call(s32[2]{0:T(128)S(1)} %pad_add_fusion.count, s32[128]{0:T(128)S(1)} %fusion.7.col_at, s32[1,128]{1,0:T(1,128)S(1)} %get-tuple-element.30.row_place, bf16[8,128,128]{2,1,0:T(8,128)(2,1)S(1)} %all_to_all.51.received, ...), custom_call_target="tpu_custom_call" | custom-call | tf_op jit(solution)/shard_map/pallas_call | solution.py:405
  162.8 4.9 %all_to_all.52 = bf16[2,128,128]{2,1,0:T(8,128)(2,1)S(1)} all-to-all(bf16[2,128,128]{2,1,0:T(8,128)(2,1)S(1)} %bitcast.28), channel_id=1, replica_groups=mesh['y'=8,'z'=8,'c'=2,'x'=4] {'c'}, dimensions={0} | all-to-all | bytes 131072 | tf_op jit(solution)/shard_map/all_to_all | solution.py:543
  167.7 14.8 %all_to_all.53 = bf16[8,128,128]{2,1,0:T(8,128)(2,1)S(1)} all-to-all(bf16[8,128,128]{2,1,0:T(8,128)(2,1)S(1)} %broadcast_in_dim.123), channel_id=1, replica_groups=mesh['y'=8,'z'=8,'c'=2,'x'=4] {'y'}, dimensions={0} | all-to-all | bytes 524288 | tf_op jit(solution)/shard_map/all_to_all | solution.py:543
  182.6 3.9 %all_to_all.54 = bf16[2,128,128]{2,1,0:T(8,128)(2,1)S(1)} all-to-all(bf16[2,128,128]{2,1,0:T(8,128)(2,1)S(1)} %broadcast_in_dim.124), channel_id=1, replica_groups=mesh['y'=8,'z'=8,'c'=2,'x'=4] {'c'}, dimensions={0} | all-to-all | bytes 131072 | tf_op jit(solution)/shard_map/all_to_all | solution.py:543
  186.5 3.4 %shard_map.91 = bf16[128,128]{1,0:T(8,128)(2,1)S(1)} custom-call(s32[2]{0:T(128)S(1)} %pad_add_fusion.count, s32[128]{0:T(128)S(1)} %get-tuple-element.23.row_at, s32[1,128]{1,0:T(1,128)S(1)} %get-tuple-element.29.col_place, bf16[256,128]{1,0:T(8,128)(2,1)S(1)} %bitcast.27, bf16[128,256,128]{2,1,0:T(8,128)(2,1)} %get-tuple-element.17.kernel), custom_call_target="tpu_custom_call" | custom-call | tf_op jit(solution)/shard_map/pallas_call | solution.py:455
  189.9 7.2 %all_to_all.55 = bf16[4,128,128]{2,1,0:T(8,128)(2,1)S(1)} all-to-all(bf16[4,128,128]{2,1,0:T(8,128)(2,1)S(1)} %broadcast_in_dim.125), channel_id=1, replica_groups=mesh['y'=8,'z'=8,'c'=2,'x'=4] {'x'}, dimensions={0} | all-to-all | bytes 262144 | tf_op jit(solution)/shard_map/all_to_all | solution.py:543
  197.2 12.2 %all_to_all.56.received = bf16[8,128,128]{2,1,0:T(8,128)(2,1)S(1)} all-to-all(bf16[8,128,128]{2,1,0:T(8,128)(2,1)S(1)} %broadcast_in_dim.126), channel_id=1, replica_groups=mesh['y'=8,'z'=8,'c'=2,'x'=4] {'z'}, dimensions={0} | all-to-all | bytes 524288 | tf_op jit(solution)/shard_map/all_to_all | solution.py:543
  209.4 4.8 %shard_map.92 = (f32[16,32,128]{2,1,0:T(8,128)S(1)}, f32[16,128]{1,0:T(8,128)}) custom-call(s32[2]{0:T(128)S(1)} %pad_add_fusion.count, s32[128]{0:T(128)S(1)} %fusion.7.col_at, s32[1,128]{1,0:T(1,128)S(1)} %get-tuple-element.30.row_place, bf16[8,128,128]{2,1,0:T(8,128)(2,1)S(1)} %all_to_all.56.received, f32[128,128]{1,0:T(8,128)S(1)} %get-tuple-element.18.column_sum, ...), custom_call_target="tpu_custom_call" | custom-call | tf_op jit(solution)/shard_map/pallas_call | solution.py:508
  214.2 16.9 %all_to_all.57 = f32[16,32,128]{2,1,0:T(8,128)S(1)} all-to-all(f32[16,32,128]{2,1,0:T(8,128)S(1)} %get-tuple-element.19), channel_id=1, replica_groups=mesh['y'=8,'z'=8,'c'=2,'x'=4] {'y','c'}, dimensions={0} | all-to-all | bytes 524288 | tf_op jit(solution)/shard_map/all_to_all | solution.py:543
  (60 shorter events, 2.9 us)
Async XLA Ops:
  7.2 28.6 %copy-start = (s32[2048]{0:T(1024)S(1)}, s32[2048]{0:T(1024)}, u32[]{:S(2)}) copy-start(s32[2048]{0:T(1024)} %param.9) | copy-start | bytes 24580
  7.2 116.3 %all-gather.3.cloned.1.call-start = ((), (), s32[]{:S(2)}) async-start(), calls=%async_computation.10 | async-start | bytes 17825792 | tf_op jit(solution)/shard_map/all_gather | solution.py:585
  16.1 107.4 %copy-start.3 = (bf16[1040,256]{1,0:T(8,128)(2,1)}, bf16[1040,256]{1,0:T(8,128)(2,1)S(1)}, u32[]{:S(2)}) copy-start(bf16[1040,256]{1,0:T(8,128)(2,1)S(1)} %get-tuple-element.25.rest_0_) | copy-start | bytes 1597444
  16.1 107.4 %copy-start.4 = (bf16[1040,256]{1,0:T(8,128)(2,1)}, bf16[1040,256]{1,0:T(8,128)(2,1)S(1)}, u32[]{:S(2)}) copy-start(bf16[1040,256]{1,0:T(8,128)(2,1)S(1)} %get-tuple-element.26.rest_1_) | copy-start | bytes 1597444
  16.1 38.3 %collective-permute-start.9 = (bf16[1040,256]{1,0:T(8,128)(2,1)S(1)}, bf16[1040,256]{1,0:T(8,128)(2,1)S(1)}, u32[]{:S(2)}, u32[]{:S(2)}) collective-permute-start(bf16[1040,256]{1,0:T(8,128)(2,1)S(1)} %get-tuple-element.25.rest_0_), channel_id=1, source_target_pairs={{0,8},{8,16},{16,24},{24,32},{32,40},{40,48},{48,56},{56,0},{1,9},... | collective-permute-start | bytes 1597448 | tf_op jit(solution)/shard_map/ppermute | solution.py:535
  21.0 42.4 %collective-permute-start.3 = (bf16[1040,256]{1,0:T(8,128)(2,1)S(1)}, bf16[1040,256]{1,0:T(8,128)(2,1)S(1)}, u32[]{:S(2)}, u32[]{:S(2)}) collective-permute-start(bf16[1040,256]{1,0:T(8,128)(2,1)S(1)} %get-tuple-element.25.rest_0_), channel_id=1, source_target_pairs={{0,56},{8,0},{16,8},{24,16},{32,24},{40,32},{48,40},{56,48},{1,57}... | collective-permute-start | bytes 1597448 | tf_op jit(solution)/shard_map/ppermute | solution.py:536
  29.5 26.8 %collective-permute-start.4 = (bf16[1040,256]{1,0:T(8,128)(2,1)S(1)}, bf16[1040,256]{1,0:T(8,128)(2,1)S(1)}, u32[]{:S(2)}, u32[]{:S(2)}) collective-permute-start(bf16[1040,256]{1,0:T(8,128)(2,1)S(1)} %get-tuple-element.26.rest_1_), channel_id=1, source_target_pairs={{0,56},{8,0},{16,8},{24,16},{32,24},{40,32},{48,40},{56,48},{1,57}... | collective-permute-start | bytes 1597448 | tf_op jit(solution)/shard_map/ppermute | solution.py:536
  32.9 28.5 %collective-permute-start = (bf16[1040,256]{1,0:T(8,128)(2,1)S(1)}, bf16[1040,256]{1,0:T(8,128)(2,1)}, u32[]{:S(2)}, u32[]{:S(2)}) collective-permute-start(bf16[1040,256]{1,0:T(8,128)(2,1)S(1)} %get-tuple-element.26.rest_1_), channel_id=1, source_target_pairs={{0,8},{8,16},{16,24},{24,32},{32,40},{40,48},{48,56},{56,0},{1,9},... | collective-permute-start | bytes 1597448 | tf_op jit(solution)/shard_map/ppermute | solution.py:535
  38.7 15.6 %all-to-all-start = ((s32[16,1,8]{2,1,0:T(1,128)}), s32[16,1,8]{2,1,0:T(1,128)S(1)}, u32[]{:S(2)}, u32[]{:S(2)}) async-start(s32[16,1,8]{2,1,0:T(1,128)} %bitcast.3), calls=%async_computation | async-start | bytes 16384 | tf_op jit(solution)/shard_map/all_to_all | solution.py:543
  54.4 69.1 %copy-start.5 = (bf16[1040,256]{1,0:T(8,128)(2,1)}, bf16[1040,256]{1,0:T(8,128)(2,1)S(1)}, u32[]{:S(2)}) copy-start(bf16[1040,256]{1,0:T(8,128)(2,1)S(1)} %collective-permute-done.9.rest_14_) | copy-start | bytes 1597444
  54.4 16.9 %collective-permute-start.10 = (bf16[1040,256]{1,0:T(8,128)(2,1)S(1)}, bf16[1040,256]{1,0:T(8,128)(2,1)}, u32[]{:S(2)}, u32[]{:S(2)}) collective-permute-start(bf16[1040,256]{1,0:T(8,128)(2,1)S(1)} %collective-permute-done.9.rest_14_), channel_id=1, source_target_pairs={{0,8},{8,16},{16,24},{24,32},{32,40},{40,48},{48,56},{56,0},{1,9},... | collective-permute-start | bytes 1597448 | tf_op jit(solution)/shard_map/ppermute | solution.py:535
  56.4 21.7 %copy-start.7 = (bf16[1040,256]{1,0:T(8,128)(2,1)}, bf16[1040,256]{1,0:T(8,128)(2,1)S(1)}, u32[]{:S(2)}) copy-start(bf16[1040,256]{1,0:T(8,128)(2,1)S(1)} %collective-permute-done.4.rest_3_) | copy-start | bytes 1597444
  56.4 16.8 %collective-permute-start.6 = (bf16[1040,256]{1,0:T(8,128)(2,1)S(1)}, bf16[1040,256]{1,0:T(8,128)(2,1)}, u32[]{:S(2)}, u32[]{:S(2)}) collective-permute-start(bf16[1040,256]{1,0:T(8,128)(2,1)S(1)} %collective-permute-done.4.rest_3_), channel_id=1, source_target_pairs={{0,56},{8,0},{16,8},{24,16},{32,24},{40,32},{48,40},{56,48},{1,57}... | collective-permute-start | bytes 1597448 | tf_op jit(solution)/shard_map/ppermute | solution.py:536
  61.4 21.3 %collective-permute-start.1 = (bf16[1040,256]{1,0:T(8,128)(2,1)}, bf16[1040,256]{1,0:T(8,128)(2,1)S(1)}, u32[]{:S(2)}, u32[]{:S(2)}) collective-permute-start(bf16[1040,256]{1,0:T(8,128)(2,1)} %collective-permute-done.rest_15_), channel_id=1, source_target_pairs={{0,8},{8,16},{16,24},{24,32},{32,40},{40,48},{48,56},{56,0},{1,9},... | collective-permute-start | bytes 1597448 | tf_op jit(solution)/shard_map/ppermute | solution.py:535
  63.4 52.7 %copy-start.6 = (bf16[1040,256]{1,0:T(8,128)(2,1)}, bf16[1040,256]{1,0:T(8,128)(2,1)S(1)}, u32[]{:S(2)}) copy-start(bf16[1040,256]{1,0:T(8,128)(2,1)S(1)} %collective-permute-done.3.rest_2_) | copy-start | bytes 1597444
  63.4 23.2 %collective-permute-start.5 = (bf16[1040,256]{1,0:T(8,128)(2,1)S(1)}, bf16[1040,256]{1,0:T(8,128)(2,1)}, u32[]{:S(2)}, u32[]{:S(2)}) collective-permute-start(bf16[1040,256]{1,0:T(8,128)(2,1)S(1)} %collective-permute-done.3.rest_2_), channel_id=1, source_target_pairs={{0,56},{8,0},{16,8},{24,16},{32,24},{40,32},{48,40},{56,48},{1,57}... | collective-permute-start | bytes 1597448 | tf_op jit(solution)/shard_map/ppermute | solution.py:536
  71.3 22.8 %collective-permute-start.11 = (bf16[1040,256]{1,0:T(8,128)(2,1)}, bf16[1040,256]{1,0:T(8,128)(2,1)}, u32[]{:S(2)}, u32[]{:S(2)}) collective-permute-start(bf16[1040,256]{1,0:T(8,128)(2,1)} %collective-permute-done.10.rest_12_), channel_id=1, source_target_pairs={{0,8},{8,16},{16,24},{24,32},{32,40},{40,48},{48,56},{56,0},{1,9},... | collective-permute-start | bytes 1597448 | tf_op jit(solution)/shard_map/ppermute | solution.py:535
  73.2 22.8 %collective-permute-start.8 = (bf16[1040,256]{1,0:T(8,128)(2,1)}, bf16[1040,256]{1,0:T(8,128)(2,1)}, u32[]{:S(2)}, u32[]{:S(2)}) collective-permute-start(bf16[1040,256]{1,0:T(8,128)(2,1)} %collective-permute-done.6.rest_5_), channel_id=1, source_target_pairs={{0,56},{8,0},{16,8},{24,16},{32,24},{40,32},{48,40},{56,48},{1,57}... | collective-permute-start | bytes 1597448 | tf_op jit(solution)/shard_map/ppermute | solution.py:536
  82.7 17.9 %copy-start.8 = (bf16[1040,256]{1,0:T(8,128)(2,1)}, bf16[1040,256]{1,0:T(8,128)(2,1)S(1)}, u32[]{:S(2)}) copy-start(bf16[1040,256]{1,0:T(8,128)(2,1)S(1)} %collective-permute-done.1.rest_13_) | copy-start | bytes 1597444
  82.7 22.8 %collective-permute-start.2 = (bf16[1040,256]{1,0:T(8,128)(2,1)S(1)}, bf16[1040,256]{1,0:T(8,128)(2,1)S(1)}, u32[]{:S(2)}, u32[]{:S(2)}) collective-permute-start(bf16[1040,256]{1,0:T(8,128)(2,1)S(1)} %collective-permute-done.1.rest_13_), channel_id=1, source_target_pairs={{0,8},{8,16},{16,24},{24,32},{32,40},{40,48},{48,56},{56,0},{1,9},... | collective-permute-start | bytes 1597448 | tf_op jit(solution)/shard_map/ppermute | solution.py:535
  86.6 36.9 %collective-permute-start.7 = (bf16[1040,256]{1,0:T(8,128)(2,1)}, bf16[1040,256]{1,0:T(8,128)(2,1)}, u32[]{:S(2)}, u32[]{:S(2)}) collective-permute-start(bf16[1040,256]{1,0:T(8,128)(2,1)} %collective-permute-done.5.rest_4_), channel_id=1, source_target_pairs={{0,56},{8,0},{16,8},{24,16},{32,24},{40,32},{48,40},{56,48},{1,57}... | collective-permute-start | bytes 1597448 | tf_op jit(solution)/shard_map/ppermute | solution.py:536
  94.1 29.4 %collective-permute-start.12 = (bf16[1040,256]{1,0:T(8,128)(2,1)}, bf16[1040,256]{1,0:T(8,128)(2,1)}, u32[]{:S(2)}, u32[]{:S(2)}) collective-permute-start(bf16[1040,256]{1,0:T(8,128)(2,1)} %collective-permute-done.11.rest_10_), channel_id=1, source_target_pairs={{0,8},{8,16},{16,24},{24,32},{32,40},{40,48},{48,56},{56,0},{1,9},... | collective-permute-start | bytes 1597448 | tf_op jit(solution)/shard_map/ppermute | solution.py:535
  96.0 27.5 %collective-permute-start.13 = (bf16[1040,256]{1,0:T(8,128)(2,1)}, bf16[1040,256]{1,0:T(8,128)(2,1)}, u32[]{:S(2)}, u32[]{:S(2)}) collective-permute-start(bf16[1040,256]{1,0:T(8,128)(2,1)} %collective-permute-done.8.rest_7_), channel_id=1, source_target_pairs={{0,56},{8,0},{16,8},{24,16},{32,24},{40,32},{48,40},{56,48},{1,57}... | collective-permute-start | bytes 1597448 | tf_op jit(solution)/shard_map/ppermute | solution.py:536
  105.5 0.8 copy-start.2
  106.4 1.2 copy-start.1
  108.9 14.3 %all-to-all-start.1 = ((f32[16,16,128]{2,1,0:T(8,128)}), f32[16,16,128]{2,1,0:T(8,128)S(1)}, u32[]{:S(2)}, u32[]{:S(2)}) async-start(f32[16,16,128]{2,1,0:T(8,128)} %broadcast_in_dim.120), calls=%async_computation.1 | async-start | bytes 262144 | tf_op jit(solution)/shard_map/all_to_all | solution.py:543
Sparse Core Ops, SparseCore 0:
  10.4 103.8 all-gather.2

commit v7 on v6

--- a/solution.py
+++ b/solution.py
@@ -120,10 +120,10 @@
     return pl.pallas_call(
         norms_kernel,
         out_shape=jax.ShapeDtypeStruct((KB, BLK), F32),
-        in_specs=[VMEM_WHOLE, IN_HBM],
+        in_specs=[VMEM_WHOLE, pl.BlockSpec(memory_space=pl.ANY)],
         out_specs=VMEM_WHOLE,
         compiler_params=pltpu.CompilerParams(vmem_limit_bytes=GRANT),
-    )(codes, in_hbm(after))
+    )(codes, after)
 
 
 def parts_kernel(received, parts, picks):
@@ -584,7 +584,7 @@
     own_codes = project_codes(rollout, projection)
     left = lax.all_gather(own_codes, ("y", "c"))
     rights = ring_pieces(project(demo, projection), "z", NZ)
-    norms = block_norms(own_codes, rights[2 * (NZ - 3) + 1])
+    norms = block_norms(own_codes, rights[2 * (NZ - 2) + 1])
     parts, picks = norm_parts(to_all(norms, ("y", "c"), SOURCES))
     turned = (lax.axis_index("z") + jnp.arange(NZ, dtype=jnp.int32)) % NZ
     pick = turned[:, None] == jnp.arange(NZ, dtype=jnp.int32)[None, :]

time: 240 us -> 238 us (level)
  waiting for transfers between devices: 29.9 us -> 24.5 us
  blocking collectives: 82.4 us -> 86.7 us
  Pallas kernels: 33.3 us -> 30.4 us
    ppermute x7, waiting for transfers between devices: 15.8 us -> 5.98 us  [ring_pieces(): right[i] = lax.ppermute(right[i], axis, up)]
    ppermute x7, waiting for transfers between devices: 0.02 us -> 4.49 us  [ring_pieces(): left[i] = lax.ppermute(left[i], axis, down)]
    all_to_all x8, blocking collectives: 82.4 us -> 86.7 us  [swap(): return lax.all_to_all(value, axes, split_axis=0, concat_axis=0, tiled=True)]
  transfers between devices with their start and end apart: 17 -> 17, of which waited for: 6 -> 5; matrix products, arithmetic and copies ran while one was open for 4% -> 4% of each run, Pallas kernels for 2% -> 2%
where the time goes in v7:
time: 238 us; the launch traced here: 236 us
  blocking collectives  86.7 us (36%)
  starting transfers between devices  67.3 us (28%)
  Pallas kernels  30.4 us (13%)
  waiting for transfers between devices  24.5 us (10%)
  between operations  14.5 us (6%)
  local copies, waits for them, and re-layouts  6.44 us (3%)
  other arithmetic  6.04 us (3%)
    all_to_all x8, blocking collectives, swap(): return lax.all_to_all(value, axes, split_axis=0, concat_axis=0, tiled=True)  86.7 us
    ppermute x7, starting transfers between devices, ring_pieces(): left[i] = lax.ppermute(left[i], axis, down)  35.5 us
    ppermute x7, starting transfers between devices, ring_pieces(): right[i] = lax.ppermute(right[i], axis, up)  16.3 us
    all_to_all x2, starting transfers between devices, swap(): return lax.all_to_all(value, axes, split_axis=0, concat_axis=0, tiled=True)  15.5 us
    all_to_all x2, waiting for transfers between devices, swap(): return lax.all_to_all(value, axes, split_axis=0, concat_axis=0, tiled=True)  14 us
    pallas_call x1, Pallas kernels, first_pass(): pl.pallas_call(first_kernel, in_specs=[SMEM_WHOLE] * 4 + [VMEM_WHOLE] * 4...  9.62 us
    ppermute x7, waiting for transfers between devices, ring_pieces(): right[i] = lax.ppermute(right[i], axis, up)  5.98 us
    pallas_call x1, Pallas kernels, second_pass(): pl.pallas_call(second_kernel, in_specs=[SMEM_WHOLE, SMEM_WHOLE, VMEM_WHOL...  4.77 us
  transfers between devices with their start and end apart: 17, of which 5 were waited for; matrix products, arithmetic and copies ran while one was open for 4% of the time, Pallas kernels for 2%

profile of v7, /device:TPU:1, one launch (start us, length us, event | category | flops | bytes accessed | tf_op | source)
XLA Modules:
  0.0 235.9 jit_solution(2747727043950129359)
XLA Ops:
  7.2 3.1 %shard_map.85.codes = bf16[2048,256]{1,0:T(8,128)(2,1)} custom-call(bf16[2048,256]{1,0:T(8,128)(2,1)} %frames.2, bf16[256,256]{1,0:T(8,128)(2,1)} %head.3), custom_call_target="tpu_custom_call" | custom-call | tf_op jit(solution)/shard_map/pallas_call | solution.py:97
  10.3 4.5 %shard_map.86 = bf16[2,1040,256]{2,1,0:T(8,128)(2,1)} custom-call(bf16[2048,256]{1,0:T(8,128)(2,1)} %frames.3, bf16[256,256]{1,0:T(8,128)(2,1)} %head.3), custom_call_target="tpu_custom_call" | custom-call | tf_op jit(solution)/shard_map/pallas_call | solution.py:184
  14.8 1.3 slice_bitcast_fusion
  16.1 4.8 %collective-permute-start.8 = (bf16[1040,256]{1,0:T(8,128)(2,1)S(1)}, bf16[1040,256]{1,0:T(8,128)(2,1)S(1)}, u32[]{:S(2)}, u32[]{:S(2)}) collective-permute-start(bf16[1040,256]{1,0:T(8,128)(2,1)S(1)} %get-tuple-element.25.rest_0_), channel_id=1, source_target_pairs={{0,8},{8,16},{16,24},{24,32},{32,40},{40,48},{48,56},{56,0},{1,9},... | collective-permute-start | bytes 1597448 | tf_op jit(solution)/shard_map/ppermute | solution.py:535
  20.9 8.6 %collective-permute-start.2 = (bf16[1040,256]{1,0:T(8,128)(2,1)S(1)}, bf16[1040,256]{1,0:T(8,128)(2,1)S(1)}, u32[]{:S(2)}, u32[]{:S(2)}) collective-permute-start(bf16[1040,256]{1,0:T(8,128)(2,1)S(1)} %get-tuple-element.25.rest_0_), channel_id=1, source_target_pairs={{0,56},{8,0},{16,8},{24,16},{32,24},{40,32},{48,40},{56,48},{1,57}... | collective-permute-start | bytes 1597448 | tf_op jit(solution)/shard_map/ppermute | solution.py:536
  29.5 3.4 %collective-permute-start.3 = (bf16[1040,256]{1,0:T(8,128)(2,1)S(1)}, bf16[1040,256]{1,0:T(8,128)(2,1)}, u32[]{:S(2)}, u32[]{:S(2)}) collective-permute-start(bf16[1040,256]{1,0:T(8,128)(2,1)S(1)} %get-tuple-element.26.rest_1_), channel_id=1, source_target_pairs={{0,56},{8,0},{16,8},{24,16},{32,24},{40,32},{48,40},{56,48},{1,57}... | collective-permute-start | bytes 1597448 | tf_op jit(solution)/shard_map/ppermute | solution.py:536
  32.9 1.9 collective-permute-start
  34.8 0.8 copy.22
  35.7 1.1 gather_fusion
  36.9 0.7 iota_compare_fusion.3
  38.0 0.7 copy.23
  38.7 8.6 %all-to-all-start = ((s32[16,1,8]{2,1,0:T(1,128)}), s32[16,1,8]{2,1,0:T(1,128)S(1)}, u32[]{:S(2)}, u32[]{:S(2)}) async-start(s32[16,1,8]{2,1,0:T(1,128)} %bitcast.3), calls=%async_computation | async-start | bytes 16384 | tf_op jit(solution)/shard_map/all_to_all | solution.py:543
  47.4 6.9 %all-to-all-done = s32[16,1,8]{2,1,0:T(1,128)S(1)} async-done(((s32[16,1,8]{2,1,0:T(1,128)}), s32[16,1,8]{2,1,0:T(1,128)S(1)}, u32[]{:S(2)}, u32[]{:S(2)}) %all-to-all-start) | async-done | bytes 544 | tf_op jit(solution)/shard_map/all_to_all | solution.py:543
  54.4 1.9 collective-permute-start.9
  56.4 4.9 %collective-permute-start.5 = (bf16[1040,256]{1,0:T(8,128)(2,1)}, bf16[1040,256]{1,0:T(8,128)(2,1)}, u32[]{:S(2)}, u32[]{:S(2)}) collective-permute-start(bf16[1040,256]{1,0:T(8,128)(2,1)} %collective-permute-done.3.rest_3_), channel_id=1, source_target_pairs={{0,56},{8,0},{16,8},{24,16},{32,24},{40,32},{48,40},{56,48},{1,57}... | collective-permute-start | bytes 1597448 | tf_op jit(solution)/shard_map/ppermute | solution.py:536
  61.4 0.6 select_reduce_fusion.3
  62.2 3.4 %collective-permute-start.4 = (bf16[1040,256]{1,0:T(8,128)(2,1)S(1)}, bf16[1040,256]{1,0:T(8,128)(2,1)}, u32[]{:S(2)}, u32[]{:S(2)}) collective-permute-start(bf16[1040,256]{1,0:T(8,128)(2,1)S(1)} %collective-permute-done.2.rest_2_), channel_id=1, source_target_pairs={{0,56},{8,0},{16,8},{24,16},{32,24},{40,32},{48,40},{56,48},{1,57}... | collective-permute-start | bytes 1597448 | tf_op jit(solution)/shard_map/ppermute | solution.py:536
  65.6 1.9 collective-permute-start.1
  67.5 3.8 %collective-permute-done.9.rest_12_ = bf16[1040,256]{1,0:T(8,128)(2,1)} collective-permute-done((bf16[1040,256]{1,0:T(8,128)(2,1)S(1)}, bf16[1040,256]{1,0:T(8,128)(2,1)}, u32[]{:S(2)}, u32[]{:S(2)}) %collective-permute-start.9) | collective-permute-done | bytes 532512 | tf_op jit(solution)/shard_map/ppermute | solution.py:535
  71.3 1.9 collective-permute-start.10
  73.2 4.6 %collective-permute-start.7 = (bf16[1040,256]{1,0:T(8,128)(2,1)}, bf16[1040,256]{1,0:T(8,128)(2,1)}, u32[]{:S(2)}, u32[]{:S(2)}) collective-permute-start(bf16[1040,256]{1,0:T(8,128)(2,1)} %collective-permute-done.5.rest_5_), channel_id=1, source_target_pairs={{0,56},{8,0},{16,8},{24,16},{32,24},{40,32},{48,40},{56,48},{1,57}... | collective-permute-start | bytes 1597448 | tf_op jit(solution)/shard_map/ppermute | solution.py:536
  77.9 1.3 fusion.9
  79.2 4.4 %collective-permute-done.4.rest_4_ = bf16[1040,256]{1,0:T(8,128)(2,1)} collective-permute-done((bf16[1040,256]{1,0:T(8,128)(2,1)S(1)}, bf16[1040,256]{1,0:T(8,128)(2,1)}, u32[]{:S(2)}, u32[]{:S(2)}) %collective-permute-start.4) | collective-permute-done | bytes 532512 | tf_op jit(solution)/shard_map/ppermute | solution.py:536
  83.7 5.4 %collective-permute-start.6 = (bf16[1040,256]{1,0:T(8,128)(2,1)}, bf16[1040,256]{1,0:T(8,128)(2,1)}, u32[]{:S(2)}, u32[]{:S(2)}) collective-permute-start(bf16[1040,256]{1,0:T(8,128)(2,1)} %collective-permute-done.4.rest_4_), channel_id=1, source_target_pairs={{0,56},{8,0},{16,8},{24,16},{32,24},{40,32},{48,40},{56,48},{1,57}... | collective-permute-start | bytes 1597448 | tf_op jit(solution)/shard_map/ppermute | solution.py:536
  89.1 1.9 collective-permute-start.13
  91.0 2.2 collective-permute-done.10.rest_10_
  93.2 1.9 collective-permute-start.11
  95.2 5.3 %collective-permute-start.12 = (bf16[1040,256]{1,0:T(8,128)(2,1)}, bf16[1040,256]{1,0:T(8,128)(2,1)}, u32[]{:S(2)}, u32[]{:S(2)}) collective-permute-start(bf16[1040,256]{1,0:T(8,128)(2,1)} %collective-permute-done.7.rest_7_), channel_id=1, source_target_pairs={{0,56},{8,0},{16,8},{24,16},{32,24},{40,32},{48,40},{56,48},{1,57}... | collective-permute-start | bytes 1597448 | tf_op jit(solution)/shard_map/ppermute | solution.py:536
  100.5 1.2 copy-done.1
  101.8 0.7 shard_map.87
  102.4 0.7 broadcast_in_dim.120
  103.1 6.8 %all-to-all-start.1 = ((f32[16,16,128]{2,1,0:T(8,128)}), f32[16,16,128]{2,1,0:T(8,128)S(1)}, u32[]{:S(2)}, u32[]{:S(2)}) async-start(f32[16,16,128]{2,1,0:T(8,128)} %broadcast_in_dim.120), calls=%async_computation.1 | async-start | bytes 262144 | tf_op jit(solution)/shard_map/all_to_all | solution.py:543
  109.9 0.7 pad_add_fusion.count
  110.6 1.3 fusion.11
  112.0 7.1 %all-to-all-done.1.received = f32[16,16,128]{2,1,0:T(8,128)S(1)} async-done(((f32[16,16,128]{2,1,0:T(8,128)}), f32[16,16,128]{2,1,0:T(8,128)S(1)}, u32[]{:S(2)}, u32[]{:S(2)}) %all-to-all-start.1) | async-done | bytes 131104 | tf_op jit(solution)/shard_map/all_to_all | solution.py:543
  119.4 9.6 %shard_map.89 = (f32[128,128,128]{2,1,0:T(8,128)}, bf16[128,128]{1,0:T(8,128)(2,1)S(1)}) custom-call(s32[2]{0:T(128)S(1)} %pad_add_fusion.count, s32[128]{0:T(128)S(1)} %get-tuple-element.24.place, s32[128]{0:T(128)S(1)} %fusion.7.col_at, s32[128]{0:T(128)S(1)} %get-tuple-element.23.row_at, s32[1,128]{1,0:T(1,128)S(1)} %get-tuple-element.29.col_place, ...), custom_call_target="tpu_custom_call" | custom-call | tf_op jit(solution)/shard_map/pallas_call | solution.py:323
  129.1 8.5 %all_to_all.50 = bf16[4,128,128]{2,1,0:T(8,128)(2,1)S(1)} all-to-all(bf16[4,128,128]{2,1,0:T(8,128)(2,1)S(1)} %broadcast_in_dim.121), channel_id=1, replica_groups=mesh['y'=8,'z'=8,'c'=2,'x'=4] {'x'}, dimensions={0} | all-to-all | bytes 262144 | tf_op jit(solution)/shard_map/all_to_all | solution.py:543
  137.7 14.4 %all_to_all.51.received = bf16[8,128,128]{2,1,0:T(8,128)(2,1)S(1)} all-to-all(bf16[8,128,128]{2,1,0:T(8,128)(2,1)S(1)} %broadcast_in_dim.122), channel_id=1, replica_groups=mesh['y'=8,'z'=8,'c'=2,'x'=4] {'z'}, dimensions={0} | all-to-all | bytes 524288 | tf_op jit(solution)/shard_map/all_to_all | solution.py:543
  152.1 4.8 %shard_map.90 = (bf16[128,256,128]{2,1,0:T(8,128)(2,1)}, bf16[256,128]{1,0:T(8,128)(2,1)S(1)}, f32[128,128]{1,0:T(8,128)S(1)}) custom-call(s32[2]{0:T(128)S(1)} %pad_add_fusion.count, s32[128]{0:T(128)S(1)} %fusion.7.col_at, s32[1,128]{1,0:T(1,128)S(1)} %get-tuple-element.30.row_place, bf16[8,128,128]{2,1,0:T(8,128)(2,1)S(1)} %all_to_all.51.received, ...), custom_call_target="tpu_custom_call" | custom-call | tf_op jit(solution)/shard_map/pallas_call | solution.py:405
  156.9 7.1 %all_to_all.52 = bf16[2,128,128]{2,1,0:T(8,128)(2,1)S(1)} all-to-all(bf16[2,128,128]{2,1,0:T(8,128)(2,1)S(1)} %bitcast.28), channel_id=1, replica_groups=mesh['y'=8,'z'=8,'c'=2,'x'=4] {'c'}, dimensions={0} | all-to-all | bytes 131072 | tf_op jit(solution)/shard_map/all_to_all | solution.py:543
  164.0 14.8 %all_to_all.53 = bf16[8,128,128]{2,1,0:T(8,128)(2,1)S(1)} all-to-all(bf16[8,128,128]{2,1,0:T(8,128)(2,1)S(1)} %broadcast_in_dim.123), channel_id=1, replica_groups=mesh['y'=8,'z'=8,'c'=2,'x'=4] {'y'}, dimensions={0} | all-to-all | bytes 524288 | tf_op jit(solution)/shard_map/all_to_all | solution.py:543
  178.9 5.1 %all_to_all.54 = bf16[2,128,128]{2,1,0:T(8,128)(2,1)S(1)} all-to-all(bf16[2,128,128]{2,1,0:T(8,128)(2,1)S(1)} %broadcast_in_dim.124), channel_id=1, replica_groups=mesh['y'=8,'z'=8,'c'=2,'x'=4] {'c'}, dimensions={0} | all-to-all | bytes 131072 | tf_op jit(solution)/shard_map/all_to_all | solution.py:543
  184.0 3.2 %shard_map.91 = bf16[128,128]{1,0:T(8,128)(2,1)S(1)} custom-call(s32[2]{0:T(128)S(1)} %pad_add_fusion.count, s32[128]{0:T(128)S(1)} %get-tuple-element.23.row_at, s32[1,128]{1,0:T(1,128)S(1)} %get-tuple-element.29.col_place, bf16[256,128]{1,0:T(8,128)(2,1)S(1)} %bitcast.27, bf16[128,256,128]{2,1,0:T(8,128)(2,1)} %get-tuple-element.17.kernel), custom_call_target="tpu_custom_call" | custom-call | tf_op jit(solution)/shard_map/pallas_call | solution.py:455
  187.2 7.2 %all_to_all.55 = bf16[4,128,128]{2,1,0:T(8,128)(2,1)S(1)} all-to-all(bf16[4,128,128]{2,1,0:T(8,128)(2,1)S(1)} %broadcast_in_dim.125), channel_id=1, replica_groups=mesh['y'=8,'z'=8,'c'=2,'x'=4] {'x'}, dimensions={0} | all-to-all | bytes 262144 | tf_op jit(solution)/shard_map/all_to_all | solution.py:543
  194.5 12.6 %all_to_all.56.received = bf16[8,128,128]{2,1,0:T(8,128)(2,1)S(1)} all-to-all(bf16[8,128,128]{2,1,0:T(8,128)(2,1)S(1)} %broadcast_in_dim.126), channel_id=1, replica_groups=mesh['y'=8,'z'=8,'c'=2,'x'=4] {'z'}, dimensions={0} | all-to-all | bytes 524288 | tf_op jit(solution)/shard_map/all_to_all | solution.py:543
  207.1 4.4 %shard_map.92 = (f32[16,32,128]{2,1,0:T(8,128)S(1)}, f32[16,128]{1,0:T(8,128)}) custom-call(s32[2]{0:T(128)S(1)} %pad_add_fusion.count, s32[128]{0:T(128)S(1)} %fusion.7.col_at, s32[1,128]{1,0:T(1,128)S(1)} %get-tuple-element.30.row_place, bf16[8,128,128]{2,1,0:T(8,128)(2,1)S(1)} %all_to_all.56.received, f32[128,128]{1,0:T(8,128)S(1)} %get-tuple-element.18.column_sum, ...), custom_call_target="tpu_custom_call" | custom-call | tf_op jit(solution)/shard_map/pallas_call | solution.py:508
  211.5 16.9 %all_to_all.57 = f32[16,32,128]{2,1,0:T(8,128)S(1)} all-to-all(f32[16,32,128]{2,1,0:T(8,128)S(1)} %get-tuple-element.19), channel_id=1, replica_groups=mesh['y'=8,'z'=8,'c'=2,'x'=4] {'y','c'}, dimensions={0} | all-to-all | bytes 524288 | tf_op jit(solution)/shard_map/all_to_all | solution.py:543
  228.4 0.6 multiply_bitcast_fusion
  (56 shorter events, 1.7 us)
Async XLA Ops:
  7.2 28.5 %copy-start = (s32[2048]{0:T(1024)S(1)}, s32[2048]{0:T(1024)}, u32[]{:S(2)}) copy-start(s32[2048]{0:T(1024)} %param.9) | copy-start | bytes 24580
  7.2 112.2 %all-gather.3.cloned.1.call-start = ((), (), s32[]{:S(2)}) async-start(), calls=%async_computation.10 | async-start | bytes 17825792 | tf_op jit(solution)/shard_map/all_gather | solution.py:585
  16.1 103.3 %copy-start.3 = (bf16[1040,256]{1,0:T(8,128)(2,1)}, bf16[1040,256]{1,0:T(8,128)(2,1)S(1)}, u32[]{:S(2)}) copy-start(bf16[1040,256]{1,0:T(8,128)(2,1)S(1)} %get-tuple-element.25.rest_0_) | copy-start | bytes 1597444
  16.1 103.3 %copy-start.4 = (bf16[1040,256]{1,0:T(8,128)(2,1)}, bf16[1040,256]{1,0:T(8,128)(2,1)S(1)}, u32[]{:S(2)}) copy-start(bf16[1040,256]{1,0:T(8,128)(2,1)S(1)} %get-tuple-element.26.rest_1_) | copy-start | bytes 1597444
  16.1 38.3 %collective-permute-start.8 = (bf16[1040,256]{1,0:T(8,128)(2,1)S(1)}, bf16[1040,256]{1,0:T(8,128)(2,1)S(1)}, u32[]{:S(2)}, u32[]{:S(2)}) collective-permute-start(bf16[1040,256]{1,0:T(8,128)(2,1)S(1)} %get-tuple-element.25.rest_0_), channel_id=1, source_target_pairs={{0,8},{8,16},{16,24},{24,32},{32,40},{40,48},{48,56},{56,0},{1,9},... | collective-permute-start | bytes 1597448 | tf_op jit(solution)/shard_map/ppermute | solution.py:535
  20.9 41.2 %collective-permute-start.2 = (bf16[1040,256]{1,0:T(8,128)(2,1)S(1)}, bf16[1040,256]{1,0:T(8,128)(2,1)S(1)}, u32[]{:S(2)}, u32[]{:S(2)}) collective-permute-start(bf16[1040,256]{1,0:T(8,128)(2,1)S(1)} %get-tuple-element.25.rest_0_), channel_id=1, source_target_pairs={{0,56},{8,0},{16,8},{24,16},{32,24},{40,32},{48,40},{56,48},{1,57}... | collective-permute-start | bytes 1597448 | tf_op jit(solution)/shard_map/ppermute | solution.py:536
  29.5 26.8 %collective-permute-start.3 = (bf16[1040,256]{1,0:T(8,128)(2,1)S(1)}, bf16[1040,256]{1,0:T(8,128)(2,1)}, u32[]{:S(2)}, u32[]{:S(2)}) collective-permute-start(bf16[1040,256]{1,0:T(8,128)(2,1)S(1)} %get-tuple-element.26.rest_1_), channel_id=1, source_target_pairs={{0,56},{8,0},{16,8},{24,16},{32,24},{40,32},{48,40},{56,48},{1,57}... | collective-permute-start | bytes 1597448 | tf_op jit(solution)/shard_map/ppermute | solution.py:536
  32.9 32.6 %collective-permute-start = (bf16[1040,256]{1,0:T(8,128)(2,1)S(1)}, bf16[1040,256]{1,0:T(8,128)(2,1)}, u32[]{:S(2)}, u32[]{:S(2)}) collective-permute-start(bf16[1040,256]{1,0:T(8,128)(2,1)S(1)} %get-tuple-element.26.rest_1_), channel_id=1, source_target_pairs={{0,8},{8,16},{16,24},{24,32},{32,40},{40,48},{48,56},{56,0},{1,9},... | collective-permute-start | bytes 1597448 | tf_op jit(solution)/shard_map/ppermute | solution.py:535
  38.7 15.7 %all-to-all-start = ((s32[16,1,8]{2,1,0:T(1,128)}), s32[16,1,8]{2,1,0:T(1,128)S(1)}, u32[]{:S(2)}, u32[]{:S(2)}) async-start(s32[16,1,8]{2,1,0:T(1,128)} %bitcast.3), calls=%async_computation | async-start | bytes 16384 | tf_op jit(solution)/shard_map/all_to_all | solution.py:543
  54.4 65.0 %copy-start.5 = (bf16[1040,256]{1,0:T(8,128)(2,1)}, bf16[1040,256]{1,0:T(8,128)(2,1)S(1)}, u32[]{:S(2)}) copy-start(bf16[1040,256]{1,0:T(8,128)(2,1)S(1)} %collective-permute-done.8.rest_14_) | copy-start | bytes 1597444
  54.4 16.9 %collective-permute-start.9 = (bf16[1040,256]{1,0:T(8,128)(2,1)S(1)}, bf16[1040,256]{1,0:T(8,128)(2,1)}, u32[]{:S(2)}, u32[]{:S(2)}) collective-permute-start(bf16[1040,256]{1,0:T(8,128)(2,1)S(1)} %collective-permute-done.8.rest_14_), channel_id=1, source_target_pairs={{0,8},{8,16},{16,24},{24,32},{32,40},{40,48},{48,56},{56,0},{1,9},... | collective-permute-start | bytes 1597448 | tf_op jit(solution)/shard_map/ppermute | solution.py:535
  56.4 16.8 %collective-permute-start.5 = (bf16[1040,256]{1,0:T(8,128)(2,1)}, bf16[1040,256]{1,0:T(8,128)(2,1)}, u32[]{:S(2)}, u32[]{:S(2)}) collective-permute-start(bf16[1040,256]{1,0:T(8,128)(2,1)} %collective-permute-done.3.rest_3_), channel_id=1, source_target_pairs={{0,56},{8,0},{16,8},{24,16},{32,24},{40,32},{48,40},{56,48},{1,57}... | collective-permute-start | bytes 1597448 | tf_op jit(solution)/shard_map/ppermute | solution.py:536
  62.2 49.8 %copy-start.6 = (bf16[1040,256]{1,0:T(8,128)(2,1)}, bf16[1040,256]{1,0:T(8,128)(2,1)S(1)}, u32[]{:S(2)}) copy-start(bf16[1040,256]{1,0:T(8,128)(2,1)S(1)} %collective-permute-done.2.rest_2_) | copy-start | bytes 1597444
  62.2 21.5 %collective-permute-start.4 = (bf16[1040,256]{1,0:T(8,128)(2,1)S(1)}, bf16[1040,256]{1,0:T(8,128)(2,1)}, u32[]{:S(2)}, u32[]{:S(2)}) collective-permute-start(bf16[1040,256]{1,0:T(8,128)(2,1)S(1)} %collective-permute-done.2.rest_2_), channel_id=1, source_target_pairs={{0,56},{8,0},{16,8},{24,16},{32,24},{40,32},{48,40},{56,48},{1,57}... | collective-permute-start | bytes 1597448 | tf_op jit(solution)/shard_map/ppermute | solution.py:536
  65.6 23.5 %collective-permute-start.1 = (bf16[1040,256]{1,0:T(8,128)(2,1)}, bf16[1040,256]{1,0:T(8,128)(2,1)S(1)}, u32[]{:S(2)}, u32[]{:S(2)}) collective-permute-start(bf16[1040,256]{1,0:T(8,128)(2,1)} %collective-permute-done.rest_15_), channel_id=1, source_target_pairs={{0,8},{8,16},{16,24},{24,32},{32,40},{40,48},{48,56},{56,0},{1,9},... | collective-permute-start | bytes 1597448 | tf_op jit(solution)/shard_map/ppermute | solution.py:535
  71.3 21.9 %collective-permute-start.10 = (bf16[1040,256]{1,0:T(8,128)(2,1)}, bf16[1040,256]{1,0:T(8,128)(2,1)}, u32[]{:S(2)}, u32[]{:S(2)}) collective-permute-start(bf16[1040,256]{1,0:T(8,128)(2,1)} %collective-permute-done.9.rest_12_), channel_id=1, source_target_pairs={{0,8},{8,16},{16,24},{24,32},{32,40},{40,48},{48,56},{56,0},{1,9},... | collective-permute-start | bytes 1597448 | tf_op jit(solution)/shard_map/ppermute | solution.py:535
  73.2 22.0 %collective-permute-start.7 = (bf16[1040,256]{1,0:T(8,128)(2,1)}, bf16[1040,256]{1,0:T(8,128)(2,1)}, u32[]{:S(2)}, u32[]{:S(2)}) collective-permute-start(bf16[1040,256]{1,0:T(8,128)(2,1)} %collective-permute-done.5.rest_5_), channel_id=1, source_target_pairs={{0,56},{8,0},{16,8},{24,16},{32,24},{40,32},{48,40},{56,48},{1,57}... | collective-permute-start | bytes 1597448 | tf_op jit(solution)/shard_map/ppermute | solution.py:536
  83.7 35.7 %collective-permute-start.6 = (bf16[1040,256]{1,0:T(8,128)(2,1)}, bf16[1040,256]{1,0:T(8,128)(2,1)}, u32[]{:S(2)}, u32[]{:S(2)}) collective-permute-start(bf16[1040,256]{1,0:T(8,128)(2,1)} %collective-permute-done.4.rest_4_), channel_id=1, source_target_pairs={{0,56},{8,0},{16,8},{24,16},{32,24},{40,32},{48,40},{56,48},{1,57}... | collective-permute-start | bytes 1597448 | tf_op jit(solution)/shard_map/ppermute | solution.py:536
  89.1 30.3 %copy-start.2 = (bf16[1040,256]{1,0:T(8,128)(2,1)}, bf16[1040,256]{1,0:T(8,128)(2,1)S(1)}, u32[]{:S(2)}) copy-start(bf16[1040,256]{1,0:T(8,128)(2,1)S(1)} %collective-permute-done.1.after.rest_13_) | copy-start | bytes 1597444
  89.1 30.2 %collective-permute-start.13 = (bf16[1040,256]{1,0:T(8,128)(2,1)S(1)}, bf16[1040,256]{1,0:T(8,128)(2,1)}, u32[]{:S(2)}, u32[]{:S(2)}) collective-permute-start(bf16[1040,256]{1,0:T(8,128)(2,1)S(1)} %collective-permute-done.1.after.rest_13_), channel_id=1, source_target_pairs={{0,8},{8,16},{16,24},{24,32},{32,40},{40,48},{48,56},{56,0},{1,9},... | collective-permute-start | bytes 1597448 | tf_op jit(solution)/shard_map/ppermute | solution.py:535
  93.2 26.1 %collective-permute-start.11 = (bf16[1040,256]{1,0:T(8,128)(2,1)}, bf16[1040,256]{1,0:T(8,128)(2,1)}, u32[]{:S(2)}, u32[]{:S(2)}) collective-permute-start(bf16[1040,256]{1,0:T(8,128)(2,1)} %collective-permute-done.10.rest_10_), channel_id=1, source_target_pairs={{0,8},{8,16},{16,24},{24,32},{32,40},{40,48},{48,56},{56,0},{1,9},... | collective-permute-start | bytes 1597448 | tf_op jit(solution)/shard_map/ppermute | solution.py:535
  95.2 24.2 %collective-permute-start.12 = (bf16[1040,256]{1,0:T(8,128)(2,1)}, bf16[1040,256]{1,0:T(8,128)(2,1)}, u32[]{:S(2)}, u32[]{:S(2)}) collective-permute-start(bf16[1040,256]{1,0:T(8,128)(2,1)} %collective-permute-done.7.rest_7_), channel_id=1, source_target_pairs={{0,56},{8,0},{16,8},{24,16},{32,24},{40,32},{48,40},{56,48},{1,57}... | collective-permute-start | bytes 1597448 | tf_op jit(solution)/shard_map/ppermute | solution.py:536
  100.5 1.2 copy-start.1
  103.1 16.0 %all-to-all-start.1 = ((f32[16,16,128]{2,1,0:T(8,128)}), f32[16,16,128]{2,1,0:T(8,128)S(1)}, u32[]{:S(2)}, u32[]{:S(2)}) async-start(f32[16,16,128]{2,1,0:T(8,128)} %broadcast_in_dim.120), calls=%async_computation.1 | async-start | bytes 262144 | tf_op jit(solution)/shard_map/all_to_all | solution.py:543
Sparse Core Ops, SparseCore 0:
  10.4 103.8 all-gather.2

commit v8 on v7

--- a/solution.py
+++ b/solution.py
@@ -149,13 +149,13 @@
     )(received)
 
 
-def project_kernel(frames, head, out, here, projection, made, norms, sems, head_sem, out_sems):
+def project_kernel(frames, head, top, bottom, here, projection, made, norms, sems, head_sem, out_sems):
     def inward(n):
         rows = pl.ds(n * PART, PART)
         return pltpu.make_async_copy(frames.at[rows], here.at[rows], sems.at[n])
 
     def outward(h):
-        return pltpu.make_async_copy(made.at[h], out.at[h], out_sems.at[h])
+        return pltpu.make_async_copy(made.at[h], (top, bottom)[h], out_sems.at[h])
 
     head_copy = pltpu.make_async_copy(head, projection, head_sem)
     inward(0).start()
@@ -183,9 +183,9 @@
 def project(frames, projection):
     return pl.pallas_call(
         project_kernel,
-        out_shape=pltpu.HBM((2, HALF, E), BF16),
+        out_shape=[pltpu.HBM((HALF, E), BF16)] * 2,
         in_specs=[IN_HBM, IN_HBM],
-        out_specs=IN_HBM,
+        out_specs=[IN_HBM] * 2,
         scratch_shapes=[
             pltpu.VMEM((ROWS, E), BF16),
             pltpu.VMEM((E, E), BF16),

time: 238 us -> 238 us (level)
    ppermute x7, waiting for transfers between devices: 5.98 us -> 9.66 us  [ring_pieces(): right[i] = lax.ppermute(right[i], axis, up)]
    ppermute x7, starting transfers between devices: 35.5 us -> 38.5 us  [ring_pieces(): left[i] = lax.ppermute(left[i], axis, down)]
    ppermute x7, starting transfers between devices: 16.3 us -> 13.4 us  [ring_pieces(): right[i] = lax.ppermute(right[i], axis, up)]
  transfers between devices with their start and end apart: 17 -> 17, of which waited for: 5 -> 6; matrix products, arithmetic and copies ran while one was open for 4% -> 4% of each run, Pallas kernels for 2% -> 2%
where the time goes in v8:
time: 238 us; the launch traced here: 237 us
  blocking collectives  87.7 us (37%)
  starting transfers between devices  67.3 us (28%)
  Pallas kernels  30.3 us (13%)
  waiting for transfers between devices  26 us (11%)
  between operations  14.5 us (6%)
  other arithmetic  6.05 us (3%)
  local copies, waits for them, and re-layouts  5.18 us (2%)
    all_to_all x8, blocking collectives, swap(): return lax.all_to_all(value, axes, split_axis=0, concat_axis=0, tiled=True)  87.7 us
    ppermute x7, starting transfers between devices, ring_pieces(): left[i] = lax.ppermute(left[i], axis, down)  38.5 us
    all_to_all x2, starting transfers between devices, swap(): return lax.all_to_all(value, axes, split_axis=0, concat_axis=0, tiled=True)  15.3 us
    all_to_all x2, waiting for transfers between devices, swap(): return lax.all_to_all(value, axes, split_axis=0, concat_axis=0, tiled=True)  14 us
    ppermute x7, starting transfers between devices, ring_pieces(): right[i] = lax.ppermute(right[i], axis, up)  13.4 us
    ppermute x7, waiting for transfers between devices, ring_pieces(): right[i] = lax.ppermute(right[i], axis, up)  9.66 us
    pallas_call x1, Pallas kernels, first_pass(): pl.pallas_call(first_kernel, in_specs=[SMEM_WHOLE] * 4 + [VMEM_WHOLE] * 4...  9.46 us
    pallas_call x1, Pallas kernels, second_pass(): pl.pallas_call(second_kernel, in_specs=[SMEM_WHOLE, SMEM_WHOLE, VMEM_WHOL...  4.77 us
  transfers between devices with their start and end apart: 17, of which 6 were waited for; matrix products, arithmetic and copies ran while one was open for 4% of the time, Pallas kernels for 2%

profile of v8, /device:TPU:1, one launch (start us, length us, event | category | flops | bytes accessed | tf_op | source)
XLA Modules:
  0.0 237.0 jit_solution(4244750602230990731)
XLA Ops:
  7.2 3.1 %shard_map.85.codes = bf16[2048,256]{1,0:T(8,128)(2,1)} custom-call(bf16[2048,256]{1,0:T(8,128)(2,1)} %frames.2, bf16[256,256]{1,0:T(8,128)(2,1)} %head.3), custom_call_target="tpu_custom_call" | custom-call | tf_op jit(solution)/shard_map/pallas_call | solution.py:97
  10.3 4.5 %shard_map.86 = (bf16[1040,256]{1,0:T(8,128)(2,1)}, bf16[1040,256]{1,0:T(8,128)(2,1)}) custom-call(bf16[2048,256]{1,0:T(8,128)(2,1)} %frames.3, bf16[256,256]{1,0:T(8,128)(2,1)} %head.3), custom_call_target="tpu_custom_call" | custom-call | tf_op jit(solution)/shard_map/pallas_call | solution.py:184
  14.9 11.5 %collective-permute-start.3 = (bf16[1040,256]{1,0:T(8,128)(2,1)}, bf16[1040,256]{1,0:T(8,128)(2,1)S(1)}, u32[]{:S(2)}, u32[]{:S(2)}) collective-permute-start(bf16[1040,256]{1,0:T(8,128)(2,1)} %get-tuple-element.14.rest_1_), channel_id=1, source_target_pairs={{0,56},{8,0},{16,8},{24,16},{32,24},{40,32},{48,40},{56,48},{1,57}... | collective-permute-start | bytes 1597448 | tf_op jit(solution)/shard_map/ppermute | solution.py:536
  26.4 1.9 collective-permute-start
  28.3 1.9 collective-permute-start.8
  30.2 4.6 %collective-permute-start.2 = (bf16[1040,256]{1,0:T(8,128)(2,1)}, bf16[1040,256]{1,0:T(8,128)(2,1)S(1)}, u32[]{:S(2)}, u32[]{:S(2)}) collective-permute-start(bf16[1040,256]{1,0:T(8,128)(2,1)} %get-tuple-element.17.rest_0_), channel_id=1, source_target_pairs={{0,56},{8,0},{16,8},{24,16},{32,24},{40,32},{48,40},{56,48},{1,57}... | collective-permute-start | bytes 1597448 | tf_op jit(solution)/shard_map/ppermute | solution.py:536
  34.8 0.8 copy.22
  35.7 1.1 gather_fusion
  36.8 0.7 iota_compare_fusion.3
  37.9 0.7 copy.23
  38.7 8.6 %all-to-all-start = ((s32[16,1,8]{2,1,0:T(1,128)}), s32[16,1,8]{2,1,0:T(1,128)S(1)}, u32[]{:S(2)}, u32[]{:S(2)}) async-start(s32[16,1,8]{2,1,0:T(1,128)} %bitcast.3), calls=%async_computation | async-start | bytes 16384 | tf_op jit(solution)/shard_map/all_to_all | solution.py:543
  47.4 6.9 %all-to-all-done = s32[16,1,8]{2,1,0:T(1,128)S(1)} async-done(((s32[16,1,8]{2,1,0:T(1,128)}), s32[16,1,8]{2,1,0:T(1,128)S(1)}, u32[]{:S(2)}, u32[]{:S(2)}) %all-to-all-start) | async-done | bytes 544 | tf_op jit(solution)/shard_map/all_to_all | solution.py:543
  54.4 3.6 %collective-permute-start.5 = (bf16[1040,256]{1,0:T(8,128)(2,1)S(1)}, bf16[1040,256]{1,0:T(8,128)(2,1)}, u32[]{:S(2)}, u32[]{:S(2)}) collective-permute-start(bf16[1040,256]{1,0:T(8,128)(2,1)S(1)} %collective-permute-done.3.rest_3_), channel_id=1, source_target_pairs={{0,56},{8,0},{16,8},{24,16},{32,24},{40,32},{48,40},{56,48},{1,57}... | collective-permute-start | bytes 1597448 | tf_op jit(solution)/shard_map/ppermute | solution.py:536
  58.0 1.9 collective-permute-start.9
  60.1 0.6 select_reduce_fusion.3
  60.9 1.9 collective-permute-start.1
  62.9 4.6 %collective-permute-start.4 = (bf16[1040,256]{1,0:T(8,128)(2,1)S(1)}, bf16[1040,256]{1,0:T(8,128)(2,1)}, u32[]{:S(2)}, u32[]{:S(2)}) collective-permute-start(bf16[1040,256]{1,0:T(8,128)(2,1)S(1)} %collective-permute-done.2.rest_2_), channel_id=1, source_target_pairs={{0,56},{8,0},{16,8},{24,16},{32,24},{40,32},{48,40},{56,48},{1,57}... | collective-permute-start | bytes 1597448 | tf_op jit(solution)/shard_map/ppermute | solution.py:536
  67.5 2.0 collective-permute-done.5.rest_5_
  69.4 4.8 %collective-permute-start.7 = (bf16[1040,256]{1,0:T(8,128)(2,1)}, bf16[1040,256]{1,0:T(8,128)(2,1)}, u32[]{:S(2)}, u32[]{:S(2)}) collective-permute-start(bf16[1040,256]{1,0:T(8,128)(2,1)} %collective-permute-done.5.rest_5_), channel_id=1, source_target_pairs={{0,56},{8,0},{16,8},{24,16},{32,24},{40,32},{48,40},{56,48},{1,57}... | collective-permute-start | bytes 1597448 | tf_op jit(solution)/shard_map/ppermute | solution.py:536
  74.3 1.9 collective-permute-start.10
  76.3 1.3 fusion.9
  77.7 7.7 %collective-permute-done.1.after.rest_13_ = bf16[1040,256]{1,0:T(8,128)(2,1)S(1)} collective-permute-done((bf16[1040,256]{1,0:T(8,128)(2,1)S(1)}, bf16[1040,256]{1,0:T(8,128)(2,1)S(1)}, u32[]{:S(2)}, u32[]{:S(2)}) %collective-permute-start.1) | collective-permute-done | bytes 532512 | tf_op jit(solution)/shard_map/ppermute | solution.py:535
  85.4 1.9 collective-permute-start.13
  87.3 4.6 %collective-permute-start.6 = (bf16[1040,256]{1,0:T(8,128)(2,1)}, bf16[1040,256]{1,0:T(8,128)(2,1)}, u32[]{:S(2)}, u32[]{:S(2)}) collective-permute-start(bf16[1040,256]{1,0:T(8,128)(2,1)} %collective-permute-done.4.rest_4_), channel_id=1, source_target_pairs={{0,56},{8,0},{16,8},{24,16},{32,24},{40,32},{48,40},{56,48},{1,57}... | collective-permute-start | bytes 1597448 | tf_op jit(solution)/shard_map/ppermute | solution.py:536
  91.9 0.3 collective-permute-done.7.rest_7_
  92.2 4.8 %collective-permute-start.12 = (bf16[1040,256]{1,0:T(8,128)(2,1)}, bf16[1040,256]{1,0:T(8,128)(2,1)}, u32[]{:S(2)}, u32[]{:S(2)}) collective-permute-start(bf16[1040,256]{1,0:T(8,128)(2,1)} %collective-permute-done.7.rest_7_), channel_id=1, source_target_pairs={{0,56},{8,0},{16,8},{24,16},{32,24},{40,32},{48,40},{56,48},{1,57}... | collective-permute-start | bytes 1597448 | tf_op jit(solution)/shard_map/ppermute | solution.py:536
  97.1 1.9 collective-permute-start.11
  99.1 1.2 copy-done.1
  100.3 0.7 shard_map.87
  101.0 0.7 broadcast_in_dim.120
  101.6 6.6 %all-to-all-start.1 = ((f32[16,16,128]{2,1,0:T(8,128)}), f32[16,16,128]{2,1,0:T(8,128)S(1)}, u32[]{:S(2)}, u32[]{:S(2)}) async-start(f32[16,16,128]{2,1,0:T(8,128)} %broadcast_in_dim.120), calls=%async_computation.1 | async-start | bytes 262144 | tf_op jit(solution)/shard_map/all_to_all | solution.py:543
  108.3 0.7 pad_add_fusion.count
  109.0 1.3 fusion.11
  110.3 7.1 %all-to-all-done.1.received = f32[16,16,128]{2,1,0:T(8,128)S(1)} async-done(((f32[16,16,128]{2,1,0:T(8,128)}), f32[16,16,128]{2,1,0:T(8,128)S(1)}, u32[]{:S(2)}, u32[]{:S(2)}) %all-to-all-start.1) | async-done | bytes 131104 | tf_op jit(solution)/shard_map/all_to_all | solution.py:543
  117.7 1.9 collective-permute-done.11.rest_8_
  119.7 9.5 %shard_map.89 = (f32[128,128,128]{2,1,0:T(8,128)}, bf16[128,128]{1,0:T(8,128)(2,1)S(1)}) custom-call(s32[2]{0:T(128)S(1)} %pad_add_fusion.count, s32[128]{0:T(128)S(1)} %get-tuple-element.28.place, s32[128]{0:T(128)S(1)} %fusion.7.col_at, s32[128]{0:T(128)S(1)} %get-tuple-element.27.row_at, s32[1,128]{1,0:T(1,128)S(1)} %get-tuple-element.31.col_place, ...), custom_call_target="tpu_custom_call" | custom-call | tf_op jit(solution)/shard_map/pallas_call | solution.py:323
  129.1 8.7 %all_to_all.50 = bf16[4,128,128]{2,1,0:T(8,128)(2,1)S(1)} all-to-all(bf16[4,128,128]{2,1,0:T(8,128)(2,1)S(1)} %broadcast_in_dim.121), channel_id=1, replica_groups=mesh['y'=8,'z'=8,'c'=2,'x'=4] {'x'}, dimensions={0} | all-to-all | bytes 262144 | tf_op jit(solution)/shard_map/all_to_all | solution.py:543
  137.9 17.0 %all_to_all.51.received = bf16[8,128,128]{2,1,0:T(8,128)(2,1)S(1)} all-to-all(bf16[8,128,128]{2,1,0:T(8,128)(2,1)S(1)} %broadcast_in_dim.122), channel_id=1, replica_groups=mesh['y'=8,'z'=8,'c'=2,'x'=4] {'z'}, dimensions={0} | all-to-all | bytes 524288 | tf_op jit(solution)/shard_map/all_to_all | solution.py:543
  154.9 4.8 %shard_map.90 = (bf16[128,256,128]{2,1,0:T(8,128)(2,1)}, bf16[256,128]{1,0:T(8,128)(2,1)S(1)}, f32[128,128]{1,0:T(8,128)S(1)}) custom-call(s32[2]{0:T(128)S(1)} %pad_add_fusion.count, s32[128]{0:T(128)S(1)} %fusion.7.col_at, s32[1,128]{1,0:T(1,128)S(1)} %get-tuple-element.32.row_place, bf16[8,128,128]{2,1,0:T(8,128)(2,1)S(1)} %all_to_all.51.received, ...), custom_call_target="tpu_custom_call" | custom-call | tf_op jit(solution)/shard_map/pallas_call | solution.py:405
  159.7 4.8 %all_to_all.52 = bf16[2,128,128]{2,1,0:T(8,128)(2,1)S(1)} all-to-all(bf16[2,128,128]{2,1,0:T(8,128)(2,1)S(1)} %bitcast.24), channel_id=1, replica_groups=mesh['y'=8,'z'=8,'c'=2,'x'=4] {'c'}, dimensions={0} | all-to-all | bytes 131072 | tf_op jit(solution)/shard_map/all_to_all | solution.py:543
  164.5 15.8 %all_to_all.53 = bf16[8,128,128]{2,1,0:T(8,128)(2,1)S(1)} all-to-all(bf16[8,128,128]{2,1,0:T(8,128)(2,1)S(1)} %broadcast_in_dim.123), channel_id=1, replica_groups=mesh['y'=8,'z'=8,'c'=2,'x'=4] {'y'}, dimensions={0} | all-to-all | bytes 524288 | tf_op jit(solution)/shard_map/all_to_all | solution.py:543
  180.4 5.1 %all_to_all.54 = bf16[2,128,128]{2,1,0:T(8,128)(2,1)S(1)} all-to-all(bf16[2,128,128]{2,1,0:T(8,128)(2,1)S(1)} %broadcast_in_dim.124), channel_id=1, replica_groups=mesh['y'=8,'z'=8,'c'=2,'x'=4] {'c'}, dimensions={0} | all-to-all | bytes 131072 | tf_op jit(solution)/shard_map/all_to_all | solution.py:543
  185.5 3.2 %shard_map.91 = bf16[128,128]{1,0:T(8,128)(2,1)S(1)} custom-call(s32[2]{0:T(128)S(1)} %pad_add_fusion.count, s32[128]{0:T(128)S(1)} %get-tuple-element.27.row_at, s32[1,128]{1,0:T(1,128)S(1)} %get-tuple-element.31.col_place, bf16[256,128]{1,0:T(8,128)(2,1)S(1)} %bitcast.23, bf16[128,256,128]{2,1,0:T(8,128)(2,1)} %get-tuple-element.21.kernel), custom_call_target="tpu_custom_call" | custom-call | tf_op jit(solution)/shard_map/pallas_call | solution.py:455
  188.7 7.2 %all_to_all.55 = bf16[4,128,128]{2,1,0:T(8,128)(2,1)S(1)} all-to-all(bf16[4,128,128]{2,1,0:T(8,128)(2,1)S(1)} %broadcast_in_dim.125), channel_id=1, replica_groups=mesh['y'=8,'z'=8,'c'=2,'x'=4] {'x'}, dimensions={0} | all-to-all | bytes 262144 | tf_op jit(solution)/shard_map/all_to_all | solution.py:543
  196.0 12.2 %all_to_all.56.received = bf16[8,128,128]{2,1,0:T(8,128)(2,1)S(1)} all-to-all(bf16[8,128,128]{2,1,0:T(8,128)(2,1)S(1)} %broadcast_in_dim.126), channel_id=1, replica_groups=mesh['y'=8,'z'=8,'c'=2,'x'=4] {'z'}, dimensions={0} | all-to-all | bytes 524288 | tf_op jit(solution)/shard_map/all_to_all | solution.py:543
  208.2 4.4 %shard_map.92 = (f32[16,32,128]{2,1,0:T(8,128)S(1)}, f32[16,128]{1,0:T(8,128)}) custom-call(s32[2]{0:T(128)S(1)} %pad_add_fusion.count, s32[128]{0:T(128)S(1)} %fusion.7.col_at, s32[1,128]{1,0:T(1,128)S(1)} %get-tuple-element.32.row_place, bf16[8,128,128]{2,1,0:T(8,128)(2,1)S(1)} %all_to_all.56.received, f32[128,128]{1,0:T(8,128)S(1)} %get-tuple-element.22.column_sum, ...), custom_call_target="tpu_custom_call" | custom-call | tf_op jit(solution)/shard_map/pallas_call | solution.py:508
  212.6 16.9 %all_to_all.57 = f32[16,32,128]{2,1,0:T(8,128)S(1)} all-to-all(f32[16,32,128]{2,1,0:T(8,128)S(1)} %get-tuple-element.23), channel_id=1, replica_groups=mesh['y'=8,'z'=8,'c'=2,'x'=4] {'y','c'}, dimensions={0} | all-to-all | bytes 524288 | tf_op jit(solution)/shard_map/all_to_all | solution.py:543
  229.5 0.6 multiply_bitcast_fusion
  (55 shorter events, 1.6 us)
Async XLA Ops:
  7.2 28.5 %copy-start = (s32[2048]{0:T(1024)S(1)}, s32[2048]{0:T(1024)}, u32[]{:S(2)}) copy-start(s32[2048]{0:T(1024)} %param.9) | copy-start | bytes 24580
  7.2 112.4 %all-gather.3.cloned.1.call-start = ((), (), s32[]{:S(2)}) async-start(), calls=%async_computation.10 | async-start | bytes 17825792 | tf_op jit(solution)/shard_map/all_gather | solution.py:585
  14.9 39.5 %collective-permute-start.3 = (bf16[1040,256]{1,0:T(8,128)(2,1)}, bf16[1040,256]{1,0:T(8,128)(2,1)S(1)}, u32[]{:S(2)}, u32[]{:S(2)}) collective-permute-start(bf16[1040,256]{1,0:T(8,128)(2,1)} %get-tuple-element.14.rest_1_), channel_id=1, source_target_pairs={{0,56},{8,0},{16,8},{24,16},{32,24},{40,32},{48,40},{56,48},{1,57}... | collective-permute-start | bytes 1597448 | tf_op jit(solution)/shard_map/ppermute | solution.py:536
  26.4 34.5 %collective-permute-start = (bf16[1040,256]{1,0:T(8,128)(2,1)}, bf16[1040,256]{1,0:T(8,128)(2,1)S(1)}, u32[]{:S(2)}, u32[]{:S(2)}) collective-permute-start(bf16[1040,256]{1,0:T(8,128)(2,1)} %get-tuple-element.14.rest_1_), channel_id=1, source_target_pairs={{0,8},{8,16},{16,24},{24,32},{32,40},{40,48},{48,56},{56,0},{1,9},... | collective-permute-start | bytes 1597448 | tf_op jit(solution)/shard_map/ppermute | solution.py:535
  28.3 29.7 %collective-permute-start.8 = (bf16[1040,256]{1,0:T(8,128)(2,1)}, bf16[1040,256]{1,0:T(8,128)(2,1)S(1)}, u32[]{:S(2)}, u32[]{:S(2)}) collective-permute-start(bf16[1040,256]{1,0:T(8,128)(2,1)} %get-tuple-element.17.rest_0_), channel_id=1, source_target_pairs={{0,8},{8,16},{16,24},{24,32},{32,40},{40,48},{48,56},{56,0},{1,9},... | collective-permute-start | bytes 1597448 | tf_op jit(solution)/shard_map/ppermute | solution.py:535
  30.2 32.6 %collective-permute-start.2 = (bf16[1040,256]{1,0:T(8,128)(2,1)}, bf16[1040,256]{1,0:T(8,128)(2,1)S(1)}, u32[]{:S(2)}, u32[]{:S(2)}) collective-permute-start(bf16[1040,256]{1,0:T(8,128)(2,1)} %get-tuple-element.17.rest_0_), channel_id=1, source_target_pairs={{0,56},{8,0},{16,8},{24,16},{32,24},{40,32},{48,40},{56,48},{1,57}... | collective-permute-start | bytes 1597448 | tf_op jit(solution)/shard_map/ppermute | solution.py:536
  38.7 15.6 %all-to-all-start = ((s32[16,1,8]{2,1,0:T(1,128)}), s32[16,1,8]{2,1,0:T(1,128)S(1)}, u32[]{:S(2)}, u32[]{:S(2)}) async-start(s32[16,1,8]{2,1,0:T(1,128)} %bitcast.3), calls=%async_computation | async-start | bytes 16384 | tf_op jit(solution)/shard_map/all_to_all | solution.py:543
  54.4 65.3 %copy-start.3 = (bf16[1040,256]{1,0:T(8,128)(2,1)}, bf16[1040,256]{1,0:T(8,128)(2,1)S(1)}, u32[]{:S(2)}) copy-start(bf16[1040,256]{1,0:T(8,128)(2,1)S(1)} %collective-permute-done.3.rest_3_) | copy-start | bytes 1597444
  54.4 15.0 %collective-permute-start.5 = (bf16[1040,256]{1,0:T(8,128)(2,1)S(1)}, bf16[1040,256]{1,0:T(8,128)(2,1)}, u32[]{:S(2)}, u32[]{:S(2)}) collective-permute-start(bf16[1040,256]{1,0:T(8,128)(2,1)S(1)} %collective-permute-done.3.rest_3_), channel_id=1, source_target_pairs={{0,56},{8,0},{16,8},{24,16},{32,24},{40,32},{48,40},{56,48},{1,57}... | collective-permute-start | bytes 1597448 | tf_op jit(solution)/shard_map/ppermute | solution.py:536
  58.0 61.6 %copy-start.5 = (bf16[1040,256]{1,0:T(8,128)(2,1)}, bf16[1040,256]{1,0:T(8,128)(2,1)S(1)}, u32[]{:S(2)}) copy-start(bf16[1040,256]{1,0:T(8,128)(2,1)S(1)} %collective-permute-done.8.rest_14_) | copy-start | bytes 1597444
  58.0 16.2 %collective-permute-start.9 = (bf16[1040,256]{1,0:T(8,128)(2,1)S(1)}, bf16[1040,256]{1,0:T(8,128)(2,1)}, u32[]{:S(2)}, u32[]{:S(2)}) collective-permute-start(bf16[1040,256]{1,0:T(8,128)(2,1)S(1)} %collective-permute-done.8.rest_14_), channel_id=1, source_target_pairs={{0,8},{8,16},{16,24},{24,32},{32,40},{40,48},{48,56},{56,0},{1,9},... | collective-permute-start | bytes 1597448 | tf_op jit(solution)/shard_map/ppermute | solution.py:535
  60.9 58.7 %copy-start.4 = (bf16[1040,256]{1,0:T(8,128)(2,1)}, bf16[1040,256]{1,0:T(8,128)(2,1)S(1)}, u32[]{:S(2)}) copy-start(bf16[1040,256]{1,0:T(8,128)(2,1)S(1)} %collective-permute-done.rest_15_) | copy-start | bytes 1597444
  60.9 24.5 %collective-permute-start.1 = (bf16[1040,256]{1,0:T(8,128)(2,1)S(1)}, bf16[1040,256]{1,0:T(8,128)(2,1)S(1)}, u32[]{:S(2)}, u32[]{:S(2)}) collective-permute-start(bf16[1040,256]{1,0:T(8,128)(2,1)S(1)} %collective-permute-done.rest_15_), channel_id=1, source_target_pairs={{0,8},{8,16},{16,24},{24,32},{32,40},{40,48},{48,56},{56,0},{1,9},... | collective-permute-start | bytes 1597448 | tf_op jit(solution)/shard_map/ppermute | solution.py:535
  62.9 38.8 %copy-start.6 = (bf16[1040,256]{1,0:T(8,128)(2,1)}, bf16[1040,256]{1,0:T(8,128)(2,1)S(1)}, u32[]{:S(2)}) copy-start(bf16[1040,256]{1,0:T(8,128)(2,1)S(1)} %collective-permute-done.2.rest_2_) | copy-start | bytes 1597444
  62.9 24.4 %collective-permute-start.4 = (bf16[1040,256]{1,0:T(8,128)(2,1)S(1)}, bf16[1040,256]{1,0:T(8,128)(2,1)}, u32[]{:S(2)}, u32[]{:S(2)}) collective-permute-start(bf16[1040,256]{1,0:T(8,128)(2,1)S(1)} %collective-permute-done.2.rest_2_), channel_id=1, source_target_pairs={{0,56},{8,0},{16,8},{24,16},{32,24},{40,32},{48,40},{56,48},{1,57}... | collective-permute-start | bytes 1597448 | tf_op jit(solution)/shard_map/ppermute | solution.py:536
  69.4 22.8 %collective-permute-start.7 = (bf16[1040,256]{1,0:T(8,128)(2,1)}, bf16[1040,256]{1,0:T(8,128)(2,1)}, u32[]{:S(2)}, u32[]{:S(2)}) collective-permute-start(bf16[1040,256]{1,0:T(8,128)(2,1)} %collective-permute-done.5.rest_5_), channel_id=1, source_target_pairs={{0,56},{8,0},{16,8},{24,16},{32,24},{40,32},{48,40},{56,48},{1,57}... | collective-permute-start | bytes 1597448 | tf_op jit(solution)/shard_map/ppermute | solution.py:536
  74.3 22.8 %collective-permute-start.10 = (bf16[1040,256]{1,0:T(8,128)(2,1)}, bf16[1040,256]{1,0:T(8,128)(2,1)}, u32[]{:S(2)}, u32[]{:S(2)}) collective-permute-start(bf16[1040,256]{1,0:T(8,128)(2,1)} %collective-permute-done.9.rest_12_), channel_id=1, source_target_pairs={{0,8},{8,16},{16,24},{24,32},{32,40},{40,48},{48,56},{56,0},{1,9},... | collective-permute-start | bytes 1597448 | tf_op jit(solution)/shard_map/ppermute | solution.py:535
  85.4 34.2 %copy-start.2 = (bf16[1040,256]{1,0:T(8,128)(2,1)}, bf16[1040,256]{1,0:T(8,128)(2,1)S(1)}, u32[]{:S(2)}) copy-start(bf16[1040,256]{1,0:T(8,128)(2,1)S(1)} %collective-permute-done.1.after.rest_13_) | copy-start | bytes 1597444
  85.4 32.3 %collective-permute-start.13 = (bf16[1040,256]{1,0:T(8,128)(2,1)S(1)}, bf16[1040,256]{1,0:T(8,128)(2,1)}, u32[]{:S(2)}, u32[]{:S(2)}) collective-permute-start(bf16[1040,256]{1,0:T(8,128)(2,1)S(1)} %collective-permute-done.1.after.rest_13_), channel_id=1, source_target_pairs={{0,8},{8,16},{16,24},{24,32},{32,40},{40,48},{48,56},{56,0},{1,9},... | collective-permute-start | bytes 1597448 | tf_op jit(solution)/shard_map/ppermute | solution.py:535
  87.3 30.4 %collective-permute-start.6 = (bf16[1040,256]{1,0:T(8,128)(2,1)}, bf16[1040,256]{1,0:T(8,128)(2,1)}, u32[]{:S(2)}, u32[]{:S(2)}) collective-permute-start(bf16[1040,256]{1,0:T(8,128)(2,1)} %collective-permute-done.4.rest_4_), channel_id=1, source_target_pairs={{0,56},{8,0},{16,8},{24,16},{32,24},{40,32},{48,40},{56,48},{1,57}... | collective-permute-start | bytes 1597448 | tf_op jit(solution)/shard_map/ppermute | solution.py:536
  92.2 25.5 %collective-permute-start.12 = (bf16[1040,256]{1,0:T(8,128)(2,1)}, bf16[1040,256]{1,0:T(8,128)(2,1)}, u32[]{:S(2)}, u32[]{:S(2)}) collective-permute-start(bf16[1040,256]{1,0:T(8,128)(2,1)} %collective-permute-done.7.rest_7_), channel_id=1, source_target_pairs={{0,56},{8,0},{16,8},{24,16},{32,24},{40,32},{48,40},{56,48},{1,57}... | collective-permute-start | bytes 1597448 | tf_op jit(solution)/shard_map/ppermute | solution.py:536
  97.1 22.5 %collective-permute-start.11 = (bf16[1040,256]{1,0:T(8,128)(2,1)}, bf16[1040,256]{1,0:T(8,128)(2,1)}, u32[]{:S(2)}, u32[]{:S(2)}) collective-permute-start(bf16[1040,256]{1,0:T(8,128)(2,1)} %collective-permute-done.10.rest_10_), channel_id=1, source_target_pairs={{0,8},{8,16},{16,24},{24,32},{32,40},{40,48},{48,56},{56,0},{1,9},... | collective-permute-start | bytes 1597448 | tf_op jit(solution)/shard_map/ppermute | solution.py:535
  99.1 1.2 copy-start.1
  101.6 15.8 %all-to-all-start.1 = ((f32[16,16,128]{2,1,0:T(8,128)}), f32[16,16,128]{2,1,0:T(8,128)S(1)}, u32[]{:S(2)}, u32[]{:S(2)}) async-start(f32[16,16,128]{2,1,0:T(8,128)} %broadcast_in_dim.120), calls=%async_computation.1 | async-start | bytes 262144 | tf_op jit(solution)/shard_map/all_to_all | solution.py:543
Sparse Core Ops, SparseCore 0:
  10.4 103.8 all-gather.2

commit v9 on v8

--- a/solution.py
+++ b/solution.py
@@ -1,3 +1,4 @@
+import functools
 import math
 
 import jax
@@ -149,54 +150,54 @@
     )(received)
 
 
-def project_kernel(frames, head, top, bottom, here, projection, made, norms, sems, head_sem, out_sems):
+def project_kernel(h, frames, head, out, here, projection, made, norms, sems, head_sem, out_sem):
     def inward(n):
         rows = pl.ds(n * PART, PART)
-        return pltpu.make_async_copy(frames.at[rows], here.at[rows], sems.at[n])
-
-    def outward(h):
-        return pltpu.make_async_copy(made.at[h], (top, bottom)[h], out_sems.at[h])
+        return pltpu.make_async_copy(
+            frames.at[pl.ds(h * HB * BLK + n * PART, PART)], here.at[rows], sems.at[n]
+        )
 
     head_copy = pltpu.make_async_copy(head, projection, head_sem)
     inward(0).start()
     head_copy.start()
-    for n in range(1, ROWS // PART):
+    for n in range(1, HB * BLK // PART):
         inward(n).start()
     head_copy.wait()
-    for h in range(2):
-        for j in range(HB):
-            k = h * HB + j
-            if k * BLK % PART == 0:
-                inward(k * BLK // PART).wait()
-            codes = dot(here[pl.ds(k * BLK, BLK), :], projection[...], NN).astype(BF16)
-            made[h, pl.ds(j * BLK, BLK), :] = codes
-            norms[j : j + 1, :] = norms_of(codes)
-        high, middle, low = three_parts(norms[...])
-        left = jnp.concatenate([high, low], axis=0)
-        right = jnp.concatenate([middle, jnp.zeros_like(low)], axis=0)
-        made[h, HB * BLK : HALF, :] = jnp.concatenate([left, right], axis=1).astype(BF16)
-        outward(h).start()
-    for h in range(2):
-        outward(h).wait()
+    for j in range(HB):
+        if j * BLK % PART == 0:
+            inward(j * BLK // PART).wait()
+        codes = dot(here[pl.ds(j * BLK, BLK), :], projection[...], NN).astype(BF16)
+        made[pl.ds(j * BLK, BLK), :] = codes
+        norms[j : j + 1, :] = norms_of(codes)
+    high, middle, low = three_parts(norms[...])
+    left = jnp.concatenate([high, low], axis=0)
+    right = jnp.concatenate([middle, jnp.zeros_like(low)], axis=0)
+    made[HB * BLK : HALF, :] = jnp.concatenate([left, right], axis=1).astype(BF16)
+    outward = pltpu.make_async_copy(made, out, out_sem)
+    outward.start()
+    outward.wait()
 
 
 def project(frames, projection):
-    return pl.pallas_call(
-        project_kernel,
-        out_shape=[pltpu.HBM((HALF, E), BF16)] * 2,
-        in_specs=[IN_HBM, IN_HBM],
-        out_specs=[IN_HBM] * 2,
-        scratch_shapes=[
-            pltpu.VMEM((ROWS, E), BF16),
-            pltpu.VMEM((E, E), BF16),
-            pltpu.VMEM((2, HALF, E), BF16),
-            pltpu.VMEM((HB, BLK), F32),
-            pltpu.SemaphoreType.DMA((ROWS // PART,)),
-            pltpu.SemaphoreType.DMA,
-            pltpu.SemaphoreType.DMA((2,)),
-        ],
-        compiler_params=pltpu.CompilerParams(vmem_limit_bytes=GRANT),
-    )(in_hbm(frames), in_hbm(projection))
+    return [
+        pl.pallas_call(
+            functools.partial(project_kernel, h),
+            out_shape=pltpu.HBM((HALF, E), BF16),
+            in_specs=[IN_HBM, IN_HBM],
+            out_specs=IN_HBM,
+            scratch_shapes=[
+                pltpu.VMEM((HB * BLK, E), BF16),
+                pltpu.VMEM((E, E), BF16),
+                pltpu.VMEM((HALF, E), BF16),
+                pltpu.VMEM((HB, BLK), F32),
+                pltpu.SemaphoreType.DMA((HB * BLK // PART,)),
+                pltpu.SemaphoreType.DMA,
+                pltpu.SemaphoreType.DMA,
+            ],
+            compiler_params=pltpu.CompilerParams(vmem_limit_bytes=GRANT),
+        )(in_hbm(frames), in_hbm(projection))
+        for h in range(2)
+    ]
 
 
 def in_hbm(value):

time: 238 us -> 238 us (level)
    pallas_call x1 -> x2, Pallas kernels: 4.53 us -> 6.21 us  [project(): pl.pallas_call(functools.partial(project_kernel, h), out_shape=pltpu.HBM(...]
  transfers between devices with their start and end apart: 17 -> 17, of which waited for: 6 -> 6; matrix products, arithmetic and copies ran while one was open for 4% -> 4% of each run, Pallas kernels for 2% -> 3%
where the time goes in v9:
time: 238 us; the launch traced here: 236 us
  blocking collectives  86.8 us (36%)
  starting transfers between devices  66.8 us (28%)
  Pallas kernels  29.9 us (13%)
  waiting for transfers between devices  26.5 us (11%)
  between operations  14.5 us (6%)
  other arithmetic  6.04 us (3%)
  local copies, waits for them, and re-layouts  5.18 us (2%)
    all_to_all x8, blocking collectives, swap(): return lax.all_to_all(value, axes, split_axis=0, concat_axis=0, tiled=True)  86.8 us
    ppermute x7, starting transfers between devices, ring_pieces(): left[i] = lax.ppermute(left[i], axis, down)  38.5 us
    all_to_all x2, starting transfers between devices, swap(): return lax.all_to_all(value, axes, split_axis=0, concat_axis=0, tiled=True)  14.8 us
    all_to_all x2, waiting for transfers between devices, swap(): return lax.all_to_all(value, axes, split_axis=0, concat_axis=0, tiled=True)  14.1 us
    ppermute x7, starting transfers between devices, ring_pieces(): right[i] = lax.ppermute(right[i], axis, up)  13.4 us
    ppermute x7, waiting for transfers between devices, ring_pieces(): right[i] = lax.ppermute(right[i], axis, up)  10.1 us
    pallas_call x1, Pallas kernels, first_pass(): pl.pallas_call(first_kernel, in_specs=[SMEM_WHOLE] * 4 + [VMEM_WHOLE] * 4...  8.44 us
    pallas_call x2, Pallas kernels, project(): pl.pallas_call(functools.partial(project_kernel, h), out_shape=pltpu.HBM(...  6.21 us
  transfers between devices with their start and end apart: 17, of which 6 were waited for; matrix products, arithmetic and copies ran while one was open for 4% of the time, Pallas kernels for 3%

profile of v9, /device:TPU:1, one launch (start us, length us, event | category | flops | bytes accessed | tf_op | source)
XLA Modules:
  0.0 235.8 jit_solution(11409896747564459101)
XLA Ops:
  7.2 3.1 %shard_map.85.codes = bf16[2048,256]{1,0:T(8,128)(2,1)} custom-call(bf16[2048,256]{1,0:T(8,128)(2,1)} %frames.3, bf16[256,256]{1,0:T(8,128)(2,1)} %head.5), custom_call_target="tpu_custom_call" | custom-call | tf_op jit(solution)/shard_map/pallas_call | solution.py:98
  10.3 3.1 %shard_map.86.rest_1_ = bf16[1040,256]{1,0:T(8,128)(2,1)} custom-call(bf16[2048,256]{1,0:T(8,128)(2,1)} %frames.5, bf16[256,256]{1,0:T(8,128)(2,1)} %head.5), custom_call_target="tpu_custom_call" | custom-call | tf_op jit(solution)/shard_map/pallas_call | solution.py:183
  13.4 11.5 %collective-permute-start.3 = (bf16[1040,256]{1,0:T(8,128)(2,1)}, bf16[1040,256]{1,0:T(8,128)(2,1)S(1)}, u32[]{:S(2)}, u32[]{:S(2)}) collective-permute-start(bf16[1040,256]{1,0:T(8,128)(2,1)} %shard_map.86.rest_1_), channel_id=1, source_target_pairs={{0,56},{8,0},{16,8},{24,16},{32,24},{40,32},{48,40},{56,48},{1,57}... | collective-permute-start | bytes 1597448 | tf_op jit(solution)/shard_map/ppermute | solution.py:537
  24.9 1.9 collective-permute-start
  26.9 3.1 %shard_map.89.rest_0_ = bf16[1040,256]{1,0:T(8,128)(2,1)} custom-call(bf16[2048,256]{1,0:T(8,128)(2,1)} %frames.5, bf16[256,256]{1,0:T(8,128)(2,1)} %head.5), custom_call_target="tpu_custom_call" | custom-call | tf_op jit(solution)/shard_map/pallas_call | solution.py:183
  30.0 1.9 collective-permute-start.8
  31.9 4.6 %collective-permute-start.2 = (bf16[1040,256]{1,0:T(8,128)(2,1)}, bf16[1040,256]{1,0:T(8,128)(2,1)S(1)}, u32[]{:S(2)}, u32[]{:S(2)}) collective-permute-start(bf16[1040,256]{1,0:T(8,128)(2,1)} %shard_map.89.rest_0_), channel_id=1, source_target_pairs={{0,56},{8,0},{16,8},{24,16},{32,24},{40,32},{48,40},{56,48},{1,57}... | collective-permute-start | bytes 1597448 | tf_op jit(solution)/shard_map/ppermute | solution.py:537
  36.5 0.8 copy.22
  37.4 1.1 gather_fusion
  38.5 0.7 iota_compare_fusion.3
  39.6 0.7 copy.23
  40.4 8.6 %all-to-all-start = ((s32[16,1,8]{2,1,0:T(1,128)}), s32[16,1,8]{2,1,0:T(1,128)S(1)}, u32[]{:S(2)}, u32[]{:S(2)}) async-start(s32[16,1,8]{2,1,0:T(1,128)} %bitcast.3), calls=%async_computation | async-start | bytes 16384 | tf_op jit(solution)/shard_map/all_to_all | solution.py:544
  49.1 6.9 %all-to-all-done = s32[16,1,8]{2,1,0:T(1,128)S(1)} async-done(((s32[16,1,8]{2,1,0:T(1,128)}), s32[16,1,8]{2,1,0:T(1,128)S(1)}, u32[]{:S(2)}, u32[]{:S(2)}) %all-to-all-start) | async-done | bytes 544 | tf_op jit(solution)/shard_map/all_to_all | solution.py:544
  56.1 3.6 %collective-permute-start.5 = (bf16[1040,256]{1,0:T(8,128)(2,1)S(1)}, bf16[1040,256]{1,0:T(8,128)(2,1)}, u32[]{:S(2)}, u32[]{:S(2)}) collective-permute-start(bf16[1040,256]{1,0:T(8,128)(2,1)S(1)} %collective-permute-done.3.rest_3_), channel_id=1, source_target_pairs={{0,56},{8,0},{16,8},{24,16},{32,24},{40,32},{48,40},{56,48},{1,57}... | collective-permute-start | bytes 1597448 | tf_op jit(solution)/shard_map/ppermute | solution.py:537
  59.7 1.9 collective-permute-start.9
  61.8 0.6 select_reduce_fusion.3
  62.6 1.9 collective-permute-start.1
  64.6 4.6 %collective-permute-start.4 = (bf16[1040,256]{1,0:T(8,128)(2,1)S(1)}, bf16[1040,256]{1,0:T(8,128)(2,1)}, u32[]{:S(2)}, u32[]{:S(2)}) collective-permute-start(bf16[1040,256]{1,0:T(8,128)(2,1)S(1)} %collective-permute-done.2.rest_2_), channel_id=1, source_target_pairs={{0,56},{8,0},{16,8},{24,16},{32,24},{40,32},{48,40},{56,48},{1,57}... | collective-permute-start | bytes 1597448 | tf_op jit(solution)/shard_map/ppermute | solution.py:537
  69.2 2.0 collective-permute-done.5.rest_5_
  71.1 4.8 %collective-permute-start.7 = (bf16[1040,256]{1,0:T(8,128)(2,1)}, bf16[1040,256]{1,0:T(8,128)(2,1)}, u32[]{:S(2)}, u32[]{:S(2)}) collective-permute-start(bf16[1040,256]{1,0:T(8,128)(2,1)} %collective-permute-done.5.rest_5_), channel_id=1, source_target_pairs={{0,56},{8,0},{16,8},{24,16},{32,24},{40,32},{48,40},{56,48},{1,57}... | collective-permute-start | bytes 1597448 | tf_op jit(solution)/shard_map/ppermute | solution.py:537
  76.0 1.9 collective-permute-start.10
  78.0 1.3 fusion.9
  79.4 7.7 %collective-permute-done.1.after.rest_13_ = bf16[1040,256]{1,0:T(8,128)(2,1)S(1)} collective-permute-done((bf16[1040,256]{1,0:T(8,128)(2,1)S(1)}, bf16[1040,256]{1,0:T(8,128)(2,1)S(1)}, u32[]{:S(2)}, u32[]{:S(2)}) %collective-permute-start.1) | collective-permute-done | bytes 532512 | tf_op jit(solution)/shard_map/ppermute | solution.py:536
  87.1 1.9 collective-permute-start.13
  89.0 4.6 %collective-permute-start.6 = (bf16[1040,256]{1,0:T(8,128)(2,1)}, bf16[1040,256]{1,0:T(8,128)(2,1)}, u32[]{:S(2)}, u32[]{:S(2)}) collective-permute-start(bf16[1040,256]{1,0:T(8,128)(2,1)} %collective-permute-done.4.rest_4_), channel_id=1, source_target_pairs={{0,56},{8,0},{16,8},{24,16},{32,24},{40,32},{48,40},{56,48},{1,57}... | collective-permute-start | bytes 1597448 | tf_op jit(solution)/shard_map/ppermute | solution.py:537
  93.9 4.8 %collective-permute-start.12 = (bf16[1040,256]{1,0:T(8,128)(2,1)}, bf16[1040,256]{1,0:T(8,128)(2,1)}, u32[]{:S(2)}, u32[]{:S(2)}) collective-permute-start(bf16[1040,256]{1,0:T(8,128)(2,1)} %collective-permute-done.7.rest_7_), channel_id=1, source_target_pairs={{0,56},{8,0},{16,8},{24,16},{32,24},{40,32},{48,40},{56,48},{1,57}... | collective-permute-start | bytes 1597448 | tf_op jit(solution)/shard_map/ppermute | solution.py:537
  98.8 1.9 collective-permute-start.11
  100.8 1.2 copy-done.1
  102.0 0.7 shard_map.87
  102.6 0.7 broadcast_in_dim.120
  103.3 6.2 %all-to-all-start.1 = ((f32[16,16,128]{2,1,0:T(8,128)}), f32[16,16,128]{2,1,0:T(8,128)S(1)}, u32[]{:S(2)}, u32[]{:S(2)}) async-start(f32[16,16,128]{2,1,0:T(8,128)} %broadcast_in_dim.120), calls=%async_computation.1 | async-start | bytes 262144 | tf_op jit(solution)/shard_map/all_to_all | solution.py:544
  109.5 0.7 pad_add_fusion.count
  110.2 1.3 fusion.11
  111.5 7.2 %all-to-all-done.1.received = f32[16,16,128]{2,1,0:T(8,128)S(1)} async-done(((f32[16,16,128]{2,1,0:T(8,128)}), f32[16,16,128]{2,1,0:T(8,128)S(1)}, u32[]{:S(2)}, u32[]{:S(2)}) %all-to-all-start.1) | async-done | bytes 131104 | tf_op jit(solution)/shard_map/all_to_all | solution.py:544
  118.9 2.4 %collective-permute-done.11.rest_8_ = bf16[1040,256]{1,0:T(8,128)(2,1)} collective-permute-done((bf16[1040,256]{1,0:T(8,128)(2,1)}, bf16[1040,256]{1,0:T(8,128)(2,1)}, u32[]{:S(2)}, u32[]{:S(2)}) %collective-permute-start.11) | collective-permute-done | bytes 532512 | tf_op jit(solution)/shard_map/ppermute | solution.py:536
  121.3 8.4 %shard_map.90 = (f32[128,128,128]{2,1,0:T(8,128)}, bf16[128,128]{1,0:T(8,128)(2,1)S(1)}) custom-call(s32[2]{0:T(128)S(1)} %pad_add_fusion.count, s32[128]{0:T(128)S(1)} %get-tuple-element.24.place, s32[128]{0:T(128)S(1)} %fusion.7.col_at, s32[128]{0:T(128)S(1)} %get-tuple-element.23.row_at, s32[1,128]{1,0:T(1,128)S(1)} %get-tuple-element.27.col_place, ...), custom_call_target="tpu_custom_call" | custom-call | tf_op jit(solution)/shard_map/pallas_call | solution.py:324
  129.8 9.7 %all_to_all.50 = bf16[4,128,128]{2,1,0:T(8,128)(2,1)S(1)} all-to-all(bf16[4,128,128]{2,1,0:T(8,128)(2,1)S(1)} %broadcast_in_dim.121), channel_id=1, replica_groups=mesh['y'=8,'z'=8,'c'=2,'x'=4] {'x'}, dimensions={0} | all-to-all | bytes 262144 | tf_op jit(solution)/shard_map/all_to_all | solution.py:544
  139.6 12.2 %all_to_all.51.received = bf16[8,128,128]{2,1,0:T(8,128)(2,1)S(1)} all-to-all(bf16[8,128,128]{2,1,0:T(8,128)(2,1)S(1)} %broadcast_in_dim.122), channel_id=1, replica_groups=mesh['y'=8,'z'=8,'c'=2,'x'=4] {'z'}, dimensions={0} | all-to-all | bytes 524288 | tf_op jit(solution)/shard_map/all_to_all | solution.py:544
  151.7 4.4 %shard_map.91 = (bf16[128,256,128]{2,1,0:T(8,128)(2,1)}, bf16[256,128]{1,0:T(8,128)(2,1)S(1)}, f32[128,128]{1,0:T(8,128)S(1)}) custom-call(s32[2]{0:T(128)S(1)} %pad_add_fusion.count, s32[128]{0:T(128)S(1)} %fusion.7.col_at, s32[1,128]{1,0:T(1,128)S(1)} %get-tuple-element.28.row_place, bf16[8,128,128]{2,1,0:T(8,128)(2,1)S(1)} %all_to_all.51.received, ...), custom_call_target="tpu_custom_call" | custom-call | tf_op jit(solution)/shard_map/pallas_call | solution.py:406
  156.1 8.2 %all_to_all.52 = bf16[2,128,128]{2,1,0:T(8,128)(2,1)S(1)} all-to-all(bf16[2,128,128]{2,1,0:T(8,128)(2,1)S(1)} %bitcast.24), channel_id=1, replica_groups=mesh['y'=8,'z'=8,'c'=2,'x'=4] {'c'}, dimensions={0} | all-to-all | bytes 131072 | tf_op jit(solution)/shard_map/all_to_all | solution.py:544
  164.3 14.4 %all_to_all.53 = bf16[8,128,128]{2,1,0:T(8,128)(2,1)S(1)} all-to-all(bf16[8,128,128]{2,1,0:T(8,128)(2,1)S(1)} %broadcast_in_dim.123), channel_id=1, replica_groups=mesh['y'=8,'z'=8,'c'=2,'x'=4] {'y'}, dimensions={0} | all-to-all | bytes 524288 | tf_op jit(solution)/shard_map/all_to_all | solution.py:544
  178.8 5.1 %all_to_all.54 = bf16[2,128,128]{2,1,0:T(8,128)(2,1)S(1)} all-to-all(bf16[2,128,128]{2,1,0:T(8,128)(2,1)S(1)} %broadcast_in_dim.124), channel_id=1, replica_groups=mesh['y'=8,'z'=8,'c'=2,'x'=4] {'c'}, dimensions={0} | all-to-all | bytes 131072 | tf_op jit(solution)/shard_map/all_to_all | solution.py:544
  183.9 2.9 %shard_map.92 = bf16[128,128]{1,0:T(8,128)(2,1)S(1)} custom-call(s32[2]{0:T(128)S(1)} %pad_add_fusion.count, s32[128]{0:T(128)S(1)} %get-tuple-element.23.row_at, s32[1,128]{1,0:T(1,128)S(1)} %get-tuple-element.27.col_place, bf16[256,128]{1,0:T(8,128)(2,1)S(1)} %bitcast.23, bf16[128,256,128]{2,1,0:T(8,128)(2,1)} %get-tuple-element.17.kernel), custom_call_target="tpu_custom_call" | custom-call | tf_op jit(solution)/shard_map/pallas_call | solution.py:456
  186.8 7.4 %all_to_all.55 = bf16[4,128,128]{2,1,0:T(8,128)(2,1)S(1)} all-to-all(bf16[4,128,128]{2,1,0:T(8,128)(2,1)S(1)} %broadcast_in_dim.125), channel_id=1, replica_groups=mesh['y'=8,'z'=8,'c'=2,'x'=4] {'x'}, dimensions={0} | all-to-all | bytes 262144 | tf_op jit(solution)/shard_map/all_to_all | solution.py:544
  194.3 11.6 %all_to_all.56.received = bf16[8,128,128]{2,1,0:T(8,128)(2,1)S(1)} all-to-all(bf16[8,128,128]{2,1,0:T(8,128)(2,1)S(1)} %broadcast_in_dim.126), channel_id=1, replica_groups=mesh['y'=8,'z'=8,'c'=2,'x'=4] {'z'}, dimensions={0} | all-to-all | bytes 524288 | tf_op jit(solution)/shard_map/all_to_all | solution.py:544
  205.9 4.0 %shard_map.93 = (f32[16,32,128]{2,1,0:T(8,128)S(1)}, f32[16,128]{1,0:T(8,128)}) custom-call(s32[2]{0:T(128)S(1)} %pad_add_fusion.count, s32[128]{0:T(128)S(1)} %fusion.7.col_at, s32[1,128]{1,0:T(1,128)S(1)} %get-tuple-element.28.row_place, bf16[8,128,128]{2,1,0:T(8,128)(2,1)S(1)} %all_to_all.56.received, f32[128,128]{1,0:T(8,128)S(1)} %get-tuple-element.18.column_sum, ...), custom_call_target="tpu_custom_call" | custom-call | tf_op jit(solution)/shard_map/pallas_call | solution.py:509
  210.0 18.3 %all_to_all.57 = f32[16,32,128]{2,1,0:T(8,128)S(1)} all-to-all(f32[16,32,128]{2,1,0:T(8,128)S(1)} %get-tuple-element.19), channel_id=1, replica_groups=mesh['y'=8,'z'=8,'c'=2,'x'=4] {'y','c'}, dimensions={0} | all-to-all | bytes 524288 | tf_op jit(solution)/shard_map/all_to_all | solution.py:544
  228.3 0.6 multiply_bitcast_fusion
  (56 shorter events, 2.0 us)
Async XLA Ops:
  7.2 30.2 %copy-start = (s32[2048]{0:T(1024)S(1)}, s32[2048]{0:T(1024)}, u32[]{:S(2)}) copy-start(s32[2048]{0:T(1024)} %param.9) | copy-start | bytes 24580
  7.2 114.1 %all-gather.3.cloned.1.call-start = ((), (), s32[]{:S(2)}) async-start(), calls=%async_computation.10 | async-start | bytes 17825792 | tf_op jit(solution)/shard_map/all_gather | solution.py:586
  13.4 42.6 %collective-permute-start.3 = (bf16[1040,256]{1,0:T(8,128)(2,1)}, bf16[1040,256]{1,0:T(8,128)(2,1)S(1)}, u32[]{:S(2)}, u32[]{:S(2)}) collective-permute-start(bf16[1040,256]{1,0:T(8,128)(2,1)} %shard_map.86.rest_1_), channel_id=1, source_target_pairs={{0,56},{8,0},{16,8},{24,16},{32,24},{40,32},{48,40},{56,48},{1,57}... | collective-permute-start | bytes 1597448 | tf_op jit(solution)/shard_map/ppermute | solution.py:537
  24.9 37.7 %collective-permute-start = (bf16[1040,256]{1,0:T(8,128)(2,1)}, bf16[1040,256]{1,0:T(8,128)(2,1)S(1)}, u32[]{:S(2)}, u32[]{:S(2)}) collective-permute-start(bf16[1040,256]{1,0:T(8,128)(2,1)} %shard_map.86.rest_1_), channel_id=1, source_target_pairs={{0,8},{8,16},{16,24},{24,32},{32,40},{40,48},{48,56},{56,0},{1,9},... | collective-permute-start | bytes 1597448 | tf_op jit(solution)/shard_map/ppermute | solution.py:536
  30.0 29.7 %collective-permute-start.8 = (bf16[1040,256]{1,0:T(8,128)(2,1)}, bf16[1040,256]{1,0:T(8,128)(2,1)S(1)}, u32[]{:S(2)}, u32[]{:S(2)}) collective-permute-start(bf16[1040,256]{1,0:T(8,128)(2,1)} %shard_map.89.rest_0_), channel_id=1, source_target_pairs={{0,8},{8,16},{16,24},{24,32},{32,40},{40,48},{48,56},{56,0},{1,9},... | collective-permute-start | bytes 1597448 | tf_op jit(solution)/shard_map/ppermute | solution.py:536
  31.9 32.6 %collective-permute-start.2 = (bf16[1040,256]{1,0:T(8,128)(2,1)}, bf16[1040,256]{1,0:T(8,128)(2,1)S(1)}, u32[]{:S(2)}, u32[]{:S(2)}) collective-permute-start(bf16[1040,256]{1,0:T(8,128)(2,1)} %shard_map.89.rest_0_), channel_id=1, source_target_pairs={{0,56},{8,0},{16,8},{24,16},{32,24},{40,32},{48,40},{56,48},{1,57}... | collective-permute-start | bytes 1597448 | tf_op jit(solution)/shard_map/ppermute | solution.py:537
  40.4 15.6 %all-to-all-start = ((s32[16,1,8]{2,1,0:T(1,128)}), s32[16,1,8]{2,1,0:T(1,128)S(1)}, u32[]{:S(2)}, u32[]{:S(2)}) async-start(s32[16,1,8]{2,1,0:T(1,128)} %bitcast.3), calls=%async_computation | async-start | bytes 16384 | tf_op jit(solution)/shard_map/all_to_all | solution.py:544
  56.1 65.2 %copy-start.3 = (bf16[1040,256]{1,0:T(8,128)(2,1)}, bf16[1040,256]{1,0:T(8,128)(2,1)S(1)}, u32[]{:S(2)}) copy-start(bf16[1040,256]{1,0:T(8,128)(2,1)S(1)} %collective-permute-done.3.rest_3_) | copy-start | bytes 1597444
  56.1 15.0 %collective-permute-start.5 = (bf16[1040,256]{1,0:T(8,128)(2,1)S(1)}, bf16[1040,256]{1,0:T(8,128)(2,1)}, u32[]{:S(2)}, u32[]{:S(2)}) collective-permute-start(bf16[1040,256]{1,0:T(8,128)(2,1)S(1)} %collective-permute-done.3.rest_3_), channel_id=1, source_target_pairs={{0,56},{8,0},{16,8},{24,16},{32,24},{40,32},{48,40},{56,48},{1,57}... | collective-permute-start | bytes 1597448 | tf_op jit(solution)/shard_map/ppermute | solution.py:537
  59.7 61.6 %copy-start.5 = (bf16[1040,256]{1,0:T(8,128)(2,1)}, bf16[1040,256]{1,0:T(8,128)(2,1)S(1)}, u32[]{:S(2)}) copy-start(bf16[1040,256]{1,0:T(8,128)(2,1)S(1)} %collective-permute-done.8.rest_14_) | copy-start | bytes 1597444
  59.7 16.2 %collective-permute-start.9 = (bf16[1040,256]{1,0:T(8,128)(2,1)S(1)}, bf16[1040,256]{1,0:T(8,128)(2,1)}, u32[]{:S(2)}, u32[]{:S(2)}) collective-permute-start(bf16[1040,256]{1,0:T(8,128)(2,1)S(1)} %collective-permute-done.8.rest_14_), channel_id=1, source_target_pairs={{0,8},{8,16},{16,24},{24,32},{32,40},{40,48},{48,56},{56,0},{1,9},... | collective-permute-start | bytes 1597448 | tf_op jit(solution)/shard_map/ppermute | solution.py:536
  62.6 58.7 %copy-start.4 = (bf16[1040,256]{1,0:T(8,128)(2,1)}, bf16[1040,256]{1,0:T(8,128)(2,1)S(1)}, u32[]{:S(2)}) copy-start(bf16[1040,256]{1,0:T(8,128)(2,1)S(1)} %collective-permute-done.rest_15_) | copy-start | bytes 1597444
  62.6 24.5 %collective-permute-start.1 = (bf16[1040,256]{1,0:T(8,128)(2,1)S(1)}, bf16[1040,256]{1,0:T(8,128)(2,1)S(1)}, u32[]{:S(2)}, u32[]{:S(2)}) collective-permute-start(bf16[1040,256]{1,0:T(8,128)(2,1)S(1)} %collective-permute-done.rest_15_), channel_id=1, source_target_pairs={{0,8},{8,16},{16,24},{24,32},{32,40},{40,48},{48,56},{56,0},{1,9},... | collective-permute-start | bytes 1597448 | tf_op jit(solution)/shard_map/ppermute | solution.py:536
  64.6 47.0 %copy-start.6 = (bf16[1040,256]{1,0:T(8,128)(2,1)}, bf16[1040,256]{1,0:T(8,128)(2,1)S(1)}, u32[]{:S(2)}) copy-start(bf16[1040,256]{1,0:T(8,128)(2,1)S(1)} %collective-permute-done.2.rest_2_) | copy-start | bytes 1597444
  64.6 24.4 %collective-permute-start.4 = (bf16[1040,256]{1,0:T(8,128)(2,1)S(1)}, bf16[1040,256]{1,0:T(8,128)(2,1)}, u32[]{:S(2)}, u32[]{:S(2)}) collective-permute-start(bf16[1040,256]{1,0:T(8,128)(2,1)S(1)} %collective-permute-done.2.rest_2_), channel_id=1, source_target_pairs={{0,56},{8,0},{16,8},{24,16},{32,24},{40,32},{48,40},{56,48},{1,57}... | collective-permute-start | bytes 1597448 | tf_op jit(solution)/shard_map/ppermute | solution.py:537
  71.1 22.8 %collective-permute-start.7 = (bf16[1040,256]{1,0:T(8,128)(2,1)}, bf16[1040,256]{1,0:T(8,128)(2,1)}, u32[]{:S(2)}, u32[]{:S(2)}) collective-permute-start(bf16[1040,256]{1,0:T(8,128)(2,1)} %collective-permute-done.5.rest_5_), channel_id=1, source_target_pairs={{0,56},{8,0},{16,8},{24,16},{32,24},{40,32},{48,40},{56,48},{1,57}... | collective-permute-start | bytes 1597448 | tf_op jit(solution)/shard_map/ppermute | solution.py:537
  76.0 22.8 %collective-permute-start.10 = (bf16[1040,256]{1,0:T(8,128)(2,1)}, bf16[1040,256]{1,0:T(8,128)(2,1)}, u32[]{:S(2)}, u32[]{:S(2)}) collective-permute-start(bf16[1040,256]{1,0:T(8,128)(2,1)} %collective-permute-done.9.rest_12_), channel_id=1, source_target_pairs={{0,8},{8,16},{16,24},{24,32},{32,40},{40,48},{48,56},{56,0},{1,9},... | collective-permute-start | bytes 1597448 | tf_op jit(solution)/shard_map/ppermute | solution.py:536
  87.1 34.2 %copy-start.2 = (bf16[1040,256]{1,0:T(8,128)(2,1)}, bf16[1040,256]{1,0:T(8,128)(2,1)S(1)}, u32[]{:S(2)}) copy-start(bf16[1040,256]{1,0:T(8,128)(2,1)S(1)} %collective-permute-done.1.after.rest_13_) | copy-start | bytes 1597444
  87.1 31.8 %collective-permute-start.13 = (bf16[1040,256]{1,0:T(8,128)(2,1)S(1)}, bf16[1040,256]{1,0:T(8,128)(2,1)}, u32[]{:S(2)}, u32[]{:S(2)}) collective-permute-start(bf16[1040,256]{1,0:T(8,128)(2,1)S(1)} %collective-permute-done.1.after.rest_13_), channel_id=1, source_target_pairs={{0,8},{8,16},{16,24},{24,32},{32,40},{40,48},{48,56},{56,0},{1,9},... | collective-permute-start | bytes 1597448 | tf_op jit(solution)/shard_map/ppermute | solution.py:536
  89.0 29.9 %collective-permute-start.6 = (bf16[1040,256]{1,0:T(8,128)(2,1)}, bf16[1040,256]{1,0:T(8,128)(2,1)}, u32[]{:S(2)}, u32[]{:S(2)}) collective-permute-start(bf16[1040,256]{1,0:T(8,128)(2,1)} %collective-permute-done.4.rest_4_), channel_id=1, source_target_pairs={{0,56},{8,0},{16,8},{24,16},{32,24},{40,32},{48,40},{56,48},{1,57}... | collective-permute-start | bytes 1597448 | tf_op jit(solution)/shard_map/ppermute | solution.py:537
  93.9 25.0 %collective-permute-start.12 = (bf16[1040,256]{1,0:T(8,128)(2,1)}, bf16[1040,256]{1,0:T(8,128)(2,1)}, u32[]{:S(2)}, u32[]{:S(2)}) collective-permute-start(bf16[1040,256]{1,0:T(8,128)(2,1)} %collective-permute-done.7.rest_7_), channel_id=1, source_target_pairs={{0,56},{8,0},{16,8},{24,16},{32,24},{40,32},{48,40},{56,48},{1,57}... | collective-permute-start | bytes 1597448 | tf_op jit(solution)/shard_map/ppermute | solution.py:537
  98.8 22.5 %collective-permute-start.11 = (bf16[1040,256]{1,0:T(8,128)(2,1)}, bf16[1040,256]{1,0:T(8,128)(2,1)}, u32[]{:S(2)}, u32[]{:S(2)}) collective-permute-start(bf16[1040,256]{1,0:T(8,128)(2,1)} %collective-permute-done.10.rest_10_), channel_id=1, source_target_pairs={{0,8},{8,16},{16,24},{24,32},{32,40},{40,48},{48,56},{56,0},{1,9},... | collective-permute-start | bytes 1597448 | tf_op jit(solution)/shard_map/ppermute | solution.py:536
  100.7 1.2 copy-start.1
  103.3 15.4 %all-to-all-start.1 = ((f32[16,16,128]{2,1,0:T(8,128)}), f32[16,16,128]{2,1,0:T(8,128)S(1)}, u32[]{:S(2)}, u32[]{:S(2)}) async-start(f32[16,16,128]{2,1,0:T(8,128)} %broadcast_in_dim.120), calls=%async_computation.1 | async-start | bytes 262144 | tf_op jit(solution)/shard_map/all_to_all | solution.py:544
Sparse Core Ops, SparseCore 0:
  10.4 103.8 all-gather.2
